TPU v7x, 32 devices: a whole 2x2x4 slice. The times are simulated.
32 devices in a mesh: grp: 2 (over y), dp: 4 (over x, core), slab: 4 (over z).
Axes of the slice: x: 2, y: 2, z: 4, core: 2. Of those that a mesh axis runs over, the one named last changes fastest.
Arguments:
- feats: bfloat16 [8, 32, 32, 128, 128], P(('grp', 'dp'), None, 'slab'), parts along dimension 0, may hold values from -6 to 6
- grains: int32 [8, 32, 128, 128], P(('grp', 'dp'), 'slab'), parts along dimension 0, may hold values from 0 to 4095
- spec_weight: bfloat16 [256, 16, 2048], P('slab'), may hold values from -0.75 to 0.75
- taps: float32 [27, 32], replicated, may hold values from -1.25 to 1.25
- point_weight: bfloat16 [32, 32], replicated, may hold values from -1 to 1
- bias: float32 [32], replicated, may hold values from -4 to 4
- cotangent: bfloat16 [8, 32, 32, 128, 128], P(('grp', 'dp'), None, 'slab'), parts along dimension 0, may hold values from -3 to 3
Outputs:
- grad_feats: bfloat16 [8, 32, 32, 128, 128], P(('grp', 'dp'), None, 'slab'), parts along dimension 0
- grad_spec: float32 [256, 32, 2048], P('slab', 'grp', 'dp'), parts along dimension 1
There are 2 independent parts, one for each index of `grp`. A program takes and returns all parts, laid end to end along the dimension named above; an argument that names none is the same for every part. Nothing has to cross between parts.
All inputs are finite; a program needn't handle non-finite values.
Results may differ from a plain program's by a relative error of at most 0.017.
Values may be sent and summed in bfloat16 or wider, within the bound.
No kernel may reach another device: no remote copies, remote signals or barrier semaphores. Data moves between devices by JAX's collectives and lax.ppermute only.
A program may use at most 192 MiB of HBM per device.

v0:
```python
import math

import jax
import jax.numpy as jnp
from jax import lax
from jax.sharding import PartitionSpec as P

NX = 128
NY = 128
NZ = 32
KX = 16
KY = 16
KZ = 16


HIGHEST = lax.Precision.HIGHEST


def extended(shard, sides, width):
    for axis, dim in sides:
        size, length = (lax.axis_size(axis), shard.shape[dim])
        up = [(i, (i + 1) % size) for i in range(size - 1)]
        down = [(j, i) for i, j in up]
        last = lax.slice_in_dim(shard, length - width, length, axis=dim)
        first = lax.slice_in_dim(shard, 0, width, axis=dim)
        before = lax.ppermute(last, axis, up)
        after = lax.ppermute(first, axis, down)
        shard = jnp.concatenate([before, shard, after], axis=dim)
    return shard


def tables(count, length, span):
    indices = jnp.arange(count, dtype=jnp.int32)
    frequency = jnp.where(indices < count // 2, indices, length - count + indices)
    position = jnp.arange(span, dtype=jnp.int32)
    phases = frequency[:, None] * position[None, :] % length
    angles = phases.astype(jnp.float32) * (2.0 * math.pi / length)
    return (jnp.cos(angles), jnp.sin(angles))


def mobility(grains):
    leading = [(0, 0)] * (grains.ndim - 2)
    along_x = (grains[..., 1:, :] != grains[..., :-1, :]).astype(jnp.float32)
    along_y = (grains[..., :, 1:] != grains[..., :, :-1]).astype(jnp.float32)
    differ = jnp.pad(along_x, leading + [(1, 0), (0, 0)]) + jnp.pad(
        along_x, leading + [(0, 1), (0, 0)]
    )
    differ = (
        differ
        + jnp.pad(along_y, leading + [(0, 0), (1, 0)])
        + jnp.pad(along_y, leading + [(0, 0), (0, 1)])
    )
    return 0.25 * (1.0 + differ)


def stencil(padded, taps, adjoint):
    planes = padded.shape[-3] - 2
    rows_x = padded.shape[-2] - 2
    rows_y = padded.shape[-1] - 2
    total = jnp.zeros(padded.shape[:-3] + (planes, rows_x, rows_y), jnp.float32)
    for offset in range(27):
        shift_z, shift_x, shift_y = (offset // 9, offset // 3 % 3, offset % 3)
        if adjoint:
            shift_z, shift_x, shift_y = (2 - shift_z, 2 - shift_x, 2 - shift_y)
        window = padded[
            ..., shift_z : shift_z + planes, shift_x : shift_x + rows_x, shift_y : shift_y + rows_y
        ]
        total = total + taps[offset][:, None, None, None] * window.astype(jnp.float32)
    return total


def plane_forward(field, cos_x, sin_x, cos_y, sin_y):
    real_y = jnp.einsum("...xy,ky->...xk", field, cos_y, precision=HIGHEST)
    imag_y = -jnp.einsum("...xy,ky->...xk", field, sin_y, precision=HIGHEST)
    real_part = jnp.einsum("...xk,jx->...jk", real_y, cos_x, precision=HIGHEST) + jnp.einsum(
        "...xk,jx->...jk", imag_y, sin_x, precision=HIGHEST
    )
    imag_part = jnp.einsum("...xk,jx->...jk", imag_y, cos_x, precision=HIGHEST) - jnp.einsum(
        "...xk,jx->...jk", real_y, sin_x, precision=HIGHEST
    )
    return (real_part, imag_part)


def plane_inverse(real_part, imag_part, cos_x, sin_x, cos_y, sin_y):
    real_x = jnp.einsum("...jk,jx->...xk", real_part, cos_x, precision=HIGHEST) - jnp.einsum(
        "...jk,jx->...xk", imag_part, sin_x, precision=HIGHEST
    )
    imag_x = jnp.einsum("...jk,jx->...xk", imag_part, cos_x, precision=HIGHEST) + jnp.einsum(
        "...jk,jx->...xk", real_part, sin_x, precision=HIGHEST
    )
    return jnp.einsum("...xk,ky->...xy", real_x, cos_y, precision=HIGHEST) - jnp.einsum(
        "...xk,ky->...xy", imag_x, sin_y, precision=HIGHEST
    )


def depth_forward(packed, cos_table, sin_table):
    width = packed.shape[-1] // 2
    real_in = packed[..., :width]
    imag_in = packed[..., width:]
    real_out = jnp.einsum("pszc,kz->pskc", real_in, cos_table, precision=HIGHEST) + jnp.einsum(
        "pszc,kz->pskc", imag_in, sin_table, precision=HIGHEST
    )
    imag_out = jnp.einsum("pszc,kz->pskc", imag_in, cos_table, precision=HIGHEST) - jnp.einsum(
        "pszc,kz->pskc", real_in, sin_table, precision=HIGHEST
    )
    return jnp.concatenate([real_out, imag_out], axis=-1)


def depth_inverse(real_modes, imag_modes, cos_table, sin_table):
    real_out = jnp.einsum("pskc,kz->pszc", real_modes, cos_table, precision=HIGHEST) - jnp.einsum(
        "pskc,kz->pszc", imag_modes, sin_table, precision=HIGHEST
    )
    imag_out = jnp.einsum("pskc,kz->pszc", imag_modes, cos_table, precision=HIGHEST) + jnp.einsum(
        "pskc,kz->pszc", real_modes, sin_table, precision=HIGHEST
    )
    return jnp.concatenate([real_out, imag_out], axis=-1)


def rim_planes(field):
    return extended(field, (("slab", 2),), 1)


def local(feats, grains, spec_weight, taps, point_weight, bias, cotangent):
    samples_here = feats.shape[0]
    channels = feats.shape[1]
    planes = feats.shape[2]
    cos_x, sin_x = tables(KX, NX, NX)
    cos_y, sin_y = tables(KY, NY, NY)
    cos_full, sin_full = tables(KZ, NZ, NZ)
    cell_scale = math.sqrt(NX * NY * NZ)
    mode_scale = math.sqrt(KX * KY * KZ)
    mode_rows = spec_weight.shape[0]
    weights = spec_weight.astype(jnp.float32).reshape(mode_rows, KZ, 2, channels, channels)
    w_real = weights[:, :, 0]
    w_imag = weights[:, :, 1]
    moving = mobility(grains)[:, None]

    def to_modes(field):
        real_plane, imag_plane = plane_forward(field, cos_x, sin_x, cos_y, sin_y)
        packed = jnp.stack([real_plane, imag_plane], axis=1)
        packed = packed.transpose(4, 5, 0, 3, 1, 2).reshape(
            KX * KY, samples_here, planes, 2 * channels
        )
        moved = lax.all_to_all(packed, "slab", split_axis=0, concat_axis=2, tiled=True)
        summed = depth_forward(moved, cos_full, sin_full)
        return (summed[..., :channels], summed[..., channels:])

    def from_modes(real_modes, imag_modes):
        planar = depth_inverse(real_modes, imag_modes, cos_full, sin_full)
        packed = lax.all_to_all(planar, "slab", split_axis=2, concat_axis=0, tiled=True)
        grouped = packed.reshape(KX, KY, samples_here, planes, 2, channels).transpose(
            2, 4, 5, 3, 0, 1
        )
        return plane_inverse(grouped[:, 0], grouped[:, 1], cos_x, sin_x, cos_y, sin_y)

    zero_rim = ((0, 0), (0, 0), (0, 0), (1, 1), (1, 1))
    padded = jnp.pad(rim_planes(feats), zero_rim)
    smooth = stencil(padded, taps, False).astype(jnp.bfloat16)
    local_part = moving * jnp.einsum(
        "sczxy,co->sozxy", smooth, point_weight, preferred_element_type=jnp.float32
    )
    spec_real, spec_imag = to_modes(feats.astype(jnp.float32))
    spec_real = spec_real / cell_scale
    spec_imag = spec_imag / cell_scale
    mixed_real = jnp.einsum("pskc,pkco->psko", spec_real, w_real, precision=HIGHEST) - jnp.einsum(
        "pskc,pkco->psko", spec_imag, w_imag, precision=HIGHEST
    )
    mixed_imag = jnp.einsum("pskc,pkco->psko", spec_real, w_imag, precision=HIGHEST) + jnp.einsum(
        "pskc,pkco->psko", spec_imag, w_real, precision=HIGHEST
    )
    spectral = from_modes(mixed_real, mixed_imag) / mode_scale
    pre = spectral + local_part + bias[None, :, None, None, None]
    gate = jax.nn.sigmoid(pre)
    delta = (cotangent.astype(jnp.float32) * gate * (1.0 + pre * (1.0 - gate))).astype(jnp.bfloat16)
    dual_real, dual_imag = to_modes(delta.astype(jnp.float32))
    dual_real = dual_real / mode_scale
    dual_imag = dual_imag / mode_scale
    batch_total = samples_here * lax.axis_size("dp")
    grad_real = jnp.einsum("pskc,psko->pkco", spec_real, dual_real, precision=HIGHEST) + jnp.einsum(
        "pskc,psko->pkco", spec_imag, dual_imag, precision=HIGHEST
    )
    grad_imag = jnp.einsum("pskc,psko->pkco", spec_real, dual_imag, precision=HIGHEST) - jnp.einsum(
        "pskc,psko->pkco", spec_imag, dual_real, precision=HIGHEST
    )
    grad_terms = (jnp.stack([grad_real, grad_imag], axis=2) / batch_total).reshape(
        mode_rows, KZ, 2 * channels * channels
    )
    grad_spec = lax.psum_scatter(
        grad_terms.astype(jnp.bfloat16), "dp", scatter_dimension=2, tiled=True
    ).astype(jnp.float32)
    back_real = jnp.einsum("psko,pkco->pskc", dual_real, w_real, precision=HIGHEST) + jnp.einsum(
        "psko,pkco->pskc", dual_imag, w_imag, precision=HIGHEST
    )
    back_imag = jnp.einsum("psko,pkco->pskc", dual_imag, w_real, precision=HIGHEST) - jnp.einsum(
        "psko,pkco->pskc", dual_real, w_imag, precision=HIGHEST
    )
    spectral_back = from_modes(back_real, back_imag) / cell_scale
    spread = (
        moving
        * jnp.einsum("sozxy,co->sczxy", delta, point_weight, preferred_element_type=jnp.float32)
    ).astype(jnp.bfloat16)
    spread_padded = jnp.pad(rim_planes(spread), zero_rim)
    local_back = stencil(spread_padded, taps, True)
    grad_feats = (spectral_back + local_back).astype(jnp.bfloat16)
    return (grad_feats, grad_spec)


def solution(mesh):
    in_specs = (
        P(("grp", "dp"), None, "slab", None, None),
        P(("grp", "dp"), "slab", None, None),
        P("slab", None, None),
        P(),
        P(),
        P(),
        P(("grp", "dp"), None, "slab", None, None),
    )
    out_specs = (P(("grp", "dp"), None, "slab", None, None), P("slab", "grp", "dp"))
    return jax.shard_map(local, mesh=mesh, in_specs=in_specs, out_specs=out_specs, check_vma=False)
```

profile of v0, /device:TPU:0, one launch (start us, length us, event | category | flops | bytes accessed | tf_op | source)
XLA Modules:
  0.0 829.7 jit_solution(2616619679292924234)
XLA Ops:
  7.2 3.3 fusion.382
  11.9 6.6 collective-permute-start
  18.5 9.4 %negate_bitcast_fusion = f32[32,8,128,16]{2,3,1,0:T(8,128)S(1)} fusion(bf16[1,32,8,128,128]{4,3,2,1,0:T(8,128)(2,1)} %param.7, s32[16]{0:T(128)S(1)} %compare_select_fusion.1), kind=kOutput, calls=%fused_computation.86 | convolution fusion | flops 805859328 | bytes 10485824 | tf_op jit(solution)/shard_map/...xy,ky->...xk/dot_general | solution.py:74
  27.9 6.8 fusion.67
  34.6 8.4 %fusion.58 = f32[16,32,8,16]{1,0,3,2:T(8,128)S(1)} fusion(f32[32,8,128,16]{2,3,1,0:T(8,128)S(1)} %negate_bitcast_fusion, s32[16]{0:T(128)S(1)} %compare_select_fusion.1), kind=kOutput, calls=%fused_computation.95 | convolution fusion | flops 100691968 | bytes 2359360 | tf_op jit(solution)/shard_map/...xk,jx->...jk/dot_general | solution.py:78
  43.0 8.6 %fusion.60 = f32[16,32,8,16]{1,0,3,2:T(8,128)S(1)} fusion(f32[32,8,128,16]{2,3,1,0:T(8,128)S(1)} %negate_bitcast_fusion, s32[16]{0:T(128)S(1)} %compare_select_fusion.1), kind=kOutput, calls=%fused_computation.97 | convolution fusion | flops 100691968 | bytes 2359360 | tf_op jit(solution)/shard_map/...xk,jx->...jk/dot_general | solution.py:75
  51.6 8.4 %fusion.81 = f32[1,1,32,8,16,16]{2,4,5,3,1,0:T(8,128)S(1)} fusion(f32[16,32,8,16]{1,0,3,2:T(8,128)S(1)} %fusion.58, f32[32,8,128,16]{2,3,1,0:T(8,128)S(1)} %fusion.67, s32[16]{0:T(128)S(1)} %compare_select_fusion.1), kind=kOutput, calls=%fused_computation.109 | convolution fusion | flops 100757504 | bytes 2621504 | tf_op jit(solution)/shard_map/...xk,jx->...jk/dot_general | solution.py:78
  59.9 8.4 %fusion.75 = f32[1,1,32,8,16,16]{2,4,5,3,1,0:T(8,128)S(1)} fusion(f32[16,32,8,16]{1,0,3,2:T(8,128)S(1)} %fusion.60, f32[32,8,128,16]{2,3,1,0:T(8,128)S(1)} %fusion.67, s32[16]{0:T(128)S(1)} %compare_select_fusion.1), kind=kOutput, calls=%fused_computation.107 | convolution fusion | flops 100757504 | bytes 2621504 | tf_op jit(solution)/shard_map/...xk,jx->...jk/dot_general | solution.py:75
  72.3 3.1 reshape.403
  75.4 4.3 all-to-all-start
  79.9 9.2 %copy.73 = bf16[64,16,2048]{0,2,1:T(8,128)(2,1)} copy(bf16[64,16,2048]{2,1,0:T(8,128)(2,1)} %param.9) | data formatting | bytes 8388608 | tf_op args[2]
  90.5 3.1 all-to-all-done
  100.2 6.4 fusion.23
  112.6 3.5 all-to-all-start.1
  116.1 23.1 %select_maximum_fusion.2 = bf16[1,32,10,130,130]{4,3,2,1,0:T(8,128)(2,1)} fusion(bf16[1,32,1,128,128]{4,3,2,1,0:T(8,128)(2,1)} %collective-permute-done.1, bf16[1,32,8,128,128]{4,3,2,1,0:T(8,128)(2,1)} %param.7, bf16[1,32,1,128,128]{4,3,2,1,0:T(8,128)(2,1)} %collective-permute-done), kind=kLoop, calls=%fused_computation.9 | loop fusion | flops 102752000 | bytes 21301760 | tf_op jit(solution)/shard_map/concatenate | solution.py:28
  139.5 183.3 %fusion.39 = bf16[32,8,128,128]{3,2,1,0:T(8,128)(2,1)} fusion(bf16[1,32,10,130,130]{4,3,2,1,0:T(8,128)(2,1)} %select_maximum_fusion.2, f32[32]{0:T(128)S(1)} %get-tuple-element.49, f32[32]{0:T(128)S(1)} %get-tuple-element.50, f32[32]{0:T(128)S(1)} %get-tuple-element.25, f32[32]{0:T(128)S(1)} %get-tuple-element.26, ...), kind=kLoop, calls=%fused_computation.69 | loop fusion | flops 348127232 | bytes 220204416 | tf_op jit(solution)/shard_map/reshape.89
  322.8 14.3 %fusion.37 = f32[8,128,128,32]{2,3,1,0:T(8,128)} fusion(bf16[32,8,128,128]{3,2,1,0:T(8,128)(2,1)} %fusion.39, bf16[32,32]{1,0:T(8,128)(2,1)S(1)} %copy-done), kind=kOutput, calls=%fused_computation.65 | convolution fusion | flops 268435456 | bytes 25167872 | tf_op jit(solution)/shard_map/sczxy,co->sozxy/dot_general | solution.py:159
  337.1 2.2 reduce.17
  342.6 3.7 fusion.108
  346.3 3.5 fusion.109
  349.8 3.5 subtract_bitcast_fusion.2
  353.3 29.0 %fusion.48 = f32[32,8,128,128]{3,2,1,0:T(8,128)} fusion(f32[32,8,128,16]{2,0,3,1:T(8,128)S(1)} %subtract_bitcast_fusion.2, s32[16]{0:T(128)S(1)} %compare_select_fusion.1), kind=kOutput, calls=%fused_computation.79 | convolution fusion | flops 805335040 | bytes 18874432 | tf_op jit(solution)/shard_map/...xk,ky->...xy/dot_general | solution.py:91
  382.4 3.5 add_bitcast_fusion.2
  386.0 44.4 %fusion.40 = bf16[32,8,128,128]{3,2,1,0:T(8,128)(2,1)S(1)} fusion(f32[32]{0:T(128)S(1)} %copy-done.68, f32[8,128,128,32]{2,3,1,0:T(8,128)} %fusion.37, f32[8,128,128]{2,1,0:T(8,128)S(1)} %copy-done.9, f32[32,8,128,128]{3,2,1,0:T(8,128)} %fusion.48, bf16[1,32,8,128,128]{4,3,2,1,0:T(8,128)(2,1)S(1)} %bitcast.461, ...), kind=kOutput, calls=%fused_computation.70 | convolution fusion | flops 868249600 | bytes 52953280 | tf_op jit(solution)/shard_map/...xk,ky->...xy/dot_general | solution.py:91
  430.4 6.8 convolution_negate_fusion
  437.3 6.8 fusion.155
  444.1 8.4 %fusion.50 = f32[16,32,8,16]{1,0,3,2:T(8,128)S(1)} fusion(f32[32,8,128,16]{2,3,1,0:T(8,128)S(1)} %convolution_negate_fusion, s32[16]{0:T(128)S(1)} %compare_select_fusion.1), kind=kOutput, calls=%fused_computation.87 | convolution fusion | flops 100691968 | bytes 2359360 | tf_op jit(solution)/shard_map/...xk,jx->...jk/dot_general | solution.py:78
  452.4 8.6 %fusion.52 = f32[16,32,8,16]{1,0,3,2:T(8,128)S(1)} fusion(f32[32,8,128,16]{2,3,1,0:T(8,128)S(1)} %convolution_negate_fusion, s32[16]{0:T(128)S(1)} %compare_select_fusion.1), kind=kOutput, calls=%fused_computation.89 | convolution fusion | flops 100691968 | bytes 2359360 | tf_op jit(solution)/shard_map/...xk,jx->...jk/dot_general | solution.py:75
  461.0 10.8 %fusion.35 = f32[8,128,128,32]{2,3,1,0:T(8,128)} fusion(bf16[32,8,128,128]{3,2,1,0:T(8,128)(2,1)S(1)} %fusion.40, bf16[32,32]{1,0:T(8,128)(2,1)S(1)} %copy-done), kind=kOutput, calls=%fused_computation.63 | convolution fusion | flops 268435456 | bytes 25167872 | tf_op jit(solution)/shard_map/sozxy,co->sczxy/dot_general | solution.py:200
  471.8 8.7 %fusion.93 = f32[1,1,32,8,16,16]{2,4,5,3,1,0:T(8,128)S(1)} fusion(f32[16,32,8,16]{1,0,3,2:T(8,128)S(1)} %fusion.50, f32[32,8,128,16]{2,3,1,0:T(8,128)S(1)} %fusion.155, s32[16]{0:T(128)S(1)} %compare_select_fusion.1), kind=kOutput, calls=%fused_computation.113 | convolution fusion | flops 100757504 | bytes 2621504 | tf_op jit(solution)/shard_map/...xk,jx->...jk/dot_general | solution.py:78
  480.6 8.4 %fusion.87 = f32[1,1,32,8,16,16]{2,4,5,3,1,0:T(8,128)S(1)} fusion(f32[16,32,8,16]{1,0,3,2:T(8,128)S(1)} %fusion.52, f32[32,8,128,16]{2,3,1,0:T(8,128)S(1)} %fusion.155, s32[16]{0:T(128)S(1)} %compare_select_fusion.1), kind=kOutput, calls=%fused_computation.111 | convolution fusion | flops 100757504 | bytes 2621504 | tf_op jit(solution)/shard_map/...xk,jx->...jk/dot_general | solution.py:75
  493.3 5.2 all-to-all-start.2
  498.6 15.2 %fusion.66 = bf16[1,32,8,128,128]{4,3,2,1,0:T(8,128)(2,1)S(1)} fusion(f32[8,128,128,32]{2,3,1,0:T(8,128)} %fusion.35, f32[8,128,128]{2,1,0:T(8,128)} %multiply_bitcast_fusion), kind=kLoop, calls=%fused_computation.103 | loop fusion | flops 8388608 | bytes 25690112 | tf_op jit(solution)/shard_map/convert_element_type | solution.py:201
  513.8 3.3 copy-done.3
  519.9 5.7 collective-permute-start.2
  531.5 10.0 %fusion.27 = (f32[64,16,32]{0,2,1:T(8,128)S(1)}, f32[64,16,32]{0,2,1:T(8,128)S(1)}, f32[64,16,32]{0,2,1:T(8,128)S(1)}, f32[64,16,32]{0,2,1:T(8,128)S(1)}) fusion(f32[64,16,32]{0,2,1:T(8,128)S(1)} %copy.156, bf16[64,16,2,32,32]{0,4,3,2,1:T(8,128)(2,1)} %bitcast.430, f32[64,16,32]{0,2,1:T(8,128)S(1)} %copy.157), kind=kLoop, calls=%fused_computation.51 | loop fusion | flops 10354688 | bytes 4980736
  547.6 4.2 all-to-all-start.3
  551.8 2.5 add_bitcast_fusion
  554.3 4.6 fusion.4
  558.9 23.5 %select_maximum_fusion = bf16[1,32,10,130,130]{4,3,2,1,0:T(8,128)(2,1)} fusion(bf16[1,32,1,128,128]{4,3,2,1,0:T(8,128)(2,1)} %collective-permute-done.3, bf16[1,32,8,128,128]{4,3,2,1,0:T(8,128)(2,1)} %copy-done.3, bf16[1,32,1,128,128]{4,3,2,1,0:T(8,128)(2,1)} %collective-permute-done.2), kind=kLoop, calls=%fused_computation.7 | loop fusion | flops 102752000 | bytes 21301760 | tf_op jit(solution)/shard_map/concatenate | solution.py:28
  582.4 2.2 reduce.19
  588.0 3.5 fusion.110
  591.5 3.5 fusion.111
  595.0 3.7 subtract_bitcast_fusion.1
  599.0 28.8 %fusion.45 = f32[32,8,128,128]{3,2,1,0:T(8,128)} fusion(f32[32,8,128,16]{2,0,3,1:T(8,128)S(1)} %subtract_bitcast_fusion.1, s32[16]{0:T(128)S(1)} %compare_select_fusion.1), kind=kOutput, calls=%fused_computation.75 | convolution fusion | flops 805335040 | bytes 18874432 | tf_op jit(solution)/shard_map/...xk,ky->...xy/dot_general | solution.py:91
  627.8 3.5 add_bitcast_fusion.1
  631.6 187.5 %fusion.22 = bf16[1,32,8,128,128]{4,3,2,1,0:T(8,128)(2,1)} fusion(f32[32,8,128,128]{3,2,1,0:T(8,128)} %fusion.45, bf16[1,32,10,130,130]{4,3,2,1,0:T(8,128)(2,1)} %select_maximum_fusion, bf16[1,32,8,128,128]{4,3,2,1,0:T(8,128)(2,1)} %copy-done.3, bf16[1,32,1,128,128]{4,3,2,1,0:T(8,128)(2,1)} %collective-permute-done.2, ...), kind=kOutput, calls=%fused_computation.38 | convolution fusion | flops 1174433792 | bytes 256380352 | tf_op jit(solution)/shard_map/...xk,ky->...xy/dot_general | solution.py:91
  819.1 3.5 copy.102
  (212 shorter events, 45.2 us)
Async XLA Ops:
  7.2 315.6 %copy-start = (bf16[32,32]{1,0:T(8,128)(2,1)S(1)}, bf16[32,32]{1,0:T(8,128)(2,1)}, u32[]{:S(2)}) copy-start(bf16[32,32]{1,0:T(8,128)(2,1)} %param.11) | copy-start | bytes 6148
  10.5 105.7 %collective-permute-start.1 = (bf16[1,32,1,128,128]{4,3,2,1,0:T(8,128)(2,1)}, bf16[1,32,1,128,128]{4,3,2,1,0:T(8,128)(2,1)}, u32[]{:S(2)}, u32[]{:S(2)}) collective-permute-start(bf16[1,32,1,128,128]{4,3,2,1,0:T(8,128)(2,1)} %get-tuple-element.21), channel_id=1, source_target_pairs={{1,0},{2,1},{3,2},{5,4},{6,5},{7,6},{9,8},{10,9},{11,10},{13,12},{... | collective-permute-start | bytes 3145736 | tf_op jit(solution)/shard_map/ppermute | solution.py:27
  11.9 104.3 %collective-permute-start = (bf16[1,32,1,128,128]{4,3,2,1,0:T(8,128)(2,1)}, bf16[1,32,1,128,128]{4,3,2,1,0:T(8,128)(2,1)}, u32[]{:S(2)}, u32[]{:S(2)}) collective-permute-start(bf16[1,32,1,128,128]{4,3,2,1,0:T(8,128)(2,1)} %get-tuple-element.20), channel_id=1, source_target_pairs={{0,1},{1,2},{2,3},{4,5},{5,6},{6,7},{8,9},{9,10},{10,11},{12,13},{... | collective-permute-start | bytes 3145736 | tf_op jit(solution)/shard_map/ppermute | solution.py:26
  34.6 45.1 %copy-start.4 = (s32[1,8,128,128]{3,2,1,0:T(8,128)S(1)}, s32[1,8,128,128]{3,2,1,0:T(8,128)}, u32[]{:S(2)}) copy-start(s32[1,8,128,128]{3,2,1,0:T(8,128)} %param.8) | copy-start | bytes 1572868
  75.4 18.2 %all-to-all-start = ((f32[4,1,32768]{2,1,0:T(1,128)}), f32[4,1,32768]{2,1,0:T(1,128)S(1)}, u32[]{:S(2)}, u32[]{:S(2)}) async-start(f32[4,1,32768]{2,1,0:T(1,128)} %reshape.403), calls=%async_computation | async-start | bytes 1048576 | tf_op jit(solution)/shard_map/all_to_all | solution.py:144
  90.2 49.0 %copy-start.14 = (f32[32]{0:T(128)}, f32[32]{0:T(128)S(1)}, u32[]{:S(2)}) copy-start(f32[32]{0:T(128)S(1)} %get-tuple-element.43) | copy-start | bytes 388
  90.2 49.0 %copy-start.16 = (f32[32]{0:T(128)}, f32[32]{0:T(128)S(1)}, u32[]{:S(2)}) copy-start(f32[32]{0:T(128)S(1)} %get-tuple-element.44) | copy-start | bytes 388
  90.3 49.0 %copy-start.18 = (f32[32]{0:T(128)}, f32[32]{0:T(128)S(1)}, u32[]{:S(2)}) copy-start(f32[32]{0:T(128)S(1)} %get-tuple-element.45) | copy-start | bytes 388
  90.3 49.0 %copy-start.20 = (f32[32]{0:T(128)}, f32[32]{0:T(128)S(1)}, u32[]{:S(2)}) copy-start(f32[32]{0:T(128)S(1)} %get-tuple-element.46) | copy-start | bytes 388
  90.3 49.0 %copy-start.22 = (f32[32]{0:T(128)}, f32[32]{0:T(128)S(1)}, u32[]{:S(2)}) copy-start(f32[32]{0:T(128)S(1)} %get-tuple-element.47) | copy-start | bytes 388
  90.3 49.0 %copy-start.24 = (f32[32]{0:T(128)}, f32[32]{0:T(128)S(1)}, u32[]{:S(2)}) copy-start(f32[32]{0:T(128)S(1)} %get-tuple-element.48) | copy-start | bytes 388
  90.3 49.0 %copy-start.26 = (f32[32]{0:T(128)}, f32[32]{0:T(128)S(1)}, u32[]{:S(2)}) copy-start(f32[32]{0:T(128)S(1)} %get-tuple-element.49) | copy-start | bytes 388
  90.3 49.0 %copy-start.28 = (f32[32]{0:T(128)}, f32[32]{0:T(128)S(1)}, u32[]{:S(2)}) copy-start(f32[32]{0:T(128)S(1)} %get-tuple-element.50) | copy-start | bytes 388
  90.3 48.9 %copy-start.30 = (f32[32]{0:T(128)}, f32[32]{0:T(128)S(1)}, u32[]{:S(2)}) copy-start(f32[32]{0:T(128)S(1)} %get-tuple-element.24) | copy-start | bytes 388
  90.3 48.9 %copy-start.32 = (f32[32]{0:T(128)}, f32[32]{0:T(128)S(1)}, u32[]{:S(2)}) copy-start(f32[32]{0:T(128)S(1)} %get-tuple-element.25) | copy-start | bytes 388
  90.4 48.9 %copy-start.34 = (f32[32]{0:T(128)}, f32[32]{0:T(128)S(1)}, u32[]{:S(2)}) copy-start(f32[32]{0:T(128)S(1)} %get-tuple-element.26) | copy-start | bytes 388
  90.4 48.9 %copy-start.36 = (f32[32]{0:T(128)}, f32[32]{0:T(128)S(1)}, u32[]{:S(2)}) copy-start(f32[32]{0:T(128)S(1)} %get-tuple-element.27) | copy-start | bytes 388
  90.4 48.9 %copy-start.38 = (f32[32]{0:T(128)}, f32[32]{0:T(128)S(1)}, u32[]{:S(2)}) copy-start(f32[32]{0:T(128)S(1)} %get-tuple-element.28) | copy-start | bytes 388
  90.4 48.9 %copy-start.40 = (f32[32]{0:T(128)}, f32[32]{0:T(128)S(1)}, u32[]{:S(2)}) copy-start(f32[32]{0:T(128)S(1)} %get-tuple-element.29) | copy-start | bytes 388
  90.4 48.9 %copy-start.42 = (f32[32]{0:T(128)}, f32[32]{0:T(128)S(1)}, u32[]{:S(2)}) copy-start(f32[32]{0:T(128)S(1)} %get-tuple-element.30) | copy-start | bytes 388
  90.4 48.9 %copy-start.44 = (f32[32]{0:T(128)}, f32[32]{0:T(128)S(1)}, u32[]{:S(2)}) copy-start(f32[32]{0:T(128)S(1)} %get-tuple-element.31) | copy-start | bytes 388
  90.4 48.9 %copy-start.46 = (f32[32]{0:T(128)}, f32[32]{0:T(128)S(1)}, u32[]{:S(2)}) copy-start(f32[32]{0:T(128)S(1)} %get-tuple-element.32) | copy-start | bytes 388
  90.4 48.9 %copy-start.48 = (f32[32]{0:T(128)}, f32[32]{0:T(128)S(1)}, u32[]{:S(2)}) copy-start(f32[32]{0:T(128)S(1)} %get-tuple-element.33) | copy-start | bytes 388
  90.4 48.9 %copy-start.50 = (f32[32]{0:T(128)}, f32[32]{0:T(128)S(1)}, u32[]{:S(2)}) copy-start(f32[32]{0:T(128)S(1)} %get-tuple-element.34) | copy-start | bytes 388
  90.4 48.9 %copy-start.52 = (f32[32]{0:T(128)}, f32[32]{0:T(128)S(1)}, u32[]{:S(2)}) copy-start(f32[32]{0:T(128)S(1)} %get-tuple-element.35) | copy-start | bytes 388
  90.5 48.9 %copy-start.54 = (f32[32]{0:T(128)}, f32[32]{0:T(128)S(1)}, u32[]{:S(2)}) copy-start(f32[32]{0:T(128)S(1)} %get-tuple-element.36) | copy-start | bytes 388
  90.5 48.9 %copy-start.56 = (f32[32]{0:T(128)}, f32[32]{0:T(128)S(1)}, u32[]{:S(2)}) copy-start(f32[32]{0:T(128)S(1)} %get-tuple-element.37) | copy-start | bytes 388
  90.5 48.9 %copy-start.58 = (f32[32]{0:T(128)}, f32[32]{0:T(128)S(1)}, u32[]{:S(2)}) copy-start(f32[32]{0:T(128)S(1)} %get-tuple-element.38) | copy-start | bytes 388
  90.5 48.9 %copy-start.60 = (f32[32]{0:T(128)}, f32[32]{0:T(128)S(1)}, u32[]{:S(2)}) copy-start(f32[32]{0:T(128)S(1)} %get-tuple-element.39) | copy-start | bytes 388
  90.5 48.9 %copy-start.62 = (f32[32]{0:T(128)}, f32[32]{0:T(128)S(1)}, u32[]{:S(2)}) copy-start(f32[32]{0:T(128)S(1)} %get-tuple-element.40) | copy-start | bytes 388
  90.5 48.9 %copy-start.64 = (f32[32]{0:T(128)}, f32[32]{0:T(128)S(1)}, u32[]{:S(2)}) copy-start(f32[32]{0:T(128)S(1)} %get-tuple-element.41) | copy-start | bytes 388
  90.5 48.9 %copy-start.66 = (f32[32]{0:T(128)}, f32[32]{0:T(128)S(1)}, u32[]{:S(2)}) copy-start(f32[32]{0:T(128)S(1)} %get-tuple-element.42) | copy-start | bytes 388
  112.6 224.4 %all-to-all-start.1 = ((f32[4,1,32768]{2,1,0:T(1,128)}), f32[4,1,32768]{2,1,0:T(1,128)S(1)}, u32[]{:S(2)}, u32[]{:S(2)}) async-start(f32[4,1,32768]{2,1,0:T(1,128)} %reshape.405), calls=%async_computation.1 | async-start | bytes 1048576 | tf_op jit(solution)/shard_map/all_to_all | solution.py:150
  349.8 36.1 %slice-start = ((s8[8388608]{0:T(1024)(128)(4,1)}), s8[4194304]{0:T(1024)(128)(4,1)S(1)}, s32[]{:S(2)}) async-start(s8[8388608]{0:T(1024)(128)(4,1)} %bitcast.460), calls=%async_computation.6 | async-start | bytes 8388608
  493.3 32.3 %all-to-all-start.2 = ((f32[4,1,32768]{2,1,0:T(1,128)}), f32[4,1,32768]{2,1,0:T(1,128)S(1)}, u32[]{:S(2)}, u32[]{:S(2)}) async-start(f32[4,1,32768]{2,1,0:T(1,128)} %reshape.407), calls=%async_computation.2 | async-start | bytes 1048576 | tf_op jit(solution)/shard_map/all_to_all | solution.py:144
  518.6 40.3 %collective-permute-start.3 = (bf16[1,32,1,128,128]{4,3,2,1,0:T(8,128)(2,1)}, bf16[1,32,1,128,128]{4,3,2,1,0:T(8,128)(2,1)}, u32[]{:S(2)}, u32[]{:S(2)}) collective-permute-start(bf16[1,32,1,128,128]{4,3,2,1,0:T(8,128)(2,1)} %get-tuple-element.19), channel_id=1, source_target_pairs={{1,0},{2,1},{3,2},{5,4},{6,5},{7,6},{9,8},{10,9},{11,10},{13,12},{... | collective-permute-start | bytes 3145736 | tf_op jit(solution)/shard_map/ppermute | solution.py:27
  519.9 39.0 %collective-permute-start.2 = (bf16[1,32,1,128,128]{4,3,2,1,0:T(8,128)(2,1)}, bf16[1,32,1,128,128]{4,3,2,1,0:T(8,128)(2,1)}, u32[]{:S(2)}, u32[]{:S(2)}) collective-permute-start(bf16[1,32,1,128,128]{4,3,2,1,0:T(8,128)(2,1)} %get-tuple-element.18), channel_id=1, source_target_pairs={{0,1},{1,2},{2,3},{4,5},{5,6},{6,7},{8,9},{9,10},{10,11},{12,13},{... | collective-permute-start | bytes 3145736 | tf_op jit(solution)/shard_map/ppermute | solution.py:26
  547.6 34.9 %all-to-all-start.3 = ((f32[4,1,32768]{2,1,0:T(1,128)}), f32[4,1,32768]{2,1,0:T(1,128)S(1)}, u32[]{:S(2)}, u32[]{:S(2)}) async-start(f32[4,1,32768]{2,1,0:T(1,128)} %reshape.409), calls=%async_computation.3 | async-start | bytes 1048576 | tf_op jit(solution)/shard_map/all_to_all | solution.py:150
  551.8 267.4 %reduce-scatter.2.cloned.1.call-start = ((), (), s32[]{:S(2)}) async-start(), calls=%async_computation.5 | async-start | bytes 10485760 | tf_op jit(solution)/shard_map/reduce_scatter | solution.py:188
  598.7 32.7 %copy-start.10 = (f32[8,128,128]{2,1,0:T(8,128)S(1)}, f32[8,128,128]{2,1,0:T(8,128)}, u32[]{:S(2)}) copy-start(f32[8,128,128]{2,1,0:T(8,128)} %multiply_bitcast_fusion) | copy-start | bytes 1572868
  598.7 32.7 %copy-start.15 = (f32[32]{0:T(128)S(1)}, f32[32]{0:T(128)}, u32[]{:S(2)}) copy-start(f32[32]{0:T(128)} %copy-done.14) | copy-start | bytes 388
  598.7 32.7 %copy-start.17 = (f32[32]{0:T(128)S(1)}, f32[32]{0:T(128)}, u32[]{:S(2)}) copy-start(f32[32]{0:T(128)} %copy-done.16) | copy-start | bytes 388
  598.7 32.7 %copy-start.19 = (f32[32]{0:T(128)S(1)}, f32[32]{0:T(128)}, u32[]{:S(2)}) copy-start(f32[32]{0:T(128)} %copy-done.18) | copy-start | bytes 388
  598.7 32.7 %copy-start.21 = (f32[32]{0:T(128)S(1)}, f32[32]{0:T(128)}, u32[]{:S(2)}) copy-start(f32[32]{0:T(128)} %copy-done.20) | copy-start | bytes 388
  598.7 32.7 %copy-start.23 = (f32[32]{0:T(128)S(1)}, f32[32]{0:T(128)}, u32[]{:S(2)}) copy-start(f32[32]{0:T(128)} %copy-done.22) | copy-start | bytes 388
  598.8 32.7 %copy-start.25 = (f32[32]{0:T(128)S(1)}, f32[32]{0:T(128)}, u32[]{:S(2)}) copy-start(f32[32]{0:T(128)} %copy-done.24) | copy-start | bytes 388
  598.8 32.7 %copy-start.27 = (f32[32]{0:T(128)S(1)}, f32[32]{0:T(128)}, u32[]{:S(2)}) copy-start(f32[32]{0:T(128)} %copy-done.26) | copy-start | bytes 388
  631.6 191.0 %copy-start.1 = (bf16[32,32]{1,0:T(8,128)(2,1)S(1)}, bf16[32,32]{1,0:T(8,128)(2,1)}, u32[]{:S(2)}) copy-start(bf16[32,32]{1,0:T(8,128)(2,1)} %param.11) | copy-start | bytes 6148
  (32 other events, 943.9 us)
Sparse Core Ops, SparseCore 0:
  559.0 73.1 reduce-scatter.1
where the time goes:
time: 833 us; the launch traced here: 830 us
  matrix products  452 us (54%)
  other arithmetic  279 us (33%)
  local copies, waits for them, and re-layouts  47.1 us (6%)
  starting transfers between devices  32.1 us (4%)
  between operations  15.8 us (2%)
    dot_general x2, matrix products, plane_inverse(): jnp.einsum('...xk,ky->...xy', imag_x, sin_y, precision=HIGHEST)  232 us
    another operation x1, other arithmetic  183 us
    dot_general x2, matrix products, plane_inverse(): jnp.einsum('...xk,ky->...xy', real_x, cos_y, precision=HIGHEST)  57.9 us
    concatenate x2, other arithmetic, extended(): shard = jnp.concatenate([before, shard, after], axis=dim)  46.6 us
    unnamed x156, local copies, waits for them, and re-layouts  26.3 us
    dot_general x2, matrix products, plane_forward(): jnp.einsum('...xk,jx->...jk', imag_y, sin_x, precision=HIGHEST)  17.1 us
    dot_general x2, matrix products, plane_forward(): jnp.einsum('...xk,jx->...jk', real_y, sin_x, precision=HIGHEST)  17.1 us
    dot_general x2, matrix products, plane_forward(): jnp.einsum('...xk,jx->...jk', imag_y, cos_x, precision=HIGHEST)  16.7 us
  transfers between devices with their start and end apart: 9, of which 1 were waited for; matrix products, arithmetic and copies ran while one was open for 74% of the time, Pallas kernels for 0%

commit v1 on v0

--- a/solution.py
+++ b/solution.py
@@ -1,8 +1,13 @@
+import functools
 import math
 
 import jax
 import jax.numpy as jnp
+import ml_dtypes
+import numpy as np
 from jax import lax
+from jax.experimental import pallas as pl
+from jax.experimental.pallas import tpu as pltpu
 from jax.sharding import PartitionSpec as P
 
 NX = 128
@@ -120,7 +125,7 @@
     return extended(field, (("slab", 2),), 1)
 
 
-def local(feats, grains, spec_weight, taps, point_weight, bias, cotangent):
+def local_any(feats, grains, spec_weight, taps, point_weight, bias, cotangent):
     samples_here = feats.shape[0]
     channels = feats.shape[1]
     planes = feats.shape[2]
@@ -205,6 +210,556 @@
     return (grad_feats, grad_spec)
 
 
+def frequencies(count, length):
+    index = np.arange(count)
+    return np.where(index < count // 2, index, length - count + index)
+
+
+def angles(count, length):
+    phases = np.outer(frequencies(count, length), np.arange(length)) % length
+    return phases * (2.0 * np.pi / length)
+
+
+def constant(array):
+    return jnp.asarray(np.asarray(array, np.float32).astype(ml_dtypes.bfloat16))
+
+
+def forward_x_table(slabs):
+    a = angles(KX, NX).reshape(slabs, KX // slabs, NX)
+    trig = np.stack([np.cos(a), np.sin(a)])
+    table = np.einsum("tsjx,cd->tscjdx", trig, np.eye(2))
+    return table.reshape(2 * slabs * 2 * (KX // slabs), 2 * NX)
+
+
+def forward_y_table(planes):
+    a = angles(KY, NY)
+    cos, sin = np.cos(a).T, np.sin(a).T
+    block = np.stack([np.stack([cos, -sin], 1), np.stack([-sin, -cos], 1)])
+    pick = np.eye(planes).reshape(planes // 2, 2, planes)
+    table = np.einsum("pqz,tyrk->pqtyzrk", pick, block)
+    return table.reshape(planes // 2, 4 * NY, planes * 2 * KY)
+
+
+def forward_z_table():
+    a = angles(KZ, NZ)
+    cos, sin = np.cos(a).T, np.sin(a).T
+    block = np.stack([np.stack([cos, -sin], 1), np.stack([sin, cos], 1)], 1)
+    table = np.einsum("zrqm,kl->zrkqlm", block, np.eye(KY))
+    return table.reshape(NZ * 2 * KY, 2 * KY * KZ)
+
+
+def inverse_z_table():
+    a = angles(KZ, NZ)
+    cos, sin = np.cos(a), np.sin(a)
+    block = np.stack([np.stack([cos, sin], 2), np.stack([-sin, cos], 2)])
+    table = np.einsum("rmzq,kl->rkmzql", block, np.eye(KY))
+    return table.reshape(2 * KY * KZ, NZ * 2 * KY)
+
+
+def inverse_y_table(planes):
+    a = angles(KY, NY)
+    cos, sin = np.cos(a), np.sin(a)
+    block = np.stack([np.stack([cos, -sin], 1), np.stack([-sin, -cos], 1)])
+    pick = np.eye(planes).reshape(planes // 2, 2, planes)
+    table = np.einsum("pqz,rkty->pzrktqy", pick, block)
+    return table.reshape(planes // 2, planes * 2 * KY, 4 * NY)
+
+
+def inverse_x_table(slabs):
+    a = angles(KX, NX).reshape(slabs, KX // slabs, NX)
+    trig = np.stack([np.cos(a), np.sin(a)])
+    table = np.einsum("tsjx,cd->cxstdj", trig, np.eye(8))
+    return table.reshape(8 * NX, 2 * KX * 8)
+
+
+def first_table(channels, depth):
+    table = np.einsum("ac,j,b->ajcb", np.eye(channels), np.ones(depth), np.ones(channels))
+    return table.reshape(channels * depth, channels * channels)
+
+
+def second_table(channels, depth):
+    table = np.einsum("ac,j,b->ajbc", np.eye(channels), np.ones(depth), np.ones(channels))
+    return table.reshape(channels * depth, channels * channels)
+
+
+def dot(a, b):
+    return jnp.dot(a, b, preferred_element_type=jnp.float32)
+
+
+def whole(shape):
+    return pl.BlockSpec(shape, lambda *_: (0,) * len(shape))
+
+
+def params(**kw):
+    return pltpu.CompilerParams(vmem_limit_bytes=48 * 2**20, **kw)
+
+
+def modes_step(load, x_table, y_table, rows, total, pair):
+    slabs = total.shape[0]
+    for i in range(rows.shape[3] // 8):
+        part = dot(x_table[...], load(i))
+        for t in range(2):
+            for s in range(slabs):
+                at = 8 * (t * slabs + s)
+                for q in range(2):
+                    rows[q, t, s, 8 * i : 8 * i + 8, :] = part[at : at + 8, q * NY : q * NY + NY]
+    for s in range(slabs):
+        left = [rows[q, t, s].astype(jnp.bfloat16) for q in range(2) for t in range(2)]
+        step = dot(jnp.concatenate(left, axis=1), y_table[0])
+        before = jnp.where(pair == 0, 0.0, total[s])
+        total[s] = before + step
+
+
+def forward_kernel(field, x_table, y_table, out, rows, total):
+    pair = pl.program_id(0)
+
+    def load(i):
+        halves = [field[2 * i : 2 * i + 2, q].reshape(2 * NX, NY) for q in range(2)]
+        return jnp.concatenate(halves, axis=1)
+
+    modes_step(load, x_table, y_table, rows, total, pair)
+
+    @pl.when(pair == pl.num_programs(0) - 1)
+    def _():
+        out[...] = total[...].astype(jnp.bfloat16)
+
+
+def forward_modes(field, slabs):
+    channels, planes = field.shape[:2]
+    lines = channels * (KX // slabs)
+    x_table = constant(forward_x_table(slabs))
+    y_table = constant(forward_y_table(planes))
+    shape = (slabs, lines, planes * 2 * KY)
+    return pl.pallas_call(
+        forward_kernel,
+        grid=(planes // 2,),
+        in_specs=[
+            pl.BlockSpec((channels, 2, NX, NY), lambda p: (0, p, 0, 0)),
+            whole(x_table.shape),
+            pl.BlockSpec((1,) + y_table.shape[1:], lambda p: (p, 0, 0)),
+        ],
+        out_specs=whole(shape),
+        out_shape=jax.ShapeDtypeStruct(shape, jnp.bfloat16),
+        scratch_shapes=[
+            pltpu.VMEM((2, 2, slabs, lines, NY), jnp.float32),
+            pltpu.VMEM(shape, jnp.float32),
+        ],
+        compiler_params=params(),
+        cost_estimate=pl.CostEstimate(flops=10**10, bytes_accessed=10**7, transcendentals=0),
+        name="forward_modes",
+    )(field, x_table, y_table)
+
+
+def mixing_kernel(scale_in, scale_out, adjoint, planar, weight, z_in, z_out, spread_table,
+                  sum_table, spectrum, out, total):
+    step = pl.program_id(0)
+    steps = pl.num_programs(0)
+    slabs = planar.shape[0]
+    width = planar.shape[2]
+    half = spectrum.shape[0] // 2
+    lanes = weight.shape[1] // 2
+
+    @pl.when(step == 0)
+    def _():
+        modes = dot(planar[0], z_in[0:width, :])
+        for s in range(1, slabs):
+            modes = modes + dot(planar[s], z_in[s * width : (s + 1) * width, :])
+        spectrum[...] = (modes.T * scale_in).astype(jnp.bfloat16)
+        total[...] = jnp.zeros_like(total)
+
+    block = 64
+    lane = lax.broadcasted_iota(jnp.int32, (1, spectrum.shape[1]), 1)
+    mine = lane % steps == step
+    for at in range(0, half, block):
+        real_in = jnp.where(mine, spectrum[at : at + block, :], 0)
+        imag_in = jnp.where(mine, spectrum[half + at : half + at + block, :], 0)
+        real_wide = dot(real_in, spread_table[...])
+        imag_wide = dot(imag_in, spread_table[...])
+        w_real = weight[at : at + block, :lanes].astype(jnp.float32)
+        w_imag = weight[at : at + block, lanes:].astype(jnp.float32)
+        if adjoint:
+            real = real_wide * w_real + imag_wide * w_imag
+            imag = imag_wide * w_real - real_wide * w_imag
+        else:
+            real = real_wide * w_real - imag_wide * w_imag
+            imag = real_wide * w_imag + imag_wide * w_real
+        real_sum = dot(real.astype(jnp.bfloat16), sum_table[...])
+        imag_sum = dot(imag.astype(jnp.bfloat16), sum_table[...])
+        total[at : at + block, :] += jnp.where(mine, real_sum, 0.0)
+        total[half + at : half + at + block, :] += jnp.where(mine, imag_sum, 0.0)
+
+    @pl.when(step == steps - 1)
+    def _():
+        modes = (total[...] * scale_out).T.astype(jnp.bfloat16)
+        for s in range(slabs):
+            out[s] = dot(modes, z_out[:, s * width : (s + 1) * width]).astype(jnp.bfloat16)
+
+
+def mix(planar, weight, scale_in, scale_out, adjoint):
+    slabs, lines, width = planar.shape
+    depth = KX // slabs
+    channels = lines // depth
+    rows = KY * KZ
+    z_in = constant(forward_z_table())
+    z_out = constant(inverse_z_table())
+    first = first_table(channels, depth)
+    second = second_table(channels, depth)
+    spread_table = constant(second if adjoint else first)
+    sum_table = constant((first if adjoint else second).T)
+    shape = (2 * rows, lines)
+    return pl.pallas_call(
+        functools.partial(mixing_kernel, scale_in, scale_out, adjoint),
+        grid=(depth,),
+        in_specs=[
+            whole(planar.shape),
+            pl.BlockSpec((rows, weight.shape[1]), lambda j: (j, 0)),
+            whole(z_in.shape),
+            whole(z_out.shape),
+            whole(spread_table.shape),
+            whole(sum_table.shape),
+        ],
+        out_specs=[whole(shape), whole(planar.shape)],
+        out_shape=[
+            jax.ShapeDtypeStruct(shape, jnp.bfloat16),
+            jax.ShapeDtypeStruct(planar.shape, jnp.bfloat16),
+        ],
+        scratch_shapes=[pltpu.VMEM(shape, jnp.float32)],
+        compiler_params=params(),
+        cost_estimate=pl.CostEstimate(flops=4 * 10**9, bytes_accessed=10**7, transcendentals=0),
+        name="mix_back" if adjoint else "mix",
+    )(planar, weight, z_in, z_out, spread_table, sum_table)
+
+
+def inverse_step(planar, x_table, y_table, waves, store):
+    slabs = planar.shape[0]
+    for s in range(slabs):
+        step = dot(planar[s], y_table[0]).astype(jnp.bfloat16)
+        for t in range(2):
+            waves[s, t] = step[:, 2 * NY * t : 2 * NY * (t + 1)]
+    group = 8 * (KX // slabs)
+    for g in range(planar.shape[1] // group):
+        right = [waves[s, t, g * group : (g + 1) * group, :] for s in range(slabs) for t in range(2)]
+        step = dot(x_table[...], jnp.concatenate(right, axis=0))
+        store(g, step.reshape(8, NX, 2 * NY))
+
+
+def plane_mobility(grains):
+    same = [
+        jnp.concatenate([grains[:1], grains[:-1]], axis=0),
+        jnp.concatenate([grains[1:], grains[-1:]], axis=0),
+        jnp.concatenate([grains[:, :1], grains[:, :-1]], axis=1),
+        jnp.concatenate([grains[:, 1:], grains[:, -1:]], axis=1),
+    ]
+    total = jnp.full(grains.shape, 0.25, jnp.float32)
+    for other in same:
+        total = total + jnp.where(grains != other, 0.25, 0.0)
+    return total
+
+
+def layer_kernel(planar, smooth, cotangent, grains, bias, mix_out, mix_in, ix_table, iy_table,
+                 x_table, y_table, spread, out, waves, spectral, moving, delta, rows, total):
+    pair = pl.program_id(0)
+    channels = smooth.shape[0]
+
+    def store(g, value):
+        spectral[8 * g : 8 * g + 8] = value
+
+    inverse_step(planar, ix_table, iy_table, waves, store)
+    for q in range(2):
+        moving[:, q * NY : (q + 1) * NY] = plane_mobility(grains[q])
+
+    def wide(ref, x):
+        halves = [ref[:, q, pl.ds(x, 16), :] for q in range(2)]
+        return jnp.concatenate(halves, axis=2).astype(jnp.float32)
+
+    def body(i, _):
+        x = pl.multiple_of(16 * i, 16)
+        smooth_here = wide(smooth, x)
+        cotangent_here = wide(cotangent, x)
+        deltas = []
+        spreads = []
+        for h in range(2):
+            at = pl.ds(pl.multiple_of(x + 8 * h, 8), 8)
+            mobile = moving[at, :][None]
+            right = smooth_here[:, 8 * h : 8 * h + 8, :].reshape(8 * channels, 2 * NY)
+            local = dot(mix_out[...], right.astype(jnp.bfloat16)).reshape(channels, 8, 2 * NY)
+            pre = spectral[:, at, :] + mobile * local + bias[...]
+            gate = 0.5 * jnp.tanh(0.5 * pre) + 0.5
+            slope = gate * (1.0 + pre * (1.0 - gate))
+            change = cotangent_here[:, 8 * h : 8 * h + 8, :] * slope
+            deltas.append(change)
+            right = change.reshape(8 * channels, 2 * NY).astype(jnp.bfloat16)
+            back = dot(mix_in[...], right).reshape(channels, 8, 2 * NY)
+            spreads.append(mobile * back)
+        delta[:, pl.ds(x, 16), :] = jnp.concatenate(deltas, axis=1).astype(jnp.bfloat16)
+        both = jnp.concatenate(spreads, axis=1).astype(jnp.bfloat16)
+        for q in range(2):
+            spread[:, q, pl.ds(x, 16), :] = both[:, :, q * NY : (q + 1) * NY]
+        return 0
+
+    lax.fori_loop(0, NX // 16, body, 0)
+
+    def load(i):
+        return delta[2 * i : 2 * i + 2].reshape(2 * NX, 2 * NY)
+
+    modes_step(load, x_table, y_table, rows, total, pair)
+
+    @pl.when(pair == pl.num_programs(0) - 1)
+    def _():
+        out[...] = total[...].astype(jnp.bfloat16)
+
+
+def layer(planar, smooth, cotangent, grains, bias, point_weight):
+    slabs, lines, width = planar.shape
+    channels, planes = smooth.shape[:2]
+    eye = jnp.eye(8, dtype=jnp.bfloat16)
+    mix_in = jnp.kron(point_weight, eye)
+    mix_out = jnp.kron(point_weight.T, eye)
+    bias_wide = jnp.broadcast_to(bias[:, None, None], (channels, 8, 2 * NY))
+    tables = [
+        constant(inverse_x_table(slabs)),
+        constant(inverse_y_table(planes)),
+        constant(forward_x_table(slabs)),
+        constant(forward_y_table(planes)),
+    ]
+
+    def paired(shape):
+        return pl.BlockSpec((1,) + shape[1:], lambda p: (p, 0, 0))
+
+    field = pl.BlockSpec((channels, 2, NX, NY), lambda p: (0, p, 0, 0))
+    return pl.pallas_call(
+        layer_kernel,
+        grid=(planes // 2,),
+        in_specs=[
+            whole(planar.shape),
+            field,
+            field,
+            pl.BlockSpec((2, NX, NY), lambda p: (p, 0, 0)),
+            whole(bias_wide.shape),
+            whole(mix_out.shape),
+            whole(mix_in.shape),
+            whole(tables[0].shape),
+            paired(tables[1].shape),
+            whole(tables[2].shape),
+            paired(tables[3].shape),
+        ],
+        out_specs=[field, whole(planar.shape)],
+        out_shape=[
+            jax.ShapeDtypeStruct(smooth.shape, jnp.bfloat16),
+            jax.ShapeDtypeStruct(planar.shape, jnp.bfloat16),
+        ],
+        scratch_shapes=[
+            pltpu.VMEM((slabs, 2, lines, 2 * NY), jnp.bfloat16),
+            pltpu.VMEM((channels, NX, 2 * NY), jnp.float32),
+            pltpu.VMEM((NX, 2 * NY), jnp.float32),
+            pltpu.VMEM((channels, NX, 2 * NY), jnp.bfloat16),
+            pltpu.VMEM((2, 2, slabs, lines, NY), jnp.float32),
+            pltpu.VMEM(planar.shape, jnp.float32),
+        ],
+        compiler_params=params(),
+        cost_estimate=pl.CostEstimate(flops=3 * 10**10, bytes_accessed=3 * 10**7, transcendentals=4 * 10**6),
+        name="layer",
+    )(planar, smooth, cotangent, grains, bias_wide, mix_out, mix_in, *tables)
+
+
+def finish_kernel(planar, near, ix_table, iy_table, out, waves):
+    def store(g, value):
+        for q in range(2):
+            here = slice(8 * g, 8 * g + 8)
+            total = value[:, :, q * NY : (q + 1) * NY] + near[here, q].astype(jnp.float32)
+            out[here, q] = total.astype(jnp.bfloat16)
+
+    inverse_step(planar, ix_table, iy_table, waves, store)
+
+
+def finish(planar, near):
+    slabs, lines, width = planar.shape
+    channels, planes = near.shape[:2]
+    ix_table = constant(inverse_x_table(slabs))
+    iy_table = constant(inverse_y_table(planes))
+    field = pl.BlockSpec((channels, 2, NX, NY), lambda p: (0, p, 0, 0))
+    return pl.pallas_call(
+        finish_kernel,
+        grid=(planes // 2,),
+        in_specs=[
+            whole(planar.shape),
+            field,
+            whole(ix_table.shape),
+            pl.BlockSpec((1,) + iy_table.shape[1:], lambda p: (p, 0, 0)),
+        ],
+        out_specs=field,
+        out_shape=jax.ShapeDtypeStruct(near.shape, jnp.bfloat16),
+        scratch_shapes=[pltpu.VMEM((slabs, 2, lines, 2 * NY), jnp.bfloat16)],
+        compiler_params=params(),
+        cost_estimate=pl.CostEstimate(flops=10**10, bytes_accessed=2 * 10**7, transcendentals=0),
+        name="finish",
+    )(planar, near, ix_table, iy_table)
+
+
+def stencil_kernel(taps, before, field, after, out, band):
+    channel = pl.program_id(0)
+    planes = field.shape[1]
+    row = lax.broadcasted_iota(jnp.int32, (NY, NY), 0)
+    column = lax.broadcasted_iota(jnp.int32, (NY, NY), 1)
+    offset = row - column
+
+    @pl.when(channel == 0)
+    def _():
+        band[...] = jnp.zeros_like(band)
+
+    for dz in range(3):
+        for dx in range(3):
+            first = 9 * dz + 3 * dx
+            block = jnp.where(offset == -1, taps[first, channel], 0.0)
+            block = jnp.where(offset == 0, taps[first + 1, channel], block)
+            block = jnp.where(offset == 1, taps[first + 2, channel], block).astype(jnp.bfloat16)
+            for q in range(2):
+                down = (q + dz) * NY
+                right = (2 * dx + q) * NY
+                band[down : down + NY, right : right + NY] = block
+    sheets = [before[0, 0]] + [field[0, z] for z in range(planes)] + [after[0, 0]]
+    left = jnp.concatenate(
+        [jnp.concatenate(sheets[z : z + 4], axis=1) for z in range(0, planes, 2)], axis=0
+    )
+    x = lax.broadcasted_iota(jnp.int32, (left.shape[0], 1), 0) % NX
+    total = dot(left, band[:, 2 * NY : 4 * NY])
+    lower = pltpu.roll(dot(left, band[:, : 2 * NY]), 1, axis=0)
+    total = total + jnp.where(x == 0, 0.0, lower)
+    upper = pltpu.roll(dot(left, band[:, 4 * NY :]), left.shape[0] - 1, axis=0)
+    total = (total + jnp.where(x == NX - 1, 0.0, upper)).astype(jnp.bfloat16)
+    for z in range(planes):
+        at = (z // 2) * NX
+        out[0, z] = total[at : at + NX, (z % 2) * NY : (z % 2 + 1) * NY]
+
+
+def stencil_planes(before, field, after, taps, name):
+    channels, planes = field.shape[:2]
+    rim = pl.BlockSpec((1, 1, NX, NY), lambda c: (c, 0, 0, 0))
+    sheets = pl.BlockSpec((1, planes, NX, NY), lambda c: (c, 0, 0, 0))
+    return pl.pallas_call(
+        stencil_kernel,
+        grid=(channels,),
+        in_specs=[pl.BlockSpec(memory_space=pltpu.SMEM), rim, sheets, rim],
+        out_specs=sheets,
+        out_shape=jax.ShapeDtypeStruct(field.shape, jnp.bfloat16),
+        scratch_shapes=[pltpu.VMEM((4 * NY, 6 * NY), jnp.bfloat16)],
+        compiler_params=params(),
+        cost_estimate=pl.CostEstimate(flops=2 * 10**10, bytes_accessed=2 * 10**7, transcendentals=0),
+        name=name,
+    )(taps, before, field, after)
+
+
+def gradient_kernel(depth, part, spectra, duals, first, second, out):
+    step = pl.program_id(0)
+    samples = spectra.shape[0]
+    half = spectra.shape[1] // 2
+    lane = lax.broadcasted_iota(jnp.int32, (1, spectra.shape[2]), 1)
+    mine = lane % depth == step
+    block = 64
+    for at in range(0, half, block):
+        total = jnp.zeros((block, out.shape[1]), jnp.float32)
+        for s in range(samples):
+            real_in = jnp.where(mine, spectra[s, at : at + block, :], 0)
+            imag_in = jnp.where(mine, spectra[s, half + at : half + at + block, :], 0)
+            real_dual = duals[s, at : at + block, :]
+            imag_dual = duals[s, half + at : half + at + block, :]
+            with_real = jnp.where(part[0] == 0, real_dual, imag_dual)
+            with_imag = jnp.where(part[0] == 0, imag_dual, -real_dual)
+            with_real = jnp.where(mine, with_real, 0)
+            with_imag = jnp.where(mine, with_imag, 0)
+            total = total + dot(real_in, first[0]) * dot(with_real, second[...])
+            total = total + dot(imag_in, first[0]) * dot(with_imag, second[...])
+        out[at : at + block, :] = total * (1.0 / samples)
+
+
+def weight_gradient(spectra, duals, depth, width, index):
+    samples, rows, lines = spectra.shape
+    channels = lines // depth
+    square = channels * channels
+    cuts = square // width
+    first = first_table(channels, depth).reshape(lines, cuts, width).transpose(1, 0, 2)
+    second = second_table(channels, depth)[:, :width]
+    first = constant(first)
+    second = constant(second)
+    where = jnp.stack([index // cuts, index % cuts]).astype(jnp.int32)
+    half = rows // 2
+    return pl.pallas_call(
+        functools.partial(gradient_kernel, depth),
+        grid_spec=pltpu.PrefetchScalarGridSpec(
+            num_scalar_prefetch=1,
+            grid=(depth,),
+            in_specs=[
+                pl.BlockSpec(spectra.shape, lambda j, w: (0, 0, 0)),
+                pl.BlockSpec(duals.shape, lambda j, w: (0, 0, 0)),
+                pl.BlockSpec((1, lines, width), lambda j, w: (w[1], 0, 0)),
+                pl.BlockSpec(second.shape, lambda j, w: (0, 0)),
+            ],
+            out_specs=pl.BlockSpec((half, width), lambda j, w: (j, 0)),
+        ),
+        out_shape=jax.ShapeDtypeStruct((depth * half, width), jnp.float32),
+        compiler_params=params(),
+        cost_estimate=pl.CostEstimate(flops=10**10, bytes_accessed=10**7, transcendentals=0),
+        name="weight_gradient",
+    )(where, spectra, duals, first, second)
+
+
+def neighbours(field):
+    size = lax.axis_size("slab")
+    up = [(i, i + 1) for i in range(size - 1)]
+    down = [(j, i) for i, j in up]
+    planes = field.shape[1]
+    before = lax.ppermute(field[:, planes - 1 :], "slab", up)
+    after = lax.ppermute(field[:, :1], "slab", down)
+    return before, after
+
+
+def swap(planar):
+    return lax.all_to_all(planar, "slab", split_axis=0, concat_axis=0)
+
+
+def local_fast(feats, grains, spec_weight, taps, point_weight, bias, cotangent):
+    slabs = lax.axis_size("slab")
+    field = feats[0]
+    channels = field.shape[0]
+    cell_scale = 1.0 / math.sqrt(NX * NY * NZ)
+    mode_scale = 1.0 / math.sqrt(KX * KY * KZ)
+    mode_rows = spec_weight.shape[0]
+    weight = spec_weight.reshape(mode_rows * KZ, 2 * channels * channels)
+    width = weight.shape[1] // lax.axis_size("dp")
+
+    before, after = neighbours(field)
+    planar = swap(forward_modes(field, slabs))
+    spectrum, planar = mix(planar, weight, cell_scale, mode_scale, False)
+    spectra = lax.all_gather(spectrum, "dp")
+    planar = swap(planar)
+    smooth = stencil_planes(before, field, after, taps, "smooth")
+    spread, planar = layer(planar, smooth, cotangent[0], grains[0], bias, point_weight)
+    before, after = neighbours(spread)
+    planar = swap(planar)
+    dual, planar = mix(planar, weight, mode_scale, cell_scale, True)
+    duals = lax.all_gather(dual, "dp")
+    planar = swap(planar)
+    near = stencil_planes(before, spread, after, taps[::-1], "near")
+    grad_feats = finish(planar, near)[None]
+    grad_spec = weight_gradient(spectra, duals, KX // slabs, width, lax.axis_index("dp"))
+    return (grad_feats, grad_spec.reshape(mode_rows, KZ, width))
+
+
+def local(feats, grains, spec_weight, taps, point_weight, bias, cotangent):
+    samples, channels, planes = feats.shape[:3]
+    width = spec_weight.shape[2] // lax.axis_size("dp")
+    fits = (
+        lax.axis_size("slab") * 4 == KX
+        and samples == 1
+        and channels == 32
+        and planes % 2 == 0
+        and channels * channels % width == 0
+        and width % 128 == 0
+    )
+    form = local_fast if fits else local_any
+    return form(feats, grains, spec_weight, taps, point_weight, bias, cotangent)
+
+
 def solution(mesh):
     in_specs = (
         P(("grp", "dp"), None, "slab", None, None),

time: 833 us -> 213 us (0.26)
  matrix products: 452 us -> 0 us
  other arithmetic: 279 us -> 2.91 us
  Pallas kernels: 0 us -> 125 us
  local copies, waits for them, and re-layouts: 47.1 us -> 26.8 us
  between operations: 15.8 us -> 0.89 us
  blocking collectives: 0 us -> 13.9 us
    dot_general x42 -> x0, matrix products: 452 us -> none  [the longest x2 232 us: plane_inverse(): jnp.einsum('...xk,ky->...xy', imag_x, sin_y, precision=HIGHEST)]
    another operation x2 -> x1, other arithmetic: 186 us -> 0.56 us  [weight_gradient(): where = jnp.stack([index // cuts, index % cuts]).astype(jnp.int32)]
    pallas_call x0 -> x8, Pallas kernels: none -> 125 us  [the longest x2 57.6 us: stencil_planes(): pl.pallas_call(stencil_kernel, grid=(channels,), in_specs=[pl.BlockSpec(m...]
    concatenate x4 -> x0, other arithmetic: 46.7 us -> none  [the longest x2 46.6 us: extended(): shard = jnp.concatenate([before, shard, after], axis=dim)]
    convert_element_type x4 -> x1, other arithmetic: 20.1 us -> 0.01 us  [layer(): eye = jnp.eye(8, dtype=jnp.bfloat16)]
    unnamed x3 -> x0, other arithmetic: 16.3 us -> none
    unnamed x156 -> x44, local copies, waits for them, and re-layouts: 26.3 us -> 12.1 us
    all_gather x0 -> x2, blocking collectives: none -> 13.9 us  [the longest x1 7.17 us: local_fast(): spectra = lax.all_gather(spectrum, 'dp')]
  transfers between devices with their start and end apart: 9 -> 8, of which waited for: 1 -> 1; matrix products, arithmetic and copies ran while one was open for 74% -> 7% of each run, Pallas kernels for 0% -> 41%
where the time goes in v1:
time: 213 us; the launch traced here: 210 us
  Pallas kernels  125 us (59%)
  starting transfers between devices  31.8 us (15%)
  local copies, waits for them, and re-layouts  26.8 us (13%)
  blocking collectives  13.9 us (7%)
  waiting for transfers between devices  8.57 us (4%)
  other arithmetic  2.91 us (1%)
    pallas_call x2, Pallas kernels, stencil_planes(): pl.pallas_call(stencil_kernel, grid=(channels,), in_specs=[pl.BlockSpec(m...  57.6 us
    pallas_call x1, Pallas kernels, layer(): pl.pallas_call(layer_kernel, grid=(planes // 2,), in_specs=[whole(planar....  30 us
    all_to_all x4, starting transfers between devices, swap(): return lax.all_to_all(planar, 'slab', split_axis=0, concat_axis=0)  20.2 us
    pallas_call x2, Pallas kernels, mix(): pl.pallas_call(functools.partial(mixing_kernel, scale_in, scale_out, adjo...  15.9 us
    unnamed x44, local copies, waits for them, and re-layouts  12.1 us
    pallas_call x1, Pallas kernels, finish(): pl.pallas_call(finish_kernel, grid=(planes // 2,), in_specs=[whole(planar...  9.01 us
    ppermute x2, starting transfers between devices, neighbours(): before = lax.ppermute(field[:, planes - 1:], 'slab', up)  8.96 us
    all_to_all x4, waiting for transfers between devices, swap(): return lax.all_to_all(planar, 'slab', split_axis=0, concat_axis=0)  8.56 us
  transfers between devices with their start and end apart: 8, of which 1 were waited for; matrix products, arithmetic and copies ran while one was open for 7% of the time, Pallas kernels for 41%

profile of v1, /device:TPU:0, one launch (start us, length us, event | category | flops | bytes accessed | tf_op | source)
XLA Modules:
  0.0 210.1 jit_solution(1351688037600018296)
XLA Ops:
  0.6 0.0 copy-start.18
  0.6 0.0 copy-start.8
  0.7 3.3 %fusion.2 = (bf16[32,1,128,128]{3,2,1,0:T(8,128)(2,1)}, bf16[32,1,128,128]{3,2,1,0:T(8,128)(2,1)}) fusion(bf16[32,8,128,128]{3,2,1,0:T(8,128)(2,1)} %bitcast.18), kind=kLoop, calls=%fused_computation.6 | loop fusion | bytes 4194304 | tf_op jit(solution)/shard_map/slice | solution.py:712
  3.9 5.0 %collective-permute-start = (bf16[32,1,128,128]{3,2,1,0:T(8,128)(2,1)}, bf16[32,1,128,128]{3,2,1,0:T(8,128)(2,1)S(1)}, u32[]{:S(2)}, u32[]{:S(2)}) collective-permute-start(bf16[32,1,128,128]{3,2,1,0:T(8,128)(2,1)} %get-tuple-element.17), channel_id=1, source_target_pairs={{0,1},{1,2},{2,3},{4,5},{5,6},{6,7},{8,9},{9,10},{10,11},{12,13},{... | collective-permute-start | bytes 3145736 | tf_op jit(solution)/shard_map/ppermute | solution.py:711
  8.9 0.0 copy-start.20
  8.9 1.3 collective-permute-start.1
  10.2 6.3 %forward_modes.1 = bf16[4,128,256]{2,1,0:T(8,128)(2,1)} custom-call(bf16[32,8,128,128]{3,2,1,0:T(8,128)(2,1)} %bitcast.19, bf16[64,256]{1,0:T(8,128)(2,1)S(1)} %copy-done.18, bf16[4,512,256]{2,1,0:T(8,128)(2,1)S(1)} %copy-done.8), custom_call_target="tpu_custom_call" | custom-call | flops 10000000000 | bytes 10000000 | tf_op jit(solution)/shard_map/forward_modes/pallas_call | solution.py:333
  16.5 5.9 %all-to-all-start = ((bf16[4,128,256]{2,1,0:T(8,128)(2,1)}), bf16[4,128,256]{2,1,0:T(8,128)(2,1)S(1)}, u32[]{:S(2)}, u32[]{:S(2)}) async-start(bf16[4,128,256]{2,1,0:T(8,128)(2,1)} %forward_modes.1), calls=%async_computation | async-start | bytes 524288 | tf_op jit(solution)/shard_map/all_to_all | solution.py:717
  22.4 0.1 copy.28
  22.5 0.0 copy-start
  22.5 0.0 copy-start.15
  22.5 0.0 copy-start.16
  22.6 2.4 %broadcast_multiply_fusion = (bf16[32,8,32,8]{3,2,1,0:T(8,128)(2,1)}, bf16[32,8,32,8]{3,2,1,0:T(8,128)(2,1)}) fusion(bf16[32,32]{1,0:T(8,128)(2,1)S(1)} %copy-done.20, bf16[8,8]{1,0:T(8,128)(2,1)S(1)} %fusion, bf16[32,32]{1,0:T(8,128)(2,1)S(1)} %copy.28), kind=kLoop, calls=%fused_computation | loop fusion | flops 131072 | bytes 266368 | tf_op jit(solution)/shard_map/jit(kron)/mul | solution.py:516
  24.9 4.1 %mul.44.mix_out = bf16[256,256]{1,0:T(8,128)(2,1)S(1)} reshape(bf16[32,8,32,8]{3,2,1,0:T(8,128)(2,1)} %get-tuple-element.19) | data formatting | bytes 262144 | tf_op jit(solution)/shard_map/jit(kron)/mul | solution.py:517
  29.0 4.1 %mul.47.mix_in = bf16[256,256]{1,0:T(8,128)(2,1)S(1)} reshape(bf16[32,8,32,8]{3,2,1,0:T(8,128)(2,1)} %get-tuple-element.18) | data formatting | bytes 262144 | tf_op jit(solution)/shard_map/jit(kron)/mul | solution.py:516
  33.1 0.6 pad_add_fusion.part
  33.6 8.6 %all-to-all-done.planar = bf16[4,128,256]{2,1,0:T(8,128)(2,1)S(1)} async-done(((bf16[4,128,256]{2,1,0:T(8,128)(2,1)}), bf16[4,128,256]{2,1,0:T(8,128)(2,1)S(1)}, u32[]{:S(2)}, u32[]{:S(2)}) %all-to-all-start) | async-done | bytes 262176 | tf_op jit(solution)/shard_map/all_to_all | solution.py:717
  42.2 1.2 copy-done.4
  43.4 1.2 copy-done.6
  44.7 7.9 %mix.1 = (bf16[512,128]{1,0:T(8,128)(2,1)S(1)}, bf16[4,128,256]{2,1,0:T(8,128)(2,1)}) custom-call(bf16[4,128,256]{2,1,0:T(8,128)(2,1)S(1)} %all-to-all-done.planar, bf16[1024,2048]{1,0:T(8,128)(2,1)} %bitcast.23, bf16[1024,512]{1,0:T(8,128)(2,1)S(1)} %copy-done.4, bf16[512,1024]{1,0:T(8,128)(2,1)S(1)} %copy-done.6, bf16[128,1024]{1,0:T(8,128)(2,1)S(1)} %copy-done.15, ...), custom_call_target="tpu_custom_call" | custom-call | flops 4000000000 | bytes 10000000 | tf_op jit(solution)/shard_map/mix/pallas_call | solution.py:410
  52.6 3.4 %all-to-all-start.1 = ((bf16[4,128,256]{2,1,0:T(8,128)(2,1)}), bf16[4,128,256]{2,1,0:T(8,128)(2,1)S(1)}, u32[]{:S(2)}, u32[]{:S(2)}) async-start(bf16[4,128,256]{2,1,0:T(8,128)(2,1)} %get-tuple-element.8), calls=%async_computation.1 | async-start | bytes 524288 | tf_op jit(solution)/shard_map/all_to_all | solution.py:717
  56.0 0.0 copy-start.21
  56.0 0.0 copy-start.1
  56.1 28.8 %smooth.1 = bf16[32,8,128,128]{3,2,1,0:T(8,128)(2,1)} custom-call(f32[27,32]{1,0:T(8,128)S(1)} %copy-done, bf16[32,1,128,128]{3,2,1,0:T(8,128)(2,1)S(1)} %collective-permute-done.before, bf16[32,8,128,128]{3,2,1,0:T(8,128)(2,1)} %bitcast.20, bf16[32,1,128,128]{3,2,1,0:T(8,128)(2,1)S(1)} %collective-permute-done.1.after), custom_call_target="tpu_custom_call" | custom-call | flops 20000000000 | bytes 20000000 | tf_op jit(solution)/shard_map/smooth/pallas_call | solution.py:639
  84.9 0.1 broadcast_in_dim.15.bias
  85.0 0.0 copy-start.2
  85.0 1.2 copy-done.2
  86.2 1.2 copy-done.9
  87.4 1.0 copy-done.10
  88.5 30.0 %layer.1 = (bf16[32,8,128,128]{3,2,1,0:T(8,128)(2,1)}, bf16[4,128,256]{2,1,0:T(8,128)(2,1)}) custom-call(bf16[4,128,256]{2,1,0:T(8,128)(2,1)S(1)} %all-to-all-done.1.planar, bf16[32,8,128,128]{3,2,1,0:T(8,128)(2,1)} %smooth.1, bf16[32,8,128,128]{3,2,1,0:T(8,128)(2,1)} %bitcast.22, s32[8,128,128]{2,1,0:T(8,128)S(1)} %bitcast.17, ...), custom_call_target="tpu_custom_call" | custom-call | flops 30000001024 | bytes 30000000 | tf_op jit(solution)/shard_map/layer/pallas_call | solution.py:530
  118.5 5.2 %all-to-all-start.2 = ((bf16[4,128,256]{2,1,0:T(8,128)(2,1)}), bf16[4,128,256]{2,1,0:T(8,128)(2,1)S(1)}, u32[]{:S(2)}, u32[]{:S(2)}) async-start(bf16[4,128,256]{2,1,0:T(8,128)(2,1)} %get-tuple-element.9), calls=%async_computation.2 | async-start | bytes 524288 | tf_op jit(solution)/shard_map/all_to_all | solution.py:717
  123.7 7.2 %all-gather = bf16[2048,128]{1,0:T(8,128)(2,1)S(1)} all-gather(bf16[512,128]{1,0:T(8,128)(2,1)S(1)} %get-tuple-element.12), channel_id=2, replica_groups=mesh['grp'=2,'dp'=4,'slab'=4] {'dp'}, dimensions={0}, use_global_device_ids=true | all-gather | bytes 655360 | tf_op jit(solution)/shard_map/all_gather | solution.py:733
  130.8 3.1 %fusion.1 = (bf16[32,1,128,128]{3,2,1,0:T(8,128)(2,1)}, bf16[32,1,128,128]{3,2,1,0:T(8,128)(2,1)}) fusion(bf16[32,8,128,128]{3,2,1,0:T(8,128)(2,1)} %get-tuple-element.11.field), kind=kLoop, calls=%fused_computation.5 | loop fusion | bytes 4194304 | tf_op jit(solution)/shard_map/slice | solution.py:712
  134.0 4.0 %collective-permute-start.2 = (bf16[32,1,128,128]{3,2,1,0:T(8,128)(2,1)}, bf16[32,1,128,128]{3,2,1,0:T(8,128)(2,1)S(1)}, u32[]{:S(2)}, u32[]{:S(2)}) collective-permute-start(bf16[32,1,128,128]{3,2,1,0:T(8,128)(2,1)} %get-tuple-element.15), channel_id=1, source_target_pairs={{0,1},{1,2},{2,3},{4,5},{5,6},{6,7},{8,9},{9,10},{10,11},{12,13},{... | collective-permute-start | bytes 3145736 | tf_op jit(solution)/shard_map/ppermute | solution.py:711
  138.0 1.3 collective-permute-start.3
  139.3 0.0 copy-start.5
  139.3 1.2 copy-done.5
  140.5 1.2 copy-done.7
  141.7 0.9 copy-done.14
  142.7 8.0 %mix_back.1 = (bf16[512,128]{1,0:T(8,128)(2,1)S(1)}, bf16[4,128,256]{2,1,0:T(8,128)(2,1)}) custom-call(bf16[4,128,256]{2,1,0:T(8,128)(2,1)S(1)} %all-to-all-done.2.planar, bf16[1024,2048]{1,0:T(8,128)(2,1)} %bitcast.24, bf16[1024,512]{1,0:T(8,128)(2,1)S(1)} %copy-done.5, bf16[512,1024]{1,0:T(8,128)(2,1)S(1)} %copy-done.7, bf16[128,1024]{1,0:T(8,128)(2,1)S(1)} %copy-done.13, ...), custom_call_target="tpu_custom_call" | custom-call | flops 4000000000 | bytes 10000000 | tf_op jit(solution)/shard_map/mix_back/pallas_call | solution.py:410
  150.7 5.7 %all-to-all-start.3 = ((bf16[4,128,256]{2,1,0:T(8,128)(2,1)}), bf16[4,128,256]{2,1,0:T(8,128)(2,1)S(1)}, u32[]{:S(2)}, u32[]{:S(2)}) async-start(bf16[4,128,256]{2,1,0:T(8,128)(2,1)} %get-tuple-element.10), calls=%async_computation.3 | async-start | bytes 524288 | tf_op jit(solution)/shard_map/all_to_all | solution.py:717
  156.4 6.7 %all-gather.1 = bf16[2048,128]{1,0:T(8,128)(2,1)S(1)} all-gather(bf16[512,128]{1,0:T(8,128)(2,1)S(1)} %get-tuple-element.13), channel_id=3, replica_groups=mesh['grp'=2,'dp'=4,'slab'=4] {'dp'}, dimensions={0}, use_global_device_ids=true | all-gather | bytes 655360 | tf_op jit(solution)/shard_map/all_gather | solution.py:740
  163.1 0.9 copy-done.17
  164.0 0.6 copy-done.19
  164.5 6.5 %weight_gradient.1 = f32[1024,512]{1,0:T(8,128)} custom-call(s32[2]{0:T(128)S(1)} %copy-done.19, bf16[4,512,128]{2,1,0:T(8,128)(2,1)S(1)} %bitcast.15, bf16[4,512,128]{2,1,0:T(8,128)(2,1)S(1)} %bitcast.16, bf16[2,128,512]{2,1,0:T(8,128)(2,1)S(1)} %copy-done.12, bf16[128,512]{1,0:T(8,128)(2,1)S(1)} %copy-done.17), custom_call_target="tpu_custom_call" | custom-call | flops 10000000000 | bytes 10000000 | tf_op jit(solution)/shard_map/weight_gradient/pallas_call | solution.py:686
  171.0 28.8 %near.1 = bf16[32,8,128,128]{3,2,1,0:T(8,128)(2,1)} custom-call(f32[27,32]{1,0:T(8,128)S(1)} %rev.3.taps, bf16[32,1,128,128]{3,2,1,0:T(8,128)(2,1)S(1)} %collective-permute-done.2.before, bf16[32,8,128,128]{3,2,1,0:T(8,128)(2,1)} %get-tuple-element.11.field, bf16[32,1,128,128]{3,2,1,0:T(8,128)(2,1)S(1)} %collective-permute-done.3.after), custom_call_target="tpu_custom_call" | custom-call | flops 20000000000 | bytes 20000000 | tf_op jit(solution)/shard_map/near/pallas_call | solution.py:639
  199.9 1.2 copy-done.3
  201.1 9.0 %finish.1 = bf16[32,8,128,128]{3,2,1,0:T(8,128)(2,1)} custom-call(bf16[4,128,256]{2,1,0:T(8,128)(2,1)S(1)} %all-to-all-done.3.planar, bf16[32,8,128,128]{3,2,1,0:T(8,128)(2,1)} %near.1, bf16[1024,256]{1,0:T(8,128)(2,1)S(1)} %copy-done.11, bf16[4,256,512]{2,1,0:T(8,128)(2,1)S(1)} %copy-done.3), custom_call_target="tpu_custom_call" | custom-call | flops 10000000000 | bytes 20000000 | tf_op jit(solution)/shard_map/finish/pallas_call | solution.py:581
  (32 shorter events, 0.1 us)
Async XLA Ops:
  0.6 9.6 %copy-start.18 = (bf16[64,256]{1,0:T(8,128)(2,1)S(1)}, bf16[64,256]{1,0:T(8,128)(2,1)}, u32[]{:S(2)}) copy-start(bf16[64,256]{1,0:T(8,128)(2,1)} %constant.53.clone.x_table) | copy-start | bytes 98308
  0.6 9.6 %copy-start.8 = (bf16[4,512,256]{2,1,0:T(8,128)(2,1)S(1)}, bf16[4,512,256]{2,1,0:T(8,128)(2,1)}, u32[]{:S(2)}) copy-start(bf16[4,512,256]{2,1,0:T(8,128)(2,1)} %constant.54.clone.y_table) | copy-start | bytes 3145732
  3.9 52.1 %collective-permute-start = (bf16[32,1,128,128]{3,2,1,0:T(8,128)(2,1)}, bf16[32,1,128,128]{3,2,1,0:T(8,128)(2,1)S(1)}, u32[]{:S(2)}, u32[]{:S(2)}) collective-permute-start(bf16[32,1,128,128]{3,2,1,0:T(8,128)(2,1)} %get-tuple-element.17), channel_id=1, source_target_pairs={{0,1},{1,2},{2,3},{4,5},{5,6},{6,7},{8,9},{9,10},{10,11},{12,13},{... | collective-permute-start | bytes 3145736 | tf_op jit(solution)/shard_map/ppermute | solution.py:711
  8.9 13.5 %copy-start.20 = (bf16[32,32]{1,0:T(8,128)(2,1)S(1)}, bf16[32,32]{1,0:T(8,128)(2,1)}, u32[]{:S(2)}) copy-start(bf16[32,32]{1,0:T(8,128)(2,1)} %param.29) | copy-start | bytes 6148
  8.9 47.1 %collective-permute-start.1 = (bf16[32,1,128,128]{3,2,1,0:T(8,128)(2,1)}, bf16[32,1,128,128]{3,2,1,0:T(8,128)(2,1)S(1)}, u32[]{:S(2)}, u32[]{:S(2)}) collective-permute-start(bf16[32,1,128,128]{3,2,1,0:T(8,128)(2,1)} %get-tuple-element.16), channel_id=1, source_target_pairs={{1,0},{2,1},{3,2},{5,4},{6,5},{7,6},{9,8},{10,9},{11,10},{13,12},{... | collective-permute-start | bytes 3145736 | tf_op jit(solution)/shard_map/ppermute | solution.py:712
  16.5 25.7 %all-to-all-start = ((bf16[4,128,256]{2,1,0:T(8,128)(2,1)}), bf16[4,128,256]{2,1,0:T(8,128)(2,1)S(1)}, u32[]{:S(2)}, u32[]{:S(2)}) async-start(bf16[4,128,256]{2,1,0:T(8,128)(2,1)} %forward_modes.1), calls=%async_computation | async-start | bytes 524288 | tf_op jit(solution)/shard_map/all_to_all | solution.py:717
  22.5 10.5 %copy-start = (f32[27,32]{1,0:T(8,128)S(1)}, f32[27,32]{1,0:T(8,128)}, u32[]{:S(2)}) copy-start(f32[27,32]{1,0:T(8,128)} %taps.1) | copy-start | bytes 10372
  22.5 19.7 %copy-start.15 = (bf16[128,1024]{1,0:T(8,128)(2,1)S(1)}, bf16[128,1024]{1,0:T(8,128)(2,1)}, u32[]{:S(2)}) copy-start(bf16[128,1024]{1,0:T(8,128)(2,1)} %constant.57.clone.spread_table) | copy-start | bytes 786436
  22.5 19.7 %copy-start.16 = (bf16[1024,128]{1,0:T(8,128)(2,1)S(1)}, bf16[1024,128]{1,0:T(8,128)(2,1)}, u32[]{:S(2)}) copy-start(bf16[1024,128]{1,0:T(8,128)(2,1)} %constant.58.clone.sum_table) | copy-start | bytes 786436
  42.2 1.2 copy-start.4
  43.4 1.2 copy-start.6
  52.6 32.3 %all-to-all-start.1 = ((bf16[4,128,256]{2,1,0:T(8,128)(2,1)}), bf16[4,128,256]{2,1,0:T(8,128)(2,1)S(1)}, u32[]{:S(2)}, u32[]{:S(2)}) async-start(bf16[4,128,256]{2,1,0:T(8,128)(2,1)} %get-tuple-element.8), calls=%async_computation.1 | async-start | bytes 524288 | tf_op jit(solution)/shard_map/all_to_all | solution.py:717
  56.0 28.9 %copy-start.21 = (f32[32]{0:T(128)S(1)}, f32[32]{0:T(128)}, u32[]{:S(2)}) copy-start(f32[32]{0:T(128)} %param.30) | copy-start | bytes 388
  56.0 28.9 %copy-start.1 = (s32[1,8,128,128]{3,2,1,0:T(8,128)S(1)}, s32[1,8,128,128]{3,2,1,0:T(8,128)}, u32[]{:S(2)}) copy-start(s32[1,8,128,128]{3,2,1,0:T(8,128)} %param.26) | copy-start | bytes 1572868
  85.0 1.2 copy-start.2
  86.2 1.2 copy-start.9
  87.4 1.0 copy-start.10
  118.5 20.8 %copy-start.13 = (bf16[128,1024]{1,0:T(8,128)(2,1)S(1)}, bf16[128,1024]{1,0:T(8,128)(2,1)}, u32[]{:S(2)}) copy-start(bf16[128,1024]{1,0:T(8,128)(2,1)} %constant.61.clone.spread_table) | copy-start | bytes 786436
  118.5 20.8 %all-to-all-start.2 = ((bf16[4,128,256]{2,1,0:T(8,128)(2,1)}), bf16[4,128,256]{2,1,0:T(8,128)(2,1)S(1)}, u32[]{:S(2)}, u32[]{:S(2)}) async-start(bf16[4,128,256]{2,1,0:T(8,128)(2,1)} %get-tuple-element.9), calls=%async_computation.2 | async-start | bytes 524288 | tf_op jit(solution)/shard_map/all_to_all | solution.py:717
  134.0 37.1 %collective-permute-start.2 = (bf16[32,1,128,128]{3,2,1,0:T(8,128)(2,1)}, bf16[32,1,128,128]{3,2,1,0:T(8,128)(2,1)S(1)}, u32[]{:S(2)}, u32[]{:S(2)}) collective-permute-start(bf16[32,1,128,128]{3,2,1,0:T(8,128)(2,1)} %get-tuple-element.15), channel_id=1, source_target_pairs={{0,1},{1,2},{2,3},{4,5},{5,6},{6,7},{8,9},{9,10},{10,11},{12,13},{... | collective-permute-start | bytes 3145736 | tf_op jit(solution)/shard_map/ppermute | solution.py:711
  138.0 33.1 %collective-permute-start.3 = (bf16[32,1,128,128]{3,2,1,0:T(8,128)(2,1)}, bf16[32,1,128,128]{3,2,1,0:T(8,128)(2,1)S(1)}, u32[]{:S(2)}, u32[]{:S(2)}) collective-permute-start(bf16[32,1,128,128]{3,2,1,0:T(8,128)(2,1)} %get-tuple-element.14), channel_id=1, source_target_pairs={{1,0},{2,1},{3,2},{5,4},{6,5},{7,6},{9,8},{10,9},{11,10},{13,12},{... | collective-permute-start | bytes 3145736 | tf_op jit(solution)/shard_map/ppermute | solution.py:712
  139.3 1.2 copy-start.5
  140.5 1.2 copy-start.7
  141.7 0.9 copy-start.14
  142.7 20.4 %copy-start.12 = (bf16[2,128,512]{2,1,0:T(8,128)(2,1)S(1)}, bf16[2,128,512]{2,1,0:T(8,128)(2,1)}, u32[]{:S(2)}) copy-start(bf16[2,128,512]{2,1,0:T(8,128)(2,1)} %constant.63.clone.first) | copy-start | bytes 786436
  150.7 49.2 %all-to-all-start.3 = ((bf16[4,128,256]{2,1,0:T(8,128)(2,1)}), bf16[4,128,256]{2,1,0:T(8,128)(2,1)S(1)}, u32[]{:S(2)}, u32[]{:S(2)}) async-start(bf16[4,128,256]{2,1,0:T(8,128)(2,1)} %get-tuple-element.10), calls=%async_computation.3 | async-start | bytes 524288 | tf_op jit(solution)/shard_map/all_to_all | solution.py:717
  163.1 0.9 copy-start.17
  164.0 0.6 copy-start.19
  171.0 28.8 %copy-start.11 = (bf16[1024,256]{1,0:T(8,128)(2,1)S(1)}, bf16[1024,256]{1,0:T(8,128)(2,1)}, u32[]{:S(2)}) copy-start(bf16[1024,256]{1,0:T(8,128)(2,1)} %constant.59.clone.ix_table) | copy-start | bytes 1572868
  199.9 1.2 copy-start.3

commit v2 on v1

--- a/solution.py
+++ b/solution.py
@@ -291,7 +291,7 @@
 
 
 def params(**kw):
-    return pltpu.CompilerParams(vmem_limit_bytes=48 * 2**20, **kw)
+    return pltpu.CompilerParams(vmem_limit_bytes=58 * 2**20, **kw)
 
 
 def modes_step(load, x_table, y_table, rows, total, pair):
@@ -310,13 +310,24 @@
         total[s] = before + step
 
 
-def forward_kernel(field, x_table, y_table, out, rows, total):
+def store_rims(field, first, last, pair):
+    @pl.when(pair == 0)
+    def _():
+        first[:, 0] = field[:, 0]
+
+    @pl.when(pair == pl.num_programs(0) - 1)
+    def _():
+        last[:, 0] = field[:, 1]
+
+
+def forward_kernel(field, x_table, y_table, out, first, last, rows, total):
     pair = pl.program_id(0)
 
     def load(i):
         halves = [field[2 * i : 2 * i + 2, q].reshape(2 * NX, NY) for q in range(2)]
         return jnp.concatenate(halves, axis=1)
 
+    store_rims(field, first, last, pair)
     modes_step(load, x_table, y_table, rows, total, pair)
 
     @pl.when(pair == pl.num_programs(0) - 1)
@@ -330,6 +341,7 @@
     x_table = constant(forward_x_table(slabs))
     y_table = constant(forward_y_table(planes))
     shape = (slabs, lines, planes * 2 * KY)
+    rim = (channels, 1, NX, NY)
     return pl.pallas_call(
         forward_kernel,
         grid=(planes // 2,),
@@ -338,8 +350,12 @@
             whole(x_table.shape),
             pl.BlockSpec((1,) + y_table.shape[1:], lambda p: (p, 0, 0)),
         ],
-        out_specs=whole(shape),
-        out_shape=jax.ShapeDtypeStruct(shape, jnp.bfloat16),
+        out_specs=[whole(shape), whole(rim), whole(rim)],
+        out_shape=[
+            jax.ShapeDtypeStruct(shape, jnp.bfloat16),
+            jax.ShapeDtypeStruct(rim, jnp.bfloat16),
+            jax.ShapeDtypeStruct(rim, jnp.bfloat16),
+        ],
         scratch_shapes=[
             pltpu.VMEM((2, 2, slabs, lines, NY), jnp.float32),
             pltpu.VMEM(shape, jnp.float32),
@@ -351,7 +367,11 @@
 
 
 def mixing_kernel(scale_in, scale_out, adjoint, planar, weight, z_in, z_out, spread_table,
-                  sum_table, spectrum, out, total):
+                  sum_table, *rest):
+    if adjoint:
+        partner, out, send, spectrum, total, wide, product = rest
+    else:
+        spectrum, out, total, wide, product = rest
     step = pl.program_id(0)
     steps = pl.num_programs(0)
     slabs = planar.shape[0]
@@ -361,20 +381,22 @@
 
     @pl.when(step == 0)
     def _():
-        modes = dot(planar[0], z_in[0:width, :])
-        for s in range(1, slabs):
-            modes = modes + dot(planar[s], z_in[s * width : (s + 1) * width, :])
-        spectrum[...] = (modes.T * scale_in).astype(jnp.bfloat16)
+        left = jnp.concatenate([planar[s] for s in range(slabs)], axis=1)
+        modes = (dot(left, z_in[...]).T * scale_in).astype(jnp.bfloat16)
+        spectrum[...] = modes
         total[...] = jnp.zeros_like(total)
-
-    block = 64
+        if adjoint:
+            for d in range(send.shape[0]):
+                send[d, : 2 * half] = partner[...]
+                send[d, 2 * half :] = modes
+
     lane = lax.broadcasted_iota(jnp.int32, (1, spectrum.shape[1]), 1)
     mine = lane % steps == step
+    wide[...] = dot(jnp.where(mine, spectrum[...], 0), spread_table[...])
+    block = 32
     for at in range(0, half, block):
-        real_in = jnp.where(mine, spectrum[at : at + block, :], 0)
-        imag_in = jnp.where(mine, spectrum[half + at : half + at + block, :], 0)
-        real_wide = dot(real_in, spread_table[...])
-        imag_wide = dot(imag_in, spread_table[...])
+        real_wide = wide[at : at + block]
+        imag_wide = wide[half + at : half + at + block]
         w_real = weight[at : at + block, :lanes].astype(jnp.float32)
         w_imag = weight[at : at + block, lanes:].astype(jnp.float32)
         if adjoint:
@@ -383,10 +405,9 @@
         else:
             real = real_wide * w_real - imag_wide * w_imag
             imag = real_wide * w_imag + imag_wide * w_real
-        real_sum = dot(real.astype(jnp.bfloat16), sum_table[...])
-        imag_sum = dot(imag.astype(jnp.bfloat16), sum_table[...])
-        total[at : at + block, :] += jnp.where(mine, real_sum, 0.0)
-        total[half + at : half + at + block, :] += jnp.where(mine, imag_sum, 0.0)
+        product[at : at + block] = real.astype(jnp.bfloat16)
+        product[half + at : half + at + block] = imag.astype(jnp.bfloat16)
+    total[...] += jnp.where(mine, dot(product[...], sum_table[...]), 0.0)
 
     @pl.when(step == steps - 1)
     def _():
@@ -395,8 +416,9 @@
             out[s] = dot(modes, z_out[:, s * width : (s + 1) * width]).astype(jnp.bfloat16)
 
 
-def mix(planar, weight, scale_in, scale_out, adjoint):
+def mix(planar, weight, scale_in, scale_out, partner=None, copies=0):
     slabs, lines, width = planar.shape
+    adjoint = partner is not None
     depth = KX // slabs
     channels = lines // depth
     rows = KY * KZ
@@ -407,27 +429,38 @@
     spread_table = constant(second if adjoint else first)
     sum_table = constant((first if adjoint else second).T)
     shape = (2 * rows, lines)
+    in_specs = [
+        whole(planar.shape),
+        pl.BlockSpec((rows, weight.shape[1]), lambda j: (j, 0)),
+        whole(z_in.shape),
+        whole(z_out.shape),
+        whole(spread_table.shape),
+        whole(sum_table.shape),
+    ]
+    operands = [planar, weight, z_in, z_out, spread_table, sum_table]
+    scratch = [
+        pltpu.VMEM(shape, jnp.float32),
+        pltpu.VMEM((2 * rows, channels * channels), jnp.float32),
+        pltpu.VMEM((2 * rows, channels * channels), jnp.bfloat16),
+    ]
+    if adjoint:
+        in_specs.append(whole(shape))
+        operands.append(partner)
+        scratch = [pltpu.VMEM(shape, jnp.bfloat16)] + scratch
+        outs = [planar.shape, (copies, 2 * shape[0], lines)]
+    else:
+        outs = [shape, planar.shape]
     return pl.pallas_call(
         functools.partial(mixing_kernel, scale_in, scale_out, adjoint),
         grid=(depth,),
-        in_specs=[
-            whole(planar.shape),
-            pl.BlockSpec((rows, weight.shape[1]), lambda j: (j, 0)),
-            whole(z_in.shape),
-            whole(z_out.shape),
-            whole(spread_table.shape),
-            whole(sum_table.shape),
-        ],
-        out_specs=[whole(shape), whole(planar.shape)],
-        out_shape=[
-            jax.ShapeDtypeStruct(shape, jnp.bfloat16),
-            jax.ShapeDtypeStruct(planar.shape, jnp.bfloat16),
-        ],
-        scratch_shapes=[pltpu.VMEM(shape, jnp.float32)],
+        in_specs=in_specs,
+        out_specs=[whole(out) for out in outs],
+        out_shape=[jax.ShapeDtypeStruct(out, jnp.bfloat16) for out in outs],
+        scratch_shapes=scratch,
         compiler_params=params(),
         cost_estimate=pl.CostEstimate(flops=4 * 10**9, bytes_accessed=10**7, transcendentals=0),
         name="mix_back" if adjoint else "mix",
-    )(planar, weight, z_in, z_out, spread_table, sum_table)
+    )(*operands)
 
 
 def inverse_step(planar, x_table, y_table, waves, store):
@@ -456,10 +489,25 @@
     return total
 
 
-def layer_kernel(planar, smooth, cotangent, grains, bias, mix_out, mix_in, ix_table, iy_table,
-                 x_table, y_table, spread, out, waves, spectral, moving, delta, rows, total):
+def layer_kernel(bias, planar, smooth, cotangent, grains, point_weight, repeat, ix_table, iy_table,
+                 x_table, y_table, spread, out, first, last, waves, spectral, moving, delta, rows,
+                 total, bias_wide, mix_out, mix_in):
     pair = pl.program_id(0)
     channels = smooth.shape[0]
+
+    @pl.when(pair == 0)
+    def _():
+        for c in range(channels):
+            bias_wide[c] = jnp.full(bias_wide.shape[1:], bias[c], jnp.float32)
+        tall = dot(repeat[...], point_weight[...]).astype(jnp.bfloat16)
+        square = lax.dot_general(
+            tall, repeat[...], (((1,), (1,)), ((), ())), preferred_element_type=jnp.float32
+        )
+        row = lax.broadcasted_iota(jnp.int32, square.shape, 0) % 8
+        column = lax.broadcasted_iota(jnp.int32, square.shape, 1) % 8
+        square = jnp.where(row == column, square, 0.0)
+        mix_in[...] = square.astype(jnp.bfloat16)
+        mix_out[...] = square.T.astype(jnp.bfloat16)
 
     def store(g, value):
         spectral[8 * g : 8 * g + 8] = value
@@ -483,7 +531,7 @@
             mobile = moving[at, :][None]
             right = smooth_here[:, 8 * h : 8 * h + 8, :].reshape(8 * channels, 2 * NY)
             local = dot(mix_out[...], right.astype(jnp.bfloat16)).reshape(channels, 8, 2 * NY)
-            pre = spectral[:, at, :] + mobile * local + bias[...]
+            pre = spectral[:, at, :] + mobile * local + bias_wide[...]
             gate = 0.5 * jnp.tanh(0.5 * pre) + 0.5
             slope = gate * (1.0 + pre * (1.0 - gate))
             change = cotangent_here[:, 8 * h : 8 * h + 8, :] * slope
@@ -497,7 +545,8 @@
             spread[:, q, pl.ds(x, 16), :] = both[:, :, q * NY : (q + 1) * NY]
         return 0
 
-    lax.fori_loop(0, NX // 16, body, 0)
+    lax.fori_loop(0, NX // 16, body, 0, unroll=2)
+    store_rims(spread, first, last, pair)
 
     def load(i):
         return delta[2 * i : 2 * i + 2].reshape(2 * NX, 2 * NY)
@@ -512,10 +561,7 @@
 def layer(planar, smooth, cotangent, grains, bias, point_weight):
     slabs, lines, width = planar.shape
     channels, planes = smooth.shape[:2]
-    eye = jnp.eye(8, dtype=jnp.bfloat16)
-    mix_in = jnp.kron(point_weight, eye)
-    mix_out = jnp.kron(point_weight.T, eye)
-    bias_wide = jnp.broadcast_to(bias[:, None, None], (channels, 8, 2 * NY))
+    repeat = constant(np.repeat(np.eye(channels), 8, axis=0))
     tables = [
         constant(inverse_x_table(slabs)),
         constant(inverse_y_table(planes)),
@@ -527,27 +573,26 @@
         return pl.BlockSpec((1,) + shape[1:], lambda p: (p, 0, 0))
 
     field = pl.BlockSpec((channels, 2, NX, NY), lambda p: (0, p, 0, 0))
+    rim = (channels, 1, NX, NY)
+    outs = [smooth.shape, planar.shape, rim, rim]
     return pl.pallas_call(
         layer_kernel,
         grid=(planes // 2,),
         in_specs=[
+            pl.BlockSpec(memory_space=pltpu.SMEM),
             whole(planar.shape),
             field,
             field,
             pl.BlockSpec((2, NX, NY), lambda p: (p, 0, 0)),
-            whole(bias_wide.shape),
-            whole(mix_out.shape),
-            whole(mix_in.shape),
+            whole(point_weight.shape),
+            whole(repeat.shape),
             whole(tables[0].shape),
             paired(tables[1].shape),
             whole(tables[2].shape),
             paired(tables[3].shape),
         ],
-        out_specs=[field, whole(planar.shape)],
-        out_shape=[
-            jax.ShapeDtypeStruct(smooth.shape, jnp.bfloat16),
-            jax.ShapeDtypeStruct(planar.shape, jnp.bfloat16),
-        ],
+        out_specs=[field, whole(planar.shape), whole(rim), whole(rim)],
+        out_shape=[jax.ShapeDtypeStruct(out, jnp.bfloat16) for out in outs],
         scratch_shapes=[
             pltpu.VMEM((slabs, 2, lines, 2 * NY), jnp.bfloat16),
             pltpu.VMEM((channels, NX, 2 * NY), jnp.float32),
@@ -555,11 +600,14 @@
             pltpu.VMEM((channels, NX, 2 * NY), jnp.bfloat16),
             pltpu.VMEM((2, 2, slabs, lines, NY), jnp.float32),
             pltpu.VMEM(planar.shape, jnp.float32),
+            pltpu.VMEM((channels, 8, 2 * NY), jnp.float32),
+            pltpu.VMEM((8 * channels, 8 * channels), jnp.bfloat16),
+            pltpu.VMEM((8 * channels, 8 * channels), jnp.bfloat16),
         ],
         compiler_params=params(),
         cost_estimate=pl.CostEstimate(flops=3 * 10**10, bytes_accessed=3 * 10**7, transcendentals=4 * 10**6),
         name="layer",
-    )(planar, smooth, cotangent, grains, bias_wide, mix_out, mix_in, *tables)
+    )(bias, planar, smooth, cotangent, grains, point_weight, repeat, *tables)
 
 
 def finish_kernel(planar, near, ix_table, iy_table, out, waves):
@@ -596,84 +644,101 @@
     )(planar, near, ix_table, iy_table)
 
 
-def stencil_kernel(taps, before, field, after, out, band):
-    channel = pl.program_id(0)
-    planes = field.shape[1]
-    row = lax.broadcasted_iota(jnp.int32, (NY, NY), 0)
-    column = lax.broadcasted_iota(jnp.int32, (NY, NY), 1)
-    offset = row - column
-
-    @pl.when(channel == 0)
-    def _():
-        band[...] = jnp.zeros_like(band)
-
+def build_band(adjoint, taps, masks, channel, band):
+    blocks = masks.shape[1] // 16
     for dz in range(3):
         for dx in range(3):
-            first = 9 * dz + 3 * dx
-            block = jnp.where(offset == -1, taps[first, channel], 0.0)
-            block = jnp.where(offset == 0, taps[first + 1, channel], block)
-            block = jnp.where(offset == 1, taps[first + 2, channel], block).astype(jnp.bfloat16)
+            block = jnp.zeros((blocks, 16, NY), jnp.bfloat16)
+            for dy in range(3):
+                number = 9 * dz + 3 * dx + dy
+                tap = taps[26 - number if adjoint else number, channel]
+                tap = jnp.full((16, NY), tap, jnp.float32).astype(jnp.bfloat16)
+                block = block + masks[dy].reshape(blocks, 16, NY) * tap[None]
+            block = block.reshape(NY, NY)
             for q in range(2):
                 down = (q + dz) * NY
                 right = (2 * dx + q) * NY
                 band[down : down + NY, right : right + NY] = block
-    sheets = [before[0, 0]] + [field[0, z] for z in range(planes)] + [after[0, 0]]
+
+
+def apply_band(before, field, after, out, band, c):
+    planes = field.shape[1]
+    sheets = [before[c, 0]] + [field[c, z] for z in range(planes)] + [after[c, 0]]
+    pairs = range(planes // 2)
     left = jnp.concatenate(
-        [jnp.concatenate(sheets[z : z + 4], axis=1) for z in range(0, planes, 2)], axis=0
-    )
-    x = lax.broadcasted_iota(jnp.int32, (left.shape[0], 1), 0) % NX
-    total = dot(left, band[:, 2 * NY : 4 * NY])
-    lower = pltpu.roll(dot(left, band[:, : 2 * NY]), 1, axis=0)
-    total = total + jnp.where(x == 0, 0.0, lower)
-    upper = pltpu.roll(dot(left, band[:, 4 * NY :]), left.shape[0] - 1, axis=0)
-    total = (total + jnp.where(x == NX - 1, 0.0, upper)).astype(jnp.bfloat16)
-    for z in range(planes):
-        at = (z // 2) * NX
-        out[0, z] = total[at : at + NX, (z % 2) * NY : (z % 2 + 1) * NY]
-
-
-def stencil_planes(before, field, after, taps, name):
+        [jnp.concatenate(sheets[2 * p : 2 * p + 4], axis=1) for p in pairs], axis=0
+    )
+    middle = dot(left, band[:, 2 * NY : 4 * NY])
+    lower = dot(left, band[:, : 2 * NY])
+    upper = dot(left, band[:, 4 * NY :])
+    row = lax.broadcasted_iota(jnp.int32, (8, 2 * NY), 0)
+    for p in pairs:
+        here = slice(p * NX, (p + 1) * NX)
+        down = pltpu.roll(lower[here], 1, axis=0)
+        up = pltpu.roll(upper[here], NX - 1, axis=0)
+        down = jnp.concatenate([jnp.where(row == 0, 0.0, down[:8]), down[8:]], axis=0)
+        up = jnp.concatenate([up[:-8], jnp.where(row == 7, 0.0, up[-8:])], axis=0)
+        total = (middle[here] + down + up).astype(jnp.bfloat16)
+        out[c, 2 * p] = total[:, :NY]
+        out[c, 2 * p + 1] = total[:, NY:]
+
+
+def stencil_kernel(adjoint, taps, masks, before, field, after, out, even, odd):
+    step = pl.program_id(0)
+    build = functools.partial(build_band, adjoint, taps, masks)
+
+    @pl.when(step == 0)
+    def _():
+        even[...] = jnp.zeros_like(even)
+        odd[...] = jnp.zeros_like(odd)
+        build(0, even)
+
+    build(2 * step + 1, odd)
+    apply_band(before, field, after, out, even, 0)
+    build(jnp.minimum(2 * step + 2, 2 * pl.num_programs(0) - 1), even)
+    apply_band(before, field, after, out, odd, 1)
+
+
+def stencil_planes(before, field, after, taps, adjoint):
     channels, planes = field.shape[:2]
-    rim = pl.BlockSpec((1, 1, NX, NY), lambda c: (c, 0, 0, 0))
-    sheets = pl.BlockSpec((1, planes, NX, NY), lambda c: (c, 0, 0, 0))
+    masks = constant(np.stack([np.eye(NY, k=1 - dy) for dy in range(3)]))
+    rim = pl.BlockSpec((2, 1, NX, NY), lambda c: (c, 0, 0, 0))
+    sheets = pl.BlockSpec((2, planes, NX, NY), lambda c: (c, 0, 0, 0))
     return pl.pallas_call(
-        stencil_kernel,
-        grid=(channels,),
-        in_specs=[pl.BlockSpec(memory_space=pltpu.SMEM), rim, sheets, rim],
+        functools.partial(stencil_kernel, adjoint),
+        grid=(channels // 2,),
+        in_specs=[pl.BlockSpec(memory_space=pltpu.SMEM), whole(masks.shape), rim, sheets, rim],
         out_specs=sheets,
         out_shape=jax.ShapeDtypeStruct(field.shape, jnp.bfloat16),
-        scratch_shapes=[pltpu.VMEM((4 * NY, 6 * NY), jnp.bfloat16)],
+        scratch_shapes=[pltpu.VMEM((4 * NY, 6 * NY), jnp.bfloat16) for _ in range(2)],
         compiler_params=params(),
         cost_estimate=pl.CostEstimate(flops=2 * 10**10, bytes_accessed=2 * 10**7, transcendentals=0),
-        name=name,
-    )(taps, before, field, after)
-
-
-def gradient_kernel(depth, part, spectra, duals, first, second, out):
+        name="near" if adjoint else "smooth",
+    )(taps, masks, before, field, after)
+
+
+def gradient_kernel(depth, where, gathered, first, second, out):
     step = pl.program_id(0)
-    samples = spectra.shape[0]
-    half = spectra.shape[1] // 2
-    lane = lax.broadcasted_iota(jnp.int32, (1, spectra.shape[2]), 1)
+    samples, rows, lines = gathered.shape
+    half = rows // 4
+    lane = lax.broadcasted_iota(jnp.int32, (1, lines), 1)
     mine = lane % depth == step
-    block = 64
-    for at in range(0, half, block):
-        total = jnp.zeros((block, out.shape[1]), jnp.float32)
-        for s in range(samples):
-            real_in = jnp.where(mine, spectra[s, at : at + block, :], 0)
-            imag_in = jnp.where(mine, spectra[s, half + at : half + at + block, :], 0)
-            real_dual = duals[s, at : at + block, :]
-            imag_dual = duals[s, half + at : half + at + block, :]
-            with_real = jnp.where(part[0] == 0, real_dual, imag_dual)
-            with_imag = jnp.where(part[0] == 0, imag_dual, -real_dual)
-            with_real = jnp.where(mine, with_real, 0)
-            with_imag = jnp.where(mine, with_imag, 0)
-            total = total + dot(real_in, first[0]) * dot(with_real, second[...])
-            total = total + dot(imag_in, first[0]) * dot(with_imag, second[...])
-        out[at : at + block, :] = total * (1.0 / samples)
-
-
-def weight_gradient(spectra, duals, depth, width, index):
-    samples, rows, lines = spectra.shape
+    total = jnp.zeros(out.shape, jnp.float32)
+    for s in range(samples):
+        spectrum = jnp.where(mine, gathered[s, : 2 * half], 0)
+        real = gathered[s, 2 * half : 3 * half]
+        imag = gathered[s, 3 * half :]
+        dual = jnp.concatenate(
+            [jnp.where(where[0] == 0, real, imag), jnp.where(where[0] == 0, imag, -real)], axis=0
+        )
+        dual = jnp.where(mine, dual, 0)
+        product = dot(spectrum, first[0]) * dot(dual, second[...])
+        total = total + product[:half] + product[half:]
+    out[...] = total * (1.0 / samples)
+
+
+def weight_gradient(gathered, depth, width, index):
+    samples, rows, lines = gathered.shape
     channels = lines // depth
     square = channels * channels
     cuts = square // width
@@ -682,15 +747,14 @@
     first = constant(first)
     second = constant(second)
     where = jnp.stack([index // cuts, index % cuts]).astype(jnp.int32)
-    half = rows // 2
+    half = rows // 4
     return pl.pallas_call(
         functools.partial(gradient_kernel, depth),
         grid_spec=pltpu.PrefetchScalarGridSpec(
             num_scalar_prefetch=1,
             grid=(depth,),
             in_specs=[
-                pl.BlockSpec(spectra.shape, lambda j, w: (0, 0, 0)),
-                pl.BlockSpec(duals.shape, lambda j, w: (0, 0, 0)),
+                pl.BlockSpec(gathered.shape, lambda j, w: (0, 0, 0)),
                 pl.BlockSpec((1, lines, width), lambda j, w: (w[1], 0, 0)),
                 pl.BlockSpec(second.shape, lambda j, w: (0, 0)),
             ],
@@ -700,17 +764,14 @@
         compiler_params=params(),
         cost_estimate=pl.CostEstimate(flops=10**10, bytes_accessed=10**7, transcendentals=0),
         name="weight_gradient",
-    )(where, spectra, duals, first, second)
-
-
-def neighbours(field):
+    )(where, gathered, first, second)
+
+
+def neighbours(first, last):
     size = lax.axis_size("slab")
     up = [(i, i + 1) for i in range(size - 1)]
     down = [(j, i) for i, j in up]
-    planes = field.shape[1]
-    before = lax.ppermute(field[:, planes - 1 :], "slab", up)
-    after = lax.ppermute(field[:, :1], "slab", down)
-    return before, after
+    return lax.ppermute(last, "slab", up), lax.ppermute(first, "slab", down)
 
 
 def swap(planar):
@@ -727,21 +788,22 @@
     weight = spec_weight.reshape(mode_rows * KZ, 2 * channels * channels)
     width = weight.shape[1] // lax.axis_size("dp")
 
-    before, after = neighbours(field)
-    planar = swap(forward_modes(field, slabs))
-    spectrum, planar = mix(planar, weight, cell_scale, mode_scale, False)
-    spectra = lax.all_gather(spectrum, "dp")
+    planar, first, last = forward_modes(field, slabs)
+    planar, first, last = lax.optimization_barrier((swap(planar), first, last))
+    before, after = neighbours(first, last)
+    spectrum, planar = mix(planar, weight, cell_scale, mode_scale)
     planar = swap(planar)
-    smooth = stencil_planes(before, field, after, taps, "smooth")
-    spread, planar = layer(planar, smooth, cotangent[0], grains[0], bias, point_weight)
-    before, after = neighbours(spread)
+    smooth = stencil_planes(before, field, after, taps, False)
+    spread, planar, first, last = layer(planar, smooth, cotangent[0], grains[0], bias, point_weight)
+    planar, first, last = lax.optimization_barrier((swap(planar), first, last))
+    before, after = neighbours(first, last)
+    copies = lax.axis_size("dp")
+    planar, send = mix(planar, weight, mode_scale, cell_scale, spectrum, copies)
     planar = swap(planar)
-    dual, planar = mix(planar, weight, mode_scale, cell_scale, True)
-    duals = lax.all_gather(dual, "dp")
-    planar = swap(planar)
-    near = stencil_planes(before, spread, after, taps[::-1], "near")
+    gathered = lax.all_to_all(send, "dp", split_axis=0, concat_axis=0)
+    near = stencil_planes(before, spread, after, taps, True)
     grad_feats = finish(planar, near)[None]
-    grad_spec = weight_gradient(spectra, duals, KX // slabs, width, lax.axis_index("dp"))
+    grad_spec = weight_gradient(gathered, KX // slabs, width, lax.axis_index("dp"))
     return (grad_feats, grad_spec.reshape(mode_rows, KZ, width))
 
 

time: 213 us -> 192 us (0.901)
  local copies, waits for them, and re-layouts: 26.8 us -> 2.39 us
  waiting for transfers between devices: 8.57 us -> 28.4 us
  Pallas kernels: 125 us -> 110 us
  blocking collectives: 13.9 us -> 27.7 us
  starting transfers between devices: 31.8 us -> 20.8 us
  other arithmetic: 2.91 us -> 0.65 us
    all_to_all x0 -> x2, blocking collectives: none -> 27.7 us  [swap(): return lax.all_to_all(planar, 'slab', split_axis=0, concat_axis=0)]
    ppermute x4, waiting for transfers between devices: 0.01 us -> 20 us  [neighbours(): return (lax.ppermute(last, 'slab', up), lax.ppermute(first, 'slab', down))]
    pallas_call x3, Pallas kernels: 87.6 us -> 69.4 us  [the longest x2 41.9 us: stencil_planes(): pl.pallas_call(functools.partial(stencil_kernel, adjoint), grid=(channels...]
    all_gather x2 -> x0, blocking collectives: 13.9 us -> none  [the longest x1 7.17 us: local_fast(): spectra = lax.all_gather(spectrum, 'dp')]
    all_to_all x4 -> x2, starting transfers between devices: 20.2 us -> 8.57 us  [swap(): return lax.all_to_all(planar, 'slab', split_axis=0, concat_axis=0)]
    unnamed x44 -> x14, local copies, waits for them, and re-layouts: 12.1 us -> 2.39 us
    all_to_all x4 -> x2, waiting for transfers between devices: 8.56 us -> 0.01 us  [swap(): return lax.all_to_all(planar, 'slab', split_axis=0, concat_axis=0)]
    all_to_all x0 -> x1, waiting for transfers between devices: none -> 8.44 us  [local_fast(): gathered = lax.all_to_all(send, 'dp', split_axis=0, concat_axis=0)]
  transfers between devices with their start and end apart: 8 -> 7, of which waited for: 1 -> 5; matrix products, arithmetic and copies ran while one was open for 7% -> 0% of each run, Pallas kernels for 41% -> 30%
where the time goes in v2:
time: 192 us; the launch traced here: 191 us
  Pallas kernels  110 us (57%)
  waiting for transfers between devices  28.4 us (15%)
  blocking collectives  27.7 us (14%)
  starting transfers between devices  20.8 us (11%)
  local copies, waits for them, and re-layouts  2.39 us (1%)
    pallas_call x2, Pallas kernels, stencil_planes(): pl.pallas_call(functools.partial(stencil_kernel, adjoint), grid=(channels...  41.9 us
    all_to_all x2, blocking collectives, swap(): return lax.all_to_all(planar, 'slab', split_axis=0, concat_axis=0)  27.7 us
    pallas_call x1, Pallas kernels, layer(): pl.pallas_call(layer_kernel, grid=(planes // 2,), in_specs=[pl.BlockSpec(...  27.5 us
    ppermute x4, waiting for transfers between devices, neighbours(): return (lax.ppermute(last, 'slab', up), lax.ppermute(first, 'slab', down))  20 us
    pallas_call x2, Pallas kernels, mix(): pl.pallas_call(functools.partial(mixing_kernel, scale_in, scale_out, adjo...  16.4 us
    pallas_call x1, Pallas kernels, finish(): pl.pallas_call(finish_kernel, grid=(planes // 2,), in_specs=[whole(planar...  9.25 us
    ppermute x4, starting transfers between devices, neighbours(): return (lax.ppermute(last, 'slab', up), lax.ppermute(first, 'slab', down))  8.76 us
    all_to_all x2, starting transfers between devices, swap(): return lax.all_to_all(planar, 'slab', split_axis=0, concat_axis=0)  8.57 us
  transfers between devices with their start and end apart: 7, of which 5 were waited for; matrix products, arithmetic and copies ran while one was open for 0% of the time, Pallas kernels for 30%

profile of v2, /device:TPU:0, one launch (start us, length us, event | category | flops | bytes accessed | tf_op | source)
XLA Modules:
  0.0 190.7 jit_solution(179887531912538831)
XLA Ops:
  0.6 7.2 %forward_modes.1 = (bf16[4,128,256]{2,1,0:T(8,128)(2,1)}, bf16[32,1,128,128]{3,2,1,0:T(8,128)(2,1)}, bf16[32,1,128,128]{3,2,1,0:T(8,128)(2,1)}) custom-call(bf16[32,8,128,128]{3,2,1,0:T(8,128)(2,1)} %bitcast.8, bf16[64,256]{1,0:T(8,128)(2,1)} %constant.57.clone.x_table, bf16[4,512,256]{2,1,0:T(8,128)(2,1)} %constant.58.clone.y_table), custom_call_target="tpu_custom_call" | custom-call | flops 10000000000 | bytes 10000000 | tf_op jit(solution)/shard_map/forward_modes/pallas_call | solution.py:345
  7.8 15.3 %all_to_all.25.planar = bf16[4,128,256]{2,1,0:T(8,128)(2,1)} all-to-all(bf16[4,128,256]{2,1,0:T(8,128)(2,1)} %get-tuple-element.19), channel_id=1, replica_groups=mesh['grp'=2,'dp'=4,'slab'=4] {'slab'}, dimensions={0} | all-to-all | bytes 524288 | tf_op jit(solution)/shard_map/all_to_all | solution.py:778
  23.1 2.2 %collective-permute-start = (bf16[32,1,128,128]{3,2,1,0:T(8,128)(2,1)}, bf16[32,1,128,128]{3,2,1,0:T(8,128)(2,1)S(1)}, u32[]{:S(2)}, u32[]{:S(2)}) collective-permute-start(bf16[32,1,128,128]{3,2,1,0:T(8,128)(2,1)} %get-tuple-element.24), channel_id=1, source_target_pairs={{0,1},{1,2},{2,3},{4,5},{5,6},{6,7},{8,9},{9,10},{10,11},{12,13},{... | collective-permute-start | bytes 3145736 | tf_op jit(solution)/shard_map/ppermute | solution.py:774
  25.3 1.3 collective-permute-start.1
  26.6 8.0 %mix.1 = (bf16[512,128]{1,0:T(8,128)(2,1)}, bf16[4,128,256]{2,1,0:T(8,128)(2,1)}) custom-call(bf16[4,128,256]{2,1,0:T(8,128)(2,1)} %all_to_all.25.planar, bf16[1024,2048]{1,0:T(8,128)(2,1)} %bitcast.11, bf16[1024,512]{1,0:T(8,128)(2,1)} %constant.59.clone.z_in, bf16[512,1024]{1,0:T(8,128)(2,1)} %constant.60.clone.z_out, ...), custom_call_target="tpu_custom_call" | custom-call | flops 4000000000 | bytes 10000000 | tf_op jit(solution)/shard_map/mix/pallas_call | solution.py:453
  34.5 5.2 %all-to-all-start.1 = ((bf16[4,128,256]{2,1,0:T(8,128)(2,1)}), bf16[4,128,256]{2,1,0:T(8,128)(2,1)S(1)}, u32[]{:S(2)}, u32[]{:S(2)}) async-start(bf16[4,128,256]{2,1,0:T(8,128)(2,1)} %get-tuple-element.23), calls=%async_computation.1 | async-start | bytes 524288 | tf_op jit(solution)/shard_map/all_to_all | solution.py:778
  39.7 8.7 %collective-permute-done.before = bf16[32,1,128,128]{3,2,1,0:T(8,128)(2,1)S(1)} collective-permute-done((bf16[32,1,128,128]{3,2,1,0:T(8,128)(2,1)}, bf16[32,1,128,128]{3,2,1,0:T(8,128)(2,1)S(1)}, u32[]{:S(2)}, u32[]{:S(2)}) %collective-permute-start) | collective-permute-done | bytes 1048608 | tf_op jit(solution)/shard_map/ppermute | solution.py:774
  48.4 0.0 copy-start.5
  48.4 3.0 %collective-permute-done.1.after = bf16[32,1,128,128]{3,2,1,0:T(8,128)(2,1)S(1)} collective-permute-done((bf16[32,1,128,128]{3,2,1,0:T(8,128)(2,1)}, bf16[32,1,128,128]{3,2,1,0:T(8,128)(2,1)S(1)}, u32[]{:S(2)}, u32[]{:S(2)}) %collective-permute-start.1) | collective-permute-done | bytes 1048608 | tf_op jit(solution)/shard_map/ppermute | solution.py:774
  51.3 0.0 copy-done.5
  51.3 0.0 copy-start.6
  51.3 1.0 copy-done.6
  52.3 21.0 %smooth.1 = bf16[32,8,128,128]{3,2,1,0:T(8,128)(2,1)} custom-call(f32[27,32]{1,0:T(8,128)} %taps.3, bf16[3,128,128]{2,1,0:T(8,128)(2,1)} %constant.63.clone.masks, bf16[32,1,128,128]{3,2,1,0:T(8,128)(2,1)} %copy-done.5, bf16[32,8,128,128]{3,2,1,0:T(8,128)(2,1)} %bitcast.9, bf16[32,1,128,128]{3,2,1,0:T(8,128)(2,1)} %copy-done.6), custom_call_target="tpu_custom_call" | custom-call | flops 20000000000 | bytes 20000000 | tf_op jit(solution)/shard_map/smooth/pallas_call | solution.py:707
  73.3 0.0 all-to-all-done.1.planar
  73.3 0.0 copy-start.2
  73.3 0.7 copy-done.2
  74.0 27.5 %layer.1 = (bf16[32,8,128,128]{3,2,1,0:T(8,128)(2,1)}, bf16[4,128,256]{2,1,0:T(8,128)(2,1)}, bf16[32,1,128,128]{3,2,1,0:T(8,128)(2,1)}, bf16[32,1,128,128]{3,2,1,0:T(8,128)(2,1)}) custom-call(f32[32]{0:T(128)} %bias.1, bf16[4,128,256]{2,1,0:T(8,128)(2,1)} %copy-done.2, bf16[32,8,128,128]{3,2,1,0:T(8,128)(2,1)} %smooth.1, bf16[32,8,128,128]{3,2,1,0:T(8,128)(2,1)} %bitcast.10, ...), custom_call_target="tpu_custom_call" | custom-call | flops 30000001024 | bytes 30000000 | tf_op jit(solution)/shard_map/layer/pallas_call | solution.py:578
  101.5 12.4 %all_to_all.26.planar = bf16[4,128,256]{2,1,0:T(8,128)(2,1)} all-to-all(bf16[4,128,256]{2,1,0:T(8,128)(2,1)} %get-tuple-element.26), channel_id=1, replica_groups=mesh['grp'=2,'dp'=4,'slab'=4] {'slab'}, dimensions={0} | all-to-all | bytes 524288 | tf_op jit(solution)/shard_map/all_to_all | solution.py:778
  113.9 0.0 copy-start.4
  113.9 0.0 copy-start.3
  113.9 8.4 %mix_back.1 = (bf16[4,128,256]{2,1,0:T(8,128)(2,1)}, bf16[4,1024,128]{2,1,0:T(8,128)(2,1)}) custom-call(bf16[4,128,256]{2,1,0:T(8,128)(2,1)} %all_to_all.26.planar, bf16[1024,2048]{1,0:T(8,128)(2,1)} %bitcast.12, bf16[1024,512]{1,0:T(8,128)(2,1)} %constant.59.clone.z_in, bf16[512,1024]{1,0:T(8,128)(2,1)} %constant.60.clone.z_out, ...), custom_call_target="tpu_custom_call" | custom-call | flops 4000000000 | bytes 10000000 | tf_op jit(solution)/shard_map/mix_back/pallas_call | solution.py:453
  122.3 3.5 %all-to-all-start.4 = ((bf16[4,1024,128]{2,1,0:T(8,128)(2,1)}), bf16[4,1024,128]{2,1,0:T(8,128)(2,1)S(1)}, u32[]{:S(2)}, u32[]{:S(2)}) async-start(bf16[4,1024,128]{2,1,0:T(8,128)(2,1)} %get-tuple-element.35), calls=%async_computation.4 | async-start | bytes 2097152 | tf_op jit(solution)/shard_map/all_to_all | solution.py:803
  125.8 0.0 copy-done.4
  125.8 4.0 %collective-permute-start.2 = (bf16[32,1,128,128]{3,2,1,0:T(8,128)(2,1)S(1)}, bf16[32,1,128,128]{3,2,1,0:T(8,128)(2,1)}, u32[]{:S(2)}, u32[]{:S(2)}) collective-permute-start(bf16[32,1,128,128]{3,2,1,0:T(8,128)(2,1)S(1)} %copy-done.4), channel_id=1, source_target_pairs={{0,1},{1,2},{2,3},{4,5},{5,6},{6,7},{8,9},{9,10},{10,11},{12,13},{... | collective-permute-start | bytes 3145736 | tf_op jit(solution)/shard_map/ppermute | solution.py:774
  129.8 0.0 copy-done.3
  129.9 1.3 collective-permute-start.3
  131.1 0.6 pad_add_fusion.where
  131.8 8.4 %all-to-all-done.4.gathered = bf16[4,1024,128]{2,1,0:T(8,128)(2,1)S(1)} async-done(((bf16[4,1024,128]{2,1,0:T(8,128)(2,1)}), bf16[4,1024,128]{2,1,0:T(8,128)(2,1)S(1)}, u32[]{:S(2)}, u32[]{:S(2)}) %all-to-all-start.4) | async-done | bytes 1048608 | tf_op jit(solution)/shard_map/all_to_all | solution.py:803
  140.2 0.0 copy-start
  140.2 3.4 %all-to-all-start.3 = ((bf16[4,128,256]{2,1,0:T(8,128)(2,1)}), bf16[4,128,256]{2,1,0:T(8,128)(2,1)S(1)}, u32[]{:S(2)}, u32[]{:S(2)}) async-start(bf16[4,128,256]{2,1,0:T(8,128)(2,1)} %get-tuple-element.31), calls=%async_computation.3 | async-start | bytes 524288 | tf_op jit(solution)/shard_map/all_to_all | solution.py:778
  143.6 0.0 copy-done
  143.7 7.8 %weight_gradient.1 = f32[1024,512]{1,0:T(8,128)} custom-call(s32[2]{0:T(128)} %pad_add_fusion.where, bf16[4,1024,128]{2,1,0:T(8,128)(2,1)} %copy-done, bf16[2,128,512]{2,1,0:T(8,128)(2,1)} %constant.69.clone.first, bf16[128,512]{1,0:T(8,128)(2,1)} %constant.70.clone.second), custom_call_target="tpu_custom_call" | custom-call | flops 10000000000 | bytes 10000000 | tf_op jit(solution)/shard_map/weight_gradient/pallas_call | solution.py:751
  151.5 0.8 collective-permute-done.2.before
  152.3 7.5 %collective-permute-done.3.after = bf16[32,1,128,128]{3,2,1,0:T(8,128)(2,1)} collective-permute-done((bf16[32,1,128,128]{3,2,1,0:T(8,128)(2,1)S(1)}, bf16[32,1,128,128]{3,2,1,0:T(8,128)(2,1)}, u32[]{:S(2)}, u32[]{:S(2)}) %collective-permute-start.3) | collective-permute-done | bytes 1048608 | tf_op jit(solution)/shard_map/ppermute | solution.py:774
  159.8 20.9 %near.1 = bf16[32,8,128,128]{3,2,1,0:T(8,128)(2,1)} custom-call(f32[27,32]{1,0:T(8,128)} %taps.3, bf16[3,128,128]{2,1,0:T(8,128)(2,1)} %constant.63.clone.masks, bf16[32,1,128,128]{3,2,1,0:T(8,128)(2,1)} %collective-permute-done.2.before, bf16[32,8,128,128]{3,2,1,0:T(8,128)(2,1)} %get-tuple-element.33.field, ...), custom_call_target="tpu_custom_call" | custom-call | flops 20000000000 | bytes 20000000 | tf_op jit(solution)/shard_map/near/pallas_call | solution.py:707
  180.7 0.0 all-to-all-done.3.planar
  180.7 0.0 copy-start.1
  180.8 0.7 copy-done.1
  181.4 9.3 %finish.1 = bf16[32,8,128,128]{3,2,1,0:T(8,128)(2,1)} custom-call(bf16[4,128,256]{2,1,0:T(8,128)(2,1)} %copy-done.1, bf16[32,8,128,128]{3,2,1,0:T(8,128)(2,1)} %near.1, bf16[1024,256]{1,0:T(8,128)(2,1)} %constant.65.clone.ix_table, bf16[4,256,512]{2,1,0:T(8,128)(2,1)} %constant.66.clone.iy_table), custom_call_target="tpu_custom_call" | custom-call | flops 10000000000 | bytes 20000000 | tf_op jit(solution)/shard_map/finish/pallas_call | solution.py:629
Async XLA Ops:
  23.1 25.3 %collective-permute-start = (bf16[32,1,128,128]{3,2,1,0:T(8,128)(2,1)}, bf16[32,1,128,128]{3,2,1,0:T(8,128)(2,1)S(1)}, u32[]{:S(2)}, u32[]{:S(2)}) collective-permute-start(bf16[32,1,128,128]{3,2,1,0:T(8,128)(2,1)} %get-tuple-element.24), channel_id=1, source_target_pairs={{0,1},{1,2},{2,3},{4,5},{5,6},{6,7},{8,9},{9,10},{10,11},{12,13},{... | collective-permute-start | bytes 3145736 | tf_op jit(solution)/shard_map/ppermute | solution.py:774
  25.3 26.1 %collective-permute-start.1 = (bf16[32,1,128,128]{3,2,1,0:T(8,128)(2,1)}, bf16[32,1,128,128]{3,2,1,0:T(8,128)(2,1)S(1)}, u32[]{:S(2)}, u32[]{:S(2)}) collective-permute-start(bf16[32,1,128,128]{3,2,1,0:T(8,128)(2,1)} %get-tuple-element.25), channel_id=1, source_target_pairs={{1,0},{2,1},{3,2},{5,4},{6,5},{7,6},{9,8},{10,9},{11,10},{13,12},{... | collective-permute-start | bytes 3145736 | tf_op jit(solution)/shard_map/ppermute | solution.py:774
  34.5 38.8 %all-to-all-start.1 = ((bf16[4,128,256]{2,1,0:T(8,128)(2,1)}), bf16[4,128,256]{2,1,0:T(8,128)(2,1)S(1)}, u32[]{:S(2)}, u32[]{:S(2)}) async-start(bf16[4,128,256]{2,1,0:T(8,128)(2,1)} %get-tuple-element.23), calls=%async_computation.1 | async-start | bytes 524288 | tf_op jit(solution)/shard_map/all_to_all | solution.py:778
  48.4 3.0 %copy-start.5 = (bf16[32,1,128,128]{3,2,1,0:T(8,128)(2,1)}, bf16[32,1,128,128]{3,2,1,0:T(8,128)(2,1)S(1)}, u32[]{:S(2)}) copy-start(bf16[32,1,128,128]{3,2,1,0:T(8,128)(2,1)S(1)} %collective-permute-done.before) | copy-start | bytes 3145732
  51.3 1.0 copy-start.6
  73.3 0.7 copy-start.2
  113.9 12.0 %copy-start.4 = (bf16[32,1,128,128]{3,2,1,0:T(8,128)(2,1)S(1)}, bf16[32,1,128,128]{3,2,1,0:T(8,128)(2,1)}, u32[]{:S(2)}) copy-start(bf16[32,1,128,128]{3,2,1,0:T(8,128)(2,1)} %get-tuple-element.32) | copy-start | bytes 3145732
  113.9 16.0 %copy-start.3 = (bf16[32,1,128,128]{3,2,1,0:T(8,128)(2,1)S(1)}, bf16[32,1,128,128]{3,2,1,0:T(8,128)(2,1)}, u32[]{:S(2)}) copy-start(bf16[32,1,128,128]{3,2,1,0:T(8,128)(2,1)} %get-tuple-element.34) | copy-start | bytes 3145732
  122.3 18.0 %all-to-all-start.4 = ((bf16[4,1024,128]{2,1,0:T(8,128)(2,1)}), bf16[4,1024,128]{2,1,0:T(8,128)(2,1)S(1)}, u32[]{:S(2)}, u32[]{:S(2)}) async-start(bf16[4,1024,128]{2,1,0:T(8,128)(2,1)} %get-tuple-element.35), calls=%async_computation.4 | async-start | bytes 2097152 | tf_op jit(solution)/shard_map/all_to_all | solution.py:803
  125.8 26.5 %collective-permute-start.2 = (bf16[32,1,128,128]{3,2,1,0:T(8,128)(2,1)S(1)}, bf16[32,1,128,128]{3,2,1,0:T(8,128)(2,1)}, u32[]{:S(2)}, u32[]{:S(2)}) collective-permute-start(bf16[32,1,128,128]{3,2,1,0:T(8,128)(2,1)S(1)} %copy-done.4), channel_id=1, source_target_pairs={{0,1},{1,2},{2,3},{4,5},{5,6},{6,7},{8,9},{9,10},{10,11},{12,13},{... | collective-permute-start | bytes 3145736 | tf_op jit(solution)/shard_map/ppermute | solution.py:774
  129.9 30.0 %collective-permute-start.3 = (bf16[32,1,128,128]{3,2,1,0:T(8,128)(2,1)S(1)}, bf16[32,1,128,128]{3,2,1,0:T(8,128)(2,1)}, u32[]{:S(2)}, u32[]{:S(2)}) collective-permute-start(bf16[32,1,128,128]{3,2,1,0:T(8,128)(2,1)S(1)} %copy-done.3), channel_id=1, source_target_pairs={{1,0},{2,1},{3,2},{5,4},{6,5},{7,6},{9,8},{10,9},{11,10},{13,12},{... | collective-permute-start | bytes 3145736 | tf_op jit(solution)/shard_map/ppermute | solution.py:774
  140.2 3.4 %copy-start = (bf16[4,1024,128]{2,1,0:T(8,128)(2,1)}, bf16[4,1024,128]{2,1,0:T(8,128)(2,1)S(1)}, u32[]{:S(2)}) copy-start(bf16[4,1024,128]{2,1,0:T(8,128)(2,1)S(1)} %all-to-all-done.4.gathered) | copy-start | bytes 3145732
  140.2 40.5 %all-to-all-start.3 = ((bf16[4,128,256]{2,1,0:T(8,128)(2,1)}), bf16[4,128,256]{2,1,0:T(8,128)(2,1)S(1)}, u32[]{:S(2)}, u32[]{:S(2)}) async-start(bf16[4,128,256]{2,1,0:T(8,128)(2,1)} %get-tuple-element.31), calls=%async_computation.3 | async-start | bytes 524288 | tf_op jit(solution)/shard_map/all_to_all | solution.py:778
  180.7 0.7 copy-start.1

commit v3 on v2

--- a/solution.py
+++ b/solution.py
@@ -282,6 +282,9 @@
     return table.reshape(channels * depth, channels * channels)
 
 
+LIGHT = pl.CostEstimate(flops=10**7, bytes_accessed=10**5, transcendentals=0)
+
+
 def dot(a, b):
     return jnp.dot(a, b, preferred_element_type=jnp.float32)
 
@@ -310,24 +313,13 @@
         total[s] = before + step
 
 
-def store_rims(field, first, last, pair):
-    @pl.when(pair == 0)
-    def _():
-        first[:, 0] = field[:, 0]
-
-    @pl.when(pair == pl.num_programs(0) - 1)
-    def _():
-        last[:, 0] = field[:, 1]
-
-
-def forward_kernel(field, x_table, y_table, out, first, last, rows, total):
+def forward_kernel(field, x_table, y_table, out, rows, total):
     pair = pl.program_id(0)
 
     def load(i):
         halves = [field[2 * i : 2 * i + 2, q].reshape(2 * NX, NY) for q in range(2)]
         return jnp.concatenate(halves, axis=1)
 
-    store_rims(field, first, last, pair)
     modes_step(load, x_table, y_table, rows, total, pair)
 
     @pl.when(pair == pl.num_programs(0) - 1)
@@ -341,7 +333,6 @@
     x_table = constant(forward_x_table(slabs))
     y_table = constant(forward_y_table(planes))
     shape = (slabs, lines, planes * 2 * KY)
-    rim = (channels, 1, NX, NY)
     return pl.pallas_call(
         forward_kernel,
         grid=(planes // 2,),
@@ -350,18 +341,14 @@
             whole(x_table.shape),
             pl.BlockSpec((1,) + y_table.shape[1:], lambda p: (p, 0, 0)),
         ],
-        out_specs=[whole(shape), whole(rim), whole(rim)],
-        out_shape=[
-            jax.ShapeDtypeStruct(shape, jnp.bfloat16),
-            jax.ShapeDtypeStruct(rim, jnp.bfloat16),
-            jax.ShapeDtypeStruct(rim, jnp.bfloat16),
-        ],
+        out_specs=whole(shape),
+        out_shape=jax.ShapeDtypeStruct(shape, jnp.bfloat16),
         scratch_shapes=[
             pltpu.VMEM((2, 2, slabs, lines, NY), jnp.float32),
             pltpu.VMEM(shape, jnp.float32),
         ],
         compiler_params=params(),
-        cost_estimate=pl.CostEstimate(flops=10**10, bytes_accessed=10**7, transcendentals=0),
+        cost_estimate=LIGHT,
         name="forward_modes",
     )(field, x_table, y_table)
 
@@ -458,7 +445,7 @@
         out_shape=[jax.ShapeDtypeStruct(out, jnp.bfloat16) for out in outs],
         scratch_shapes=scratch,
         compiler_params=params(),
-        cost_estimate=pl.CostEstimate(flops=4 * 10**9, bytes_accessed=10**7, transcendentals=0),
+        cost_estimate=LIGHT,
         name="mix_back" if adjoint else "mix",
     )(*operands)
 
@@ -490,8 +477,8 @@
 
 
 def layer_kernel(bias, planar, smooth, cotangent, grains, point_weight, repeat, ix_table, iy_table,
-                 x_table, y_table, spread, out, first, last, waves, spectral, moving, delta, rows,
-                 total, bias_wide, mix_out, mix_in):
+                 x_table, y_table, spread, out, waves, spectral, moving, delta, rows, total,
+                 bias_wide, mix_out, mix_in):
     pair = pl.program_id(0)
     channels = smooth.shape[0]
 
@@ -545,8 +532,7 @@
             spread[:, q, pl.ds(x, 16), :] = both[:, :, q * NY : (q + 1) * NY]
         return 0
 
-    lax.fori_loop(0, NX // 16, body, 0, unroll=2)
-    store_rims(spread, first, last, pair)
+    lax.fori_loop(0, NX // 16, body, 0, unroll=4)
 
     def load(i):
         return delta[2 * i : 2 * i + 2].reshape(2 * NX, 2 * NY)
@@ -573,15 +559,14 @@
         return pl.BlockSpec((1,) + shape[1:], lambda p: (p, 0, 0))
 
     field = pl.BlockSpec((channels, 2, NX, NY), lambda p: (0, p, 0, 0))
-    rim = (channels, 1, NX, NY)
-    outs = [smooth.shape, planar.shape, rim, rim]
+    outs = [smooth.shape, planar.shape]
     return pl.pallas_call(
         layer_kernel,
         grid=(planes // 2,),
         in_specs=[
             pl.BlockSpec(memory_space=pltpu.SMEM),
             whole(planar.shape),
-            field,
+            pl.BlockSpec((channels, 2, NX, NY), lambda p: (0, kept(p, planes // 2), 0, 0)),
             field,
             pl.BlockSpec((2, NX, NY), lambda p: (p, 0, 0)),
             whole(point_weight.shape),
@@ -591,7 +576,7 @@
             whole(tables[2].shape),
             paired(tables[3].shape),
         ],
-        out_specs=[field, whole(planar.shape), whole(rim), whole(rim)],
+        out_specs=[field, whole(planar.shape)],
         out_shape=[jax.ShapeDtypeStruct(out, jnp.bfloat16) for out in outs],
         scratch_shapes=[
             pltpu.VMEM((slabs, 2, lines, 2 * NY), jnp.bfloat16),
@@ -605,7 +590,7 @@
             pltpu.VMEM((8 * channels, 8 * channels), jnp.bfloat16),
         ],
         compiler_params=params(),
-        cost_estimate=pl.CostEstimate(flops=3 * 10**10, bytes_accessed=3 * 10**7, transcendentals=4 * 10**6),
+        cost_estimate=LIGHT,
         name="layer",
     )(bias, planar, smooth, cotangent, grains, point_weight, repeat, *tables)
 
@@ -631,7 +616,7 @@
         grid=(planes // 2,),
         in_specs=[
             whole(planar.shape),
-            field,
+            pl.BlockSpec((channels, 2, NX, NY), lambda p: (0, kept(p, planes // 2), 0, 0)),
             whole(ix_table.shape),
             pl.BlockSpec((1,) + iy_table.shape[1:], lambda p: (p, 0, 0)),
         ],
@@ -639,7 +624,7 @@
         out_shape=jax.ShapeDtypeStruct(near.shape, jnp.bfloat16),
         scratch_shapes=[pltpu.VMEM((slabs, 2, lines, 2 * NY), jnp.bfloat16)],
         compiler_params=params(),
-        cost_estimate=pl.CostEstimate(flops=10**10, bytes_accessed=2 * 10**7, transcendentals=0),
+        cost_estimate=LIGHT,
         name="finish",
     )(planar, near, ix_table, iy_table)
 
@@ -661,18 +646,17 @@
                 band[down : down + NY, right : right + NY] = block
 
 
-def apply_band(before, field, after, out, band, c):
-    planes = field.shape[1]
-    sheets = [before[c, 0]] + [field[c, z] for z in range(planes)] + [after[c, 0]]
-    pairs = range(planes // 2)
-    left = jnp.concatenate(
-        [jnp.concatenate(sheets[2 * p : 2 * p + 4], axis=1) for p in pairs], axis=0
-    )
+def kept(pair, pairs):
+    return jnp.where(pair == 0, pairs - 2, jnp.where(pair == pairs - 1, pair, pair - 1))
+
+
+def apply_band(quads, out, band, c):
+    left = jnp.concatenate([jnp.concatenate(quad, axis=1) for quad in quads], axis=0)
     middle = dot(left, band[:, 2 * NY : 4 * NY])
     lower = dot(left, band[:, : 2 * NY])
     upper = dot(left, band[:, 4 * NY :])
     row = lax.broadcasted_iota(jnp.int32, (8, 2 * NY), 0)
-    for p in pairs:
+    for p in range(len(quads)):
         here = slice(p * NX, (p + 1) * NX)
         down = pltpu.roll(lower[here], 1, axis=0)
         up = pltpu.roll(upper[here], NX - 1, axis=0)
@@ -683,38 +667,95 @@
         out[c, 2 * p + 1] = total[:, NY:]
 
 
-def stencil_kernel(adjoint, taps, masks, before, field, after, out, even, odd):
+def inner_quads(field, c):
+    planes = field.shape[1]
+    return [[field[c, z + k] for k in range(4)] for z in range(1, planes - 3, 2)]
+
+
+def outer_quads(before, field, after, c):
+    planes = field.shape[1]
+    low = [before[c, 0]] + [field[c, z] for z in range(3)]
+    high = [field[c, z] for z in range(planes - 3, planes)] + [after[c, 0]]
+    return [low, high]
+
+
+def stencil_kernel(adjoint, rims, inner, start, taps, masks, *refs):
+    if rims:
+        low, high, field, out, first, last, even, odd = refs
+        first[...] = low[...]
+        last[...] = high[...]
+    elif inner:
+        _, field, out, even, odd = refs
+    else:
+        _, field, before, after, out, even, odd = refs
     step = pl.program_id(0)
+    steps = pl.num_programs(0)
     build = functools.partial(build_band, adjoint, taps, masks)
+
+    def quads(c):
+        return inner_quads(field, c) if inner else outer_quads(before, field, after, c)
 
     @pl.when(step == 0)
     def _():
         even[...] = jnp.zeros_like(even)
         odd[...] = jnp.zeros_like(odd)
-        build(0, even)
-
-    build(2 * step + 1, odd)
-    apply_band(before, field, after, out, even, 0)
-    build(jnp.minimum(2 * step + 2, 2 * pl.num_programs(0) - 1), even)
-    apply_band(before, field, after, out, odd, 1)
-
-
-def stencil_planes(before, field, after, taps, adjoint):
+        build(start, even)
+
+    build(start + 2 * step + 1, odd)
+    apply_band(quads(0), out, even, 0)
+    build(start + jnp.minimum(2 * step + 2, 2 * steps - 1), even)
+    apply_band(quads(1), out, odd, 1)
+
+
+def stencil_planes(kind, taps, adjoint, field, near=None, rims=None):
     channels, planes = field.shape[:2]
     masks = constant(np.stack([np.eye(NY, k=1 - dy) for dy in range(3)]))
-    rim = pl.BlockSpec((2, 1, NX, NY), lambda c: (c, 0, 0, 0))
-    sheets = pl.BlockSpec((2, planes, NX, NY), lambda c: (c, 0, 0, 0))
-    return pl.pallas_call(
-        functools.partial(stencil_kernel, adjoint),
-        grid=(channels // 2,),
-        in_specs=[pl.BlockSpec(memory_space=pltpu.SMEM), whole(masks.shape), rim, sheets, rim],
-        out_specs=sheets,
-        out_shape=jax.ShapeDtypeStruct(field.shape, jnp.bfloat16),
+    quarter = channels // 4
+    start = quarter if kind == "inner" else 0
+    count = {"rims": quarter, "inner": channels - quarter, "outer": channels}[kind]
+    steps = count // 2
+    skip = start // 2
+    sheets = pl.BlockSpec((2, planes, NX, NY), lambda c: (c + skip, 0, 0, 0))
+    if kind == "outer":
+        out_spec = pl.BlockSpec((2, 4, NX, NY), lambda c: (c, planes // 4 - 1, 0, 0))
+    else:
+        out_spec = pl.BlockSpec((2, planes - 4, NX, NY), lambda c: (c + skip, 0, 0, 0))
+    in_specs = [pl.BlockSpec(memory_space=pltpu.SMEM), whole(masks.shape)]
+    operands = [taps, masks]
+    out_specs = [out_spec]
+    out_shape = [jax.ShapeDtypeStruct(field.shape, jnp.bfloat16)]
+    aliases = {}
+    if kind == "rims":
+        wide = channels // steps
+        rim = (wide, 1, NX, NY)
+        in_specs.append(pl.BlockSpec(rim, lambda c: (c, 0, 0, 0)))
+        in_specs.append(pl.BlockSpec(rim, lambda c: (c, planes - 1, 0, 0)))
+        operands += [field, field]
+        for _ in range(2):
+            out_specs.append(pl.BlockSpec(rim, lambda c: (c, 0, 0, 0)))
+            out_shape.append(jax.ShapeDtypeStruct((channels, 1, NX, NY), jnp.bfloat16))
+    else:
+        in_specs.append(pl.BlockSpec(memory_space=pl.ANY))
+        operands.append(near)
+        aliases = {2: 0}
+    in_specs.append(sheets)
+    operands.append(field)
+    if kind == "outer":
+        in_specs += [pl.BlockSpec((2, 1, NX, NY), lambda c: (c, 0, 0, 0))] * 2
+        operands += list(rims)
+    result = pl.pallas_call(
+        functools.partial(stencil_kernel, adjoint, kind == "rims", kind != "outer", start),
+        grid=(steps,),
+        in_specs=in_specs,
+        out_specs=out_specs,
+        out_shape=out_shape,
+        input_output_aliases=aliases,
         scratch_shapes=[pltpu.VMEM((4 * NY, 6 * NY), jnp.bfloat16) for _ in range(2)],
         compiler_params=params(),
-        cost_estimate=pl.CostEstimate(flops=2 * 10**10, bytes_accessed=2 * 10**7, transcendentals=0),
-        name="near" if adjoint else "smooth",
-    )(taps, masks, before, field, after)
+        cost_estimate=LIGHT,
+        name=("near_" if adjoint else "smooth_") + kind,
+    )(*operands)
+    return result if kind == "rims" else result[0]
 
 
 def gradient_kernel(depth, where, gathered, first, second, out):
@@ -762,7 +803,7 @@
         ),
         out_shape=jax.ShapeDtypeStruct((depth * half, width), jnp.float32),
         compiler_params=params(),
-        cost_estimate=pl.CostEstimate(flops=10**10, bytes_accessed=10**7, transcendentals=0),
+        cost_estimate=LIGHT,
         name="weight_gradient",
     )(where, gathered, first, second)
 
@@ -788,20 +829,30 @@
     weight = spec_weight.reshape(mode_rows * KZ, 2 * channels * channels)
     width = weight.shape[1] // lax.axis_size("dp")
 
-    planar, first, last = forward_modes(field, slabs)
-    planar, first, last = lax.optimization_barrier((swap(planar), first, last))
-    before, after = neighbours(first, last)
+    copies = lax.axis_size("dp")
+    barrier = lax.optimization_barrier
+
+    planar, field = barrier((forward_modes(field, slabs), field))
+    smooth, first, last = stencil_planes("rims", taps, False, field)
+    rims = neighbours(first, last)
+    smooth = stencil_planes("inner", taps, False, field, smooth)
+    planar, smooth = barrier((swap(planar), smooth))
     spectrum, planar = mix(planar, weight, cell_scale, mode_scale)
+    planar, smooth = barrier((planar, smooth))
     planar = swap(planar)
-    smooth = stencil_planes(before, field, after, taps, False)
-    spread, planar, first, last = layer(planar, smooth, cotangent[0], grains[0], bias, point_weight)
-    planar, first, last = lax.optimization_barrier((swap(planar), first, last))
-    before, after = neighbours(first, last)
-    copies = lax.axis_size("dp")
+    smooth = stencil_planes("outer", taps, False, field, smooth, rims)
+    planar, smooth = barrier((planar, smooth))
+    spread, planar = layer(planar, smooth, cotangent[0], grains[0], bias, point_weight)
+    near, first, last = stencil_planes("rims", taps, True, spread)
+    rims = neighbours(first, last)
+    near = stencil_planes("inner", taps, True, spread, near)
+    planar, near = barrier((swap(planar), near))
     planar, send = mix(planar, weight, mode_scale, cell_scale, spectrum, copies)
+    planar, near = barrier((planar, near))
     planar = swap(planar)
+    near = stencil_planes("outer", taps, True, spread, near, rims)
+    planar, near, send = barrier((planar, near, send))
     gathered = lax.all_to_all(send, "dp", split_axis=0, concat_axis=0)
-    near = stencil_planes(before, spread, after, taps, True)
     grad_feats = finish(planar, near)[None]
     grad_spec = weight_gradient(gathered, KX // slabs, width, lax.axis_index("dp"))
     return (grad_feats, grad_spec.reshape(mode_rows, KZ, width))
@@ -814,7 +865,7 @@
         lax.axis_size("slab") * 4 == KX
         and samples == 1
         and channels == 32
-        and planes % 2 == 0
+        and planes == 8
         and channels * channels % width == 0
         and width % 128 == 0
     )

time: 192 us -> 207 us (1.078)
  blocking collectives: 27.7 us -> 0 us
  Pallas kernels: 110 us -> 135 us
  starting transfers between devices: 20.8 us -> 33.7 us
  local copies, waits for them, and re-layouts: 2.39 us -> 7.04 us
    pallas_call x2 -> x6, Pallas kernels: 41.9 us -> 71.1 us  [stencil_planes(): pl.pallas_call(functools.partial(stencil_kernel, adjoint, kind == 'rims',...]
    all_to_all x2 -> x0, blocking collectives: 27.7 us -> none  [swap(): return lax.all_to_all(planar, 'slab', split_axis=0, concat_axis=0)]
    all_to_all x2 -> x4, waiting for transfers between devices: 0.01 us -> 22.9 us  [swap(): return lax.all_to_all(planar, 'slab', split_axis=0, concat_axis=0)]
    ppermute x4, waiting for transfers between devices: 20 us -> 0.01 us  [neighbours(): return (lax.ppermute(last, 'slab', up), lax.ppermute(first, 'slab', down))]
    all_to_all x2 -> x4, starting transfers between devices: 8.57 us -> 18.7 us  [swap(): return lax.all_to_all(planar, 'slab', split_axis=0, concat_axis=0)]
    unnamed x14 -> x18, local copies, waits for them, and re-layouts: 2.39 us -> 7.04 us
    all_to_all x1, waiting for transfers between devices: 8.44 us -> 4.49 us  [local_fast(): gathered = lax.all_to_all(send, 'dp', split_axis=0, concat_axis=0)]
    ppermute x4, starting transfers between devices: 8.76 us -> 11.5 us  [neighbours(): return (lax.ppermute(last, 'slab', up), lax.ppermute(first, 'slab', down))]
  transfers between devices with their start and end apart: 7 -> 9, of which waited for: 5 -> 3; matrix products, arithmetic and copies ran while one was open for 0% -> 0% of each run, Pallas kernels for 30% -> 41%
where the time goes in v3:
time: 207 us; the launch traced here: 205 us
  Pallas kernels  135 us (65%)
  starting transfers between devices  33.7 us (16%)
  waiting for transfers between devices  27.4 us (13%)
  local copies, waits for them, and re-layouts  7.04 us (3%)
    pallas_call x6, Pallas kernels, stencil_planes(): pl.pallas_call(functools.partial(stencil_kernel, adjoint, kind == 'rims',...  71.1 us
    pallas_call x1, Pallas kernels, layer(): pl.pallas_call(layer_kernel, grid=(planes // 2,), in_specs=[pl.BlockSpec(...  24.8 us
    all_to_all x4, waiting for transfers between devices, swap(): return lax.all_to_all(planar, 'slab', split_axis=0, concat_axis=0)  22.9 us
    all_to_all x4, starting transfers between devices, swap(): return lax.all_to_all(planar, 'slab', split_axis=0, concat_axis=0)  18.7 us
    pallas_call x2, Pallas kernels, mix(): pl.pallas_call(functools.partial(mixing_kernel, scale_in, scale_out, adjo...  16.2 us
    ppermute x4, starting transfers between devices, neighbours(): return (lax.ppermute(last, 'slab', up), lax.ppermute(first, 'slab', down))  11.5 us
    pallas_call x1, Pallas kernels, finish(): pl.pallas_call(finish_kernel, grid=(planes // 2,), in_specs=[whole(planar...  9.27 us
    pallas_call x1, Pallas kernels, weight_gradient(): pl.pallas_call(functools.partial(gradient_kernel, depth), grid_spec=pltpu...  7.82 us
  transfers between devices with their start and end apart: 9, of which 3 were waited for; matrix products, arithmetic and copies ran while one was open for 0% of the time, Pallas kernels for 41%

profile of v3, /device:TPU:0, one launch (start us, length us, event | category | flops | bytes accessed | tf_op | source)
XLA Modules:
  0.0 204.9 jit_solution(3960585976004907105)
XLA Ops:
  0.6 6.3 %forward_modes.1 = bf16[4,128,256]{2,1,0:T(8,128)(2,1)} custom-call(bf16[32,8,128,128]{3,2,1,0:T(8,128)(2,1)} %bitcast.8, bf16[64,256]{1,0:T(8,128)(2,1)} %constant.57.clone.x_table, bf16[4,512,256]{2,1,0:T(8,128)(2,1)} %constant.58.clone.y_table), custom_call_target="tpu_custom_call" | custom-call | flops 10000000 | bytes 100000 | tf_op jit(solution)/shard_map/forward_modes/pallas_call | solution.py:336
  6.9 6.1 %smooth_rims.1 = (bf16[32,8,128,128]{3,2,1,0:T(8,128)(2,1)}, bf16[32,1,128,128]{3,2,1,0:T(8,128)(2,1)}, bf16[32,1,128,128]{3,2,1,0:T(8,128)(2,1)}) custom-call(f32[27,32]{1,0:T(8,128)} %taps.11, bf16[3,128,128]{2,1,0:T(8,128)(2,1)} %constant.59.clone.masks, bf16[32,8,128,128]{3,2,1,0:T(8,128)(2,1)} %bitcast.9, bf16[32,8,128,128]{3,2,1,0:T(8,128)(2,1)} %bitcast.10, ...), custom_call_target="tpu_custom_call" | custom-call | flops 10000000 | bytes 100000 | tf_op jit(solution)/shard_map/smooth_rims/pallas_call | solution.py:746
  13.0 5.0 %collective-permute-start = (bf16[32,1,128,128]{3,2,1,0:T(8,128)(2,1)}, bf16[32,1,128,128]{3,2,1,0:T(8,128)(2,1)S(1)}, u32[]{:S(2)}, u32[]{:S(2)}) collective-permute-start(bf16[32,1,128,128]{3,2,1,0:T(8,128)(2,1)} %get-tuple-element.37), channel_id=1, source_target_pairs={{0,1},{1,2},{2,3},{4,5},{5,6},{6,7},{8,9},{9,10},{10,11},{12,13},{... | collective-permute-start | bytes 3145736 | tf_op jit(solution)/shard_map/ppermute | solution.py:815
  18.0 1.3 collective-permute-start.1
  19.3 5.9 %all-to-all-start = ((bf16[4,128,256]{2,1,0:T(8,128)(2,1)}), bf16[4,128,256]{2,1,0:T(8,128)(2,1)S(1)}, u32[]{:S(2)}, u32[]{:S(2)}) async-start(bf16[4,128,256]{2,1,0:T(8,128)(2,1)} %forward_modes.1), calls=%async_computation | async-start | bytes 524288 | tf_op jit(solution)/shard_map/all_to_all | solution.py:819
  25.2 12.7 %smooth_inner.1.refs_0_ = bf16[32,8,128,128]{3,2,1,0:T(8,128)(2,1)} custom-call(f32[27,32]{1,0:T(8,128)} %taps.11, bf16[3,128,128]{2,1,0:T(8,128)(2,1)} %constant.59.clone.masks, bf16[32,8,128,128]{3,2,1,0:T(8,128)(2,1)} %get-tuple-element.31.refs_0_, bf16[32,8,128,128]{3,2,1,0:T(8,128)(2,1)} %bitcast.12), custom_call_target="tpu_custom_call", output_to_operand_aliasing={{}: (2, {})} | custom-call | flops 10000000 | bytes 100000 | tf_op jit(solution)/shard_map/smooth_inner/pallas_call | solution.py:746
  37.9 13.3 %all-to-all-done.planar = bf16[4,128,256]{2,1,0:T(8,128)(2,1)S(1)} async-done(((bf16[4,128,256]{2,1,0:T(8,128)(2,1)}), bf16[4,128,256]{2,1,0:T(8,128)(2,1)S(1)}, u32[]{:S(2)}, u32[]{:S(2)}) %all-to-all-start) | async-done | bytes 262176 | tf_op jit(solution)/shard_map/all_to_all | solution.py:819
  51.3 0.0 copy-start.4
  51.3 0.7 copy-done.4
  52.0 7.9 %mix.1 = (bf16[512,128]{1,0:T(8,128)(2,1)}, bf16[4,128,256]{2,1,0:T(8,128)(2,1)}) custom-call(bf16[4,128,256]{2,1,0:T(8,128)(2,1)} %copy-done.4, bf16[1024,2048]{1,0:T(8,128)(2,1)} %bitcast.14, bf16[1024,512]{1,0:T(8,128)(2,1)} %constant.60.clone.z_in, bf16[512,1024]{1,0:T(8,128)(2,1)} %constant.61.clone.z_out, ...), custom_call_target="tpu_custom_call" | custom-call | flops 10000000 | bytes 100000 | tf_op jit(solution)/shard_map/mix/pallas_call | solution.py:440
  59.9 3.4 %all-to-all-start.1 = ((bf16[4,128,256]{2,1,0:T(8,128)(2,1)}), bf16[4,128,256]{2,1,0:T(8,128)(2,1)S(1)}, u32[]{:S(2)}, u32[]{:S(2)}) async-start(bf16[4,128,256]{2,1,0:T(8,128)(2,1)} %get-tuple-element.35), calls=%async_computation.1 | async-start | bytes 524288 | tf_op jit(solution)/shard_map/all_to_all | solution.py:819
  63.3 0.0 collective-permute-done.refs_2_
  63.3 0.0 copy-start.7
  63.3 0.0 collective-permute-done.1.refs_3_
  63.3 1.0 copy-done.7
  64.3 0.0 copy-start.8
  64.3 1.0 copy-done.8
  65.3 16.7 %smooth_outer.1.smooth = bf16[32,8,128,128]{3,2,1,0:T(8,128)(2,1)} custom-call(f32[27,32]{1,0:T(8,128)} %taps.11, bf16[3,128,128]{2,1,0:T(8,128)(2,1)} %constant.59.clone.masks, bf16[32,8,128,128]{3,2,1,0:T(8,128)(2,1)} %smooth_inner.1.refs_0_, bf16[32,8,128,128]{3,2,1,0:T(8,128)(2,1)} %bitcast.13, ...), custom_call_target="tpu_custom_call", output_to_operand_aliasing={{}: (2, {})} | custom-call | flops 10000000 | bytes 100000 | tf_op jit(solution)/shard_map/smooth_outer/pallas_call | solution.py:746
  82.0 0.0 all-to-all-done.1.planar
  82.0 0.0 copy-start.2
  82.0 0.7 copy-done.2
  82.7 24.8 %layer.1 = (bf16[32,8,128,128]{3,2,1,0:T(8,128)(2,1)}, bf16[4,128,256]{2,1,0:T(8,128)(2,1)}) custom-call(f32[32]{0:T(128)} %bias.1, bf16[4,128,256]{2,1,0:T(8,128)(2,1)} %copy-done.2, bf16[32,8,128,128]{3,2,1,0:T(8,128)(2,1)} %smooth_outer.1.smooth, bf16[32,8,128,128]{3,2,1,0:T(8,128)(2,1)} %bitcast.16, s32[8,128,128]{2,1,0:T(8,128)} %bitcast.19, ...), custom_call_target="tpu_custom_call" | custom-call | flops 10000000 | bytes 100000 | tf_op jit(solution)/shard_map/layer/pallas_call | solution.py:563
  107.5 6.1 %near_rims.1 = (bf16[32,8,128,128]{3,2,1,0:T(8,128)(2,1)}, bf16[32,1,128,128]{3,2,1,0:T(8,128)(2,1)}, bf16[32,1,128,128]{3,2,1,0:T(8,128)(2,1)}) custom-call(f32[27,32]{1,0:T(8,128)} %taps.11, bf16[3,128,128]{2,1,0:T(8,128)(2,1)} %constant.59.clone.masks, bf16[32,8,128,128]{3,2,1,0:T(8,128)(2,1)} %get-tuple-element.42.refs_0_.refs_1_.refs_2_, ...), custom_call_target="tpu_custom_call" | custom-call | flops 10000000 | bytes 100000 | tf_op jit(solution)/shard_map/near_rims/pallas_call | solution.py:746
  113.6 3.9 %collective-permute-start.2 = (bf16[32,1,128,128]{3,2,1,0:T(8,128)(2,1)}, bf16[32,1,128,128]{3,2,1,0:T(8,128)(2,1)S(1)}, u32[]{:S(2)}, u32[]{:S(2)}) collective-permute-start(bf16[32,1,128,128]{3,2,1,0:T(8,128)(2,1)} %get-tuple-element.50), channel_id=1, source_target_pairs={{0,1},{1,2},{2,3},{4,5},{5,6},{6,7},{8,9},{9,10},{10,11},{12,13},{... | collective-permute-start | bytes 3145736 | tf_op jit(solution)/shard_map/ppermute | solution.py:815
  117.5 1.3 collective-permute-start.3
  118.8 5.7 %all-to-all-start.2 = ((bf16[4,128,256]{2,1,0:T(8,128)(2,1)}), bf16[4,128,256]{2,1,0:T(8,128)(2,1)S(1)}, u32[]{:S(2)}, u32[]{:S(2)}) async-start(bf16[4,128,256]{2,1,0:T(8,128)(2,1)} %get-tuple-element.41), calls=%async_computation.2 | async-start | bytes 524288 | tf_op jit(solution)/shard_map/all_to_all | solution.py:819
  124.6 12.7 %near_inner.1.refs_0_ = bf16[32,8,128,128]{3,2,1,0:T(8,128)(2,1)} custom-call(f32[27,32]{1,0:T(8,128)} %taps.11, bf16[3,128,128]{2,1,0:T(8,128)(2,1)} %constant.59.clone.masks, bf16[32,8,128,128]{3,2,1,0:T(8,128)(2,1)} %get-tuple-element.43.refs_0_, bf16[32,8,128,128]{3,2,1,0:T(8,128)(2,1)} %get-tuple-element.42.refs_0_.refs_1_.refs_2_), custom_call_target="tpu_custom_call", output_to_operand_aliasing={{}: (2, {})} | custom-call | flops 10000000 | bytes 100000 | tf_op jit(solution)/shard_map/near_inner/pallas_call | solution.py:746
  137.3 9.6 %all-to-all-done.2.planar = bf16[4,128,256]{2,1,0:T(8,128)(2,1)S(1)} async-done(((bf16[4,128,256]{2,1,0:T(8,128)(2,1)}), bf16[4,128,256]{2,1,0:T(8,128)(2,1)S(1)}, u32[]{:S(2)}, u32[]{:S(2)}) %all-to-all-start.2) | async-done | bytes 262176 | tf_op jit(solution)/shard_map/all_to_all | solution.py:819
  146.9 0.0 copy-start.3
  146.9 0.7 copy-done.3
  147.6 8.2 %mix_back.1 = (bf16[4,128,256]{2,1,0:T(8,128)(2,1)}, bf16[4,1024,128]{2,1,0:T(8,128)(2,1)}) custom-call(bf16[4,128,256]{2,1,0:T(8,128)(2,1)} %copy-done.3, bf16[1024,2048]{1,0:T(8,128)(2,1)} %bitcast.15, bf16[1024,512]{1,0:T(8,128)(2,1)} %constant.60.clone.z_in, bf16[512,1024]{1,0:T(8,128)(2,1)} %constant.61.clone.z_out, ...), custom_call_target="tpu_custom_call" | custom-call | flops 10000000 | bytes 100000 | tf_op jit(solution)/shard_map/mix_back/pallas_call | solution.py:440
  155.8 3.6 %all-to-all-start.3 = ((bf16[4,128,256]{2,1,0:T(8,128)(2,1)}), bf16[4,128,256]{2,1,0:T(8,128)(2,1)S(1)}, u32[]{:S(2)}, u32[]{:S(2)}) async-start(bf16[4,128,256]{2,1,0:T(8,128)(2,1)} %get-tuple-element.48), calls=%async_computation.3 | async-start | bytes 524288 | tf_op jit(solution)/shard_map/all_to_all | solution.py:819
  159.4 0.0 collective-permute-done.2.refs_2_
  159.4 0.0 copy-start.5
  159.4 0.0 collective-permute-done.3.refs_3_
  159.4 1.0 copy-done.5
  160.4 0.0 copy-start.6
  160.4 1.0 copy-done.6
  161.4 16.7 %near_outer.1.near = bf16[32,8,128,128]{3,2,1,0:T(8,128)(2,1)} custom-call(f32[27,32]{1,0:T(8,128)} %taps.11, bf16[3,128,128]{2,1,0:T(8,128)(2,1)} %constant.59.clone.masks, bf16[32,8,128,128]{3,2,1,0:T(8,128)(2,1)} %near_inner.1.refs_0_, bf16[32,8,128,128]{3,2,1,0:T(8,128)(2,1)} %get-tuple-element.42.refs_0_.refs_1_.refs_2_, ...), custom_call_target="tpu_custom_call", output_to_operand_aliasing={{}: (2, {})} | custom-call | flops 10000000 | bytes 100000 | tf_op jit(solution)/shard_map/near_outer/pallas_call | solution.py:746
  178.1 0.0 all-to-all-done.3.planar
  178.1 0.0 copy-start.1
  178.1 3.5 %all-to-all-start.4 = ((bf16[4,1024,128]{2,1,0:T(8,128)(2,1)}), bf16[4,1024,128]{2,1,0:T(8,128)(2,1)S(1)}, u32[]{:S(2)}, u32[]{:S(2)}) async-start(bf16[4,1024,128]{2,1,0:T(8,128)(2,1)} %get-tuple-element.55), calls=%async_computation.4 | async-start | bytes 2097152 | tf_op jit(solution)/shard_map/all_to_all | solution.py:855
  181.7 0.6 pad_add_fusion.where
  182.3 0.0 copy-done.1
  182.3 9.3 %finish.1 = bf16[32,8,128,128]{3,2,1,0:T(8,128)(2,1)} custom-call(bf16[4,128,256]{2,1,0:T(8,128)(2,1)} %copy-done.1, bf16[32,8,128,128]{3,2,1,0:T(8,128)(2,1)} %near_outer.1.near, bf16[1024,256]{1,0:T(8,128)(2,1)} %constant.65.clone.ix_table, bf16[4,256,512]{2,1,0:T(8,128)(2,1)} %constant.66.clone.iy_table), custom_call_target="tpu_custom_call" | custom-call | flops 10000000 | bytes 100000 | tf_op jit(solution)/shard_map/finish/pallas_call | solution.py:614
  191.6 4.5 %all-to-all-done.4.gathered = bf16[4,1024,128]{2,1,0:T(8,128)(2,1)S(1)} async-done(((bf16[4,1024,128]{2,1,0:T(8,128)(2,1)}), bf16[4,1024,128]{2,1,0:T(8,128)(2,1)S(1)}, u32[]{:S(2)}, u32[]{:S(2)}) %all-to-all-start.4) | async-done | bytes 1048608 | tf_op jit(solution)/shard_map/all_to_all | solution.py:855
  196.1 1.0 copy-done
  197.1 7.8 %weight_gradient.1 = f32[1024,512]{1,0:T(8,128)} custom-call(s32[2]{0:T(128)} %pad_add_fusion.where, bf16[4,1024,128]{2,1,0:T(8,128)(2,1)} %copy-done, bf16[2,128,512]{2,1,0:T(8,128)(2,1)} %constant.69.clone.first, bf16[128,512]{1,0:T(8,128)(2,1)} %constant.70.clone.second), custom_call_target="tpu_custom_call" | custom-call | flops 10000000 | bytes 100000 | tf_op jit(solution)/shard_map/weight_gradient/pallas_call | solution.py:792
  (1 shorter events, 0.0 us)
Async XLA Ops:
  13.0 50.3 %collective-permute-start = (bf16[32,1,128,128]{3,2,1,0:T(8,128)(2,1)}, bf16[32,1,128,128]{3,2,1,0:T(8,128)(2,1)S(1)}, u32[]{:S(2)}, u32[]{:S(2)}) collective-permute-start(bf16[32,1,128,128]{3,2,1,0:T(8,128)(2,1)} %get-tuple-element.37), channel_id=1, source_target_pairs={{0,1},{1,2},{2,3},{4,5},{5,6},{6,7},{8,9},{9,10},{10,11},{12,13},{... | collective-permute-start | bytes 3145736 | tf_op jit(solution)/shard_map/ppermute | solution.py:815
  18.0 45.3 %collective-permute-start.1 = (bf16[32,1,128,128]{3,2,1,0:T(8,128)(2,1)}, bf16[32,1,128,128]{3,2,1,0:T(8,128)(2,1)S(1)}, u32[]{:S(2)}, u32[]{:S(2)}) collective-permute-start(bf16[32,1,128,128]{3,2,1,0:T(8,128)(2,1)} %get-tuple-element.38), channel_id=1, source_target_pairs={{1,0},{2,1},{3,2},{5,4},{6,5},{7,6},{9,8},{10,9},{11,10},{13,12},{... | collective-permute-start | bytes 3145736 | tf_op jit(solution)/shard_map/ppermute | solution.py:815
  19.3 32.0 %all-to-all-start = ((bf16[4,128,256]{2,1,0:T(8,128)(2,1)}), bf16[4,128,256]{2,1,0:T(8,128)(2,1)S(1)}, u32[]{:S(2)}, u32[]{:S(2)}) async-start(bf16[4,128,256]{2,1,0:T(8,128)(2,1)} %forward_modes.1), calls=%async_computation | async-start | bytes 524288 | tf_op jit(solution)/shard_map/all_to_all | solution.py:819
  51.3 0.7 copy-start.4
  59.9 22.1 %all-to-all-start.1 = ((bf16[4,128,256]{2,1,0:T(8,128)(2,1)}), bf16[4,128,256]{2,1,0:T(8,128)(2,1)S(1)}, u32[]{:S(2)}, u32[]{:S(2)}) async-start(bf16[4,128,256]{2,1,0:T(8,128)(2,1)} %get-tuple-element.35), calls=%async_computation.1 | async-start | bytes 524288 | tf_op jit(solution)/shard_map/all_to_all | solution.py:819
  63.3 1.0 copy-start.7
  64.3 1.0 copy-start.8
  82.0 0.7 copy-start.2
  113.6 45.8 %collective-permute-start.2 = (bf16[32,1,128,128]{3,2,1,0:T(8,128)(2,1)}, bf16[32,1,128,128]{3,2,1,0:T(8,128)(2,1)S(1)}, u32[]{:S(2)}, u32[]{:S(2)}) collective-permute-start(bf16[32,1,128,128]{3,2,1,0:T(8,128)(2,1)} %get-tuple-element.50), channel_id=1, source_target_pairs={{0,1},{1,2},{2,3},{4,5},{5,6},{6,7},{8,9},{9,10},{10,11},{12,13},{... | collective-permute-start | bytes 3145736 | tf_op jit(solution)/shard_map/ppermute | solution.py:815
  117.5 41.9 %collective-permute-start.3 = (bf16[32,1,128,128]{3,2,1,0:T(8,128)(2,1)}, bf16[32,1,128,128]{3,2,1,0:T(8,128)(2,1)S(1)}, u32[]{:S(2)}, u32[]{:S(2)}) collective-permute-start(bf16[32,1,128,128]{3,2,1,0:T(8,128)(2,1)} %get-tuple-element.51), channel_id=1, source_target_pairs={{1,0},{2,1},{3,2},{5,4},{6,5},{7,6},{9,8},{10,9},{11,10},{13,12},{... | collective-permute-start | bytes 3145736 | tf_op jit(solution)/shard_map/ppermute | solution.py:815
  118.8 28.0 %all-to-all-start.2 = ((bf16[4,128,256]{2,1,0:T(8,128)(2,1)}), bf16[4,128,256]{2,1,0:T(8,128)(2,1)S(1)}, u32[]{:S(2)}, u32[]{:S(2)}) async-start(bf16[4,128,256]{2,1,0:T(8,128)(2,1)} %get-tuple-element.41), calls=%async_computation.2 | async-start | bytes 524288 | tf_op jit(solution)/shard_map/all_to_all | solution.py:819
  146.9 0.7 copy-start.3
  155.8 22.3 %all-to-all-start.3 = ((bf16[4,128,256]{2,1,0:T(8,128)(2,1)}), bf16[4,128,256]{2,1,0:T(8,128)(2,1)S(1)}, u32[]{:S(2)}, u32[]{:S(2)}) async-start(bf16[4,128,256]{2,1,0:T(8,128)(2,1)} %get-tuple-element.48), calls=%async_computation.3 | async-start | bytes 524288 | tf_op jit(solution)/shard_map/all_to_all | solution.py:819
  159.4 1.0 copy-start.5
  160.4 1.0 copy-start.6
  178.1 4.2 %copy-start.1 = (bf16[4,128,256]{2,1,0:T(8,128)(2,1)}, bf16[4,128,256]{2,1,0:T(8,128)(2,1)S(1)}, u32[]{:S(2)}) copy-start(bf16[4,128,256]{2,1,0:T(8,128)(2,1)S(1)} %all-to-all-done.3.planar) | copy-start | bytes 786436
  178.1 18.0 %all-to-all-start.4 = ((bf16[4,1024,128]{2,1,0:T(8,128)(2,1)}), bf16[4,1024,128]{2,1,0:T(8,128)(2,1)S(1)}, u32[]{:S(2)}, u32[]{:S(2)}) async-start(bf16[4,1024,128]{2,1,0:T(8,128)(2,1)} %get-tuple-element.55), calls=%async_computation.4 | async-start | bytes 2097152 | tf_op jit(solution)/shard_map/all_to_all | solution.py:855
  196.1 1.0 copy-start

commit v4 on v2

--- a/solution.py
+++ b/solution.py
@@ -224,20 +224,20 @@
     return jnp.asarray(np.asarray(array, np.float32).astype(ml_dtypes.bfloat16))
 
 
-def forward_x_table(slabs):
+def forward_x_table(slabs, split):
     a = angles(KX, NX).reshape(slabs, KX // slabs, NX)
     trig = np.stack([np.cos(a), np.sin(a)])
-    table = np.einsum("tsjx,cd->tscjdx", trig, np.eye(2))
-    return table.reshape(2 * slabs * 2 * (KX // slabs), 2 * NX)
+    table = np.einsum("tsjx,cd->tscjdx", trig, np.eye(2)).reshape(-1, 2, NX // 8, 8)
+    if split:
+        table = table.transpose(0, 2, 1, 3)
+    return table.reshape(4 * KX, 2 * NX)
 
 
 def forward_y_table(planes):
     a = angles(KY, NY)
-    cos, sin = np.cos(a).T, np.sin(a).T
-    block = np.stack([np.stack([cos, -sin], 1), np.stack([-sin, -cos], 1)])
-    pick = np.eye(planes).reshape(planes // 2, 2, planes)
-    table = np.einsum("pqz,tyrk->pqtyzrk", pick, block)
-    return table.reshape(planes // 2, 4 * NY, planes * 2 * KY)
+    trig = np.stack([np.cos(a), np.sin(a)])
+    table = np.einsum("zw,tky->zywtk", np.eye(planes), trig)
+    return table.reshape(planes * NY, planes * 2 * KY)
 
 
 def forward_z_table():
@@ -256,20 +256,20 @@
     return table.reshape(2 * KY * KZ, NZ * 2 * KY)
 
 
-def inverse_y_table(planes):
+def inverse_y_table(planes, group):
     a = angles(KY, NY)
     cos, sin = np.cos(a), np.sin(a)
     block = np.stack([np.stack([cos, -sin], 1), np.stack([-sin, -cos], 1)])
-    pick = np.eye(planes).reshape(planes // 2, 2, planes)
+    pick = np.eye(planes).reshape(planes // group, group, planes)
     table = np.einsum("pqz,rkty->pzrktqy", pick, block)
-    return table.reshape(planes // 2, planes * 2 * KY, 4 * NY)
-
-
-def inverse_x_table(slabs):
+    return table.reshape(planes // group, planes * 2 * KY, 2 * group * NY)
+
+
+def inverse_x_table(slabs, group):
     a = angles(KX, NX).reshape(slabs, KX // slabs, NX)
     trig = np.stack([np.cos(a), np.sin(a)])
-    table = np.einsum("tsjx,cd->cxstdj", trig, np.eye(8))
-    return table.reshape(8 * NX, 2 * KX * 8)
+    table = np.einsum("tsjx,cd->cxstdj", trig, np.eye(group))
+    return table.reshape(group * NX, 2 * KX * group)
 
 
 def first_table(channels, depth):
@@ -282,6 +282,9 @@
     return table.reshape(channels * depth, channels * channels)
 
 
+LIGHT = pl.CostEstimate(flops=10**7, bytes_accessed=10**5, transcendentals=0)
+
+
 def dot(a, b):
     return jnp.dot(a, b, preferred_element_type=jnp.float32)
 
@@ -294,74 +297,61 @@
     return pltpu.CompilerParams(vmem_limit_bytes=58 * 2**20, **kw)
 
 
-def modes_step(load, x_table, y_table, rows, total, pair):
-    slabs = total.shape[0]
-    for i in range(rows.shape[3] // 8):
-        part = dot(x_table[...], load(i))
-        for t in range(2):
-            for s in range(slabs):
-                at = 8 * (t * slabs + s)
-                for q in range(2):
-                    rows[q, t, s, 8 * i : 8 * i + 8, :] = part[at : at + 8, q * NY : q * NY + NY]
-    for s in range(slabs):
-        left = [rows[q, t, s].astype(jnp.bfloat16) for q in range(2) for t in range(2)]
-        step = dot(jnp.concatenate(left, axis=1), y_table[0])
-        before = jnp.where(pair == 0, 0.0, total[s])
-        total[s] = before + step
-
-
-def store_rims(field, first, last, pair):
-    @pl.when(pair == 0)
-    def _():
-        first[:, 0] = field[:, 0]
-
-    @pl.when(pair == pl.num_programs(0) - 1)
-    def _():
-        last[:, 0] = field[:, 1]
-
-
-def forward_kernel(field, x_table, y_table, out, first, last, rows, total):
-    pair = pl.program_id(0)
-
-    def load(i):
-        halves = [field[2 * i : 2 * i + 2, q].reshape(2 * NX, NY) for q in range(2)]
-        return jnp.concatenate(halves, axis=1)
-
-    store_rims(field, first, last, pair)
-    modes_step(load, x_table, y_table, rows, total, pair)
-
-    @pl.when(pair == pl.num_programs(0) - 1)
-    def _():
-        out[...] = total[...].astype(jnp.bfloat16)
+def modes_of(left, y_table, x_table):
+    waves = dot(left, y_table[...]).astype(jnp.bfloat16)
+    both = dot(x_table[...], waves)
+    half = both.shape[0] // 2
+    lane = lax.broadcasted_iota(jnp.int32, (half, 128), 1)
+    real = (lane // KY) % 2 == 0
+    parts = []
+    for at in range(0, both.shape[1], 128):
+        cos = both[:half, at : at + 128]
+        sin = both[half:, at : at + 128]
+        other = jnp.where(real, pltpu.roll(sin, 128 - KY, axis=1), pltpu.roll(sin, KY, axis=1))
+        parts.append(jnp.where(real, cos, -cos) - other)
+    return jnp.concatenate(parts, axis=1)
+
+
+def store_modes(out, at, first, second):
+    rows = first.shape[0] // out.shape[0]
+    for s in range(out.shape[0]):
+        here = slice(s * rows, (s + 1) * rows)
+        both = jnp.concatenate([first[here], second[here]], axis=0)
+        out[s, pl.ds(at, 2 * rows), :] = both.astype(jnp.bfloat16)
+
+
+def forward_kernel(field, x_table, y_table, out, first, last):
+    step = pl.program_id(0)
+    planes = field.shape[1]
+    first[:, 0] = field[:, 0]
+    last[:, 0] = field[:, planes - 1]
+    modes = []
+    for i in range(2):
+        sheets = [field[2 * i : 2 * i + 2, z].reshape(2 * NX, NY) for z in range(planes)]
+        modes.append(modes_of(jnp.concatenate(sheets, axis=1), y_table, x_table))
+    store_modes(out, pl.multiple_of(16 * step, 16), *modes)
 
 
 def forward_modes(field, slabs):
     channels, planes = field.shape[:2]
     lines = channels * (KX // slabs)
-    x_table = constant(forward_x_table(slabs))
+    x_table = constant(forward_x_table(slabs, False))
     y_table = constant(forward_y_table(planes))
     shape = (slabs, lines, planes * 2 * KY)
-    rim = (channels, 1, NX, NY)
+    rim = pl.BlockSpec((4, 1, NX, NY), lambda c: (c, 0, 0, 0))
+    rims = jax.ShapeDtypeStruct((channels, 1, NX, NY), jnp.bfloat16)
     return pl.pallas_call(
         forward_kernel,
-        grid=(planes // 2,),
+        grid=(channels // 4,),
         in_specs=[
-            pl.BlockSpec((channels, 2, NX, NY), lambda p: (0, p, 0, 0)),
+            pl.BlockSpec((4, planes, NX, NY), lambda c: (c, 0, 0, 0)),
             whole(x_table.shape),
-            pl.BlockSpec((1,) + y_table.shape[1:], lambda p: (p, 0, 0)),
+            whole(y_table.shape),
         ],
-        out_specs=[whole(shape), whole(rim), whole(rim)],
-        out_shape=[
-            jax.ShapeDtypeStruct(shape, jnp.bfloat16),
-            jax.ShapeDtypeStruct(rim, jnp.bfloat16),
-            jax.ShapeDtypeStruct(rim, jnp.bfloat16),
-        ],
-        scratch_shapes=[
-            pltpu.VMEM((2, 2, slabs, lines, NY), jnp.float32),
-            pltpu.VMEM(shape, jnp.float32),
-        ],
+        out_specs=[whole(shape), rim, rim],
+        out_shape=[jax.ShapeDtypeStruct(shape, jnp.bfloat16), rims, rims],
         compiler_params=params(),
-        cost_estimate=pl.CostEstimate(flops=10**10, bytes_accessed=10**7, transcendentals=0),
+        cost_estimate=LIGHT,
         name="forward_modes",
     )(field, x_table, y_table)
 
@@ -458,22 +448,9 @@
         out_shape=[jax.ShapeDtypeStruct(out, jnp.bfloat16) for out in outs],
         scratch_shapes=scratch,
         compiler_params=params(),
-        cost_estimate=pl.CostEstimate(flops=4 * 10**9, bytes_accessed=10**7, transcendentals=0),
+        cost_estimate=LIGHT,
         name="mix_back" if adjoint else "mix",
     )(*operands)
-
-
-def inverse_step(planar, x_table, y_table, waves, store):
-    slabs = planar.shape[0]
-    for s in range(slabs):
-        step = dot(planar[s], y_table[0]).astype(jnp.bfloat16)
-        for t in range(2):
-            waves[s, t] = step[:, 2 * NY * t : 2 * NY * (t + 1)]
-    group = 8 * (KX // slabs)
-    for g in range(planar.shape[1] // group):
-        right = [waves[s, t, g * group : (g + 1) * group, :] for s in range(slabs) for t in range(2)]
-        step = dot(x_table[...], jnp.concatenate(right, axis=0))
-        store(g, step.reshape(8, NX, 2 * NY))
 
 
 def plane_mobility(grains):
@@ -490,15 +467,17 @@
 
 
 def layer_kernel(bias, planar, smooth, cotangent, grains, point_weight, repeat, ix_table, iy_table,
-                 x_table, y_table, spread, out, first, last, waves, spectral, moving, delta, rows,
-                 total, bias_wide, mix_out, mix_in):
+                 x_table, y_table, spread, out, first, last, waves, spectral, moving, delta,
+                 bias_wide, mix_out, mix_in):
     pair = pl.program_id(0)
-    channels = smooth.shape[0]
+    pairs = delta.shape[0]
+    channels = cotangent.shape[0]
+    slabs = planar.shape[0]
 
     @pl.when(pair == 0)
     def _():
         for c in range(channels):
-            bias_wide[c] = jnp.full(bias_wide.shape[1:], bias[c], jnp.float32)
+            bias_wide[c] = jnp.full(bias_wide.shape[1:], 0.5 * bias[c], jnp.float32)
         tall = dot(repeat[...], point_weight[...]).astype(jnp.bfloat16)
         square = lax.dot_general(
             tall, repeat[...], (((1,), (1,)), ((), ())), preferred_element_type=jnp.float32
@@ -509,87 +488,85 @@
         mix_in[...] = square.astype(jnp.bfloat16)
         mix_out[...] = square.T.astype(jnp.bfloat16)
 
-    def store(g, value):
-        spectral[8 * g : 8 * g + 8] = value
-
-    inverse_step(planar, ix_table, iy_table, waves, store)
+    for s in range(slabs):
+        step = dot(planar[s], iy_table[0]).astype(jnp.bfloat16)
+        for t in range(2):
+            waves[s, t] = step[:, 2 * NY * t : 2 * NY * (t + 1)]
+    group = 8 * (KX // slabs)
+    for g in range(channels // 8):
+        right = [waves[s, t, g * group : (g + 1) * group, :] for s in range(slabs) for t in range(2)]
+        step = dot(ix_table[...], jnp.concatenate(right, axis=0))
+        spectral[8 * g : 8 * g + 8] = step.reshape(8, NX, 2 * NY)
     for q in range(2):
-        moving[:, q * NY : (q + 1) * NY] = plane_mobility(grains[q])
-
-    def wide(ref, x):
-        halves = [ref[:, q, pl.ds(x, 16), :] for q in range(2)]
-        return jnp.concatenate(halves, axis=2).astype(jnp.float32)
+        moving[:, q * NY : (q + 1) * NY] = 0.5 * plane_mobility(grains[q])
 
     def body(i, _):
         x = pl.multiple_of(16 * i, 16)
-        smooth_here = wide(smooth, x)
-        cotangent_here = wide(cotangent, x)
-        deltas = []
+        halves = [cotangent[:, q, pl.ds(x, 16), :] for q in range(2)]
+        cotangent_here = jnp.concatenate(halves, axis=2).astype(jnp.float32)
         spreads = []
         for h in range(2):
             at = pl.ds(pl.multiple_of(x + 8 * h, 8), 8)
             mobile = moving[at, :][None]
-            right = smooth_here[:, 8 * h : 8 * h + 8, :].reshape(8 * channels, 2 * NY)
-            local = dot(mix_out[...], right.astype(jnp.bfloat16)).reshape(channels, 8, 2 * NY)
-            pre = spectral[:, at, :] + mobile * local + bias_wide[...]
-            gate = 0.5 * jnp.tanh(0.5 * pre) + 0.5
-            slope = gate * (1.0 + pre * (1.0 - gate))
+            local = dot(mix_out[...], smooth[0, 2 * i + h]).reshape(channels, 8, 2 * NY)
+            half = spectral[:, at, :] + mobile * local + bias_wide[...]
+            wave = jnp.tanh(half)
+            slope = (1.0 + wave) * (1.0 + (half - half * wave))
             change = cotangent_here[:, 8 * h : 8 * h + 8, :] * slope
-            deltas.append(change)
             right = change.reshape(8 * channels, 2 * NY).astype(jnp.bfloat16)
+            delta[pair, 2 * i + h] = right
             back = dot(mix_in[...], right).reshape(channels, 8, 2 * NY)
             spreads.append(mobile * back)
-        delta[:, pl.ds(x, 16), :] = jnp.concatenate(deltas, axis=1).astype(jnp.bfloat16)
         both = jnp.concatenate(spreads, axis=1).astype(jnp.bfloat16)
         for q in range(2):
             spread[:, q, pl.ds(x, 16), :] = both[:, :, q * NY : (q + 1) * NY]
         return 0
 
-    lax.fori_loop(0, NX // 16, body, 0, unroll=2)
-    store_rims(spread, first, last, pair)
-
-    def load(i):
-        return delta[2 * i : 2 * i + 2].reshape(2 * NX, 2 * NY)
-
-    modes_step(load, x_table, y_table, rows, total, pair)
-
-    @pl.when(pair == pl.num_programs(0) - 1)
+    lax.fori_loop(0, NX // 16, body, 0, unroll=4)
+
+    @pl.when(pair == 0)
     def _():
-        out[...] = total[...].astype(jnp.bfloat16)
+        first[:, 0] = spread[:, 0]
+
+    @pl.when(pair == pairs - 1)
+    def _():
+        last[:, 0] = spread[:, 1]
+        for step in range(channels // 4):
+            modes = []
+            for i in range(2):
+                here = slice(32 * step + 16 * i, 32 * step + 16 * i + 16)
+                sheets = [delta[p, :, here, :].reshape(2 * NX, 2 * NY) for p in range(pairs)]
+                modes.append(modes_of(jnp.concatenate(sheets, axis=1), y_table, x_table))
+            store_modes(out, 16 * step, *modes)
 
 
 def layer(planar, smooth, cotangent, grains, bias, point_weight):
     slabs, lines, width = planar.shape
-    channels, planes = smooth.shape[:2]
+    channels, planes = cotangent.shape[:2]
+    pairs = planes // 2
     repeat = constant(np.repeat(np.eye(channels), 8, axis=0))
-    tables = [
-        constant(inverse_x_table(slabs)),
-        constant(inverse_y_table(planes)),
-        constant(forward_x_table(slabs)),
-        constant(forward_y_table(planes)),
-    ]
-
-    def paired(shape):
-        return pl.BlockSpec((1,) + shape[1:], lambda p: (p, 0, 0))
-
+    ix_table = constant(inverse_x_table(slabs, 8))
+    iy_table = constant(inverse_y_table(planes, 2))
+    x_table = constant(forward_x_table(slabs, True))
+    y_table = constant(forward_y_table(planes))
     field = pl.BlockSpec((channels, 2, NX, NY), lambda p: (0, p, 0, 0))
     rim = (channels, 1, NX, NY)
-    outs = [smooth.shape, planar.shape, rim, rim]
+    outs = [cotangent.shape, planar.shape, rim, rim]
     return pl.pallas_call(
         layer_kernel,
-        grid=(planes // 2,),
+        grid=(pairs,),
         in_specs=[
             pl.BlockSpec(memory_space=pltpu.SMEM),
             whole(planar.shape),
-            field,
+            pl.BlockSpec((1,) + smooth.shape[1:], lambda p: (kept(p, pairs), 0, 0, 0)),
             field,
             pl.BlockSpec((2, NX, NY), lambda p: (p, 0, 0)),
             whole(point_weight.shape),
             whole(repeat.shape),
-            whole(tables[0].shape),
-            paired(tables[1].shape),
-            whole(tables[2].shape),
-            paired(tables[3].shape),
+            whole(ix_table.shape),
+            pl.BlockSpec((1,) + iy_table.shape[1:], lambda p: (p, 0, 0)),
+            whole(x_table.shape),
+            whole(y_table.shape),
         ],
         out_specs=[field, whole(planar.shape), whole(rim), whole(rim)],
         out_shape=[jax.ShapeDtypeStruct(out, jnp.bfloat16) for out in outs],
@@ -597,124 +574,195 @@
             pltpu.VMEM((slabs, 2, lines, 2 * NY), jnp.bfloat16),
             pltpu.VMEM((channels, NX, 2 * NY), jnp.float32),
             pltpu.VMEM((NX, 2 * NY), jnp.float32),
-            pltpu.VMEM((channels, NX, 2 * NY), jnp.bfloat16),
-            pltpu.VMEM((2, 2, slabs, lines, NY), jnp.float32),
-            pltpu.VMEM(planar.shape, jnp.float32),
+            pltpu.VMEM((pairs, NX // 8, 8 * channels, 2 * NY), jnp.bfloat16),
             pltpu.VMEM((channels, 8, 2 * NY), jnp.float32),
             pltpu.VMEM((8 * channels, 8 * channels), jnp.bfloat16),
             pltpu.VMEM((8 * channels, 8 * channels), jnp.bfloat16),
         ],
         compiler_params=params(),
-        cost_estimate=pl.CostEstimate(flops=3 * 10**10, bytes_accessed=3 * 10**7, transcendentals=4 * 10**6),
+        cost_estimate=LIGHT,
         name="layer",
-    )(bias, planar, smooth, cotangent, grains, point_weight, repeat, *tables)
-
-
-def finish_kernel(planar, near, ix_table, iy_table, out, waves):
-    def store(g, value):
-        for q in range(2):
-            here = slice(8 * g, 8 * g + 8)
-            total = value[:, :, q * NY : (q + 1) * NY] + near[here, q].astype(jnp.float32)
-            out[here, q] = total.astype(jnp.bfloat16)
-
-    inverse_step(planar, ix_table, iy_table, waves, store)
-
-
-def finish(planar, near):
-    slabs, lines, width = planar.shape
-    channels, planes = near.shape[:2]
-    ix_table = constant(inverse_x_table(slabs))
-    iy_table = constant(inverse_y_table(planes))
-    field = pl.BlockSpec((channels, 2, NX, NY), lambda p: (0, p, 0, 0))
-    return pl.pallas_call(
-        finish_kernel,
-        grid=(planes // 2,),
-        in_specs=[
-            whole(planar.shape),
-            field,
-            whole(ix_table.shape),
-            pl.BlockSpec((1,) + iy_table.shape[1:], lambda p: (p, 0, 0)),
-        ],
-        out_specs=field,
-        out_shape=jax.ShapeDtypeStruct(near.shape, jnp.bfloat16),
-        scratch_shapes=[pltpu.VMEM((slabs, 2, lines, 2 * NY), jnp.bfloat16)],
-        compiler_params=params(),
-        cost_estimate=pl.CostEstimate(flops=10**10, bytes_accessed=2 * 10**7, transcendentals=0),
-        name="finish",
-    )(planar, near, ix_table, iy_table)
-
-
-def build_band(adjoint, taps, masks, channel, band):
-    blocks = masks.shape[1] // 16
+    )(bias, planar, smooth, cotangent, grains, point_weight, repeat, ix_table, iy_table, x_table,
+      y_table)
+
+
+def kept(pair, pairs):
+    return jnp.where(pair == 0, pairs - 2, jnp.where(pair == pairs - 1, pair, pair - 1))
+
+
+def build_band(adjoint, taps, channel, band):
+    row = lax.broadcasted_iota(jnp.int32, (8, NY), 0)
+    lane = lax.broadcasted_iota(jnp.int32, (8, NY), 1)
+    offset = row - lane
     for dz in range(3):
         for dx in range(3):
-            block = jnp.zeros((blocks, 16, NY), jnp.bfloat16)
+            tile = jnp.zeros((8, NY), jnp.float32)
             for dy in range(3):
                 number = 9 * dz + 3 * dx + dy
                 tap = taps[26 - number if adjoint else number, channel]
-                tap = jnp.full((16, NY), tap, jnp.float32).astype(jnp.bfloat16)
-                block = block + masks[dy].reshape(blocks, 16, NY) * tap[None]
-            block = block.reshape(NY, NY)
+                hit = (offset == dy - 1) | (offset == dy - 1 - NY)
+                tile = jnp.where(hit, tap, tile)
+            tiles = [pltpu.roll(tile, 8 * k, axis=1) if k > 0 else tile for k in range(NY // 8)]
+            tiles[0] = jnp.where((row == 0) & (lane == NY - 1), 0.0, tiles[0])
+            tiles[-1] = jnp.where((row == 7) & (lane == 0), 0.0, tiles[-1])
+            block = jnp.concatenate(tiles, axis=0).astype(jnp.bfloat16)
             for q in range(2):
                 down = (q + dz) * NY
                 right = (2 * dx + q) * NY
                 band[down : down + NY, right : right + NY] = block
 
 
-def apply_band(before, field, after, out, band, c):
-    planes = field.shape[1]
-    sheets = [before[c, 0]] + [field[c, z] for z in range(planes)] + [after[c, 0]]
-    pairs = range(planes // 2)
-    left = jnp.concatenate(
-        [jnp.concatenate(sheets[2 * p : 2 * p + 4], axis=1) for p in pairs], axis=0
-    )
+def apply_band(quads, band):
+    left = jnp.concatenate([jnp.concatenate(quad, axis=1) for quad in quads], axis=0)
     middle = dot(left, band[:, 2 * NY : 4 * NY])
     lower = dot(left, band[:, : 2 * NY])
     upper = dot(left, band[:, 4 * NY :])
     row = lax.broadcasted_iota(jnp.int32, (8, 2 * NY), 0)
-    for p in pairs:
+    totals = []
+    for p in range(len(quads)):
         here = slice(p * NX, (p + 1) * NX)
         down = pltpu.roll(lower[here], 1, axis=0)
         up = pltpu.roll(upper[here], NX - 1, axis=0)
         down = jnp.concatenate([jnp.where(row == 0, 0.0, down[:8]), down[8:]], axis=0)
         up = jnp.concatenate([up[:-8], jnp.where(row == 7, 0.0, up[-8:])], axis=0)
-        total = (middle[here] + down + up).astype(jnp.bfloat16)
-        out[c, 2 * p] = total[:, :NY]
-        out[c, 2 * p + 1] = total[:, NY:]
-
-
-def stencil_kernel(adjoint, taps, masks, before, field, after, out, even, odd):
+        totals.append(middle[here] + down + up)
+    return totals
+
+
+def banded(adjoint, taps, even, odd, channels):
     step = pl.program_id(0)
-    build = functools.partial(build_band, adjoint, taps, masks)
+    final = channels * pl.num_programs(0) - 1
+    bands = (even, odd)
 
     @pl.when(step == 0)
     def _():
         even[...] = jnp.zeros_like(even)
         odd[...] = jnp.zeros_like(odd)
-        build(0, even)
-
-    build(2 * step + 1, odd)
-    apply_band(before, field, after, out, even, 0)
-    build(jnp.minimum(2 * step + 2, 2 * pl.num_programs(0) - 1), even)
-    apply_band(before, field, after, out, odd, 1)
-
-
-def stencil_planes(before, field, after, taps, adjoint):
+        build_band(adjoint, taps, 0, even)
+
+    def run(visit):
+        for c in range(channels):
+            following = jnp.minimum(channels * step + c + 1, final)
+            build_band(adjoint, taps, following, bands[(c + 1) % 2])
+            visit(c, bands[c % 2])
+
+    return run
+
+
+def smooth_kernel(inner, taps, field, *refs):
+    if inner:
+        out, even, odd = refs
+    else:
+        _, before, after, out, even, odd = refs
+    planes = field.shape[1]
+    totals = []
+
+    def visit(c, band):
+        if inner:
+            quads = [[field[c, z + k] for k in range(4)] for z in range(1, planes - 3, 2)]
+        else:
+            low = [before[c, 0]] + [field[c, z] for z in range(3)]
+            high = [field[c, z] for z in range(planes - 3, planes)] + [after[c, 0]]
+            quads = [low, high]
+        totals.append(apply_band(quads, band))
+
+    banded(False, taps, even, odd, 2)(visit)
+    for p in range(len(totals[0])):
+        both = [totals[c][p].reshape(NX // 8, 8, 2 * NY) for c in range(2)]
+        out[p] = jnp.concatenate(both, axis=1).astype(jnp.bfloat16)
+
+
+def smooth_planes(field, taps, inner=None, rims=None):
     channels, planes = field.shape[:2]
-    masks = constant(np.stack([np.eye(NY, k=1 - dy) for dy in range(3)]))
-    rim = pl.BlockSpec((2, 1, NX, NY), lambda c: (c, 0, 0, 0))
-    sheets = pl.BlockSpec((2, planes, NX, NY), lambda c: (c, 0, 0, 0))
+    pairs = planes // 2
+    shape = (pairs, NX // 8, 8 * channels, 2 * NY)
+    in_specs = [
+        pl.BlockSpec(memory_space=pltpu.SMEM),
+        pl.BlockSpec((2, planes, NX, NY), lambda c: (c, 0, 0, 0)),
+    ]
+    operands = [taps, field]
+    place = 0
+    if inner is not None:
+        in_specs.append(pl.BlockSpec(memory_space=pl.ANY))
+        in_specs += [pl.BlockSpec((2, 1, NX, NY), lambda c: (c, 0, 0, 0))] * 2
+        operands += [inner, *rims]
+        place = 1
     return pl.pallas_call(
-        functools.partial(stencil_kernel, adjoint),
+        functools.partial(smooth_kernel, inner is None),
         grid=(channels // 2,),
-        in_specs=[pl.BlockSpec(memory_space=pltpu.SMEM), whole(masks.shape), rim, sheets, rim],
-        out_specs=sheets,
-        out_shape=jax.ShapeDtypeStruct(field.shape, jnp.bfloat16),
+        in_specs=in_specs,
+        out_specs=pl.BlockSpec((pairs // 2, NX // 8, 16, 2 * NY), lambda c: (place, 0, c, 0)),
+        out_shape=jax.ShapeDtypeStruct(shape, jnp.bfloat16),
+        input_output_aliases={} if inner is None else {2: 0},
         scratch_shapes=[pltpu.VMEM((4 * NY, 6 * NY), jnp.bfloat16) for _ in range(2)],
         compiler_params=params(),
-        cost_estimate=pl.CostEstimate(flops=2 * 10**10, bytes_accessed=2 * 10**7, transcendentals=0),
-        name="near" if adjoint else "smooth",
-    )(taps, masks, before, field, after)
+        cost_estimate=LIGHT,
+        name="smooth_inner" if inner is None else "smooth_outer",
+    )(*operands)
+
+
+def finish_kernel(taps, before, field, after, planar, ix_table, iy_table, out, waves, spectral,
+                  even, odd):
+    step = pl.program_id(0)
+    slabs = planar.shape[0]
+    planes = field.shape[1]
+    span = planes * NY
+
+    @pl.when(step == 0)
+    def _():
+        for s in range(slabs):
+            for t in range(2):
+                right = iy_table[0, :, t * span : (t + 1) * span]
+                waves[s, t] = dot(planar[s], right).astype(jnp.bfloat16)
+
+    rows = 4 * (KX // slabs)
+    here = pl.ds(pl.multiple_of(rows * step, rows), rows)
+    right = [waves[s, t, here, :] for s in range(slabs) for t in range(2)]
+    spectral[...] = dot(ix_table[...], jnp.concatenate(right, axis=0))
+
+    def visit(c, band):
+        sheets = [before[c, 0]] + [field[c, z] for z in range(planes)] + [after[c, 0]]
+        totals = apply_band([sheets[z : z + 4] for z in range(0, planes, 2)], band)
+        for p in range(planes // 2):
+            wide = slice(2 * p * NY, 2 * (p + 1) * NY)
+            total = (totals[p] + spectral[c * NX : (c + 1) * NX, wide]).astype(jnp.bfloat16)
+            out[c, 2 * p] = total[:, :NY]
+            out[c, 2 * p + 1] = total[:, NY:]
+
+    banded(True, taps, even, odd, 4)(visit)
+
+
+def finish(planar, spread, rims, taps):
+    slabs, lines, width = planar.shape
+    channels, planes = spread.shape[:2]
+    ix_table = constant(inverse_x_table(slabs, 4))
+    iy_table = constant(inverse_y_table(planes, planes))
+    rim = pl.BlockSpec((4, 1, NX, NY), lambda c: (c, 0, 0, 0))
+    sheets = pl.BlockSpec((4, planes, NX, NY), lambda c: (c, 0, 0, 0))
+    return pl.pallas_call(
+        finish_kernel,
+        grid=(channels // 4,),
+        in_specs=[
+            pl.BlockSpec(memory_space=pltpu.SMEM),
+            rim,
+            sheets,
+            rim,
+            whole(planar.shape),
+            whole(ix_table.shape),
+            whole(iy_table.shape),
+        ],
+        out_specs=sheets,
+        out_shape=jax.ShapeDtypeStruct(spread.shape, jnp.bfloat16),
+        scratch_shapes=[
+            pltpu.VMEM((slabs, 2, lines, planes * NY), jnp.bfloat16),
+            pltpu.VMEM((4 * NX, planes * NY), jnp.float32),
+            pltpu.VMEM((4 * NY, 6 * NY), jnp.bfloat16),
+            pltpu.VMEM((4 * NY, 6 * NY), jnp.bfloat16),
+        ],
+        compiler_params=params(),
+        cost_estimate=LIGHT,
+        name="finish",
+    )(taps, rims[0], spread, rims[1], planar, ix_table, iy_table)
 
 
 def gradient_kernel(depth, where, gathered, first, second, out):
@@ -762,7 +810,7 @@
         ),
         out_shape=jax.ShapeDtypeStruct((depth * half, width), jnp.float32),
         compiler_params=params(),
-        cost_estimate=pl.CostEstimate(flops=10**10, bytes_accessed=10**7, transcendentals=0),
+        cost_estimate=LIGHT,
         name="weight_gradient",
     )(where, gathered, first, second)
 
@@ -780,30 +828,32 @@
 
 def local_fast(feats, grains, spec_weight, taps, point_weight, bias, cotangent):
     slabs = lax.axis_size("slab")
+    copies = lax.axis_size("dp")
+    barrier = lax.optimization_barrier
     field = feats[0]
     channels = field.shape[0]
     cell_scale = 1.0 / math.sqrt(NX * NY * NZ)
     mode_scale = 1.0 / math.sqrt(KX * KY * KZ)
     mode_rows = spec_weight.shape[0]
     weight = spec_weight.reshape(mode_rows * KZ, 2 * channels * channels)
-    width = weight.shape[1] // lax.axis_size("dp")
+    width = weight.shape[1] // copies
 
     planar, first, last = forward_modes(field, slabs)
-    planar, first, last = lax.optimization_barrier((swap(planar), first, last))
-    before, after = neighbours(first, last)
-    spectrum, planar = mix(planar, weight, cell_scale, mode_scale)
+    rims = neighbours(first, last)
+    spectrum, planar = mix(swap(planar), weight, cell_scale, 0.5 * mode_scale)
+    planar, field = barrier((planar, field))
     planar = swap(planar)
-    smooth = stencil_planes(before, field, after, taps, False)
+    smooth = smooth_planes(field, taps)
+    smooth = smooth_planes(field, taps, smooth, rims)
+    planar, smooth = barrier((planar, smooth))
     spread, planar, first, last = layer(planar, smooth, cotangent[0], grains[0], bias, point_weight)
-    planar, first, last = lax.optimization_barrier((swap(planar), first, last))
-    before, after = neighbours(first, last)
-    copies = lax.axis_size("dp")
-    planar, send = mix(planar, weight, mode_scale, cell_scale, spectrum, copies)
+    rims = neighbours(first, last)
+    planar, send = mix(swap(planar), weight, 0.5 * mode_scale, cell_scale, spectrum, copies)
     planar = swap(planar)
     gathered = lax.all_to_all(send, "dp", split_axis=0, concat_axis=0)
-    near = stencil_planes(before, spread, after, taps, True)
-    grad_feats = finish(planar, near)[None]
     grad_spec = weight_gradient(gathered, KX // slabs, width, lax.axis_index("dp"))
+    planar, grad_spec = barrier((planar, grad_spec))
+    grad_feats = finish(planar, spread, rims, taps)[None]
     return (grad_feats, grad_spec.reshape(mode_rows, KZ, width))
 
 
@@ -814,7 +864,7 @@
         lax.axis_size("slab") * 4 == KX
         and samples == 1
         and channels == 32
-        and planes % 2 == 0
+        and planes == 8
         and channels * channels % width == 0
         and width % 128 == 0
     )

time: 192 us -> 209 us (1.089)
  blocking collectives: 27.7 us -> 44.3 us
  waiting for transfers between devices: 28.4 us -> 19.3 us
  Pallas kernels: 110 us -> 117 us
    ppermute x4, waiting for transfers between devices: 20 us -> 0.01 us  [neighbours(): return (lax.ppermute(last, 'slab', up), lax.ppermute(first, 'slab', down))]
    all_to_all x2, blocking collectives: 27.7 us -> 44.3 us  [swap(): return lax.all_to_all(planar, 'slab', split_axis=0, concat_axis=0)]
    all_to_all x2, waiting for transfers between devices: 0.01 us -> 9.25 us  [swap(): return lax.all_to_all(planar, 'slab', split_axis=0, concat_axis=0)]
    pallas_call x5, Pallas kernels: 85.8 us -> 93.4 us  [the longest x2 32.1 us: smooth_planes(): pl.pallas_call(functools.partial(smooth_kernel, inner is None), grid=(cha...]
  transfers between devices with their start and end apart: 7 -> 7, of which waited for: 5 -> 2; matrix products, arithmetic and copies ran while one was open for 0% -> 0% of each run, Pallas kernels for 30% -> 23%
where the time goes in v4:
time: 209 us; the launch traced here: 208 us
  Pallas kernels  117 us (56%)
  blocking collectives  44.3 us (21%)
  starting transfers between devices  21.2 us (10%)
  waiting for transfers between devices  19.3 us (9%)
  local copies, waits for them, and re-layouts  4.14 us (2%)
    all_to_all x2, blocking collectives, swap(): return lax.all_to_all(planar, 'slab', split_axis=0, concat_axis=0)  44.3 us
    pallas_call x2, Pallas kernels, smooth_planes(): pl.pallas_call(functools.partial(smooth_kernel, inner is None), grid=(cha...  32.1 us
    pallas_call x1, Pallas kernels, layer(): pl.pallas_call(layer_kernel, grid=(pairs,), in_specs=[pl.BlockSpec(memory...  27.6 us
    pallas_call x1, Pallas kernels, finish(): pl.pallas_call(finish_kernel, grid=(channels // 4,), in_specs=[pl.BlockSp...  22.4 us
    pallas_call x2, Pallas kernels, mix(): pl.pallas_call(functools.partial(mixing_kernel, scale_in, scale_out, adjo...  16.2 us
    pallas_call x1, Pallas kernels, forward_modes(): pl.pallas_call(forward_kernel, grid=(channels // 4,), in_specs=[pl.BlockS...  11.2 us
    ppermute x4, starting transfers between devices, neighbours(): return (lax.ppermute(last, 'slab', up), lax.ppermute(first, 'slab', down))  10.7 us
    all_to_all x1, waiting for transfers between devices, local_fast(): gathered = lax.all_to_all(send, 'dp', split_axis=0, concat_axis=0)  10 us
  transfers between devices with their start and end apart: 7, of which 2 were waited for; matrix products, arithmetic and copies ran while one was open for 0% of the time, Pallas kernels for 23%

profile of v4, /device:TPU:0, one launch (start us, length us, event | category | flops | bytes accessed | tf_op | source)
XLA Modules:
  0.0 207.7 jit_solution(3869456349301814850)
XLA Ops:
  0.6 11.2 %forward_modes.1 = (bf16[4,128,256]{2,1,0:T(8,128)(2,1)}, bf16[32,1,128,128]{3,2,1,0:T(8,128)(2,1)}, bf16[32,1,128,128]{3,2,1,0:T(8,128)(2,1)}) custom-call(bf16[32,8,128,128]{3,2,1,0:T(8,128)(2,1)} %bitcast.8, bf16[64,256]{1,0:T(8,128)(2,1)} %constant.61.clone.x_table, bf16[1024,256]{1,0:T(8,128)(2,1)} %constant.62.clone.y_table), custom_call_target="tpu_custom_call" | custom-call | flops 10000000 | bytes 100000 | tf_op jit(solution)/shard_map/forward_modes/pallas_call | solution.py:343
  11.8 5.0 %collective-permute-start = (bf16[32,1,128,128]{3,2,1,0:T(8,128)(2,1)}, bf16[32,1,128,128]{3,2,1,0:T(8,128)(2,1)S(1)}, u32[]{:S(2)}, u32[]{:S(2)}) collective-permute-start(bf16[32,1,128,128]{3,2,1,0:T(8,128)(2,1)} %get-tuple-element.23), channel_id=1, source_target_pairs={{0,1},{1,2},{2,3},{4,5},{5,6},{6,7},{8,9},{9,10},{10,11},{12,13},{... | collective-permute-start | bytes 3145736 | tf_op jit(solution)/shard_map/ppermute | solution.py:822
  16.8 1.3 collective-permute-start.1
  18.1 32.1 %all_to_all.25.planar = bf16[4,128,256]{2,1,0:T(8,128)(2,1)} all-to-all(bf16[4,128,256]{2,1,0:T(8,128)(2,1)} %get-tuple-element.19), channel_id=1, replica_groups=mesh['grp'=2,'dp'=4,'slab'=4] {'slab'}, dimensions={0} | all-to-all | bytes 524288 | tf_op jit(solution)/shard_map/all_to_all | solution.py:826
  50.2 7.9 %mix.1 = (bf16[512,128]{1,0:T(8,128)(2,1)}, bf16[4,128,256]{2,1,0:T(8,128)(2,1)}) custom-call(bf16[4,128,256]{2,1,0:T(8,128)(2,1)} %all_to_all.25.planar, bf16[1024,2048]{1,0:T(8,128)(2,1)} %bitcast.11, bf16[1024,512]{1,0:T(8,128)(2,1)} %constant.63.clone.z_in, bf16[512,1024]{1,0:T(8,128)(2,1)} %constant.64.clone.z_out, ...), custom_call_target="tpu_custom_call" | custom-call | flops 10000000 | bytes 100000 | tf_op jit(solution)/shard_map/mix/pallas_call | solution.py:443
  58.2 3.4 %all-to-all-start.1 = ((bf16[4,128,256]{2,1,0:T(8,128)(2,1)}), bf16[4,128,256]{2,1,0:T(8,128)(2,1)S(1)}, u32[]{:S(2)}, u32[]{:S(2)}) async-start(bf16[4,128,256]{2,1,0:T(8,128)(2,1)} %get-tuple-element.21), calls=%async_computation.1 | async-start | bytes 524288 | tf_op jit(solution)/shard_map/all_to_all | solution.py:826
  61.6 15.9 %smooth_inner.1.refs_0_ = bf16[4,16,256,256]{3,2,1,0:T(8,128)(2,1)} custom-call(f32[27,32]{1,0:T(8,128)} %taps.5, bf16[32,8,128,128]{3,2,1,0:T(8,128)(2,1)} %bitcast.9), custom_call_target="tpu_custom_call" | custom-call | flops 10000000 | bytes 100000 | tf_op jit(solution)/shard_map/smooth_inner/pallas_call | solution.py:690
  77.5 0.0 collective-permute-done.refs_1_
  77.5 0.0 copy-start.5
  77.5 0.0 collective-permute-done.1.refs_2_
  77.5 1.0 copy-done.5
  78.5 0.0 copy-start.6
  78.5 1.0 copy-done.6
  79.5 16.2 %smooth_outer.1.smooth = bf16[4,16,256,256]{3,2,1,0:T(8,128)(2,1)} custom-call(f32[27,32]{1,0:T(8,128)} %taps.5, bf16[32,8,128,128]{3,2,1,0:T(8,128)(2,1)} %bitcast.10, bf16[4,16,256,256]{3,2,1,0:T(8,128)(2,1)} %smooth_inner.1.refs_0_, bf16[32,1,128,128]{3,2,1,0:T(8,128)(2,1)} %copy-done.5, ...), custom_call_target="tpu_custom_call", output_to_operand_aliasing={{}: (2, {})} | custom-call | flops 10000000 | bytes 100000 | tf_op jit(solution)/shard_map/smooth_outer/pallas_call | solution.py:690
  95.7 0.0 all-to-all-done.1.planar
  95.7 0.0 copy-start.2
  95.7 0.7 copy-done.2
  96.4 27.6 %layer.1 = (bf16[32,8,128,128]{3,2,1,0:T(8,128)(2,1)}, bf16[4,128,256]{2,1,0:T(8,128)(2,1)}, bf16[32,1,128,128]{3,2,1,0:T(8,128)(2,1)}, bf16[32,1,128,128]{3,2,1,0:T(8,128)(2,1)}) custom-call(f32[32]{0:T(128)} %bias.1, bf16[4,128,256]{2,1,0:T(8,128)(2,1)} %copy-done.2, bf16[4,16,256,256]{3,2,1,0:T(8,128)(2,1)} %smooth_outer.1.smooth, ...), custom_call_target="tpu_custom_call" | custom-call | flops 10000000 | bytes 100000 | tf_op jit(solution)/shard_map/layer/pallas_call | solution.py:555
  124.0 12.3 %all_to_all.26.planar = bf16[4,128,256]{2,1,0:T(8,128)(2,1)} all-to-all(bf16[4,128,256]{2,1,0:T(8,128)(2,1)} %get-tuple-element.30), channel_id=1, replica_groups=mesh['grp'=2,'dp'=4,'slab'=4] {'slab'}, dimensions={0} | all-to-all | bytes 524288 | tf_op jit(solution)/shard_map/all_to_all | solution.py:826
  136.3 8.3 %mix_back.1 = (bf16[4,128,256]{2,1,0:T(8,128)(2,1)}, bf16[4,1024,128]{2,1,0:T(8,128)(2,1)}) custom-call(bf16[4,128,256]{2,1,0:T(8,128)(2,1)} %all_to_all.26.planar, bf16[1024,2048]{1,0:T(8,128)(2,1)} %bitcast.12, bf16[1024,512]{1,0:T(8,128)(2,1)} %constant.63.clone.z_in, bf16[512,1024]{1,0:T(8,128)(2,1)} %constant.64.clone.z_out, ...), custom_call_target="tpu_custom_call" | custom-call | flops 10000000 | bytes 100000 | tf_op jit(solution)/shard_map/mix_back/pallas_call | solution.py:443
  144.5 3.5 %all-to-all-start.4 = ((bf16[4,1024,128]{2,1,0:T(8,128)(2,1)}), bf16[4,1024,128]{2,1,0:T(8,128)(2,1)S(1)}, u32[]{:S(2)}, u32[]{:S(2)}) async-start(bf16[4,1024,128]{2,1,0:T(8,128)(2,1)} %get-tuple-element.33), calls=%async_computation.4 | async-start | bytes 2097152 | tf_op jit(solution)/shard_map/all_to_all | solution.py:853
  148.0 3.1 %collective-permute-start.2 = (bf16[32,1,128,128]{3,2,1,0:T(8,128)(2,1)}, bf16[32,1,128,128]{3,2,1,0:T(8,128)(2,1)S(1)}, u32[]{:S(2)}, u32[]{:S(2)}) collective-permute-start(bf16[32,1,128,128]{3,2,1,0:T(8,128)(2,1)} %get-tuple-element.27), channel_id=1, source_target_pairs={{0,1},{1,2},{2,3},{4,5},{5,6},{6,7},{8,9},{9,10},{10,11},{12,13},{... | collective-permute-start | bytes 3145736 | tf_op jit(solution)/shard_map/ppermute | solution.py:822
  151.1 1.3 collective-permute-start.3
  152.4 10.0 %all-to-all-done.4.gathered = bf16[4,1024,128]{2,1,0:T(8,128)(2,1)S(1)} async-done(((bf16[4,1024,128]{2,1,0:T(8,128)(2,1)}), bf16[4,1024,128]{2,1,0:T(8,128)(2,1)S(1)}, u32[]{:S(2)}, u32[]{:S(2)}) %all-to-all-start.4) | async-done | bytes 1048608 | tf_op jit(solution)/shard_map/all_to_all | solution.py:853
  162.5 0.0 copy-start
  162.5 3.6 %all-to-all-start.3 = ((bf16[4,128,256]{2,1,0:T(8,128)(2,1)}), bf16[4,128,256]{2,1,0:T(8,128)(2,1)S(1)}, u32[]{:S(2)}, u32[]{:S(2)}) async-start(bf16[4,128,256]{2,1,0:T(8,128)(2,1)} %get-tuple-element.32), calls=%async_computation.3 | async-start | bytes 524288 | tf_op jit(solution)/shard_map/all_to_all | solution.py:826
  166.1 0.6 pad_add_fusion.where
  166.7 0.0 copy-done
  166.7 7.8 %weight_gradient.1 = f32[1024,512]{1,0:T(8,128)} custom-call(s32[2]{0:T(128)} %pad_add_fusion.where, bf16[4,1024,128]{2,1,0:T(8,128)(2,1)} %copy-done, bf16[2,128,512]{2,1,0:T(8,128)(2,1)} %constant.73.clone.first, bf16[128,512]{1,0:T(8,128)(2,1)} %constant.74.clone.second), custom_call_target="tpu_custom_call" | custom-call | flops 10000000 | bytes 100000 | tf_op jit(solution)/shard_map/weight_gradient/pallas_call | solution.py:799
  174.5 9.3 %all-to-all-done.3.planar = bf16[4,128,256]{2,1,0:T(8,128)(2,1)S(1)} async-done(((bf16[4,128,256]{2,1,0:T(8,128)(2,1)}), bf16[4,128,256]{2,1,0:T(8,128)(2,1)S(1)}, u32[]{:S(2)}, u32[]{:S(2)}) %all-to-all-start.3) | async-done | bytes 262176 | tf_op jit(solution)/shard_map/all_to_all | solution.py:826
  183.8 0.0 copy-start.1
  183.8 0.0 collective-permute-done.2.before
  183.8 0.0 copy-start.3
  183.8 0.0 collective-permute-done.3.after
  183.8 0.0 copy-start.4
  183.8 0.7 copy-done.1
  184.5 0.4 copy-done.3
  184.8 0.4 copy-done.4
  185.3 22.4 %finish.1 = bf16[32,8,128,128]{3,2,1,0:T(8,128)(2,1)} custom-call(f32[27,32]{1,0:T(8,128)} %taps.5, bf16[32,1,128,128]{3,2,1,0:T(8,128)(2,1)} %copy-done.3, bf16[32,8,128,128]{3,2,1,0:T(8,128)(2,1)} %get-tuple-element.28.field, bf16[32,1,128,128]{3,2,1,0:T(8,128)(2,1)} %copy-done.4, bf16[4,128,256]{2,1,0:T(8,128)(2,1)} %copy-done.1, ...), custom_call_target="tpu_custom_call" | custom-call | flops 10000000 | bytes 100000 | tf_op jit(solution)/shard_map/finish/pallas_call | solution.py:742
Async XLA Ops:
  11.8 65.7 %collective-permute-start = (bf16[32,1,128,128]{3,2,1,0:T(8,128)(2,1)}, bf16[32,1,128,128]{3,2,1,0:T(8,128)(2,1)S(1)}, u32[]{:S(2)}, u32[]{:S(2)}) collective-permute-start(bf16[32,1,128,128]{3,2,1,0:T(8,128)(2,1)} %get-tuple-element.23), channel_id=1, source_target_pairs={{0,1},{1,2},{2,3},{4,5},{5,6},{6,7},{8,9},{9,10},{10,11},{12,13},{... | collective-permute-start | bytes 3145736 | tf_op jit(solution)/shard_map/ppermute | solution.py:822
  16.8 60.7 %collective-permute-start.1 = (bf16[32,1,128,128]{3,2,1,0:T(8,128)(2,1)}, bf16[32,1,128,128]{3,2,1,0:T(8,128)(2,1)S(1)}, u32[]{:S(2)}, u32[]{:S(2)}) collective-permute-start(bf16[32,1,128,128]{3,2,1,0:T(8,128)(2,1)} %get-tuple-element.24), channel_id=1, source_target_pairs={{1,0},{2,1},{3,2},{5,4},{6,5},{7,6},{9,8},{10,9},{11,10},{13,12},{... | collective-permute-start | bytes 3145736 | tf_op jit(solution)/shard_map/ppermute | solution.py:822
  58.2 37.5 %all-to-all-start.1 = ((bf16[4,128,256]{2,1,0:T(8,128)(2,1)}), bf16[4,128,256]{2,1,0:T(8,128)(2,1)S(1)}, u32[]{:S(2)}, u32[]{:S(2)}) async-start(bf16[4,128,256]{2,1,0:T(8,128)(2,1)} %get-tuple-element.21), calls=%async_computation.1 | async-start | bytes 524288 | tf_op jit(solution)/shard_map/all_to_all | solution.py:826
  77.5 1.0 copy-start.5
  78.5 1.0 copy-start.6
  95.7 0.7 copy-start.2
  144.5 18.0 %all-to-all-start.4 = ((bf16[4,1024,128]{2,1,0:T(8,128)(2,1)}), bf16[4,1024,128]{2,1,0:T(8,128)(2,1)S(1)}, u32[]{:S(2)}, u32[]{:S(2)}) async-start(bf16[4,1024,128]{2,1,0:T(8,128)(2,1)} %get-tuple-element.33), calls=%async_computation.4 | async-start | bytes 2097152 | tf_op jit(solution)/shard_map/all_to_all | solution.py:853
  148.0 35.7 %collective-permute-start.2 = (bf16[32,1,128,128]{3,2,1,0:T(8,128)(2,1)}, bf16[32,1,128,128]{3,2,1,0:T(8,128)(2,1)S(1)}, u32[]{:S(2)}, u32[]{:S(2)}) collective-permute-start(bf16[32,1,128,128]{3,2,1,0:T(8,128)(2,1)} %get-tuple-element.27), channel_id=1, source_target_pairs={{0,1},{1,2},{2,3},{4,5},{5,6},{6,7},{8,9},{9,10},{10,11},{12,13},{... | collective-permute-start | bytes 3145736 | tf_op jit(solution)/shard_map/ppermute | solution.py:822
  151.1 32.6 %collective-permute-start.3 = (bf16[32,1,128,128]{3,2,1,0:T(8,128)(2,1)}, bf16[32,1,128,128]{3,2,1,0:T(8,128)(2,1)S(1)}, u32[]{:S(2)}, u32[]{:S(2)}) collective-permute-start(bf16[32,1,128,128]{3,2,1,0:T(8,128)(2,1)} %get-tuple-element.29), channel_id=1, source_target_pairs={{1,0},{2,1},{3,2},{5,4},{6,5},{7,6},{9,8},{10,9},{11,10},{13,12},{... | collective-permute-start | bytes 3145736 | tf_op jit(solution)/shard_map/ppermute | solution.py:822
  162.5 4.2 %copy-start = (bf16[4,1024,128]{2,1,0:T(8,128)(2,1)}, bf16[4,1024,128]{2,1,0:T(8,128)(2,1)S(1)}, u32[]{:S(2)}) copy-start(bf16[4,1024,128]{2,1,0:T(8,128)(2,1)S(1)} %all-to-all-done.4.gathered) | copy-start | bytes 3145732
  162.5 21.3 %all-to-all-start.3 = ((bf16[4,128,256]{2,1,0:T(8,128)(2,1)}), bf16[4,128,256]{2,1,0:T(8,128)(2,1)S(1)}, u32[]{:S(2)}, u32[]{:S(2)}) async-start(bf16[4,128,256]{2,1,0:T(8,128)(2,1)} %get-tuple-element.32), calls=%async_computation.3 | async-start | bytes 524288 | tf_op jit(solution)/shard_map/all_to_all | solution.py:826
  183.8 0.7 copy-start.1
  183.8 1.1 copy-start.3
  183.8 1.5 copy-start.4

commit v5 on v4

--- a/solution.py
+++ b/solution.py
@@ -235,9 +235,11 @@
 
 def forward_y_table(planes):
     a = angles(KY, NY)
-    trig = np.stack([np.cos(a), np.sin(a)])
-    table = np.einsum("zw,tky->zywtk", np.eye(planes), trig)
-    return table.reshape(planes * NY, planes * 2 * KY)
+    cos, sin = np.cos(a).T, np.sin(a).T
+    block = np.stack([np.stack([cos, -sin], 1), np.stack([-sin, -cos], 1)])
+    pick = np.eye(planes).reshape(planes // 2, 2, planes)
+    table = np.einsum("pqz,tyrk->ptqyzrk", pick, block)
+    return table.reshape(planes * 2 * NY, planes * 2 * KY)
 
 
 def forward_z_table():
@@ -283,6 +285,7 @@
 
 
 LIGHT = pl.CostEstimate(flops=10**7, bytes_accessed=10**5, transcendentals=0)
+HEAVY = pl.CostEstimate(flops=10**11, bytes_accessed=10**8, transcendentals=0)
 
 
 def dot(a, b):
@@ -297,39 +300,44 @@
     return pltpu.CompilerParams(vmem_limit_bytes=58 * 2**20, **kw)
 
 
-def modes_of(left, y_table, x_table):
-    waves = dot(left, y_table[...]).astype(jnp.bfloat16)
-    both = dot(x_table[...], waves)
-    half = both.shape[0] // 2
-    lane = lax.broadcasted_iota(jnp.int32, (half, 128), 1)
-    real = (lane // KY) % 2 == 0
-    parts = []
-    for at in range(0, both.shape[1], 128):
-        cos = both[:half, at : at + 128]
-        sin = both[half:, at : at + 128]
-        other = jnp.where(real, pltpu.roll(sin, 128 - KY, axis=1), pltpu.roll(sin, KY, axis=1))
-        parts.append(jnp.where(real, cos, -cos) - other)
-    return jnp.concatenate(parts, axis=1)
-
-
-def store_modes(out, at, first, second):
-    rows = first.shape[0] // out.shape[0]
-    for s in range(out.shape[0]):
-        here = slice(s * rows, (s + 1) * rows)
-        both = jnp.concatenate([first[here], second[here]], axis=0)
-        out[s, pl.ds(at, 2 * rows), :] = both.astype(jnp.bfloat16)
-
-
-def forward_kernel(field, x_table, y_table, out, first, last):
+def store_rows(rows, at, parts):
+    for p, part in parts:
+        for t in range(2):
+            for s in range(rows.shape[2]):
+                here = slice(8 * (t * rows.shape[2] + s), 8 * (t * rows.shape[2] + s) + 8)
+                both = jnp.concatenate([part[0][here], part[1][here]], axis=0)
+                rows[p, t, s, pl.ds(at, 16), :] = both.astype(jnp.bfloat16)
+
+
+def store_modes(rows, y_table, out):
+    pairs, _, slabs, lines, _ = rows.shape
+    left = [
+        jnp.concatenate([rows[p, t, s] for p in range(pairs) for t in range(2)], axis=1)
+        for s in range(slabs)
+    ]
+    modes = dot(jnp.concatenate(left, axis=0), y_table[...])
+    for s in range(slabs):
+        out[s] = modes[s * lines : (s + 1) * lines].astype(jnp.bfloat16)
+
+
+def forward_kernel(field, x_table, y_table, out, first, last, rows):
     step = pl.program_id(0)
     planes = field.shape[1]
     first[:, 0] = field[:, 0]
     last[:, 0] = field[:, planes - 1]
-    modes = []
+    products = []
     for i in range(2):
         sheets = [field[2 * i : 2 * i + 2, z].reshape(2 * NX, NY) for z in range(planes)]
-        modes.append(modes_of(jnp.concatenate(sheets, axis=1), y_table, x_table))
-    store_modes(out, pl.multiple_of(16 * step, 16), *modes)
+        products.append(dot(x_table[...], jnp.concatenate(sheets, axis=1)))
+    parts = [
+        (p, [product[:, 2 * NY * p : 2 * NY * (p + 1)] for product in products])
+        for p in range(planes // 2)
+    ]
+    store_rows(rows, pl.multiple_of(16 * step, 16), parts)
+
+    @pl.when(step == pl.num_programs(0) - 1)
+    def _():
+        store_modes(rows, y_table, out)
 
 
 def forward_modes(field, slabs):
@@ -350,6 +358,7 @@
         ],
         out_specs=[whole(shape), rim, rim],
         out_shape=[jax.ShapeDtypeStruct(shape, jnp.bfloat16), rims, rims],
+        scratch_shapes=[pltpu.VMEM((planes // 2, 2, slabs, lines, 2 * NY), jnp.bfloat16)],
         compiler_params=params(),
         cost_estimate=LIGHT,
         name="forward_modes",
@@ -401,9 +410,9 @@
 
     @pl.when(step == steps - 1)
     def _():
-        modes = (total[...] * scale_out).T.astype(jnp.bfloat16)
+        modes = dot((total[...] * scale_out).T.astype(jnp.bfloat16), z_out[...])
         for s in range(slabs):
-            out[s] = dot(modes, z_out[:, s * width : (s + 1) * width]).astype(jnp.bfloat16)
+            out[s] = modes[:, s * width : (s + 1) * width].astype(jnp.bfloat16)
 
 
 def mix(planar, weight, scale_in, scale_out, partner=None, copies=0):
@@ -448,7 +457,7 @@
         out_shape=[jax.ShapeDtypeStruct(out, jnp.bfloat16) for out in outs],
         scratch_shapes=scratch,
         compiler_params=params(),
-        cost_estimate=LIGHT,
+        cost_estimate=HEAVY,
         name="mix_back" if adjoint else "mix",
     )(*operands)
 
@@ -468,9 +477,9 @@
 
 def layer_kernel(bias, planar, smooth, cotangent, grains, point_weight, repeat, ix_table, iy_table,
                  x_table, y_table, spread, out, first, last, waves, spectral, moving, delta,
-                 bias_wide, mix_out, mix_in):
+                 rows, bias_wide, mix_out, mix_in):
     pair = pl.program_id(0)
-    pairs = delta.shape[0]
+    pairs = rows.shape[0]
     channels = cotangent.shape[0]
     slabs = planar.shape[0]
 
@@ -488,15 +497,22 @@
         mix_in[...] = square.astype(jnp.bfloat16)
         mix_out[...] = square.T.astype(jnp.bfloat16)
 
+    lines = planar.shape[1]
+    step = jnp.concatenate([planar[s] for s in range(slabs)], axis=0)
+    step = dot(step, iy_table[0]).astype(jnp.bfloat16)
     for s in range(slabs):
-        step = dot(planar[s], iy_table[0]).astype(jnp.bfloat16)
         for t in range(2):
-            waves[s, t] = step[:, 2 * NY * t : 2 * NY * (t + 1)]
+            waves[s, t] = step[s * lines : (s + 1) * lines, 2 * NY * t : 2 * NY * (t + 1)]
     group = 8 * (KX // slabs)
+    right = []
     for g in range(channels // 8):
-        right = [waves[s, t, g * group : (g + 1) * group, :] for s in range(slabs) for t in range(2)]
-        step = dot(ix_table[...], jnp.concatenate(right, axis=0))
-        spectral[8 * g : 8 * g + 8] = step.reshape(8, NX, 2 * NY)
+        here = slice(g * group, (g + 1) * group)
+        wave = [waves[s, t, here, :] for s in range(slabs) for t in range(2)]
+        right.append(jnp.concatenate(wave, axis=0))
+    step = dot(ix_table[...], jnp.concatenate(right, axis=1))
+    for g in range(channels // 8):
+        here = step[:, 2 * NY * g : 2 * NY * (g + 1)]
+        spectral[8 * g : 8 * g + 8] = here.reshape(8, NX, 2 * NY)
     for q in range(2):
         moving[:, q * NY : (q + 1) * NY] = 0.5 * plane_mobility(grains[q])
 
@@ -504,19 +520,24 @@
         x = pl.multiple_of(16 * i, 16)
         halves = [cotangent[:, q, pl.ds(x, 16), :] for q in range(2)]
         cotangent_here = jnp.concatenate(halves, axis=2).astype(jnp.float32)
-        spreads = []
+        rights = []
+        mobiles = []
+        right = jnp.concatenate([smooth[0, 2 * i + h] for h in range(2)], axis=1)
+        local = dot(mix_out[...], right).reshape(channels, 8, 4 * NY)
         for h in range(2):
             at = pl.ds(pl.multiple_of(x + 8 * h, 8), 8)
             mobile = moving[at, :][None]
-            local = dot(mix_out[...], smooth[0, 2 * i + h]).reshape(channels, 8, 2 * NY)
-            half = spectral[:, at, :] + mobile * local + bias_wide[...]
+            local_here = local[:, :, 2 * NY * h : 2 * NY * (h + 1)]
+            half = spectral[:, at, :] + mobile * local_here + bias_wide[...]
             wave = jnp.tanh(half)
             slope = (1.0 + wave) * (1.0 + (half - half * wave))
             change = cotangent_here[:, 8 * h : 8 * h + 8, :] * slope
             right = change.reshape(8 * channels, 2 * NY).astype(jnp.bfloat16)
-            delta[pair, 2 * i + h] = right
-            back = dot(mix_in[...], right).reshape(channels, 8, 2 * NY)
-            spreads.append(mobile * back)
+            delta[2 * i + h] = right
+            rights.append(right)
+            mobiles.append(mobile)
+        back = dot(mix_in[...], jnp.concatenate(rights, axis=1)).reshape(channels, 8, 4 * NY)
+        spreads = [mobiles[h] * back[:, :, 2 * NY * h : 2 * NY * (h + 1)] for h in range(2)]
         both = jnp.concatenate(spreads, axis=1).astype(jnp.bfloat16)
         for q in range(2):
             spread[:, q, pl.ds(x, 16), :] = both[:, :, q * NY : (q + 1) * NY]
@@ -524,6 +545,16 @@
 
     lax.fori_loop(0, NX // 16, body, 0, unroll=4)
 
+    for step in range(channels // 8):
+        right = [
+            delta[:, 16 * i : 16 * i + 16, :].reshape(2 * NX, 2 * NY)
+            for i in range(4 * step, 4 * step + 4)
+        ]
+        product = dot(x_table[...], jnp.concatenate(right, axis=1))
+        parts = [product[:, 2 * NY * i : 2 * NY * (i + 1)] for i in range(4)]
+        for i in range(2):
+            store_rows(rows, 32 * step + 16 * i, [(pair, parts[2 * i : 2 * i + 2])])
+
     @pl.when(pair == 0)
     def _():
         first[:, 0] = spread[:, 0]
@@ -531,13 +562,7 @@
     @pl.when(pair == pairs - 1)
     def _():
         last[:, 0] = spread[:, 1]
-        for step in range(channels // 4):
-            modes = []
-            for i in range(2):
-                here = slice(32 * step + 16 * i, 32 * step + 16 * i + 16)
-                sheets = [delta[p, :, here, :].reshape(2 * NX, 2 * NY) for p in range(pairs)]
-                modes.append(modes_of(jnp.concatenate(sheets, axis=1), y_table, x_table))
-            store_modes(out, 16 * step, *modes)
+        store_modes(rows, y_table, out)
 
 
 def layer(planar, smooth, cotangent, grains, bias, point_weight):
@@ -558,7 +583,7 @@
         in_specs=[
             pl.BlockSpec(memory_space=pltpu.SMEM),
             whole(planar.shape),
-            pl.BlockSpec((1,) + smooth.shape[1:], lambda p: (kept(p, pairs), 0, 0, 0)),
+            pl.BlockSpec((1,) + smooth.shape[1:], lambda p: (p, 0, 0, 0)),
             field,
             pl.BlockSpec((2, NX, NY), lambda p: (p, 0, 0)),
             whole(point_weight.shape),
@@ -574,7 +599,8 @@
             pltpu.VMEM((slabs, 2, lines, 2 * NY), jnp.bfloat16),
             pltpu.VMEM((channels, NX, 2 * NY), jnp.float32),
             pltpu.VMEM((NX, 2 * NY), jnp.float32),
-            pltpu.VMEM((pairs, NX // 8, 8 * channels, 2 * NY), jnp.bfloat16),
+            pltpu.VMEM((NX // 8, 8 * channels, 2 * NY), jnp.bfloat16),
+            pltpu.VMEM((pairs, 2, slabs, lines, 2 * NY), jnp.bfloat16),
             pltpu.VMEM((channels, 8, 2 * NY), jnp.float32),
             pltpu.VMEM((8 * channels, 8 * channels), jnp.bfloat16),
             pltpu.VMEM((8 * channels, 8 * channels), jnp.bfloat16),
@@ -584,10 +610,6 @@
         name="layer",
     )(bias, planar, smooth, cotangent, grains, point_weight, repeat, ix_table, iy_table, x_table,
       y_table)
-
-
-def kept(pair, pairs):
-    return jnp.where(pair == 0, pairs - 2, jnp.where(pair == pairs - 1, pair, pair - 1))
 
 
 def build_band(adjoint, taps, channel, band):
@@ -614,9 +636,8 @@
 
 def apply_band(quads, band):
     left = jnp.concatenate([jnp.concatenate(quad, axis=1) for quad in quads], axis=0)
-    middle = dot(left, band[:, 2 * NY : 4 * NY])
-    lower = dot(left, band[:, : 2 * NY])
-    upper = dot(left, band[:, 4 * NY :])
+    wide = dot(left, band[...])
+    lower, middle, upper = (wide[:, 2 * NY * dx : 2 * NY * (dx + 1)] for dx in range(3))
     row = lax.broadcasted_iota(jnp.int32, (8, 2 * NY), 0)
     totals = []
     for p in range(len(quads)):
@@ -649,56 +670,40 @@
     return run
 
 
-def smooth_kernel(inner, taps, field, *refs):
-    if inner:
-        out, even, odd = refs
-    else:
-        _, before, after, out, even, odd = refs
+def smooth_kernel(taps, before, field, after, out, even, odd):
     planes = field.shape[1]
     totals = []
 
     def visit(c, band):
-        if inner:
-            quads = [[field[c, z + k] for k in range(4)] for z in range(1, planes - 3, 2)]
-        else:
-            low = [before[c, 0]] + [field[c, z] for z in range(3)]
-            high = [field[c, z] for z in range(planes - 3, planes)] + [after[c, 0]]
-            quads = [low, high]
-        totals.append(apply_band(quads, band))
+        sheets = [before[c, 0]] + [field[c, z] for z in range(planes)] + [after[c, 0]]
+        totals.append(apply_band([sheets[z : z + 4] for z in range(0, planes, 2)], band))
 
     banded(False, taps, even, odd, 2)(visit)
-    for p in range(len(totals[0])):
+    for p in range(planes // 2):
         both = [totals[c][p].reshape(NX // 8, 8, 2 * NY) for c in range(2)]
         out[p] = jnp.concatenate(both, axis=1).astype(jnp.bfloat16)
 
 
-def smooth_planes(field, taps, inner=None, rims=None):
+def smooth_planes(field, rims, taps):
     channels, planes = field.shape[:2]
     pairs = planes // 2
-    shape = (pairs, NX // 8, 8 * channels, 2 * NY)
-    in_specs = [
-        pl.BlockSpec(memory_space=pltpu.SMEM),
-        pl.BlockSpec((2, planes, NX, NY), lambda c: (c, 0, 0, 0)),
-    ]
-    operands = [taps, field]
-    place = 0
-    if inner is not None:
-        in_specs.append(pl.BlockSpec(memory_space=pl.ANY))
-        in_specs += [pl.BlockSpec((2, 1, NX, NY), lambda c: (c, 0, 0, 0))] * 2
-        operands += [inner, *rims]
-        place = 1
+    rim = pl.BlockSpec((2, 1, NX, NY), lambda c: (c, 0, 0, 0))
     return pl.pallas_call(
-        functools.partial(smooth_kernel, inner is None),
+        smooth_kernel,
         grid=(channels // 2,),
-        in_specs=in_specs,
-        out_specs=pl.BlockSpec((pairs // 2, NX // 8, 16, 2 * NY), lambda c: (place, 0, c, 0)),
-        out_shape=jax.ShapeDtypeStruct(shape, jnp.bfloat16),
-        input_output_aliases={} if inner is None else {2: 0},
+        in_specs=[
+            pl.BlockSpec(memory_space=pltpu.SMEM),
+            rim,
+            pl.BlockSpec((2, planes, NX, NY), lambda c: (c, 0, 0, 0)),
+            rim,
+        ],
+        out_specs=pl.BlockSpec((pairs, NX // 8, 16, 2 * NY), lambda c: (0, 0, c, 0)),
+        out_shape=jax.ShapeDtypeStruct((pairs, NX // 8, 8 * channels, 2 * NY), jnp.bfloat16),
         scratch_shapes=[pltpu.VMEM((4 * NY, 6 * NY), jnp.bfloat16) for _ in range(2)],
         compiler_params=params(),
         cost_estimate=LIGHT,
-        name="smooth_inner" if inner is None else "smooth_outer",
-    )(*operands)
+        name="smooth",
+    )(taps, rims[0], field, rims[1])
 
 
 def finish_kernel(taps, before, field, after, planar, ix_table, iy_table, out, waves, spectral,
@@ -710,10 +715,12 @@
 
     @pl.when(step == 0)
     def _():
-        for s in range(slabs):
-            for t in range(2):
-                right = iy_table[0, :, t * span : (t + 1) * span]
-                waves[s, t] = dot(planar[s], right).astype(jnp.bfloat16)
+        lines = planar.shape[1]
+        left = jnp.concatenate([planar[s] for s in range(slabs)], axis=0)
+        for t in range(2):
+            wave = dot(left, iy_table[0, :, t * span : (t + 1) * span]).astype(jnp.bfloat16)
+            for s in range(slabs):
+                waves[s, t] = wave[s * lines : (s + 1) * lines]
 
     rows = 4 * (KX // slabs)
     here = pl.ds(pl.multiple_of(rows * step, rows), rows)
@@ -760,7 +767,7 @@
             pltpu.VMEM((4 * NY, 6 * NY), jnp.bfloat16),
         ],
         compiler_params=params(),
-        cost_estimate=LIGHT,
+        cost_estimate=HEAVY,
         name="finish",
     )(taps, rims[0], spread, rims[1], planar, ix_table, iy_table)
 
@@ -839,21 +846,20 @@
     width = weight.shape[1] // copies
 
     planar, first, last = forward_modes(field, slabs)
+    planar, first, last = barrier((swap(planar), first, last))
     rims = neighbours(first, last)
-    spectrum, planar = mix(swap(planar), weight, cell_scale, 0.5 * mode_scale)
-    planar, field = barrier((planar, field))
+    spectrum, planar = mix(planar, weight, cell_scale, 0.5 * mode_scale)
     planar = swap(planar)
-    smooth = smooth_planes(field, taps)
-    smooth = smooth_planes(field, taps, smooth, rims)
-    planar, smooth = barrier((planar, smooth))
+    smooth = smooth_planes(field, rims, taps)
     spread, planar, first, last = layer(planar, smooth, cotangent[0], grains[0], bias, point_weight)
     rims = neighbours(first, last)
     planar, send = mix(swap(planar), weight, 0.5 * mode_scale, cell_scale, spectrum, copies)
     planar = swap(planar)
     gathered = lax.all_to_all(send, "dp", split_axis=0, concat_axis=0)
+    grad_feats = finish(planar, spread, rims, taps)
+    grad_feats, gathered = barrier((grad_feats, gathered))
+    grad_feats = grad_feats[None]
     grad_spec = weight_gradient(gathered, KX // slabs, width, lax.axis_index("dp"))
-    planar, grad_spec = barrier((planar, grad_spec))
-    grad_feats = finish(planar, spread, rims, taps)[None]
     return (grad_feats, grad_spec.reshape(mode_rows, KZ, width))
 
 

time: 209 us -> 181 us (0.87)
  blocking collectives: 44.3 us -> 15.3 us
  Pallas kernels: 117 us -> 103 us
  waiting for transfers between devices: 19.3 us -> 28.7 us
  starting transfers between devices: 21.2 us -> 26.4 us
    all_to_all x2 -> x1, blocking collectives: 44.3 us -> 15.3 us  [swap(): return lax.all_to_all(planar, 'slab', split_axis=0, concat_axis=0)]
    pallas_call x2 -> x1, Pallas kernels: 32.1 us -> 20.3 us  [smooth_planes(): pl.pallas_call(smooth_kernel, grid=(channels // 2,), in_specs=[pl.BlockSp...]
    ppermute x4, waiting for transfers between devices: 0.01 us -> 11.7 us  [neighbours(): return (lax.ppermute(last, 'slab', up), lax.ppermute(first, 'slab', down))]
    all_to_all x1, waiting for transfers between devices: 10 us -> 0.01 us  [local_fast(): gathered = lax.all_to_all(send, 'dp', split_axis=0, concat_axis=0)]
    all_to_all x2 -> x3, waiting for transfers between devices: 9.25 us -> 17 us  [swap(): return lax.all_to_all(planar, 'slab', split_axis=0, concat_axis=0)]
    all_to_all x2 -> x3, starting transfers between devices: 6.99 us -> 14 us  [swap(): return lax.all_to_all(planar, 'slab', split_axis=0, concat_axis=0)]
    unnamed x14 -> x16, local copies, waits for them, and re-layouts: 4.14 us -> 4.65 us
  transfers between devices with their start and end apart: 7 -> 8, of which waited for: 2 -> 4; matrix products, arithmetic and copies ran while one was open for 0% -> 0% of each run, Pallas kernels for 23% -> 33%
where the time goes in v5:
time: 181 us; the launch traced here: 179 us
  Pallas kernels  103 us (57%)
  waiting for transfers between devices  28.7 us (16%)
  starting transfers between devices  26.4 us (15%)
  blocking collectives  15.3 us (8%)
  local copies, waits for them, and re-layouts  4.65 us (3%)
    pallas_call x1, Pallas kernels, layer(): pl.pallas_call(layer_kernel, grid=(pairs,), in_specs=[pl.BlockSpec(memory...  27.1 us
    pallas_call x1, Pallas kernels, finish(): pl.pallas_call(finish_kernel, grid=(channels // 4,), in_specs=[pl.BlockSp...  22.4 us
    pallas_call x1, Pallas kernels, smooth_planes(): pl.pallas_call(smooth_kernel, grid=(channels // 2,), in_specs=[pl.BlockSp...  20.3 us
    all_to_all x3, waiting for transfers between devices, swap(): return lax.all_to_all(planar, 'slab', split_axis=0, concat_axis=0)  17 us
    pallas_call x2, Pallas kernels, mix(): pl.pallas_call(functools.partial(mixing_kernel, scale_in, scale_out, adjo...  16.2 us
    all_to_all x1, blocking collectives, swap(): return lax.all_to_all(planar, 'slab', split_axis=0, concat_axis=0)  15.3 us
    all_to_all x3, starting transfers between devices, swap(): return lax.all_to_all(planar, 'slab', split_axis=0, concat_axis=0)  14 us
    ppermute x4, waiting for transfers between devices, neighbours(): return (lax.ppermute(last, 'slab', up), lax.ppermute(first, 'slab', down))  11.7 us
  transfers between devices with their start and end apart: 8, of which 4 were waited for; matrix products, arithmetic and copies ran while one was open for 0% of the time, Pallas kernels for 33%

profile of v5, /device:TPU:0, one launch (start us, length us, event | category | flops | bytes accessed | tf_op | source)
XLA Modules:
  0.0 179.5 jit_solution(17490113702483334846)
XLA Ops:
  0.6 9.2 %forward_modes.1 = (bf16[4,128,256]{2,1,0:T(8,128)(2,1)}, bf16[32,1,128,128]{3,2,1,0:T(8,128)(2,1)}, bf16[32,1,128,128]{3,2,1,0:T(8,128)(2,1)}) custom-call(bf16[32,8,128,128]{3,2,1,0:T(8,128)(2,1)} %bitcast.8, bf16[64,256]{1,0:T(8,128)(2,1)} %constant.61.clone.x_table, bf16[2048,256]{1,0:T(8,128)(2,1)} %constant.62.clone.y_table), custom_call_target="tpu_custom_call" | custom-call | flops 10000000 | bytes 100000 | tf_op jit(solution)/shard_map/forward_modes/pallas_call | solution.py:351
  9.8 15.3 %all_to_all.25.planar = bf16[4,128,256]{2,1,0:T(8,128)(2,1)} all-to-all(bf16[4,128,256]{2,1,0:T(8,128)(2,1)} %get-tuple-element.18), channel_id=1, replica_groups=mesh['grp'=2,'dp'=4,'slab'=4] {'slab'}, dimensions={0} | all-to-all | bytes 524288 | tf_op jit(solution)/shard_map/all_to_all | solution.py:833
  25.1 2.2 %collective-permute-start = (bf16[32,1,128,128]{3,2,1,0:T(8,128)(2,1)}, bf16[32,1,128,128]{3,2,1,0:T(8,128)(2,1)S(1)}, u32[]{:S(2)}, u32[]{:S(2)}) collective-permute-start(bf16[32,1,128,128]{3,2,1,0:T(8,128)(2,1)} %get-tuple-element.23), channel_id=1, source_target_pairs={{0,1},{1,2},{2,3},{4,5},{5,6},{6,7},{8,9},{9,10},{10,11},{12,13},{... | collective-permute-start | bytes 3145736 | tf_op jit(solution)/shard_map/ppermute | solution.py:829
  27.3 1.3 collective-permute-start.1
  28.6 7.9 %mix.1 = (bf16[512,128]{1,0:T(8,128)(2,1)}, bf16[4,128,256]{2,1,0:T(8,128)(2,1)}) custom-call(bf16[4,128,256]{2,1,0:T(8,128)(2,1)} %all_to_all.25.planar, bf16[1024,2048]{1,0:T(8,128)(2,1)} %bitcast.13, bf16[1024,512]{1,0:T(8,128)(2,1)} %constant.63.clone.z_in, bf16[512,1024]{1,0:T(8,128)(2,1)} %constant.64.clone.z_out, ...), custom_call_target="tpu_custom_call" | custom-call | flops 99999997952 | bytes 100000000 | tf_op jit(solution)/shard_map/mix/pallas_call | solution.py:452
  36.5 5.2 %all-to-all-start.1 = ((bf16[4,128,256]{2,1,0:T(8,128)(2,1)}), bf16[4,128,256]{2,1,0:T(8,128)(2,1)S(1)}, u32[]{:S(2)}, u32[]{:S(2)}) async-start(bf16[4,128,256]{2,1,0:T(8,128)(2,1)} %get-tuple-element.22), calls=%async_computation.1 | async-start | bytes 524288 | tf_op jit(solution)/shard_map/all_to_all | solution.py:833
  41.7 8.7 %collective-permute-done.before = bf16[32,1,128,128]{3,2,1,0:T(8,128)(2,1)S(1)} collective-permute-done((bf16[32,1,128,128]{3,2,1,0:T(8,128)(2,1)}, bf16[32,1,128,128]{3,2,1,0:T(8,128)(2,1)S(1)}, u32[]{:S(2)}, u32[]{:S(2)}) %collective-permute-start) | collective-permute-done | bytes 1048608 | tf_op jit(solution)/shard_map/ppermute | solution.py:829
  50.4 0.0 copy-start.2
  50.4 3.0 %collective-permute-done.1.after = bf16[32,1,128,128]{3,2,1,0:T(8,128)(2,1)S(1)} collective-permute-done((bf16[32,1,128,128]{3,2,1,0:T(8,128)(2,1)}, bf16[32,1,128,128]{3,2,1,0:T(8,128)(2,1)S(1)}, u32[]{:S(2)}, u32[]{:S(2)}) %collective-permute-start.1) | collective-permute-done | bytes 1048608 | tf_op jit(solution)/shard_map/ppermute | solution.py:829
  53.4 0.0 copy-done.2
  53.4 0.0 copy-start.3
  53.4 1.0 copy-done.3
  54.3 20.3 %smooth.1 = bf16[4,16,256,256]{3,2,1,0:T(8,128)(2,1)} custom-call(f32[27,32]{1,0:T(8,128)} %taps.3, bf16[32,1,128,128]{3,2,1,0:T(8,128)(2,1)} %copy-done.2, bf16[32,8,128,128]{3,2,1,0:T(8,128)(2,1)} %bitcast.9, bf16[32,1,128,128]{3,2,1,0:T(8,128)(2,1)} %copy-done.3), custom_call_target="tpu_custom_call" | custom-call | flops 10000000 | bytes 100000 | tf_op jit(solution)/shard_map/smooth/pallas_call | solution.py:691
  74.6 0.0 all-to-all-done.1.planar
  74.6 0.0 copy-start.1
  74.6 0.7 copy-done.1
  75.3 27.1 %layer.1 = (bf16[32,8,128,128]{3,2,1,0:T(8,128)(2,1)}, bf16[4,128,256]{2,1,0:T(8,128)(2,1)}, bf16[32,1,128,128]{3,2,1,0:T(8,128)(2,1)}, bf16[32,1,128,128]{3,2,1,0:T(8,128)(2,1)}) custom-call(f32[32]{0:T(128)} %bias.1, bf16[4,128,256]{2,1,0:T(8,128)(2,1)} %copy-done.1, bf16[4,16,256,256]{3,2,1,0:T(8,128)(2,1)} %smooth.1, bf16[32,8,128,128]{3,2,1,0:T(8,128)(2,1)} %bitcast.10, ...), custom_call_target="tpu_custom_call" | custom-call | flops 10000000 | bytes 100000 | tf_op jit(solution)/shard_map/layer/pallas_call | solution.py:580
  102.5 5.2 %all-to-all-start.2 = ((bf16[4,128,256]{2,1,0:T(8,128)(2,1)}), bf16[4,128,256]{2,1,0:T(8,128)(2,1)S(1)}, u32[]{:S(2)}, u32[]{:S(2)}) async-start(bf16[4,128,256]{2,1,0:T(8,128)(2,1)} %get-tuple-element.28), calls=%async_computation.2 | async-start | bytes 524288 | tf_op jit(solution)/shard_map/all_to_all | solution.py:833
  107.6 4.0 %collective-permute-start.2 = (bf16[32,1,128,128]{3,2,1,0:T(8,128)(2,1)}, bf16[32,1,128,128]{3,2,1,0:T(8,128)(2,1)S(1)}, u32[]{:S(2)}, u32[]{:S(2)}) collective-permute-start(bf16[32,1,128,128]{3,2,1,0:T(8,128)(2,1)} %get-tuple-element.25), channel_id=1, source_target_pairs={{0,1},{1,2},{2,3},{4,5},{5,6},{6,7},{8,9},{9,10},{10,11},{12,13},{... | collective-permute-start | bytes 3145736 | tf_op jit(solution)/shard_map/ppermute | solution.py:829
  111.6 1.3 collective-permute-start.3
  112.9 2.7 %all-to-all-done.2.planar = bf16[4,128,256]{2,1,0:T(8,128)(2,1)S(1)} async-done(((bf16[4,128,256]{2,1,0:T(8,128)(2,1)}), bf16[4,128,256]{2,1,0:T(8,128)(2,1)S(1)}, u32[]{:S(2)}, u32[]{:S(2)}) %all-to-all-start.2) | async-done | bytes 262176 | tf_op jit(solution)/shard_map/all_to_all | solution.py:833
  115.6 0.0 copy-start.5
  115.6 0.7 copy-done.5
  116.3 8.3 %mix_back.1 = (bf16[4,128,256]{2,1,0:T(8,128)(2,1)}, bf16[4,1024,128]{2,1,0:T(8,128)(2,1)}) custom-call(bf16[4,128,256]{2,1,0:T(8,128)(2,1)} %copy-done.5, bf16[1024,2048]{1,0:T(8,128)(2,1)} %bitcast.14, bf16[1024,512]{1,0:T(8,128)(2,1)} %constant.63.clone.z_in, bf16[512,1024]{1,0:T(8,128)(2,1)} %constant.64.clone.z_out, ...), custom_call_target="tpu_custom_call" | custom-call | flops 99999997952 | bytes 100000000 | tf_op jit(solution)/shard_map/mix_back/pallas_call | solution.py:452
  124.6 3.7 %all-to-all-start.3 = ((bf16[4,128,256]{2,1,0:T(8,128)(2,1)}), bf16[4,128,256]{2,1,0:T(8,128)(2,1)S(1)}, u32[]{:S(2)}, u32[]{:S(2)}) async-start(bf16[4,128,256]{2,1,0:T(8,128)(2,1)} %get-tuple-element.30), calls=%async_computation.3 | async-start | bytes 524288 | tf_op jit(solution)/shard_map/all_to_all | solution.py:833
  128.3 0.6 pad_add_fusion.where
  128.9 14.3 %all-to-all-done.3.planar = bf16[4,128,256]{2,1,0:T(8,128)(2,1)S(1)} async-done(((bf16[4,128,256]{2,1,0:T(8,128)(2,1)}), bf16[4,128,256]{2,1,0:T(8,128)(2,1)S(1)}, u32[]{:S(2)}, u32[]{:S(2)}) %all-to-all-start.3) | async-done | bytes 262176 | tf_op jit(solution)/shard_map/all_to_all | solution.py:833
  143.2 0.0 copy-start.4
  143.2 3.7 %all-to-all-start.4 = ((bf16[4,1024,128]{2,1,0:T(8,128)(2,1)}), bf16[4,1024,128]{2,1,0:T(8,128)(2,1)S(1)}, u32[]{:S(2)}, u32[]{:S(2)}) async-start(bf16[4,1024,128]{2,1,0:T(8,128)(2,1)} %get-tuple-element.31), calls=%async_computation.4 | async-start | bytes 2097152 | tf_op jit(solution)/shard_map/all_to_all | solution.py:858
  146.9 0.0 collective-permute-done.2.before
  146.9 0.0 copy-start.6
  146.9 0.0 collective-permute-done.3.after
  146.9 0.0 copy-start.7
  147.0 0.0 copy-done.4
  147.0 1.0 copy-done.6
  148.0 0.3 copy-done.7
  148.2 22.4 %finish.1 = bf16[32,8,128,128]{3,2,1,0:T(8,128)(2,1)} custom-call(f32[27,32]{1,0:T(8,128)} %taps.3, bf16[32,1,128,128]{3,2,1,0:T(8,128)(2,1)} %copy-done.6, bf16[32,8,128,128]{3,2,1,0:T(8,128)(2,1)} %get-tuple-element.26.field, bf16[32,1,128,128]{3,2,1,0:T(8,128)(2,1)} %copy-done.7, bf16[4,128,256]{2,1,0:T(8,128)(2,1)} %copy-done.4, ...), custom_call_target="tpu_custom_call" | custom-call | flops 99999997952 | bytes 100000000 | tf_op jit(solution)/shard_map/finish/pallas_call | solution.py:749
  170.6 0.0 all-to-all-done.4.gathered
  170.6 0.0 copy-start
  170.7 1.0 copy-done
  171.6 7.8 %weight_gradient.1 = f32[1024,512]{1,0:T(8,128)} custom-call(s32[2]{0:T(128)} %pad_add_fusion.where, bf16[4,1024,128]{2,1,0:T(8,128)(2,1)} %copy-done, bf16[2,128,512]{2,1,0:T(8,128)(2,1)} %constant.75.clone.first, bf16[128,512]{1,0:T(8,128)(2,1)} %constant.76.clone.second), custom_call_target="tpu_custom_call" | custom-call | flops 10000000 | bytes 100000 | tf_op jit(solution)/shard_map/weight_gradient/pallas_call | solution.py:806
Async XLA Ops:
  25.1 25.3 %collective-permute-start = (bf16[32,1,128,128]{3,2,1,0:T(8,128)(2,1)}, bf16[32,1,128,128]{3,2,1,0:T(8,128)(2,1)S(1)}, u32[]{:S(2)}, u32[]{:S(2)}) collective-permute-start(bf16[32,1,128,128]{3,2,1,0:T(8,128)(2,1)} %get-tuple-element.23), channel_id=1, source_target_pairs={{0,1},{1,2},{2,3},{4,5},{5,6},{6,7},{8,9},{9,10},{10,11},{12,13},{... | collective-permute-start | bytes 3145736 | tf_op jit(solution)/shard_map/ppermute | solution.py:829
  27.3 26.1 %collective-permute-start.1 = (bf16[32,1,128,128]{3,2,1,0:T(8,128)(2,1)}, bf16[32,1,128,128]{3,2,1,0:T(8,128)(2,1)S(1)}, u32[]{:S(2)}, u32[]{:S(2)}) collective-permute-start(bf16[32,1,128,128]{3,2,1,0:T(8,128)(2,1)} %get-tuple-element.24), channel_id=1, source_target_pairs={{1,0},{2,1},{3,2},{5,4},{6,5},{7,6},{9,8},{10,9},{11,10},{13,12},{... | collective-permute-start | bytes 3145736 | tf_op jit(solution)/shard_map/ppermute | solution.py:829
  36.5 38.1 %all-to-all-start.1 = ((bf16[4,128,256]{2,1,0:T(8,128)(2,1)}), bf16[4,128,256]{2,1,0:T(8,128)(2,1)S(1)}, u32[]{:S(2)}, u32[]{:S(2)}) async-start(bf16[4,128,256]{2,1,0:T(8,128)(2,1)} %get-tuple-element.22), calls=%async_computation.1 | async-start | bytes 524288 | tf_op jit(solution)/shard_map/all_to_all | solution.py:833
  50.4 3.0 %copy-start.2 = (bf16[32,1,128,128]{3,2,1,0:T(8,128)(2,1)}, bf16[32,1,128,128]{3,2,1,0:T(8,128)(2,1)S(1)}, u32[]{:S(2)}) copy-start(bf16[32,1,128,128]{3,2,1,0:T(8,128)(2,1)S(1)} %collective-permute-done.before) | copy-start | bytes 3145732
  53.4 1.0 copy-start.3
  74.6 0.7 copy-start.1
  102.5 13.2 %all-to-all-start.2 = ((bf16[4,128,256]{2,1,0:T(8,128)(2,1)}), bf16[4,128,256]{2,1,0:T(8,128)(2,1)S(1)}, u32[]{:S(2)}, u32[]{:S(2)}) async-start(bf16[4,128,256]{2,1,0:T(8,128)(2,1)} %get-tuple-element.28), calls=%async_computation.2 | async-start | bytes 524288 | tf_op jit(solution)/shard_map/all_to_all | solution.py:833
  107.6 39.3 %collective-permute-start.2 = (bf16[32,1,128,128]{3,2,1,0:T(8,128)(2,1)}, bf16[32,1,128,128]{3,2,1,0:T(8,128)(2,1)S(1)}, u32[]{:S(2)}, u32[]{:S(2)}) collective-permute-start(bf16[32,1,128,128]{3,2,1,0:T(8,128)(2,1)} %get-tuple-element.25), channel_id=1, source_target_pairs={{0,1},{1,2},{2,3},{4,5},{5,6},{6,7},{8,9},{9,10},{10,11},{12,13},{... | collective-permute-start | bytes 3145736 | tf_op jit(solution)/shard_map/ppermute | solution.py:829
  111.6 35.3 %collective-permute-start.3 = (bf16[32,1,128,128]{3,2,1,0:T(8,128)(2,1)}, bf16[32,1,128,128]{3,2,1,0:T(8,128)(2,1)S(1)}, u32[]{:S(2)}, u32[]{:S(2)}) collective-permute-start(bf16[32,1,128,128]{3,2,1,0:T(8,128)(2,1)} %get-tuple-element.27), channel_id=1, source_target_pairs={{1,0},{2,1},{3,2},{5,4},{6,5},{7,6},{9,8},{10,9},{11,10},{13,12},{... | collective-permute-start | bytes 3145736 | tf_op jit(solution)/shard_map/ppermute | solution.py:829
  115.6 0.7 copy-start.5
  124.6 18.6 %all-to-all-start.3 = ((bf16[4,128,256]{2,1,0:T(8,128)(2,1)}), bf16[4,128,256]{2,1,0:T(8,128)(2,1)S(1)}, u32[]{:S(2)}, u32[]{:S(2)}) async-start(bf16[4,128,256]{2,1,0:T(8,128)(2,1)} %get-tuple-element.30), calls=%async_computation.3 | async-start | bytes 524288 | tf_op jit(solution)/shard_map/all_to_all | solution.py:833
  143.2 3.8 %copy-start.4 = (bf16[4,128,256]{2,1,0:T(8,128)(2,1)}, bf16[4,128,256]{2,1,0:T(8,128)(2,1)S(1)}, u32[]{:S(2)}) copy-start(bf16[4,128,256]{2,1,0:T(8,128)(2,1)S(1)} %all-to-all-done.3.planar) | copy-start | bytes 786436
  143.2 27.4 %all-to-all-start.4 = ((bf16[4,1024,128]{2,1,0:T(8,128)(2,1)}), bf16[4,1024,128]{2,1,0:T(8,128)(2,1)S(1)}, u32[]{:S(2)}, u32[]{:S(2)}) async-start(bf16[4,1024,128]{2,1,0:T(8,128)(2,1)} %get-tuple-element.31), calls=%async_computation.4 | async-start | bytes 2097152 | tf_op jit(solution)/shard_map/all_to_all | solution.py:858
  146.9 1.1 copy-start.6
  146.9 1.3 copy-start.7
  170.6 1.0 copy-start

commit v6 on v5

--- a/solution.py
+++ b/solution.py
@@ -300,13 +300,15 @@
     return pltpu.CompilerParams(vmem_limit_bytes=58 * 2**20, **kw)
 
 
-def store_rows(rows, at, parts):
-    for p, part in parts:
+def store_rows(rows, pair, x_table, load):
+    slabs, lines = rows.shape[2:4]
+    for i in range(lines // 16):
+        parts = [dot(x_table[...], load(2 * i + k)) for k in range(2)]
         for t in range(2):
-            for s in range(rows.shape[2]):
-                here = slice(8 * (t * rows.shape[2] + s), 8 * (t * rows.shape[2] + s) + 8)
-                both = jnp.concatenate([part[0][here], part[1][here]], axis=0)
-                rows[p, t, s, pl.ds(at, 16), :] = both.astype(jnp.bfloat16)
+            for s in range(slabs):
+                here = slice(8 * (t * slabs + s), 8 * (t * slabs + s) + 8)
+                both = jnp.concatenate([part[here] for part in parts], axis=0)
+                rows[pair, t, s, 16 * i : 16 * i + 16, :] = both.astype(jnp.bfloat16)
 
 
 def store_modes(rows, y_table, out):
@@ -320,22 +322,33 @@
         out[s] = modes[s * lines : (s + 1) * lines].astype(jnp.bfloat16)
 
 
-def forward_kernel(field, x_table, y_table, out, first, last, rows):
-    step = pl.program_id(0)
-    planes = field.shape[1]
-    first[:, 0] = field[:, 0]
-    last[:, 0] = field[:, planes - 1]
-    products = []
-    for i in range(2):
-        sheets = [field[2 * i : 2 * i + 2, z].reshape(2 * NX, NY) for z in range(planes)]
-        products.append(dot(x_table[...], jnp.concatenate(sheets, axis=1)))
-    parts = [
-        (p, [product[:, 2 * NY * p : 2 * NY * (p + 1)] for product in products])
-        for p in range(planes // 2)
-    ]
-    store_rows(rows, pl.multiple_of(16 * step, 16), parts)
-
-    @pl.when(step == pl.num_programs(0) - 1)
+def store_rims(field, rims, pair, pairs):
+    half = field.shape[0] // 2
+
+    @pl.when(pair == 0)
+    def _():
+        for i in range(2):
+            rims[i][:, 0] = field[half * i : half * (i + 1), 0]
+
+    @pl.when(pair == pairs - 1)
+    def _():
+        for i in range(2):
+            rims[2 + i][:, 0] = field[half * i : half * (i + 1), 1]
+
+
+def forward_kernel(field, x_table, y_table, out, *rest):
+    *rims, rows = rest
+    pair = pl.program_id(0)
+    pairs = rows.shape[0]
+    store_rims(field, rims, pair, pairs)
+
+    def load(i):
+        halves = [field[2 * i : 2 * i + 2, q].reshape(2 * NX, NY) for q in range(2)]
+        return jnp.concatenate(halves, axis=1)
+
+    store_rows(rows, pair, x_table, load)
+
+    @pl.when(pair == pairs - 1)
     def _():
         store_modes(rows, y_table, out)
 
@@ -345,19 +358,17 @@
     lines = channels * (KX // slabs)
     x_table = constant(forward_x_table(slabs, False))
     y_table = constant(forward_y_table(planes))
-    shape = (slabs, lines, planes * 2 * KY)
-    rim = pl.BlockSpec((4, 1, NX, NY), lambda c: (c, 0, 0, 0))
-    rims = jax.ShapeDtypeStruct((channels, 1, NX, NY), jnp.bfloat16)
+    outs = [(slabs, lines, planes * 2 * KY)] + [(channels // 2, 1, NX, NY)] * 4
     return pl.pallas_call(
         forward_kernel,
-        grid=(channels // 4,),
+        grid=(planes // 2,),
         in_specs=[
-            pl.BlockSpec((4, planes, NX, NY), lambda c: (c, 0, 0, 0)),
+            pl.BlockSpec((channels, 2, NX, NY), lambda p: (0, p, 0, 0)),
             whole(x_table.shape),
             whole(y_table.shape),
         ],
-        out_specs=[whole(shape), rim, rim],
-        out_shape=[jax.ShapeDtypeStruct(shape, jnp.bfloat16), rims, rims],
+        out_specs=[whole(out) for out in outs],
+        out_shape=[jax.ShapeDtypeStruct(out, jnp.bfloat16) for out in outs],
         scratch_shapes=[pltpu.VMEM((planes // 2, 2, slabs, lines, 2 * NY), jnp.bfloat16)],
         compiler_params=params(),
         cost_estimate=LIGHT,
@@ -393,19 +404,29 @@
     mine = lane % steps == step
     wide[...] = dot(jnp.where(mine, spectrum[...], 0), spread_table[...])
     block = 32
+    tile = wide.shape[1]
     for at in range(0, half, block):
-        real_wide = wide[at : at + block]
-        imag_wide = wide[half + at : half + at + block]
-        w_real = weight[at : at + block, :lanes].astype(jnp.float32)
-        w_imag = weight[at : at + block, lanes:].astype(jnp.float32)
-        if adjoint:
-            real = real_wide * w_real + imag_wide * w_imag
-            imag = imag_wide * w_real - real_wide * w_imag
-        else:
-            real = real_wide * w_real - imag_wide * w_imag
-            imag = real_wide * w_imag + imag_wide * w_real
-        product[at : at + block] = real.astype(jnp.bfloat16)
-        product[half + at : half + at + block] = imag.astype(jnp.bfloat16)
+        sums = [0.0, 0.0]
+        for column in range(0, lanes, 128):
+            here = slice(column, column + 128) if tile == lanes else slice(None)
+            real_wide = wide[at : at + block, here]
+            imag_wide = wide[half + at : half + at + block, here]
+            w_real = weight[at : at + block, column : column + 128].astype(jnp.float32)
+            imag_column = lanes + column
+            w_imag = weight[at : at + block, imag_column : imag_column + 128].astype(jnp.float32)
+            if adjoint:
+                real = real_wide * w_real + imag_wide * w_imag
+                imag = imag_wide * w_real - real_wide * w_imag
+                product[at : at + block, column : column + 128] = real.astype(jnp.bfloat16)
+                product[half + at : half + at + block, column : column + 128] = imag.astype(
+                    jnp.bfloat16
+                )
+            else:
+                sums[0] = sums[0] + (real_wide * w_real - imag_wide * w_imag)
+                sums[1] = sums[1] + (real_wide * w_imag + imag_wide * w_real)
+        if not adjoint:
+            product[at : at + block] = sums[0].astype(jnp.bfloat16)
+            product[half + at : half + at + block] = sums[1].astype(jnp.bfloat16)
     total[...] += jnp.where(mine, dot(product[...], sum_table[...]), 0.0)
 
     @pl.when(step == steps - 1)
@@ -425,8 +446,8 @@
     z_out = constant(inverse_z_table())
     first = first_table(channels, depth)
     second = second_table(channels, depth)
-    spread_table = constant(second if adjoint else first)
-    sum_table = constant((first if adjoint else second).T)
+    spread_table = constant(second[:, :128] if adjoint else first)
+    sum_table = constant(first.T if adjoint else second[:, :128].T)
     shape = (2 * rows, lines)
     in_specs = [
         whole(planar.shape),
@@ -439,8 +460,8 @@
     operands = [planar, weight, z_in, z_out, spread_table, sum_table]
     scratch = [
         pltpu.VMEM(shape, jnp.float32),
-        pltpu.VMEM((2 * rows, channels * channels), jnp.float32),
-        pltpu.VMEM((2 * rows, channels * channels), jnp.bfloat16),
+        pltpu.VMEM((2 * rows, spread_table.shape[1]), jnp.float32),
+        pltpu.VMEM((2 * rows, sum_table.shape[0]), jnp.bfloat16),
     ]
     if adjoint:
         in_specs.append(whole(shape))
@@ -476,9 +497,10 @@
 
 
 def layer_kernel(bias, planar, smooth, cotangent, grains, point_weight, repeat, ix_table, iy_table,
-                 x_table, y_table, spread, out, first, last, waves, spectral, moving, delta,
-                 rows, bias_wide, mix_out, mix_in):
+                 x_table, y_table, spread, out, *rest):
     pair = pl.program_id(0)
+    rims, rest = rest[:4], rest[4:]
+    waves, spectral, moving, delta, rows, bias_wide, mix_out, mix_in = rest
     pairs = rows.shape[0]
     channels = cotangent.shape[0]
     slabs = planar.shape[0]
@@ -504,15 +526,11 @@
         for t in range(2):
             waves[s, t] = step[s * lines : (s + 1) * lines, 2 * NY * t : 2 * NY * (t + 1)]
     group = 8 * (KX // slabs)
-    right = []
     for g in range(channels // 8):
         here = slice(g * group, (g + 1) * group)
         wave = [waves[s, t, here, :] for s in range(slabs) for t in range(2)]
-        right.append(jnp.concatenate(wave, axis=0))
-    step = dot(ix_table[...], jnp.concatenate(right, axis=1))
-    for g in range(channels // 8):
-        here = step[:, 2 * NY * g : 2 * NY * (g + 1)]
-        spectral[8 * g : 8 * g + 8] = here.reshape(8, NX, 2 * NY)
+        step = dot(ix_table[...], jnp.concatenate(wave, axis=0))
+        spectral[8 * g : 8 * g + 8] = step.reshape(8, NX, 2 * NY)
     for q in range(2):
         moving[:, q * NY : (q + 1) * NY] = 0.5 * plane_mobility(grains[q])
 
@@ -520,24 +538,19 @@
         x = pl.multiple_of(16 * i, 16)
         halves = [cotangent[:, q, pl.ds(x, 16), :] for q in range(2)]
         cotangent_here = jnp.concatenate(halves, axis=2).astype(jnp.float32)
-        rights = []
-        mobiles = []
-        right = jnp.concatenate([smooth[0, 2 * i + h] for h in range(2)], axis=1)
-        local = dot(mix_out[...], right).reshape(channels, 8, 4 * NY)
+        spreads = []
         for h in range(2):
             at = pl.ds(pl.multiple_of(x + 8 * h, 8), 8)
             mobile = moving[at, :][None]
-            local_here = local[:, :, 2 * NY * h : 2 * NY * (h + 1)]
-            half = spectral[:, at, :] + mobile * local_here + bias_wide[...]
+            local = dot(mix_out[...], smooth[0, 2 * i + h]).reshape(channels, 8, 2 * NY)
+            half = spectral[:, at, :] + mobile * local + bias_wide[...]
             wave = jnp.tanh(half)
             slope = (1.0 + wave) * (1.0 + (half - half * wave))
             change = cotangent_here[:, 8 * h : 8 * h + 8, :] * slope
             right = change.reshape(8 * channels, 2 * NY).astype(jnp.bfloat16)
             delta[2 * i + h] = right
-            rights.append(right)
-            mobiles.append(mobile)
-        back = dot(mix_in[...], jnp.concatenate(rights, axis=1)).reshape(channels, 8, 4 * NY)
-        spreads = [mobiles[h] * back[:, :, 2 * NY * h : 2 * NY * (h + 1)] for h in range(2)]
+            back = dot(mix_in[...], right).reshape(channels, 8, 2 * NY)
+            spreads.append(mobile * back)
         both = jnp.concatenate(spreads, axis=1).astype(jnp.bfloat16)
         for q in range(2):
             spread[:, q, pl.ds(x, 16), :] = both[:, :, q * NY : (q + 1) * NY]
@@ -545,23 +558,15 @@
 
     lax.fori_loop(0, NX // 16, body, 0, unroll=4)
 
-    for step in range(channels // 8):
-        right = [
-            delta[:, 16 * i : 16 * i + 16, :].reshape(2 * NX, 2 * NY)
-            for i in range(4 * step, 4 * step + 4)
-        ]
-        product = dot(x_table[...], jnp.concatenate(right, axis=1))
-        parts = [product[:, 2 * NY * i : 2 * NY * (i + 1)] for i in range(4)]
-        for i in range(2):
-            store_rows(rows, 32 * step + 16 * i, [(pair, parts[2 * i : 2 * i + 2])])
-
-    @pl.when(pair == 0)
-    def _():
-        first[:, 0] = spread[:, 0]
+    store_rims(spread, rims, pair, pairs)
+
+    def load(i):
+        return delta[:, 16 * i : 16 * i + 16, :].reshape(2 * NX, 2 * NY)
+
+    store_rows(rows, pair, x_table, load)
 
     @pl.when(pair == pairs - 1)
     def _():
-        last[:, 0] = spread[:, 1]
         store_modes(rows, y_table, out)
 
 
@@ -575,8 +580,7 @@
     x_table = constant(forward_x_table(slabs, True))
     y_table = constant(forward_y_table(planes))
     field = pl.BlockSpec((channels, 2, NX, NY), lambda p: (0, p, 0, 0))
-    rim = (channels, 1, NX, NY)
-    outs = [cotangent.shape, planar.shape, rim, rim]
+    outs = [cotangent.shape, planar.shape] + [(channels // 2, 1, NX, NY)] * 4
     return pl.pallas_call(
         layer_kernel,
         grid=(pairs,),
@@ -593,7 +597,7 @@
             whole(x_table.shape),
             whole(y_table.shape),
         ],
-        out_specs=[field, whole(planar.shape), whole(rim), whole(rim)],
+        out_specs=[field] + [whole(out) for out in outs[1:]],
         out_shape=[jax.ShapeDtypeStruct(out, jnp.bfloat16) for out in outs],
         scratch_shapes=[
             pltpu.VMEM((slabs, 2, lines, 2 * NY), jnp.bfloat16),
@@ -650,72 +654,89 @@
     return totals
 
 
-def banded(adjoint, taps, even, odd, channels):
+def banded(adjoint, taps, start, even, odd, channels):
     step = pl.program_id(0)
-    final = channels * pl.num_programs(0) - 1
+    final = start + channels * pl.num_programs(0) - 1
     bands = (even, odd)
 
     @pl.when(step == 0)
     def _():
         even[...] = jnp.zeros_like(even)
         odd[...] = jnp.zeros_like(odd)
-        build_band(adjoint, taps, 0, even)
+        build_band(adjoint, taps, start, even)
 
     def run(visit):
         for c in range(channels):
-            following = jnp.minimum(channels * step + c + 1, final)
+            following = jnp.minimum(start + channels * step + c + 1, final)
             build_band(adjoint, taps, following, bands[(c + 1) % 2])
             visit(c, bands[c % 2])
 
     return run
 
 
-def smooth_kernel(taps, before, field, after, out, even, odd):
+def stencil_kernel(adjoint, start, taps, before, field, after, *rest):
+    out, even, odd = rest[-3:]
     planes = field.shape[1]
     totals = []
 
     def visit(c, band):
         sheets = [before[c, 0]] + [field[c, z] for z in range(planes)] + [after[c, 0]]
-        totals.append(apply_band([sheets[z : z + 4] for z in range(0, planes, 2)], band))
-
-    banded(False, taps, even, odd, 2)(visit)
-    for p in range(planes // 2):
-        both = [totals[c][p].reshape(NX // 8, 8, 2 * NY) for c in range(2)]
-        out[p] = jnp.concatenate(both, axis=1).astype(jnp.bfloat16)
-
-
-def smooth_planes(field, rims, taps):
+        pairs = apply_band([sheets[z : z + 4] for z in range(0, planes, 2)], band)
+        if adjoint:
+            for p, total in enumerate(pairs):
+                total = total.astype(jnp.bfloat16)
+                out[c, 2 * p] = total[:, :NY]
+                out[c, 2 * p + 1] = total[:, NY:]
+        else:
+            totals.append(pairs)
+
+    banded(adjoint, taps, start, even, odd, 2)(visit)
+    if not adjoint:
+        for p in range(planes // 2):
+            both = [totals[c][p].reshape(NX // 8, 8, 2 * NY) for c in range(2)]
+            out[p] = jnp.concatenate(both, axis=1).astype(jnp.bfloat16)
+
+
+def stencil_planes(field, rims, taps, adjoint, done=None):
     channels, planes = field.shape[:2]
     pairs = planes // 2
+    start = 0 if done is None else channels // 2
+    skip = start // 2
     rim = pl.BlockSpec((2, 1, NX, NY), lambda c: (c, 0, 0, 0))
+    sheets = pl.BlockSpec((2, planes, NX, NY), lambda c: (c + skip, 0, 0, 0))
+    in_specs = [pl.BlockSpec(memory_space=pltpu.SMEM), rim, sheets, rim]
+    operands = [taps, rims[0], field, rims[1]]
+    if done is not None:
+        in_specs.append(pl.BlockSpec(memory_space=pl.ANY))
+        operands.append(done)
+    if adjoint:
+        out_spec, shape = sheets, field.shape
+    else:
+        out_spec = pl.BlockSpec((pairs, NX // 8, 16, 2 * NY), lambda c: (0, 0, c + skip, 0))
+        shape = (pairs, NX // 8, 8 * channels, 2 * NY)
+    name = "near" if adjoint else "smooth"
     return pl.pallas_call(
-        smooth_kernel,
-        grid=(channels // 2,),
-        in_specs=[
-            pl.BlockSpec(memory_space=pltpu.SMEM),
-            rim,
-            pl.BlockSpec((2, planes, NX, NY), lambda c: (c, 0, 0, 0)),
-            rim,
-        ],
-        out_specs=pl.BlockSpec((pairs, NX // 8, 16, 2 * NY), lambda c: (0, 0, c, 0)),
-        out_shape=jax.ShapeDtypeStruct((pairs, NX // 8, 8 * channels, 2 * NY), jnp.bfloat16),
+        functools.partial(stencil_kernel, adjoint, start),
+        grid=(channels // 4,),
+        in_specs=in_specs,
+        out_specs=out_spec,
+        out_shape=jax.ShapeDtypeStruct(shape, jnp.bfloat16),
+        input_output_aliases={} if done is None else {4: 0},
         scratch_shapes=[pltpu.VMEM((4 * NY, 6 * NY), jnp.bfloat16) for _ in range(2)],
         compiler_params=params(),
         cost_estimate=LIGHT,
-        name="smooth",
-    )(taps, rims[0], field, rims[1])
-
-
-def finish_kernel(taps, before, field, after, planar, ix_table, iy_table, out, waves, spectral,
-                  even, odd):
+        name=name + ("_low" if done is None else "_high"),
+    )(*operands)
+
+
+def finish_kernel(planar, near, ix_table, iy_table, out, waves):
     step = pl.program_id(0)
-    slabs = planar.shape[0]
-    planes = field.shape[1]
+    slabs, lines = planar.shape[:2]
+    planes = near.shape[1]
     span = planes * NY
 
     @pl.when(step == 0)
     def _():
-        lines = planar.shape[1]
         left = jnp.concatenate([planar[s] for s in range(slabs)], axis=0)
         for t in range(2):
             wave = dot(left, iy_table[0, :, t * span : (t + 1) * span]).astype(jnp.bfloat16)
@@ -725,51 +746,33 @@
     rows = 4 * (KX // slabs)
     here = pl.ds(pl.multiple_of(rows * step, rows), rows)
     right = [waves[s, t, here, :] for s in range(slabs) for t in range(2)]
-    spectral[...] = dot(ix_table[...], jnp.concatenate(right, axis=0))
-
-    def visit(c, band):
-        sheets = [before[c, 0]] + [field[c, z] for z in range(planes)] + [after[c, 0]]
-        totals = apply_band([sheets[z : z + 4] for z in range(0, planes, 2)], band)
-        for p in range(planes // 2):
-            wide = slice(2 * p * NY, 2 * (p + 1) * NY)
-            total = (totals[p] + spectral[c * NX : (c + 1) * NX, wide]).astype(jnp.bfloat16)
-            out[c, 2 * p] = total[:, :NY]
-            out[c, 2 * p + 1] = total[:, NY:]
-
-    banded(True, taps, even, odd, 4)(visit)
-
-
-def finish(planar, spread, rims, taps):
+    right = jnp.concatenate(right, axis=0)
+    for p in range(planes // 2):
+        spectral = dot(ix_table[...], right[:, 2 * p * NY : 2 * (p + 1) * NY])
+        for c in range(4):
+            for q in range(2):
+                far = spectral[c * NX : (c + 1) * NX, q * NY : (q + 1) * NY]
+                total = far + near[c, 2 * p + q].astype(jnp.float32)
+                out[c, 2 * p + q] = total.astype(jnp.bfloat16)
+
+
+def finish(planar, near):
     slabs, lines, width = planar.shape
-    channels, planes = spread.shape[:2]
+    channels, planes = near.shape[:2]
     ix_table = constant(inverse_x_table(slabs, 4))
     iy_table = constant(inverse_y_table(planes, planes))
-    rim = pl.BlockSpec((4, 1, NX, NY), lambda c: (c, 0, 0, 0))
     sheets = pl.BlockSpec((4, planes, NX, NY), lambda c: (c, 0, 0, 0))
     return pl.pallas_call(
         finish_kernel,
         grid=(channels // 4,),
-        in_specs=[
-            pl.BlockSpec(memory_space=pltpu.SMEM),
-            rim,
-            sheets,
-            rim,
-            whole(planar.shape),
-            whole(ix_table.shape),
-            whole(iy_table.shape),
-        ],
+        in_specs=[whole(planar.shape), sheets, whole(ix_table.shape), whole(iy_table.shape)],
         out_specs=sheets,
-        out_shape=jax.ShapeDtypeStruct(spread.shape, jnp.bfloat16),
-        scratch_shapes=[
-            pltpu.VMEM((slabs, 2, lines, planes * NY), jnp.bfloat16),
-            pltpu.VMEM((4 * NX, planes * NY), jnp.float32),
-            pltpu.VMEM((4 * NY, 6 * NY), jnp.bfloat16),
-            pltpu.VMEM((4 * NY, 6 * NY), jnp.bfloat16),
-        ],
+        out_shape=jax.ShapeDtypeStruct(near.shape, jnp.bfloat16),
+        scratch_shapes=[pltpu.VMEM((slabs, 2, lines, planes * NY), jnp.bfloat16)],
         compiler_params=params(),
         cost_estimate=HEAVY,
         name="finish",
-    )(taps, rims[0], spread, rims[1], planar, ix_table, iy_table)
+    )(planar, near, ix_table, iy_table)
 
 
 def gradient_kernel(depth, where, gathered, first, second, out):
@@ -778,18 +781,24 @@
     half = rows // 4
     lane = lax.broadcasted_iota(jnp.int32, (1, lines), 1)
     mine = lane % depth == step
-    total = jnp.zeros(out.shape, jnp.float32)
+    spectra = [gathered[s, : 2 * half] for s in range(samples)]
+    duals = []
     for s in range(samples):
-        spectrum = jnp.where(mine, gathered[s, : 2 * half], 0)
         real = gathered[s, 2 * half : 3 * half]
         imag = gathered[s, 3 * half :]
-        dual = jnp.concatenate(
-            [jnp.where(where[0] == 0, real, imag), jnp.where(where[0] == 0, imag, -real)], axis=0
-        )
-        dual = jnp.where(mine, dual, 0)
-        product = dot(spectrum, first[0]) * dot(dual, second[...])
-        total = total + product[:half] + product[half:]
-    out[...] = total * (1.0 / samples)
+        duals.append(jnp.where(where[0] == 0, real, imag))
+        duals.append(jnp.where(where[0] == 0, imag, -real))
+    spectra = jnp.where(mine, jnp.concatenate(spectra, axis=0), 0)
+    duals = jnp.where(mine, jnp.concatenate(duals, axis=0), 0)
+    wide = dot(duals, second[...])
+    for column in range(0, out.shape[1], 256):
+        product = dot(spectra, first[0, :, column : column + 256])
+        for at in range(0, 256, 128):
+            total = 0.0
+            for s in range(2 * samples):
+                here = slice(s * half, (s + 1) * half)
+                total = total + product[here, at : at + 128] * wide[here]
+            out[:, column + at : column + at + 128] = total * (1.0 / samples)
 
 
 def weight_gradient(gathered, depth, width, index):
@@ -798,9 +807,8 @@
     square = channels * channels
     cuts = square // width
     first = first_table(channels, depth).reshape(lines, cuts, width).transpose(1, 0, 2)
-    second = second_table(channels, depth)[:, :width]
     first = constant(first)
-    second = constant(second)
+    second = constant(second_table(channels, depth)[:, :128])
     where = jnp.stack([index // cuts, index % cuts]).astype(jnp.int32)
     half = rows // 4
     return pl.pallas_call(
@@ -822,7 +830,7 @@
     )(where, gathered, first, second)
 
 
-def neighbours(first, last):
+def exchange(first, last):
     size = lax.axis_size("slab")
     up = [(i, i + 1) for i in range(size - 1)]
     down = [(j, i) for i, j in up]
@@ -845,18 +853,27 @@
     weight = spec_weight.reshape(mode_rows * KZ, 2 * channels * channels)
     width = weight.shape[1] // copies
 
-    planar, first, last = forward_modes(field, slabs)
+    planar, first, first_high, last, last_high = forward_modes(field, slabs)
     planar, first, last = barrier((swap(planar), first, last))
-    rims = neighbours(first, last)
+    rims = exchange(first, last)
     spectrum, planar = mix(planar, weight, cell_scale, 0.5 * mode_scale)
     planar = swap(planar)
-    smooth = smooth_planes(field, rims, taps)
-    spread, planar, first, last = layer(planar, smooth, cotangent[0], grains[0], bias, point_weight)
-    rims = neighbours(first, last)
+    rims, first, last, spectrum = barrier((rims, first_high, last_high, spectrum))
+    rims_high = exchange(first, last)
+    smooth = stencil_planes(field, rims, taps, False)
+    smooth = stencil_planes(field, rims_high, taps, False, smooth)
+    spread, planar, first, first_high, last, last_high = layer(
+        planar, smooth, cotangent[0], grains[0], bias, point_weight
+    )
+    rims = exchange(first, last)
     planar, send = mix(swap(planar), weight, 0.5 * mode_scale, cell_scale, spectrum, copies)
     planar = swap(planar)
+    rims, first, last, send = barrier((rims, first_high, last_high, send))
+    rims_high = exchange(first, last)
+    near, send = barrier((stencil_planes(spread, rims, taps, True), send))
+    near = stencil_planes(spread, rims_high, taps, True, near)
     gathered = lax.all_to_all(send, "dp", split_axis=0, concat_axis=0)
-    grad_feats = finish(planar, spread, rims, taps)
+    grad_feats = finish(planar, near)
     grad_feats, gathered = barrier((grad_feats, gathered))
     grad_feats = grad_feats[None]
     grad_spec = weight_gradient(gathered, KX // slabs, width, lax.axis_index("dp"))

time: 181 us -> 181 us (level)
  waiting for transfers between devices: 28.7 us -> 11.8 us
  starting transfers between devices: 26.4 us -> 36.4 us
  Pallas kernels: 103 us -> 108 us
    all_to_all x3, waiting for transfers between devices: 17 us -> 1.84 us  [swap(): return lax.all_to_all(planar, 'slab', split_axis=0, concat_axis=0)]
    pallas_call x3 -> x6, Pallas kernels: 51.9 us -> 63.4 us  [the longest x4 44.5 us: stencil_planes(): pl.pallas_call(functools.partial(stencil_kernel, adjoint, start), grid=(c...]
    ppermute x4 -> x8, starting transfers between devices: 8.74 us -> 18.7 us  [exchange(): return (lax.ppermute(last, 'slab', up), lax.ppermute(first, 'slab', down))]
    ppermute x4 -> x8, waiting for transfers between devices: 11.7 us -> 7 us  [exchange(): return (lax.ppermute(last, 'slab', up), lax.ppermute(first, 'slab', down))]
    pallas_call x1, Pallas kernels: 27.1 us -> 23.3 us  [layer(): pl.pallas_call(layer_kernel, grid=(pairs,), in_specs=[pl.BlockSpec(memory...]
    all_to_all x1, waiting for transfers between devices: 0.01 us -> 2.93 us  [local_fast(): gathered = lax.all_to_all(send, 'dp', split_axis=0, concat_axis=0)]
    unnamed x16 -> x32, local copies, waits for them, and re-layouts: 4.65 us -> 5.55 us
  transfers between devices with their start and end apart: 8 -> 12, of which waited for: 4 -> 5; matrix products, arithmetic and copies ran while one was open for 0% -> 0% of each run, Pallas kernels for 33% -> 40%
where the time goes in v6:
time: 181 us; the launch traced here: 179 us
  Pallas kernels  108 us (60%)
  starting transfers between devices  36.4 us (20%)
  blocking collectives  15.3 us (8%)
  waiting for transfers between devices  11.8 us (7%)
  local copies, waits for them, and re-layouts  5.55 us (3%)
    pallas_call x4, Pallas kernels, stencil_planes(): pl.pallas_call(functools.partial(stencil_kernel, adjoint, start), grid=(c...  44.5 us
    pallas_call x1, Pallas kernels, layer(): pl.pallas_call(layer_kernel, grid=(pairs,), in_specs=[pl.BlockSpec(memory...  23.3 us
    ppermute x8, starting transfers between devices, exchange(): return (lax.ppermute(last, 'slab', up), lax.ppermute(first, 'slab', down))  18.7 us
    all_to_all x1, blocking collectives, swap(): return lax.all_to_all(planar, 'slab', split_axis=0, concat_axis=0)  15.3 us
    pallas_call x2, Pallas kernels, mix(): pl.pallas_call(functools.partial(mixing_kernel, scale_in, scale_out, adjo...  15.2 us
    all_to_all x3, starting transfers between devices, swap(): return lax.all_to_all(planar, 'slab', split_axis=0, concat_axis=0)  14.2 us
    pallas_call x1, Pallas kernels, finish(): pl.pallas_call(finish_kernel, grid=(channels // 4,), in_specs=[whole(plan...  11.5 us
    pallas_call x1, Pallas kernels, forward_modes(): pl.pallas_call(forward_kernel, grid=(planes // 2,), in_specs=[pl.BlockSpe...  7.46 us
  transfers between devices with their start and end apart: 12, of which 5 were waited for; matrix products, arithmetic and copies ran while one was open for 0% of the time, Pallas kernels for 40%

profile of v6, /device:TPU:0, one launch (start us, length us, event | category | flops | bytes accessed | tf_op | source)
XLA Modules:
  0.0 178.7 jit_solution(3075196310088043206)
XLA Ops:
  0.6 7.5 %forward_modes.1 = (bf16[4,128,256]{2,1,0:T(8,128)(2,1)}, bf16[16,1,128,128]{3,2,1,0:T(8,128)(2,1)}, bf16[16,1,128,128]{3,2,1,0:T(8,128)(2,1)}, bf16[16,1,128,12...) custom-call(bf16[32,8,128,128]{3,2,1,0:T(8,128)(2,1)} %bitcast.8, bf16[64,256]{1,0:T(8,128)(2,1)} %constant.59.clone.x_table, ...), custom_call_target="tpu_custom_call" | custom-call | flops 10000000 | bytes 100000 | tf_op jit(solution)/shard_map/forward_modes/pallas_call | solution.py:362
  8.1 15.3 %all_to_all.25.planar = bf16[4,128,256]{2,1,0:T(8,128)(2,1)} all-to-all(bf16[4,128,256]{2,1,0:T(8,128)(2,1)} %get-tuple-element.34), channel_id=1, replica_groups=mesh['grp'=2,'dp'=4,'slab'=4] {'slab'}, dimensions={0} | all-to-all | bytes 524288 | tf_op jit(solution)/shard_map/all_to_all | solution.py:841
  23.4 2.1 %collective-permute-start = (bf16[16,1,128,128]{3,2,1,0:T(8,128)(2,1)}, bf16[16,1,128,128]{3,2,1,0:T(8,128)(2,1)S(1)}, u32[]{:S(2)}, u32[]{:S(2)}) collective-permute-start(bf16[16,1,128,128]{3,2,1,0:T(8,128)(2,1)} %get-tuple-element.39), channel_id=1, source_target_pairs={{0,1},{1,2},{2,3},{4,5},{5,6},{6,7},{8,9},{9,10},{10,11},{12,13},{... | collective-permute-start | bytes 1572872 | tf_op jit(solution)/shard_map/ppermute | solution.py:837
  25.5 1.3 collective-permute-start.1
  26.8 0.0 copy-start.15
  26.8 0.0 copy-start.14
  26.9 7.3 %mix.1 = (bf16[512,128]{1,0:T(8,128)(2,1)}, bf16[4,128,256]{2,1,0:T(8,128)(2,1)}) custom-call(bf16[4,128,256]{2,1,0:T(8,128)(2,1)} %all_to_all.25.planar, bf16[1024,2048]{1,0:T(8,128)(2,1)} %bitcast.14, bf16[1024,512]{1,0:T(8,128)(2,1)} %constant.61.clone.z_in, bf16[512,1024]{1,0:T(8,128)(2,1)} %constant.62.clone.z_out, ...), custom_call_target="tpu_custom_call" | custom-call | flops 99999997952 | bytes 100000000 | tf_op jit(solution)/shard_map/mix/pallas_call | solution.py:473
  34.2 1.1 collective-permute-done.before
  35.3 4.0 %collective-permute-done.1.after = bf16[16,1,128,128]{3,2,1,0:T(8,128)(2,1)S(1)} collective-permute-done((bf16[16,1,128,128]{3,2,1,0:T(8,128)(2,1)}, bf16[16,1,128,128]{3,2,1,0:T(8,128)(2,1)S(1)}, u32[]{:S(2)}, u32[]{:S(2)}) %collective-permute-start.1) | collective-permute-done | bytes 524320 | tf_op jit(solution)/shard_map/ppermute | solution.py:837
  39.4 0.0 copy-done.15
  39.4 3.7 %collective-permute-start.2 = (bf16[16,1,128,128]{3,2,1,0:T(8,128)(2,1)S(1)}, bf16[16,1,128,128]{3,2,1,0:T(8,128)(2,1)S(1)}, u32[]{:S(2)}, u32[]{:S(2)}) collective-permute-start(bf16[16,1,128,128]{3,2,1,0:T(8,128)(2,1)S(1)} %copy-done.15), channel_id=1, source_target_pairs={{0,1},{1,2},{2,3},{4,5},{5,6},{6,7},{8,9},{9,10},{10,11},{12,13},{... | collective-permute-start | bytes 1572872 | tf_op jit(solution)/shard_map/ppermute | solution.py:837
  43.1 1.3 collective-permute-start.3
  44.4 5.1 %all-to-all-start.1 = ((bf16[4,128,256]{2,1,0:T(8,128)(2,1)}), bf16[4,128,256]{2,1,0:T(8,128)(2,1)S(1)}, u32[]{:S(2)}, u32[]{:S(2)}) async-start(bf16[4,128,256]{2,1,0:T(8,128)(2,1)} %get-tuple-element.38), calls=%async_computation.1 | async-start | bytes 524288 | tf_op jit(solution)/shard_map/all_to_all | solution.py:841
  49.5 0.0 copy-done.6
  49.5 11.1 %smooth_low.1.rest_0_ = bf16[4,16,256,256]{3,2,1,0:T(8,128)(2,1)} custom-call(f32[27,32]{1,0:T(8,128)} %taps.7, bf16[16,1,128,128]{3,2,1,0:T(8,128)(2,1)} %copy-done.6, bf16[32,8,128,128]{3,2,1,0:T(8,128)(2,1)} %bitcast.9, bf16[16,1,128,128]{3,2,1,0:T(8,128)(2,1)} %copy-done.7), custom_call_target="tpu_custom_call" | custom-call | flops 10000000 | bytes 100000 | tf_op jit(solution)/shard_map/smooth_low/pallas_call | solution.py:718
  60.6 0.0 collective-permute-done.2.before
  60.6 0.0 collective-permute-done.3.after
  60.6 0.8 copy-done.8
  61.4 0.8 copy-done.9
  62.2 11.1 %smooth_high.1.smooth = bf16[4,16,256,256]{3,2,1,0:T(8,128)(2,1)} custom-call(f32[27,32]{1,0:T(8,128)} %taps.7, bf16[16,1,128,128]{3,2,1,0:T(8,128)(2,1)} %copy-done.8, bf16[32,8,128,128]{3,2,1,0:T(8,128)(2,1)} %bitcast.10, bf16[16,1,128,128]{3,2,1,0:T(8,128)(2,1)} %copy-done.9, ...), custom_call_target="tpu_custom_call", output_to_operand_aliasing={{}: (4, {})} | custom-call | flops 10000000 | bytes 100000 | tf_op jit(solution)/shard_map/smooth_high/pallas_call | solution.py:718
  73.3 0.0 all-to-all-done.1.planar
  73.3 0.7 copy-done.1
  74.0 23.3 %layer.1 = (bf16[32,8,128,128]{3,2,1,0:T(8,128)(2,1)}, bf16[4,128,256]{2,1,0:T(8,128)(2,1)}, bf16[16,1,128,128]{3,2,1,0:T(8,128)(2,1)}, bf16[16,1,128,128]{3,2,1...) custom-call(f32[32]{0:T(128)} %bias.1, bf16[4,128,256]{2,1,0:T(8,128)(2,1)} %copy-done.1, ...), custom_call_target="tpu_custom_call" | custom-call | flops 10000000 | bytes 100000 | tf_op jit(solution)/shard_map/layer/pallas_call | solution.py:584
  97.3 5.1 %all-to-all-start.2 = ((bf16[4,128,256]{2,1,0:T(8,128)(2,1)}), bf16[4,128,256]{2,1,0:T(8,128)(2,1)S(1)}, u32[]{:S(2)}, u32[]{:S(2)}) async-start(bf16[4,128,256]{2,1,0:T(8,128)(2,1)} %get-tuple-element.48), calls=%async_computation.2 | async-start | bytes 524288 | tf_op jit(solution)/shard_map/all_to_all | solution.py:841
  102.4 3.9 %collective-permute-start.4 = (bf16[16,1,128,128]{3,2,1,0:T(8,128)(2,1)}, bf16[16,1,128,128]{3,2,1,0:T(8,128)(2,1)S(1)}, u32[]{:S(2)}, u32[]{:S(2)}) collective-permute-start(bf16[16,1,128,128]{3,2,1,0:T(8,128)(2,1)} %get-tuple-element.51), channel_id=1, source_target_pairs={{0,1},{1,2},{2,3},{4,5},{5,6},{6,7},{8,9},{9,10},{10,11},{12,13},{... | collective-permute-start | bytes 1572872 | tf_op jit(solution)/shard_map/ppermute | solution.py:837
  106.4 1.4 collective-permute-start.5
  107.8 1.8 %all-to-all-done.2.planar = bf16[4,128,256]{2,1,0:T(8,128)(2,1)S(1)} async-done(((bf16[4,128,256]{2,1,0:T(8,128)(2,1)}), bf16[4,128,256]{2,1,0:T(8,128)(2,1)S(1)}, u32[]{:S(2)}, u32[]{:S(2)}) %all-to-all-start.2) | async-done | bytes 262176 | tf_op jit(solution)/shard_map/all_to_all | solution.py:841
  109.7 0.7 copy-done.11
  110.4 7.9 %mix_back.1 = (bf16[4,128,256]{2,1,0:T(8,128)(2,1)}, bf16[4,1024,128]{2,1,0:T(8,128)(2,1)}) custom-call(bf16[4,128,256]{2,1,0:T(8,128)(2,1)} %copy-done.11, bf16[1024,2048]{1,0:T(8,128)(2,1)} %bitcast.15, bf16[1024,512]{1,0:T(8,128)(2,1)} %constant.61.clone.z_in, bf16[512,1024]{1,0:T(8,128)(2,1)} %constant.62.clone.z_out, ...), custom_call_target="tpu_custom_call" | custom-call | flops 99999997952 | bytes 100000000 | tf_op jit(solution)/shard_map/mix_back/pallas_call | solution.py:473
  118.2 0.0 collective-permute-done.4.before
  118.2 1.8 %collective-permute-done.5.after = bf16[16,1,128,128]{3,2,1,0:T(8,128)(2,1)S(1)} collective-permute-done((bf16[16,1,128,128]{3,2,1,0:T(8,128)(2,1)}, bf16[16,1,128,128]{3,2,1,0:T(8,128)(2,1)S(1)}, u32[]{:S(2)}, u32[]{:S(2)}) %collective-permute-start.5) | collective-permute-done | bytes 524320 | tf_op jit(solution)/shard_map/ppermute | solution.py:837
  120.0 3.6 %collective-permute-start.6 = (bf16[16,1,128,128]{3,2,1,0:T(8,128)(2,1)S(1)}, bf16[16,1,128,128]{3,2,1,0:T(8,128)(2,1)S(1)}, u32[]{:S(2)}, u32[]{:S(2)}) collective-permute-start(bf16[16,1,128,128]{3,2,1,0:T(8,128)(2,1)S(1)} %copy-done.13), channel_id=1, source_target_pairs={{0,1},{1,2},{2,3},{4,5},{5,6},{6,7},{8,9},{9,10},{10,11},{12,13},{... | collective-permute-start | bytes 1572872 | tf_op jit(solution)/shard_map/ppermute | solution.py:837
  123.7 1.3 collective-permute-start.7
  125.0 4.0 %all-to-all-start.3 = ((bf16[4,128,256]{2,1,0:T(8,128)(2,1)}), bf16[4,128,256]{2,1,0:T(8,128)(2,1)S(1)}, u32[]{:S(2)}, u32[]{:S(2)}) async-start(bf16[4,128,256]{2,1,0:T(8,128)(2,1)} %get-tuple-element.50), calls=%async_computation.3 | async-start | bytes 524288 | tf_op jit(solution)/shard_map/all_to_all | solution.py:841
  129.0 0.7 pad_add_fusion.where
  129.7 0.0 copy-done.3
  129.7 11.1 %near_low.1.rest_0_ = bf16[32,8,128,128]{3,2,1,0:T(8,128)(2,1)} custom-call(f32[27,32]{1,0:T(8,128)} %taps.7, bf16[16,1,128,128]{3,2,1,0:T(8,128)(2,1)} %copy-done.2, bf16[32,8,128,128]{3,2,1,0:T(8,128)(2,1)} %get-tuple-element.57.field, bf16[16,1,128,128]{3,2,1,0:T(8,128)(2,1)} %copy-done.3), custom_call_target="tpu_custom_call" | custom-call | flops 10000000 | bytes 100000 | tf_op jit(solution)/shard_map/near_low/pallas_call | solution.py:718
  140.8 0.0 collective-permute-done.6.before
  140.8 0.0 collective-permute-done.7.after
  140.8 0.8 copy-done.4
  141.6 0.8 copy-done.5
  142.4 11.1 %near_high.1.near = bf16[32,8,128,128]{3,2,1,0:T(8,128)(2,1)} custom-call(f32[27,32]{1,0:T(8,128)} %taps.7, bf16[16,1,128,128]{3,2,1,0:T(8,128)(2,1)} %copy-done.4, bf16[32,8,128,128]{3,2,1,0:T(8,128)(2,1)} %get-tuple-element.57.field, bf16[16,1,128,128]{3,2,1,0:T(8,128)(2,1)} %copy-done.5, ...), custom_call_target="tpu_custom_call", output_to_operand_aliasing={{}: (4, {})} | custom-call | flops 10000000 | bytes 100000 | tf_op jit(solution)/shard_map/near_high/pallas_call | solution.py:718
  153.5 0.0 all-to-all-done.3.planar
  153.5 3.5 %all-to-all-start.4 = ((bf16[4,1024,128]{2,1,0:T(8,128)(2,1)}), bf16[4,1024,128]{2,1,0:T(8,128)(2,1)S(1)}, u32[]{:S(2)}, u32[]{:S(2)}) async-start(bf16[4,1024,128]{2,1,0:T(8,128)(2,1)} %get-tuple-element.63), calls=%async_computation.4 | async-start | bytes 2097152 | tf_op jit(solution)/shard_map/all_to_all | solution.py:875
  157.0 11.5 %finish.1 = bf16[32,8,128,128]{3,2,1,0:T(8,128)(2,1)} custom-call(bf16[4,128,256]{2,1,0:T(8,128)(2,1)} %copy-done.10, bf16[32,8,128,128]{3,2,1,0:T(8,128)(2,1)} %near_high.1.near, bf16[512,128]{1,0:T(8,128)(2,1)} %constant.71.clone.ix_table, bf16[1,256,2048]{2,1,0:T(8,128)(2,1)} %constant.72.clone.iy_table), custom_call_target="tpu_custom_call" | custom-call | flops 99999997952 | bytes 100000000 | tf_op jit(solution)/shard_map/finish/pallas_call | solution.py:765
  168.5 2.9 %all-to-all-done.4.gathered = bf16[4,1024,128]{2,1,0:T(8,128)(2,1)S(1)} async-done(((bf16[4,1024,128]{2,1,0:T(8,128)(2,1)}), bf16[4,1024,128]{2,1,0:T(8,128)(2,1)S(1)}, u32[]{:S(2)}, u32[]{:S(2)}) %all-to-all-start.4) | async-done | bytes 1048608 | tf_op jit(solution)/shard_map/all_to_all | solution.py:875
  171.5 1.0 copy-done
  172.4 6.2 %weight_gradient.1 = f32[1024,512]{1,0:T(8,128)} custom-call(s32[2]{0:T(128)} %pad_add_fusion.where, bf16[4,1024,128]{2,1,0:T(8,128)(2,1)} %copy-done, bf16[2,128,512]{2,1,0:T(8,128)(2,1)} %constant.73.clone.first, bf16[128,128]{1,0:T(8,128)(2,1)} %constant.69.clone.spread_table.second), custom_call_target="tpu_custom_call" | custom-call | flops 10000000 | bytes 100000 | tf_op jit(solution)/shard_map/weight_gradient/pallas_call | solution.py:814
  (20 shorter events, 0.0 us)
Async XLA Ops:
  23.4 12.0 %collective-permute-start = (bf16[16,1,128,128]{3,2,1,0:T(8,128)(2,1)}, bf16[16,1,128,128]{3,2,1,0:T(8,128)(2,1)S(1)}, u32[]{:S(2)}, u32[]{:S(2)}) collective-permute-start(bf16[16,1,128,128]{3,2,1,0:T(8,128)(2,1)} %get-tuple-element.39), channel_id=1, source_target_pairs={{0,1},{1,2},{2,3},{4,5},{5,6},{6,7},{8,9},{9,10},{10,11},{12,13},{... | collective-permute-start | bytes 1572872 | tf_op jit(solution)/shard_map/ppermute | solution.py:837
  25.5 13.8 %collective-permute-start.1 = (bf16[16,1,128,128]{3,2,1,0:T(8,128)(2,1)}, bf16[16,1,128,128]{3,2,1,0:T(8,128)(2,1)S(1)}, u32[]{:S(2)}, u32[]{:S(2)}) collective-permute-start(bf16[16,1,128,128]{3,2,1,0:T(8,128)(2,1)} %get-tuple-element.40), channel_id=1, source_target_pairs={{1,0},{2,1},{3,2},{5,4},{6,5},{7,6},{9,8},{10,9},{11,10},{13,12},{... | collective-permute-start | bytes 1572872 | tf_op jit(solution)/shard_map/ppermute | solution.py:837
  26.8 12.6 %copy-start.15 = (bf16[16,1,128,128]{3,2,1,0:T(8,128)(2,1)S(1)}, bf16[16,1,128,128]{3,2,1,0:T(8,128)(2,1)}, u32[]{:S(2)}) copy-start(bf16[16,1,128,128]{3,2,1,0:T(8,128)(2,1)} %get-tuple-element.44) | copy-start | bytes 1572868
  26.8 16.3 %copy-start.14 = (bf16[16,1,128,128]{3,2,1,0:T(8,128)(2,1)S(1)}, bf16[16,1,128,128]{3,2,1,0:T(8,128)(2,1)}, u32[]{:S(2)}) copy-start(bf16[16,1,128,128]{3,2,1,0:T(8,128)(2,1)} %get-tuple-element.45) | copy-start | bytes 1572868
  35.3 14.1 %copy-start.6 = (bf16[16,1,128,128]{3,2,1,0:T(8,128)(2,1)}, bf16[16,1,128,128]{3,2,1,0:T(8,128)(2,1)S(1)}, u32[]{:S(2)}) copy-start(bf16[16,1,128,128]{3,2,1,0:T(8,128)(2,1)S(1)} %collective-permute-done.before) | copy-start | bytes 1572868
  39.4 10.1 %copy-start.7 = (bf16[16,1,128,128]{3,2,1,0:T(8,128)(2,1)}, bf16[16,1,128,128]{3,2,1,0:T(8,128)(2,1)S(1)}, u32[]{:S(2)}) copy-start(bf16[16,1,128,128]{3,2,1,0:T(8,128)(2,1)S(1)} %collective-permute-done.1.after) | copy-start | bytes 1572868
  39.4 21.2 %collective-permute-start.2 = (bf16[16,1,128,128]{3,2,1,0:T(8,128)(2,1)S(1)}, bf16[16,1,128,128]{3,2,1,0:T(8,128)(2,1)S(1)}, u32[]{:S(2)}, u32[]{:S(2)}) collective-permute-start(bf16[16,1,128,128]{3,2,1,0:T(8,128)(2,1)S(1)} %copy-done.15), channel_id=1, source_target_pairs={{0,1},{1,2},{2,3},{4,5},{5,6},{6,7},{8,9},{9,10},{10,11},{12,13},{... | collective-permute-start | bytes 1572872 | tf_op jit(solution)/shard_map/ppermute | solution.py:837
  43.1 17.5 %collective-permute-start.3 = (bf16[16,1,128,128]{3,2,1,0:T(8,128)(2,1)S(1)}, bf16[16,1,128,128]{3,2,1,0:T(8,128)(2,1)S(1)}, u32[]{:S(2)}, u32[]{:S(2)}) collective-permute-start(bf16[16,1,128,128]{3,2,1,0:T(8,128)(2,1)S(1)} %copy-done.14), channel_id=1, source_target_pairs={{1,0},{2,1},{3,2},{5,4},{6,5},{7,6},{9,8},{10,9},{11,10},{13,12},{... | collective-permute-start | bytes 1572872 | tf_op jit(solution)/shard_map/ppermute | solution.py:837
  44.4 28.9 %all-to-all-start.1 = ((bf16[4,128,256]{2,1,0:T(8,128)(2,1)}), bf16[4,128,256]{2,1,0:T(8,128)(2,1)S(1)}, u32[]{:S(2)}, u32[]{:S(2)}) async-start(bf16[4,128,256]{2,1,0:T(8,128)(2,1)} %get-tuple-element.38), calls=%async_computation.1 | async-start | bytes 524288 | tf_op jit(solution)/shard_map/all_to_all | solution.py:841
  60.6 0.8 copy-start.8
  61.4 0.8 copy-start.9
  73.3 0.7 copy-start.1
  97.3 12.3 %all-to-all-start.2 = ((bf16[4,128,256]{2,1,0:T(8,128)(2,1)}), bf16[4,128,256]{2,1,0:T(8,128)(2,1)S(1)}, u32[]{:S(2)}, u32[]{:S(2)}) async-start(bf16[4,128,256]{2,1,0:T(8,128)(2,1)} %get-tuple-element.48), calls=%async_computation.2 | async-start | bytes 524288 | tf_op jit(solution)/shard_map/all_to_all | solution.py:841
  102.4 15.8 %collective-permute-start.4 = (bf16[16,1,128,128]{3,2,1,0:T(8,128)(2,1)}, bf16[16,1,128,128]{3,2,1,0:T(8,128)(2,1)S(1)}, u32[]{:S(2)}, u32[]{:S(2)}) collective-permute-start(bf16[16,1,128,128]{3,2,1,0:T(8,128)(2,1)} %get-tuple-element.51), channel_id=1, source_target_pairs={{0,1},{1,2},{2,3},{4,5},{5,6},{6,7},{8,9},{9,10},{10,11},{12,13},{... | collective-permute-start | bytes 1572872 | tf_op jit(solution)/shard_map/ppermute | solution.py:837
  106.4 13.7 %copy-start.13 = (bf16[16,1,128,128]{3,2,1,0:T(8,128)(2,1)S(1)}, bf16[16,1,128,128]{3,2,1,0:T(8,128)(2,1)}, u32[]{:S(2)}) copy-start(bf16[16,1,128,128]{3,2,1,0:T(8,128)(2,1)} %get-tuple-element.56) | copy-start | bytes 1572868
  106.4 17.3 %copy-start.12 = (bf16[16,1,128,128]{3,2,1,0:T(8,128)(2,1)S(1)}, bf16[16,1,128,128]{3,2,1,0:T(8,128)(2,1)}, u32[]{:S(2)}) copy-start(bf16[16,1,128,128]{3,2,1,0:T(8,128)(2,1)} %get-tuple-element.58) | copy-start | bytes 1572868
  106.4 13.7 %collective-permute-start.5 = (bf16[16,1,128,128]{3,2,1,0:T(8,128)(2,1)}, bf16[16,1,128,128]{3,2,1,0:T(8,128)(2,1)S(1)}, u32[]{:S(2)}, u32[]{:S(2)}) collective-permute-start(bf16[16,1,128,128]{3,2,1,0:T(8,128)(2,1)} %get-tuple-element.52), channel_id=1, source_target_pairs={{1,0},{2,1},{3,2},{5,4},{6,5},{7,6},{9,8},{10,9},{11,10},{13,12},{... | collective-permute-start | bytes 1572872 | tf_op jit(solution)/shard_map/ppermute | solution.py:837
  109.6 0.7 copy-start.11
  118.2 11.4 %copy-start.2 = (bf16[16,1,128,128]{3,2,1,0:T(8,128)(2,1)}, bf16[16,1,128,128]{3,2,1,0:T(8,128)(2,1)S(1)}, u32[]{:S(2)}) copy-start(bf16[16,1,128,128]{3,2,1,0:T(8,128)(2,1)S(1)} %collective-permute-done.4.before) | copy-start | bytes 1572868
  120.0 9.6 %copy-start.3 = (bf16[16,1,128,128]{3,2,1,0:T(8,128)(2,1)}, bf16[16,1,128,128]{3,2,1,0:T(8,128)(2,1)S(1)}, u32[]{:S(2)}) copy-start(bf16[16,1,128,128]{3,2,1,0:T(8,128)(2,1)S(1)} %collective-permute-done.5.after) | copy-start | bytes 1572868
  120.0 20.8 %collective-permute-start.6 = (bf16[16,1,128,128]{3,2,1,0:T(8,128)(2,1)S(1)}, bf16[16,1,128,128]{3,2,1,0:T(8,128)(2,1)S(1)}, u32[]{:S(2)}, u32[]{:S(2)}) collective-permute-start(bf16[16,1,128,128]{3,2,1,0:T(8,128)(2,1)S(1)} %copy-done.13), channel_id=1, source_target_pairs={{0,1},{1,2},{2,3},{4,5},{5,6},{6,7},{8,9},{9,10},{10,11},{12,13},{... | collective-permute-start | bytes 1572872 | tf_op jit(solution)/shard_map/ppermute | solution.py:837
  123.7 17.2 %collective-permute-start.7 = (bf16[16,1,128,128]{3,2,1,0:T(8,128)(2,1)S(1)}, bf16[16,1,128,128]{3,2,1,0:T(8,128)(2,1)S(1)}, u32[]{:S(2)}, u32[]{:S(2)}) collective-permute-start(bf16[16,1,128,128]{3,2,1,0:T(8,128)(2,1)S(1)} %copy-done.12), channel_id=1, source_target_pairs={{1,0},{2,1},{3,2},{5,4},{6,5},{7,6},{9,8},{10,9},{11,10},{13,12},{... | collective-permute-start | bytes 1572872 | tf_op jit(solution)/shard_map/ppermute | solution.py:837
  125.0 28.5 %all-to-all-start.3 = ((bf16[4,128,256]{2,1,0:T(8,128)(2,1)}), bf16[4,128,256]{2,1,0:T(8,128)(2,1)S(1)}, u32[]{:S(2)}, u32[]{:S(2)}) async-start(bf16[4,128,256]{2,1,0:T(8,128)(2,1)} %get-tuple-element.50), calls=%async_computation.3 | async-start | bytes 524288 | tf_op jit(solution)/shard_map/all_to_all | solution.py:841
  140.8 0.8 copy-start.4
  141.6 0.8 copy-start.5
  153.5 3.5 %copy-start.10 = (bf16[4,128,256]{2,1,0:T(8,128)(2,1)}, bf16[4,128,256]{2,1,0:T(8,128)(2,1)S(1)}, u32[]{:S(2)}) copy-start(bf16[4,128,256]{2,1,0:T(8,128)(2,1)S(1)} %all-to-all-done.3.planar) | copy-start | bytes 786436
  153.5 18.0 %all-to-all-start.4 = ((bf16[4,1024,128]{2,1,0:T(8,128)(2,1)}), bf16[4,1024,128]{2,1,0:T(8,128)(2,1)S(1)}, u32[]{:S(2)}, u32[]{:S(2)}) async-start(bf16[4,1024,128]{2,1,0:T(8,128)(2,1)} %get-tuple-element.63), calls=%async_computation.4 | async-start | bytes 2097152 | tf_op jit(solution)/shard_map/all_to_all | solution.py:875
  171.5 1.0 copy-start

commit v7 on v6

--- a/solution.py
+++ b/solution.py
@@ -322,25 +322,38 @@
         out[s] = modes[s * lines : (s + 1) * lines].astype(jnp.bfloat16)
 
 
-def store_rims(field, rims, pair, pairs):
+def rims_kernel(field, *refs):
+    rims, done = refs[:4], refs[4]
     half = field.shape[0] // 2
-
-    @pl.when(pair == 0)
-    def _():
-        for i in range(2):
-            rims[i][:, 0] = field[half * i : half * (i + 1), 0]
-
-    @pl.when(pair == pairs - 1)
-    def _():
-        for i in range(2):
-            rims[2 + i][:, 0] = field[half * i : half * (i + 1), 1]
-
-
-def forward_kernel(field, x_table, y_table, out, *rest):
-    *rims, rows = rest
+    last = field.shape[1] - 1
+    copies = []
+    for k in range(4):
+        source = field.at[pl.ds(half * (k % 2), half), pl.ds(last * (k // 2), 1)]
+        copies.append(pltpu.make_async_copy(source, rims[k], done.at[k]))
+    for copy in copies:
+        copy.start()
+    for copy in copies:
+        copy.wait()
+
+
+def cut_rims(field):
+    channels = field.shape[0]
+    rim = jax.ShapeDtypeStruct((channels // 2, 1, NX, NY), jnp.bfloat16)
+    return pl.pallas_call(
+        rims_kernel,
+        in_specs=[pl.BlockSpec(memory_space=pl.ANY)],
+        out_specs=[pl.BlockSpec(memory_space=pl.ANY)] * 4,
+        out_shape=[rim] * 4,
+        scratch_shapes=[pltpu.SemaphoreType.DMA((4,))],
+        compiler_params=params(),
+        cost_estimate=LIGHT,
+        name="rims",
+    )(field)
+
+
+def forward_kernel(field, x_table, y_table, out, rows):
     pair = pl.program_id(0)
     pairs = rows.shape[0]
-    store_rims(field, rims, pair, pairs)
 
     def load(i):
         halves = [field[2 * i : 2 * i + 2, q].reshape(2 * NX, NY) for q in range(2)]
@@ -358,7 +371,7 @@
     lines = channels * (KX // slabs)
     x_table = constant(forward_x_table(slabs, False))
     y_table = constant(forward_y_table(planes))
-    outs = [(slabs, lines, planes * 2 * KY)] + [(channels // 2, 1, NX, NY)] * 4
+    shape = (slabs, lines, planes * 2 * KY)
     return pl.pallas_call(
         forward_kernel,
         grid=(planes // 2,),
@@ -367,8 +380,8 @@
             whole(x_table.shape),
             whole(y_table.shape),
         ],
-        out_specs=[whole(out) for out in outs],
-        out_shape=[jax.ShapeDtypeStruct(out, jnp.bfloat16) for out in outs],
+        out_specs=whole(shape),
+        out_shape=jax.ShapeDtypeStruct(shape, jnp.bfloat16),
         scratch_shapes=[pltpu.VMEM((planes // 2, 2, slabs, lines, 2 * NY), jnp.bfloat16)],
         compiler_params=params(),
         cost_estimate=LIGHT,
@@ -396,9 +409,8 @@
         spectrum[...] = modes
         total[...] = jnp.zeros_like(total)
         if adjoint:
-            for d in range(send.shape[0]):
-                send[d, : 2 * half] = partner[...]
-                send[d, 2 * half :] = modes
+            send[: 2 * half] = partner[...]
+            send[2 * half :] = modes
 
     lane = lax.broadcasted_iota(jnp.int32, (1, spectrum.shape[1]), 1)
     mine = lane % steps == step
@@ -436,7 +448,7 @@
             out[s] = modes[:, s * width : (s + 1) * width].astype(jnp.bfloat16)
 
 
-def mix(planar, weight, scale_in, scale_out, partner=None, copies=0):
+def mix(planar, weight, scale_in, scale_out, partner=None):
     slabs, lines, width = planar.shape
     adjoint = partner is not None
     depth = KX // slabs
@@ -467,7 +479,7 @@
         in_specs.append(whole(shape))
         operands.append(partner)
         scratch = [pltpu.VMEM(shape, jnp.bfloat16)] + scratch
-        outs = [planar.shape, (copies, 2 * shape[0], lines)]
+        outs = [planar.shape, (2 * shape[0], lines)]
     else:
         outs = [shape, planar.shape]
     return pl.pallas_call(
@@ -497,9 +509,8 @@
 
 
 def layer_kernel(bias, planar, smooth, cotangent, grains, point_weight, repeat, ix_table, iy_table,
-                 x_table, y_table, spread, out, *rest):
+                 x_table, y_table, spread, out, first, last, *rest):
     pair = pl.program_id(0)
-    rims, rest = rest[:4], rest[4:]
     waves, spectral, moving, delta, rows, bias_wide, mix_out, mix_in = rest
     pairs = rows.shape[0]
     channels = cotangent.shape[0]
@@ -558,7 +569,14 @@
 
     lax.fori_loop(0, NX // 16, body, 0, unroll=4)
 
-    store_rims(spread, rims, pair, pairs)
+
+    @pl.when(pair == 0)
+    def _():
+        first[:, 0] = spread[:, 0]
+
+    @pl.when(pair == pairs - 1)
+    def _():
+        last[:, 0] = spread[:, 1]
 
     def load(i):
         return delta[:, 16 * i : 16 * i + 16, :].reshape(2 * NX, 2 * NY)
@@ -580,7 +598,7 @@
     x_table = constant(forward_x_table(slabs, True))
     y_table = constant(forward_y_table(planes))
     field = pl.BlockSpec((channels, 2, NX, NY), lambda p: (0, p, 0, 0))
-    outs = [cotangent.shape, planar.shape] + [(channels // 2, 1, NX, NY)] * 4
+    outs = [cotangent.shape, planar.shape] + [(channels, 1, NX, NY)] * 2
     return pl.pallas_call(
         layer_kernel,
         grid=(pairs,),
@@ -617,40 +635,68 @@
 
 
 def build_band(adjoint, taps, channel, band):
-    row = lax.broadcasted_iota(jnp.int32, (8, NY), 0)
-    lane = lax.broadcasted_iota(jnp.int32, (8, NY), 1)
-    offset = row - lane
-    for dz in range(3):
-        for dx in range(3):
-            tile = jnp.zeros((8, NY), jnp.float32)
-            for dy in range(3):
-                number = 9 * dz + 3 * dx + dy
-                tap = taps[26 - number if adjoint else number, channel]
-                hit = (offset == dy - 1) | (offset == dy - 1 - NY)
-                tile = jnp.where(hit, tap, tile)
-            tiles = [pltpu.roll(tile, 8 * k, axis=1) if k > 0 else tile for k in range(NY // 8)]
-            tiles[0] = jnp.where((row == 0) & (lane == NY - 1), 0.0, tiles[0])
-            tiles[-1] = jnp.where((row == 7) & (lane == 0), 0.0, tiles[-1])
-            block = jnp.concatenate(tiles, axis=0).astype(jnp.bfloat16)
+    row = lax.broadcasted_iota(jnp.int32, (8, 128), 0)
+    lane = lax.broadcasted_iota(jnp.int32, (8, 128), 1)
+    for dy in range(3):
+        for q in range(2):
+            halves = []
+            for side in range(2):
+                tile = jnp.zeros((8, 128), jnp.float32)
+                for k in range(2):
+                    dz = 2 * side + k - q
+                    if not 0 <= dz <= 2:
+                        continue
+                    for dx in range(3):
+                        number = 9 * dz + 3 * dx + dy
+                        tap = taps[26 - number if adjoint else number, channel]
+                        hit = lane == (64 * k + row + (dx - 1)) % 128
+                        tile = jnp.where(hit, tap, tile)
+                tiles = [pltpu.roll(tile, 8 * k, axis=1) if k > 0 else tile for k in range(8)]
+                low = (row == 0) & (lane % 64 == 63)
+                high = (row == 7) & (lane % 64 == 0)
+                tiles[0] = jnp.where(low, 0.0, tiles[0])
+                tiles[7] = jnp.where(high, 0.0, tiles[7])
+                halves.append(jnp.concatenate(tiles[1:7] + [tiles[0], tiles[7]], axis=0))
+            at = 64 * (2 * dy + q)
+            band[at : at + 64, :] = jnp.concatenate(halves, axis=1).astype(jnp.bfloat16)
+
+
+def apply_band(sheets, band):
+    blocks = range(6)
+    lefts = [
+        band[...],
+        jnp.concatenate([band[64 * b : 64 * b + 48, :] for b in blocks], axis=0),
+        jnp.concatenate([band[64 * b + 32 : 64 * b + 64, :] for b in blocks], axis=0),
+    ]
+    lane = lax.broadcasted_iota(jnp.int32, (NX, NY), 1)
+    totals = []
+    for group in range(0, len(sheets) - 2, 4):
+        products = []
+        for left, x in zip(lefts, (0, 48, 64)):
+            right = [
+                jnp.concatenate([sheets[group + 2 * p + k][x : x + 64] for k in range(4)], axis=0)
+                for p in range(2)
+            ]
+            products.append(dot(left, jnp.concatenate(right, axis=1)))
+        for p in range(2):
+            wide = slice(NY * p, NY * (p + 1))
+            pair = []
             for q in range(2):
-                down = (q + dz) * NY
-                right = (2 * dx + q) * NY
-                band[down : down + NY, right : right + NY] = block
-
-
-def apply_band(quads, band):
-    left = jnp.concatenate([jnp.concatenate(quad, axis=1) for quad in quads], axis=0)
-    wide = dot(left, band[...])
-    lower, middle, upper = (wide[:, 2 * NY * dx : 2 * NY * (dx + 1)] for dx in range(3))
-    row = lax.broadcasted_iota(jnp.int32, (8, 2 * NY), 0)
-    totals = []
-    for p in range(len(quads)):
-        here = slice(p * NX, (p + 1) * NX)
-        down = pltpu.roll(lower[here], 1, axis=0)
-        up = pltpu.roll(upper[here], NX - 1, axis=0)
-        down = jnp.concatenate([jnp.where(row == 0, 0.0, down[:8]), down[8:]], axis=0)
-        up = jnp.concatenate([up[:-8], jnp.where(row == 7, 0.0, up[-8:])], axis=0)
-        totals.append(middle[here] + down + up)
+                shifted = []
+                for dy in range(3):
+                    b = 2 * dy + q
+                    pieces = [
+                        products[0][64 * b + 48 : 64 * b + 56, wide],
+                        products[0][64 * b : 64 * b + 48, wide],
+                        products[1][48 * b : 48 * b + 48, wide],
+                        products[2][32 * b : 32 * b + 16, wide],
+                        products[2][32 * b + 24 : 32 * b + 32, wide],
+                    ]
+                    shifted.append(jnp.concatenate(pieces, axis=0))
+                before = jnp.where(lane == 0, 0.0, pltpu.roll(shifted[0], 1, axis=1))
+                after = jnp.where(lane == NY - 1, 0.0, pltpu.roll(shifted[2], NY - 1, axis=1))
+                pair.append(shifted[1] + before + after)
+            totals.append(jnp.concatenate(pair, axis=1))
     return totals
 
 
@@ -674,30 +720,22 @@
     return run
 
 
-def stencil_kernel(adjoint, start, taps, before, field, after, *rest):
+def smooth_kernel(start, taps, before, field, after, *rest):
     out, even, odd = rest[-3:]
     planes = field.shape[1]
     totals = []
 
     def visit(c, band):
         sheets = [before[c, 0]] + [field[c, z] for z in range(planes)] + [after[c, 0]]
-        pairs = apply_band([sheets[z : z + 4] for z in range(0, planes, 2)], band)
-        if adjoint:
-            for p, total in enumerate(pairs):
-                total = total.astype(jnp.bfloat16)
-                out[c, 2 * p] = total[:, :NY]
-                out[c, 2 * p + 1] = total[:, NY:]
-        else:
-            totals.append(pairs)
-
-    banded(adjoint, taps, start, even, odd, 2)(visit)
-    if not adjoint:
-        for p in range(planes // 2):
-            both = [totals[c][p].reshape(NX // 8, 8, 2 * NY) for c in range(2)]
-            out[p] = jnp.concatenate(both, axis=1).astype(jnp.bfloat16)
-
-
-def stencil_planes(field, rims, taps, adjoint, done=None):
+        totals.append(apply_band(sheets, band))
+
+    banded(False, taps, start, even, odd, 2)(visit)
+    for p in range(planes // 2):
+        both = [totals[c][p].reshape(NX // 8, 8, 2 * NY) for c in range(2)]
+        out[p] = jnp.concatenate(both, axis=1).astype(jnp.bfloat16)
+
+
+def smooth_planes(field, rims, taps, done=None):
     channels, planes = field.shape[:2]
     pairs = planes // 2
     start = 0 if done is None else channels // 2
@@ -709,30 +747,24 @@
     if done is not None:
         in_specs.append(pl.BlockSpec(memory_space=pl.ANY))
         operands.append(done)
-    if adjoint:
-        out_spec, shape = sheets, field.shape
-    else:
-        out_spec = pl.BlockSpec((pairs, NX // 8, 16, 2 * NY), lambda c: (0, 0, c + skip, 0))
-        shape = (pairs, NX // 8, 8 * channels, 2 * NY)
-    name = "near" if adjoint else "smooth"
     return pl.pallas_call(
-        functools.partial(stencil_kernel, adjoint, start),
+        functools.partial(smooth_kernel, start),
         grid=(channels // 4,),
         in_specs=in_specs,
-        out_specs=out_spec,
-        out_shape=jax.ShapeDtypeStruct(shape, jnp.bfloat16),
+        out_specs=pl.BlockSpec((pairs, NX // 8, 16, 2 * NY), lambda c: (0, 0, c + skip, 0)),
+        out_shape=jax.ShapeDtypeStruct((pairs, NX // 8, 8 * channels, 2 * NY), jnp.bfloat16),
         input_output_aliases={} if done is None else {4: 0},
-        scratch_shapes=[pltpu.VMEM((4 * NY, 6 * NY), jnp.bfloat16) for _ in range(2)],
+        scratch_shapes=[pltpu.VMEM((6 * 64, 4 * 64), jnp.bfloat16) for _ in range(2)],
         compiler_params=params(),
         cost_estimate=LIGHT,
-        name=name + ("_low" if done is None else "_high"),
+        name="smooth_low" if done is None else "smooth_high",
     )(*operands)
 
 
-def finish_kernel(planar, near, ix_table, iy_table, out, waves):
+def finish_kernel(taps, before, field, after, planar, ix_table, iy_table, out, waves, even, odd):
     step = pl.program_id(0)
     slabs, lines = planar.shape[:2]
-    planes = near.shape[1]
+    planes = field.shape[1]
     span = planes * NY
 
     @pl.when(step == 0)
@@ -747,32 +779,50 @@
     here = pl.ds(pl.multiple_of(rows * step, rows), rows)
     right = [waves[s, t, here, :] for s in range(slabs) for t in range(2)]
     right = jnp.concatenate(right, axis=0)
-    for p in range(planes // 2):
-        spectral = dot(ix_table[...], right[:, 2 * p * NY : 2 * (p + 1) * NY])
-        for c in range(4):
-            for q in range(2):
-                far = spectral[c * NX : (c + 1) * NX, q * NY : (q + 1) * NY]
-                total = far + near[c, 2 * p + q].astype(jnp.float32)
-                out[c, 2 * p + q] = total.astype(jnp.bfloat16)
-
-
-def finish(planar, near):
+    far = [
+        dot(ix_table[...], right[:, 2 * p * NY : 2 * (p + 1) * NY]) for p in range(planes // 2)
+    ]
+
+    def visit(c, band):
+        sheets = [before[c, 0]] + [field[c, z] for z in range(planes)] + [after[c, 0]]
+        for p, near in enumerate(apply_band(sheets, band)):
+            total = (near + far[p][c * NX : (c + 1) * NX]).astype(jnp.bfloat16)
+            out[c, 2 * p] = total[:, :NY]
+            out[c, 2 * p + 1] = total[:, NY:]
+
+    banded(True, taps, 0, even, odd, 4)(visit)
+
+
+def finish(planar, spread, rims, taps):
     slabs, lines, width = planar.shape
-    channels, planes = near.shape[:2]
+    channels, planes = spread.shape[:2]
     ix_table = constant(inverse_x_table(slabs, 4))
     iy_table = constant(inverse_y_table(planes, planes))
+    rim = pl.BlockSpec((4, 1, NX, NY), lambda c: (c, 0, 0, 0))
     sheets = pl.BlockSpec((4, planes, NX, NY), lambda c: (c, 0, 0, 0))
     return pl.pallas_call(
         finish_kernel,
         grid=(channels // 4,),
-        in_specs=[whole(planar.shape), sheets, whole(ix_table.shape), whole(iy_table.shape)],
+        in_specs=[
+            pl.BlockSpec(memory_space=pltpu.SMEM),
+            rim,
+            sheets,
+            rim,
+            whole(planar.shape),
+            whole(ix_table.shape),
+            whole(iy_table.shape),
+        ],
         out_specs=sheets,
-        out_shape=jax.ShapeDtypeStruct(near.shape, jnp.bfloat16),
-        scratch_shapes=[pltpu.VMEM((slabs, 2, lines, planes * NY), jnp.bfloat16)],
+        out_shape=jax.ShapeDtypeStruct(spread.shape, jnp.bfloat16),
+        scratch_shapes=[
+            pltpu.VMEM((slabs, 2, lines, planes * NY), jnp.bfloat16),
+            pltpu.VMEM((6 * 64, 4 * 64), jnp.bfloat16),
+            pltpu.VMEM((6 * 64, 4 * 64), jnp.bfloat16),
+        ],
         compiler_params=params(),
         cost_estimate=HEAVY,
         name="finish",
-    )(planar, near, ix_table, iy_table)
+    )(taps, rims[0], spread, rims[1], planar, ix_table, iy_table)
 
 
 def gradient_kernel(depth, where, gathered, first, second, out):
@@ -853,30 +903,24 @@
     weight = spec_weight.reshape(mode_rows * KZ, 2 * channels * channels)
     width = weight.shape[1] // copies
 
-    planar, first, first_high, last, last_high = forward_modes(field, slabs)
-    planar, first, last = barrier((swap(planar), first, last))
+    first, first_high, last, last_high = cut_rims(field)
     rims = exchange(first, last)
+    planar = swap(forward_modes(field, slabs))
+    rims, first, last = barrier((rims, first_high, last_high))
+    rims_high = exchange(first, last)
+    planar, smooth = barrier((planar, smooth_planes(field, rims, taps)))
     spectrum, planar = mix(planar, weight, cell_scale, 0.5 * mode_scale)
+    smooth, spectrum = barrier((smooth, spectrum))
     planar = swap(planar)
-    rims, first, last, spectrum = barrier((rims, first_high, last_high, spectrum))
-    rims_high = exchange(first, last)
-    smooth = stencil_planes(field, rims, taps, False)
-    smooth = stencil_planes(field, rims_high, taps, False, smooth)
-    spread, planar, first, first_high, last, last_high = layer(
-        planar, smooth, cotangent[0], grains[0], bias, point_weight
-    )
+    smooth = smooth_planes(field, rims_high, taps, smooth)
+    spread, planar, first, last = layer(planar, smooth, cotangent[0], grains[0], bias, point_weight)
     rims = exchange(first, last)
-    planar, send = mix(swap(planar), weight, 0.5 * mode_scale, cell_scale, spectrum, copies)
+    planar, send = mix(swap(planar), weight, 0.5 * mode_scale, cell_scale, spectrum)
     planar = swap(planar)
-    rims, first, last, send = barrier((rims, first_high, last_high, send))
-    rims_high = exchange(first, last)
-    near, send = barrier((stencil_planes(spread, rims, taps, True), send))
-    near = stencil_planes(spread, rims_high, taps, True, near)
-    gathered = lax.all_to_all(send, "dp", split_axis=0, concat_axis=0)
-    grad_feats = finish(planar, near)
-    grad_feats, gathered = barrier((grad_feats, gathered))
-    grad_feats = grad_feats[None]
+    gathered = lax.all_gather(send, "dp")
     grad_spec = weight_gradient(gathered, KX // slabs, width, lax.axis_index("dp"))
+    planar, grad_spec = barrier((planar, grad_spec))
+    grad_feats = finish(planar, spread, rims, taps)[None]
     return (grad_feats, grad_spec.reshape(mode_rows, KZ, width))
 
 

time: 181 us -> 236 us (1.30)
  Pallas kernels: 108 us -> 156 us
  between operations: 0.81 us -> 14.2 us
  starting transfers between devices: 36.4 us -> 31.7 us
  waiting for transfers between devices: 11.8 us -> 16 us
  blocking collectives: 15.3 us -> 12.3 us
    pallas_call x5 -> x4, Pallas kernels: 55.9 us -> 104 us  [the longest x1 64.7 us: cut_rims(): pl.pallas_call(rims_kernel, in_specs=[pl.BlockSpec(memory_space=pl.ANY)],...]
    all_to_all x3, waiting for transfers between devices: 1.84 us -> 8.78 us  [swap(): return lax.all_to_all(planar, 'slab', split_axis=0, concat_axis=0)]
    all_gather x0 -> x1, waiting for transfers between devices: none -> 5.69 us  [local_fast(): gathered = lax.all_gather(send, 'dp')]
    ppermute x8 -> x6, waiting for transfers between devices: 7 us -> 1.55 us  [exchange(): return (lax.ppermute(last, 'slab', up), lax.ppermute(first, 'slab', down))]
    all_to_all x1 -> x0, starting transfers between devices: 3.53 us -> none  [local_fast(): gathered = lax.all_to_all(send, 'dp', split_axis=0, concat_axis=0)]
    ppermute x8 -> x6, starting transfers between devices: 18.7 us -> 15.5 us  [exchange(): return (lax.ppermute(last, 'slab', up), lax.ppermute(first, 'slab', down))]
    all_to_all x1, blocking collectives: 15.3 us -> 12.3 us  [swap(): return lax.all_to_all(planar, 'slab', split_axis=0, concat_axis=0)]
    all_to_all x1 -> x0, waiting for transfers between devices: 2.93 us -> none  [local_fast(): gathered = lax.all_to_all(send, 'dp', split_axis=0, concat_axis=0)]
  transfers between devices with their start and end apart: 12 -> 10, of which waited for: 5 -> 3; matrix products, arithmetic and copies ran while one was open for 0% -> 0% of each run, Pallas kernels for 40% -> 17%
where the time goes in v7:
time: 236 us; the launch traced here: 235 us
  Pallas kernels  156 us (66%)
  starting transfers between devices  31.7 us (13%)
  waiting for transfers between devices  16 us (7%)
  between operations  14.2 us (6%)
  blocking collectives  12.3 us (5%)
  local copies, waits for them, and re-layouts  4.11 us (2%)
    pallas_call x1, Pallas kernels, cut_rims(): pl.pallas_call(rims_kernel, in_specs=[pl.BlockSpec(memory_space=pl.ANY)],...  64.7 us
    pallas_call x1, Pallas kernels, layer(): pl.pallas_call(layer_kernel, grid=(pairs,), in_specs=[pl.BlockSpec(memory...  23.3 us
    pallas_call x2, Pallas kernels, smooth_planes(): pl.pallas_call(functools.partial(smooth_kernel, start), grid=(channels //...  20 us
    pallas_call x1, Pallas kernels, finish(): pl.pallas_call(finish_kernel, grid=(channels // 4,), in_specs=[pl.BlockSp...  19.6 us
    all_to_all x3, starting transfers between devices, swap(): return lax.all_to_all(planar, 'slab', split_axis=0, concat_axis=0)  16.2 us
    ppermute x6, starting transfers between devices, exchange(): return (lax.ppermute(last, 'slab', up), lax.ppermute(first, 'slab', down))  15.5 us
    pallas_call x2, Pallas kernels, mix(): pl.pallas_call(functools.partial(mixing_kernel, scale_in, scale_out, adjo...  15 us
    all_to_all x1, blocking collectives, swap(): return lax.all_to_all(planar, 'slab', split_axis=0, concat_axis=0)  12.3 us
  transfers between devices with their start and end apart: 10, of which 3 were waited for; matrix products, arithmetic and copies ran while one was open for 0% of the time, Pallas kernels for 17%

profile of v7, /device:TPU:0, one launch (start us, length us, event | category | flops | bytes accessed | tf_op | source)
XLA Modules:
  0.0 234.6 jit_solution(5950469112328107458)
XLA Ops:
  7.2 64.7 %rims.1 = (bf16[16,1,128,128]{3,2,1,0:T(8,128)(2,1)}, bf16[16,1,128,128]{3,2,1,0:T(8,128)(2,1)}, bf16[16,1,128,128]{3,2,1,0:T(8,128)(2,1)}, bf16[16,1,128,128]{3,2,1,0:T(8,128)(2,1)}) custom-call(bf16[32,8,128,128]{3,2,1,0:T(8,128)(2,1)} %bitcast.9), custom_call_target="tpu_custom_call" | custom-call | flops 10000000 | bytes 100000 | tf_op jit(solution)/shard_map/rims/pallas_call | solution.py:342
  71.8 0.0 copy-start.11
  71.8 0.0 copy-start.10
  71.9 5.1 %collective-permute-start = (bf16[16,1,128,128]{3,2,1,0:T(8,128)(2,1)}, bf16[16,1,128,128]{3,2,1,0:T(8,128)(2,1)S(1)}, u32[]{:S(2)}, u32[]{:S(2)}) collective-permute-start(bf16[16,1,128,128]{3,2,1,0:T(8,128)(2,1)} %get-tuple-element.24), channel_id=1, source_target_pairs={{0,1},{1,2},{2,3},{4,5},{5,6},{6,7},{8,9},{9,10},{10,11},{12,13},{... | collective-permute-start | bytes 1572872 | tf_op jit(solution)/shard_map/ppermute | solution.py:887
  77.0 1.3 collective-permute-start.1
  78.3 6.7 %forward_modes.1 = bf16[4,128,256]{2,1,0:T(8,128)(2,1)} custom-call(bf16[32,8,128,128]{3,2,1,0:T(8,128)(2,1)} %bitcast.10, bf16[64,256]{1,0:T(8,128)(2,1)} %constant.59.clone.x_table, bf16[2048,256]{1,0:T(8,128)(2,1)} %constant.60.clone.y_table), custom_call_target="tpu_custom_call" | custom-call | flops 10000000 | bytes 100000 | tf_op jit(solution)/shard_map/forward_modes/pallas_call | solution.py:375
  85.0 5.9 %all-to-all-start = ((bf16[4,128,256]{2,1,0:T(8,128)(2,1)}), bf16[4,128,256]{2,1,0:T(8,128)(2,1)S(1)}, u32[]{:S(2)}, u32[]{:S(2)}) async-start(bf16[4,128,256]{2,1,0:T(8,128)(2,1)} %forward_modes.1), calls=%async_computation | async-start | bytes 524288 | tf_op jit(solution)/shard_map/all_to_all | solution.py:891
  90.9 0.0 collective-permute-done.before
  90.9 0.0 copy-start.3
  90.9 1.5 collective-permute-done.1.after
  92.5 0.0 copy-done.11
  92.5 3.5 %collective-permute-start.2 = (bf16[16,1,128,128]{3,2,1,0:T(8,128)(2,1)S(1)}, bf16[16,1,128,128]{3,2,1,0:T(8,128)(2,1)S(1)}, u32[]{:S(2)}, u32[]{:S(2)}) collective-permute-start(bf16[16,1,128,128]{3,2,1,0:T(8,128)(2,1)S(1)} %copy-done.11), channel_id=1, source_target_pairs={{0,1},{1,2},{2,3},{4,5},{5,6},{6,7},{8,9},{9,10},{10,11},{12,13},{... | collective-permute-start | bytes 1572872 | tf_op jit(solution)/shard_map/ppermute | solution.py:887
  95.9 0.0 copy-done.10
  95.9 1.3 collective-permute-start.3
  97.2 0.0 copy-done.3
  97.3 0.0 copy-done.4
  97.3 10.0 %smooth_low.1.rest_0_ = bf16[4,16,256,256]{3,2,1,0:T(8,128)(2,1)} custom-call(f32[27,32]{1,0:T(8,128)} %taps.5, bf16[16,1,128,128]{3,2,1,0:T(8,128)(2,1)} %copy-done.3, bf16[32,8,128,128]{3,2,1,0:T(8,128)(2,1)} %bitcast.11, bf16[16,1,128,128]{3,2,1,0:T(8,128)(2,1)} %copy-done.4), custom_call_target="tpu_custom_call" | custom-call | flops 10000000 | bytes 100000 | tf_op jit(solution)/shard_map/smooth_low/pallas_call | solution.py:750
  107.3 0.0 all-to-all-done.planar
  107.3 0.7 copy-done.6
  108.0 7.3 %mix.1 = (bf16[512,128]{1,0:T(8,128)(2,1)}, bf16[4,128,256]{2,1,0:T(8,128)(2,1)}) custom-call(bf16[4,128,256]{2,1,0:T(8,128)(2,1)} %copy-done.6, bf16[1024,2048]{1,0:T(8,128)(2,1)} %bitcast.17, bf16[1024,512]{1,0:T(8,128)(2,1)} %constant.61.clone.z_in, bf16[512,1024]{1,0:T(8,128)(2,1)} %constant.62.clone.z_out, ...), custom_call_target="tpu_custom_call" | custom-call | flops 99999997952 | bytes 100000000 | tf_op jit(solution)/shard_map/mix/pallas_call | solution.py:485
  115.2 4.9 %all-to-all-start.1 = ((bf16[4,128,256]{2,1,0:T(8,128)(2,1)}), bf16[4,128,256]{2,1,0:T(8,128)(2,1)S(1)}, u32[]{:S(2)}, u32[]{:S(2)}) async-start(bf16[4,128,256]{2,1,0:T(8,128)(2,1)} %get-tuple-element.31), calls=%async_computation.1 | async-start | bytes 524288 | tf_op jit(solution)/shard_map/all_to_all | solution.py:891
  120.1 0.0 all-gather.3.cloned.1.call-start
  120.1 0.0 collective-permute-done.2.before
  120.1 0.0 copy-start.1
  120.2 0.0 collective-permute-done.3.after
  120.2 0.8 copy-done.1
  120.9 0.8 copy-done.2
  121.8 10.0 %smooth_high.1.smooth = bf16[4,16,256,256]{3,2,1,0:T(8,128)(2,1)} custom-call(f32[27,32]{1,0:T(8,128)} %taps.5, bf16[16,1,128,128]{3,2,1,0:T(8,128)(2,1)} %copy-done.1, bf16[32,8,128,128]{3,2,1,0:T(8,128)(2,1)} %bitcast.12, bf16[16,1,128,128]{3,2,1,0:T(8,128)(2,1)} %copy-done.2, ...), custom_call_target="tpu_custom_call", output_to_operand_aliasing={{}: (4, {})} | custom-call | flops 10000000 | bytes 100000 | tf_op jit(solution)/shard_map/smooth_high/pallas_call | solution.py:750
  131.8 0.0 all-to-all-done.1.planar
  131.8 0.7 copy-done
  132.5 23.3 %layer.1 = (bf16[32,8,128,128]{3,2,1,0:T(8,128)(2,1)}, bf16[4,128,256]{2,1,0:T(8,128)(2,1)}, bf16[32,1,128,128]{3,2,1,0:T(8,128)(2,1)}, bf16[32,1,128,128]{3,2,1,0:T(8,128)(2,1)}) custom-call(f32[32]{0:T(128)} %bias.1, bf16[4,128,256]{2,1,0:T(8,128)(2,1)} %copy-done, bf16[4,16,256,256]{3,2,1,0:T(8,128)(2,1)} %smooth_high.1.smooth, ...), custom_call_target="tpu_custom_call" | custom-call | flops 10000000 | bytes 100000 | tf_op jit(solution)/shard_map/layer/pallas_call | solution.py:602
  155.8 12.3 %all_to_all.20.planar = bf16[4,128,256]{2,1,0:T(8,128)(2,1)} all-to-all(bf16[4,128,256]{2,1,0:T(8,128)(2,1)} %get-tuple-element.40), channel_id=1, replica_groups=mesh['grp'=2,'dp'=4,'slab'=4] {'slab'}, dimensions={0} | all-to-all | bytes 524288 | tf_op jit(solution)/shard_map/all_to_all | solution.py:891
  168.1 7.8 %mix_back.1 = (bf16[4,128,256]{2,1,0:T(8,128)(2,1)}, bf16[1024,128]{1,0:T(8,128)(2,1)}) custom-call(bf16[4,128,256]{2,1,0:T(8,128)(2,1)} %all_to_all.20.planar, bf16[1024,2048]{1,0:T(8,128)(2,1)} %bitcast.18, bf16[1024,512]{1,0:T(8,128)(2,1)} %constant.61.clone.z_in, bf16[512,1024]{1,0:T(8,128)(2,1)} %constant.62.clone.z_out, ...), custom_call_target="tpu_custom_call" | custom-call | flops 99999997952 | bytes 100000000 | tf_op jit(solution)/shard_map/mix_back/pallas_call | solution.py:485
  175.9 0.0 all-gather.3.cloned.1.call-update
  175.9 0.0 copy-done.8
  175.9 3.1 %collective-permute-start.4 = (bf16[32,1,128,128]{3,2,1,0:T(8,128)(2,1)S(1)}, bf16[32,1,128,128]{3,2,1,0:T(8,128)(2,1)S(1)}, u32[]{:S(2)}, u32[]{:S(2)}) collective-permute-start(bf16[32,1,128,128]{3,2,1,0:T(8,128)(2,1)S(1)} %copy-done.8), channel_id=1, source_target_pairs={{0,1},{1,2},{2,3},{4,5},{5,6},{6,7},{8,9},{9,10},{10,11},{12,13},{... | collective-permute-start | bytes 3145736 | tf_op jit(solution)/shard_map/ppermute | solution.py:887
  179.0 0.0 copy-done.7
  179.0 1.3 collective-permute-start.5
  180.3 5.4 %all-to-all-start.3 = ((bf16[4,128,256]{2,1,0:T(8,128)(2,1)}), bf16[4,128,256]{2,1,0:T(8,128)(2,1)S(1)}, u32[]{:S(2)}, u32[]{:S(2)}) async-start(bf16[4,128,256]{2,1,0:T(8,128)(2,1)} %get-tuple-element.42), calls=%async_computation.3 | async-start | bytes 524288 | tf_op jit(solution)/shard_map/all_to_all | solution.py:891
  185.7 0.7 pad_add_fusion.where
  186.4 5.7 %all-gather.3.cloned.1.call-done = bf16[4096,128]{1,0:T(8,128)(2,1)} async-done(((bf16[1024,128]{1,0:T(8,128)(2,1)}), bf16[4096,128]{1,0:T(8,128)(2,1)}) %all-gather.3.cloned.1.call-update) | async-done | bytes 1048592 | tf_op jit(solution)/shard_map/all_gather | solution.py:920
  192.1 6.2 %weight_gradient.1 = f32[1024,512]{1,0:T(8,128)} custom-call(s32[2]{0:T(128)} %pad_add_fusion.where, bf16[4,1024,128]{2,1,0:T(8,128)(2,1)} %bitcast.15, bf16[2,128,512]{2,1,0:T(8,128)(2,1)} %constant.71.clone.first, bf16[128,128]{1,0:T(8,128)(2,1)} %constant.69.clone.spread_table.second), custom_call_target="tpu_custom_call" | custom-call | flops 10000000 | bytes 100000 | tf_op jit(solution)/shard_map/weight_gradient/pallas_call | solution.py:864
  198.3 8.8 %all-to-all-done.3.planar = bf16[4,128,256]{2,1,0:T(8,128)(2,1)S(1)} async-done(((bf16[4,128,256]{2,1,0:T(8,128)(2,1)}), bf16[4,128,256]{2,1,0:T(8,128)(2,1)S(1)}, u32[]{:S(2)}, u32[]{:S(2)}) %all-to-all-start.3) | async-done | bytes 262176 | tf_op jit(solution)/shard_map/all_to_all | solution.py:891
  207.1 0.0 collective-permute-done.4.before
  207.1 0.0 collective-permute-done.5.after
  207.1 0.7 copy-done.5
  207.8 0.4 copy-done.9
  208.2 19.6 %finish.1 = bf16[32,8,128,128]{3,2,1,0:T(8,128)(2,1)} custom-call(f32[27,32]{1,0:T(8,128)} %taps.5, bf16[32,1,128,128]{3,2,1,0:T(8,128)(2,1)} %copy-done.9, bf16[32,8,128,128]{3,2,1,0:T(8,128)(2,1)} %get-tuple-element.38.field, bf16[32,1,128,128]{3,2,1,0:T(8,128)(2,1)} %collective-permute-done.5.after, bf16[4,128,256]{2,1,0:T(8,128)(2,1)} %copy-done.5, ...), custom_call_target="tpu_custom_call" | custom-call | flops 99999997952 | bytes 100000000 | tf_op jit(solution)/shard_map/finish/pallas_call | solution.py:803
  (8 shorter events, 0.0 us)
Async XLA Ops:
  71.8 20.6 %copy-start.11 = (bf16[16,1,128,128]{3,2,1,0:T(8,128)(2,1)S(1)}, bf16[16,1,128,128]{3,2,1,0:T(8,128)(2,1)}, u32[]{:S(2)}) copy-start(bf16[16,1,128,128]{3,2,1,0:T(8,128)(2,1)} %get-tuple-element.32) | copy-start | bytes 1572868
  71.8 24.1 %copy-start.10 = (bf16[16,1,128,128]{3,2,1,0:T(8,128)(2,1)S(1)}, bf16[16,1,128,128]{3,2,1,0:T(8,128)(2,1)}, u32[]{:S(2)}) copy-start(bf16[16,1,128,128]{3,2,1,0:T(8,128)(2,1)} %get-tuple-element.33) | copy-start | bytes 1572868
  71.9 19.1 %collective-permute-start = (bf16[16,1,128,128]{3,2,1,0:T(8,128)(2,1)}, bf16[16,1,128,128]{3,2,1,0:T(8,128)(2,1)S(1)}, u32[]{:S(2)}, u32[]{:S(2)}) collective-permute-start(bf16[16,1,128,128]{3,2,1,0:T(8,128)(2,1)} %get-tuple-element.24), channel_id=1, source_target_pairs={{0,1},{1,2},{2,3},{4,5},{5,6},{6,7},{8,9},{9,10},{10,11},{12,13},{... | collective-permute-start | bytes 1572872 | tf_op jit(solution)/shard_map/ppermute | solution.py:887
  77.0 15.5 %collective-permute-start.1 = (bf16[16,1,128,128]{3,2,1,0:T(8,128)(2,1)}, bf16[16,1,128,128]{3,2,1,0:T(8,128)(2,1)S(1)}, u32[]{:S(2)}, u32[]{:S(2)}) collective-permute-start(bf16[16,1,128,128]{3,2,1,0:T(8,128)(2,1)} %get-tuple-element.25), channel_id=1, source_target_pairs={{1,0},{2,1},{3,2},{5,4},{6,5},{7,6},{9,8},{10,9},{11,10},{13,12},{... | collective-permute-start | bytes 1572872 | tf_op jit(solution)/shard_map/ppermute | solution.py:887
  85.0 22.3 %all-to-all-start = ((bf16[4,128,256]{2,1,0:T(8,128)(2,1)}), bf16[4,128,256]{2,1,0:T(8,128)(2,1)S(1)}, u32[]{:S(2)}, u32[]{:S(2)}) async-start(bf16[4,128,256]{2,1,0:T(8,128)(2,1)} %forward_modes.1), calls=%async_computation | async-start | bytes 524288 | tf_op jit(solution)/shard_map/all_to_all | solution.py:891
  90.9 6.3 %copy-start.3 = (bf16[16,1,128,128]{3,2,1,0:T(8,128)(2,1)}, bf16[16,1,128,128]{3,2,1,0:T(8,128)(2,1)S(1)}, u32[]{:S(2)}) copy-start(bf16[16,1,128,128]{3,2,1,0:T(8,128)(2,1)S(1)} %collective-permute-done.before) | copy-start | bytes 1572868
  92.4 4.8 %copy-start.4 = (bf16[16,1,128,128]{3,2,1,0:T(8,128)(2,1)}, bf16[16,1,128,128]{3,2,1,0:T(8,128)(2,1)S(1)}, u32[]{:S(2)}) copy-start(bf16[16,1,128,128]{3,2,1,0:T(8,128)(2,1)S(1)} %collective-permute-done.1.after) | copy-start | bytes 1572868
  92.5 27.7 %collective-permute-start.2 = (bf16[16,1,128,128]{3,2,1,0:T(8,128)(2,1)S(1)}, bf16[16,1,128,128]{3,2,1,0:T(8,128)(2,1)S(1)}, u32[]{:S(2)}, u32[]{:S(2)}) collective-permute-start(bf16[16,1,128,128]{3,2,1,0:T(8,128)(2,1)S(1)} %copy-done.11), channel_id=1, source_target_pairs={{0,1},{1,2},{2,3},{4,5},{5,6},{6,7},{8,9},{9,10},{10,11},{12,13},{... | collective-permute-start | bytes 1572872 | tf_op jit(solution)/shard_map/ppermute | solution.py:887
  95.9 24.2 %collective-permute-start.3 = (bf16[16,1,128,128]{3,2,1,0:T(8,128)(2,1)S(1)}, bf16[16,1,128,128]{3,2,1,0:T(8,128)(2,1)S(1)}, u32[]{:S(2)}, u32[]{:S(2)}) collective-permute-start(bf16[16,1,128,128]{3,2,1,0:T(8,128)(2,1)S(1)} %copy-done.10), channel_id=1, source_target_pairs={{1,0},{2,1},{3,2},{5,4},{6,5},{7,6},{9,8},{10,9},{11,10},{13,12},{... | collective-permute-start | bytes 1572872 | tf_op jit(solution)/shard_map/ppermute | solution.py:887
  107.3 0.7 copy-start.6
  115.2 16.5 %all-to-all-start.1 = ((bf16[4,128,256]{2,1,0:T(8,128)(2,1)}), bf16[4,128,256]{2,1,0:T(8,128)(2,1)S(1)}, u32[]{:S(2)}, u32[]{:S(2)}) async-start(bf16[4,128,256]{2,1,0:T(8,128)(2,1)} %get-tuple-element.31), calls=%async_computation.1 | async-start | bytes 524288 | tf_op jit(solution)/shard_map/all_to_all | solution.py:891
  120.1 71.9 %all-gather.3.cloned.1.call-start = ((), (), s32[]{:S(2)}) async-start(), calls=%async_computation.4 | async-start | bytes 1310720 | tf_op jit(solution)/shard_map/all_gather | solution.py:920
  120.1 0.8 copy-start.1
  120.9 0.8 copy-start.2
  131.8 0.7 copy-start
  168.1 7.8 %copy-start.8 = (bf16[32,1,128,128]{3,2,1,0:T(8,128)(2,1)S(1)}, bf16[32,1,128,128]{3,2,1,0:T(8,128)(2,1)}, u32[]{:S(2)}) copy-start(bf16[32,1,128,128]{3,2,1,0:T(8,128)(2,1)} %get-tuple-element.37) | copy-start | bytes 3145732
  168.1 10.9 %copy-start.7 = (bf16[32,1,128,128]{3,2,1,0:T(8,128)(2,1)S(1)}, bf16[32,1,128,128]{3,2,1,0:T(8,128)(2,1)}, u32[]{:S(2)}) copy-start(bf16[32,1,128,128]{3,2,1,0:T(8,128)(2,1)} %get-tuple-element.39) | copy-start | bytes 3145732
  175.9 31.2 %collective-permute-start.4 = (bf16[32,1,128,128]{3,2,1,0:T(8,128)(2,1)S(1)}, bf16[32,1,128,128]{3,2,1,0:T(8,128)(2,1)S(1)}, u32[]{:S(2)}, u32[]{:S(2)}) collective-permute-start(bf16[32,1,128,128]{3,2,1,0:T(8,128)(2,1)S(1)} %copy-done.8), channel_id=1, source_target_pairs={{0,1},{1,2},{2,3},{4,5},{5,6},{6,7},{8,9},{9,10},{10,11},{12,13},{... | collective-permute-start | bytes 3145736 | tf_op jit(solution)/shard_map/ppermute | solution.py:887
  179.0 28.1 %collective-permute-start.5 = (bf16[32,1,128,128]{3,2,1,0:T(8,128)(2,1)S(1)}, bf16[32,1,128,128]{3,2,1,0:T(8,128)(2,1)}, u32[]{:S(2)}, u32[]{:S(2)}) collective-permute-start(bf16[32,1,128,128]{3,2,1,0:T(8,128)(2,1)S(1)} %copy-done.7), channel_id=1, source_target_pairs={{1,0},{2,1},{3,2},{5,4},{6,5},{7,6},{9,8},{10,9},{11,10},{13,12},{... | collective-permute-start | bytes 3145736 | tf_op jit(solution)/shard_map/ppermute | solution.py:887
  180.3 26.7 %all-to-all-start.3 = ((bf16[4,128,256]{2,1,0:T(8,128)(2,1)}), bf16[4,128,256]{2,1,0:T(8,128)(2,1)S(1)}, u32[]{:S(2)}, u32[]{:S(2)}) async-start(bf16[4,128,256]{2,1,0:T(8,128)(2,1)} %get-tuple-element.42), calls=%async_computation.3 | async-start | bytes 524288 | tf_op jit(solution)/shard_map/all_to_all | solution.py:891
  207.1 0.7 copy-start.5
  207.1 1.1 copy-start.9
Sparse Core Ops, SparseCore 0:
  176.0 15.9 all-gather.2

commit v8 on v7

--- a/solution.py
+++ b/solution.py
@@ -322,33 +322,42 @@
         out[s] = modes[s * lines : (s + 1) * lines].astype(jnp.bfloat16)
 
 
-def rims_kernel(field, *refs):
-    rims, done = refs[:4], refs[4]
-    half = field.shape[0] // 2
-    last = field.shape[1] - 1
-    copies = []
-    for k in range(4):
-        source = field.at[pl.ds(half * (k % 2), half), pl.ds(last * (k // 2), 1)]
-        copies.append(pltpu.make_async_copy(source, rims[k], done.at[k]))
-    for copy in copies:
-        copy.start()
-    for copy in copies:
-        copy.wait()
+def rims_kernel(low, high, *rims):
+    step = pl.program_id(0)
+    half = pl.num_programs(0) // 2
+    for k, source in enumerate((low, high)):
+
+        @pl.when(step < half)
+        def _():
+            rims[2 * k][...] = source[...]
+
+        @pl.when(step >= half)
+        def _():
+            rims[2 * k + 1][...] = source[...]
 
 
 def cut_rims(field):
-    channels = field.shape[0]
+    channels, planes = field.shape[:2]
+    steps = 4
     rim = jax.ShapeDtypeStruct((channels // 2, 1, NX, NY), jnp.bfloat16)
+    block = (channels // steps, 1, NX, NY)
+    outs = [
+        pl.BlockSpec(block, lambda c: (jnp.minimum(c, steps // 2 - 1), 0, 0, 0)),
+        pl.BlockSpec(block, lambda c: (jnp.maximum(c - steps // 2, 0), 0, 0, 0)),
+    ]
     return pl.pallas_call(
         rims_kernel,
-        in_specs=[pl.BlockSpec(memory_space=pl.ANY)],
-        out_specs=[pl.BlockSpec(memory_space=pl.ANY)] * 4,
+        grid=(steps,),
+        in_specs=[
+            pl.BlockSpec(block, lambda c: (c, 0, 0, 0)),
+            pl.BlockSpec(block, lambda c: (c, planes - 1, 0, 0)),
+        ],
+        out_specs=outs + outs,
         out_shape=[rim] * 4,
-        scratch_shapes=[pltpu.SemaphoreType.DMA((4,))],
         compiler_params=params(),
         cost_estimate=LIGHT,
         name="rims",
-    )(field)
+    )(field, field)
 
 
 def forward_kernel(field, x_table, y_table, out, rows):
@@ -661,7 +670,7 @@
             band[at : at + 64, :] = jnp.concatenate(halves, axis=1).astype(jnp.bfloat16)
 
 
-def apply_band(sheets, band):
+def apply_band(quads, band):
     blocks = range(6)
     lefts = [
         band[...],
@@ -670,11 +679,11 @@
     ]
     lane = lax.broadcasted_iota(jnp.int32, (NX, NY), 1)
     totals = []
-    for group in range(0, len(sheets) - 2, 4):
+    for group in range(0, len(quads), 2):
         products = []
         for left, x in zip(lefts, (0, 48, 64)):
             right = [
-                jnp.concatenate([sheets[group + 2 * p + k][x : x + 64] for k in range(4)], axis=0)
+                jnp.concatenate([sheet[x : x + 64] for sheet in quads[group + p]], axis=0)
                 for p in range(2)
             ]
             products.append(dot(left, jnp.concatenate(right, axis=1)))
@@ -727,7 +736,7 @@
 
     def visit(c, band):
         sheets = [before[c, 0]] + [field[c, z] for z in range(planes)] + [after[c, 0]]
-        totals.append(apply_band(sheets, band))
+        totals.append(apply_band([sheets[z : z + 4] for z in range(0, planes, 2)], band))
 
     banded(False, taps, start, even, odd, 2)(visit)
     for p in range(planes // 2):
@@ -761,7 +770,40 @@
     )(*operands)
 
 
-def finish_kernel(taps, before, field, after, planar, ix_table, iy_table, out, waves, even, odd):
+def inner_kernel(taps, field, out, even, odd):
+    planes = field.shape[1]
+
+    def visit(c, band):
+        quads = [[field[c, z + k] for k in range(4)] for z in range(1, planes - 3, 2)]
+        for p, near in enumerate(apply_band(quads, band)):
+            total = near.astype(jnp.bfloat16)
+            out[c, 2 * p] = total[:, :NY]
+            out[c, 2 * p + 1] = total[:, NY:]
+
+    banded(True, taps, 0, even, odd, 2)(visit)
+
+
+def near_inner(field, taps):
+    channels, planes = field.shape[:2]
+    shape = (channels, planes - 4, NX, NY)
+    return pl.pallas_call(
+        inner_kernel,
+        grid=(channels // 2,),
+        in_specs=[
+            pl.BlockSpec(memory_space=pltpu.SMEM),
+            pl.BlockSpec((2, planes, NX, NY), lambda c: (c, 0, 0, 0)),
+        ],
+        out_specs=pl.BlockSpec((2,) + shape[1:], lambda c: (c, 0, 0, 0)),
+        out_shape=jax.ShapeDtypeStruct(shape, jnp.bfloat16),
+        scratch_shapes=[pltpu.VMEM((6 * 64, 4 * 64), jnp.bfloat16) for _ in range(2)],
+        compiler_params=params(),
+        cost_estimate=LIGHT,
+        name="near_inner",
+    )(taps, field)
+
+
+def finish_kernel(taps, before, field, after, inner, planar, ix_table, iy_table, out, waves, even,
+                  odd):
     step = pl.program_id(0)
     slabs, lines = planar.shape[:2]
     planes = field.shape[1]
@@ -783,17 +825,23 @@
         dot(ix_table[...], right[:, 2 * p * NY : 2 * (p + 1) * NY]) for p in range(planes // 2)
     ]
 
+    def store(c, p, near):
+        for q in range(2):
+            total = near[q] + far[p][c * NX : (c + 1) * NX, q * NY : (q + 1) * NY]
+            out[c, 2 * p + q] = total.astype(jnp.bfloat16)
+
     def visit(c, band):
-        sheets = [before[c, 0]] + [field[c, z] for z in range(planes)] + [after[c, 0]]
-        for p, near in enumerate(apply_band(sheets, band)):
-            total = (near + far[p][c * NX : (c + 1) * NX]).astype(jnp.bfloat16)
-            out[c, 2 * p] = total[:, :NY]
-            out[c, 2 * p + 1] = total[:, NY:]
+        low = [before[c, 0]] + [field[c, z] for z in range(3)]
+        high = [field[c, z] for z in range(planes - 3, planes)] + [after[c, 0]]
+        for p, near in zip((0, planes // 2 - 1), apply_band([low, high], band)):
+            store(c, p, [near[:, :NY], near[:, NY:]])
+        for p in range(1, planes // 2 - 1):
+            store(c, p, [inner[c, 2 * p - 2 + q].astype(jnp.float32) for q in range(2)])
 
     banded(True, taps, 0, even, odd, 4)(visit)
 
 
-def finish(planar, spread, rims, taps):
+def finish(planar, spread, rims, inner, taps):
     slabs, lines, width = planar.shape
     channels, planes = spread.shape[:2]
     ix_table = constant(inverse_x_table(slabs, 4))
@@ -808,6 +856,7 @@
             rim,
             sheets,
             rim,
+            pl.BlockSpec((4,) + inner.shape[1:], lambda c: (c, 0, 0, 0)),
             whole(planar.shape),
             whole(ix_table.shape),
             whole(iy_table.shape),
@@ -822,7 +871,7 @@
         compiler_params=params(),
         cost_estimate=HEAVY,
         name="finish",
-    )(taps, rims[0], spread, rims[1], planar, ix_table, iy_table)
+    )(taps, rims[0], spread, rims[1], inner, planar, ix_table, iy_table)
 
 
 def gradient_kernel(depth, where, gathered, first, second, out):
@@ -917,10 +966,13 @@
     rims = exchange(first, last)
     planar, send = mix(swap(planar), weight, 0.5 * mode_scale, cell_scale, spectrum)
     planar = swap(planar)
+    send, spread = barrier((send, spread))
+    inner = near_inner(spread, taps)
+    grad_feats = finish(planar, spread, rims, inner, taps)
     gathered = lax.all_gather(send, "dp")
+    grad_feats, gathered = barrier((grad_feats, gathered))
+    grad_feats = grad_feats[None]
     grad_spec = weight_gradient(gathered, KX // slabs, width, lax.axis_index("dp"))
-    planar, grad_spec = barrier((planar, grad_spec))
-    grad_feats = finish(planar, spread, rims, taps)[None]
     return (grad_feats, grad_spec.reshape(mode_rows, KZ, width))
 
 

time: 236 us -> 170 us (0.72)
  Pallas kernels: 156 us -> 107 us
  blocking collectives: 12.3 us -> 0 us
  waiting for transfers between devices: 16 us -> 4.39 us
  starting transfers between devices: 31.7 us -> 36.3 us
    pallas_call x1 -> x2, Pallas kernels: 64.7 us -> 19.2 us  [the longest x1 15.2 us: near_inner(): pl.pallas_call(inner_kernel, grid=(channels // 2,), in_specs=[pl.BlockSpe...]
    all_to_all x1 -> x0, blocking collectives: 12.3 us -> none  [swap(): return lax.all_to_all(planar, 'slab', split_axis=0, concat_axis=0)]
    all_to_all x3 -> x4, waiting for transfers between devices: 8.78 us -> 2.2 us  [swap(): return lax.all_to_all(planar, 'slab', split_axis=0, concat_axis=0)]
    all_gather x1, waiting for transfers between devices: 5.69 us -> 0.01 us  [local_fast(): gathered = lax.all_gather(send, 'dp')]
    all_to_all x3 -> x4, starting transfers between devices: 16.2 us -> 20 us  [swap(): return lax.all_to_all(planar, 'slab', split_axis=0, concat_axis=0)]
    pallas_call x1, Pallas kernels: 19.6 us -> 17.1 us  [finish(): pl.pallas_call(finish_kernel, grid=(channels // 4,), in_specs=[pl.BlockSp...]
  transfers between devices with their start and end apart: 10 -> 11, of which waited for: 3 -> 3; matrix products, arithmetic and copies ran while one was open for 0% -> 0% of each run, Pallas kernels for 17% -> 44%
where the time goes in v8:
time: 170 us; the launch traced here: 168 us
  Pallas kernels  107 us (63%)
  starting transfers between devices  36.3 us (21%)
  between operations  14.1 us (8%)
  local copies, waits for them, and re-layouts  5.25 us (3%)
  waiting for transfers between devices  4.39 us (3%)
    pallas_call x1, Pallas kernels, layer(): pl.pallas_call(layer_kernel, grid=(pairs,), in_specs=[pl.BlockSpec(memory...  23.2 us
    pallas_call x2, Pallas kernels, smooth_planes(): pl.pallas_call(functools.partial(smooth_kernel, start), grid=(channels //...  20.1 us
    all_to_all x4, starting transfers between devices, swap(): return lax.all_to_all(planar, 'slab', split_axis=0, concat_axis=0)  20 us
    pallas_call x1, Pallas kernels, finish(): pl.pallas_call(finish_kernel, grid=(channels // 4,), in_specs=[pl.BlockSp...  17.1 us
    ppermute x6, starting transfers between devices, exchange(): return (lax.ppermute(last, 'slab', up), lax.ppermute(first, 'slab', down))  16.3 us
    pallas_call x1, Pallas kernels, near_inner(): pl.pallas_call(inner_kernel, grid=(channels // 2,), in_specs=[pl.BlockSpe...  15.2 us
    pallas_call x2, Pallas kernels, mix(): pl.pallas_call(functools.partial(mixing_kernel, scale_in, scale_out, adjo...  14.9 us
    pallas_call x1, Pallas kernels, forward_modes(): pl.pallas_call(forward_kernel, grid=(planes // 2,), in_specs=[pl.BlockSpe...  6.74 us
  transfers between devices with their start and end apart: 11, of which 3 were waited for; matrix products, arithmetic and copies ran while one was open for 0% of the time, Pallas kernels for 44%

profile of v8, /device:TPU:0, one launch (start us, length us, event | category | flops | bytes accessed | tf_op | source)
XLA Modules:
  0.0 168.2 jit_solution(500876875327496750)
XLA Ops:
  7.2 4.0 %rims.1 = (bf16[16,1,128,128]{3,2,1,0:T(8,128)(2,1)}, bf16[16,1,128,128]{3,2,1,0:T(8,128)(2,1)}, bf16[16,1,128,128]{3,2,1,0:T(8,128)(2,1)}, bf16[16,1,128,128]{3,2,1,0:T(8,128)(2,1)}) custom-call(bf16[32,8,128,128]{3,2,1,0:T(8,128)(2,1)} %bitcast.9, bf16[32,8,128,128]{3,2,1,0:T(8,128)(2,1)} %bitcast.10), custom_call_target="tpu_custom_call" | custom-call | flops 10000000 | bytes 100000 | tf_op jit(solution)/shard_map/rims/pallas_call | solution.py:348
  11.2 4.9 %collective-permute-start = (bf16[16,1,128,128]{3,2,1,0:T(8,128)(2,1)}, bf16[16,1,128,128]{3,2,1,0:T(8,128)(2,1)S(1)}, u32[]{:S(2)}, u32[]{:S(2)}) collective-permute-start(bf16[16,1,128,128]{3,2,1,0:T(8,128)(2,1)} %get-tuple-element.26), channel_id=1, source_target_pairs={{0,1},{1,2},{2,3},{4,5},{5,6},{6,7},{8,9},{9,10},{10,11},{12,13},{... | collective-permute-start | bytes 1572872 | tf_op jit(solution)/shard_map/ppermute | solution.py:936
  16.1 1.3 collective-permute-start.1
  17.4 6.7 %forward_modes.1 = bf16[4,128,256]{2,1,0:T(8,128)(2,1)} custom-call(bf16[32,8,128,128]{3,2,1,0:T(8,128)(2,1)} %bitcast.11, bf16[64,256]{1,0:T(8,128)(2,1)} %constant.59.clone.x_table, bf16[2048,256]{1,0:T(8,128)(2,1)} %constant.60.clone.y_table), custom_call_target="tpu_custom_call" | custom-call | flops 10000000 | bytes 100000 | tf_op jit(solution)/shard_map/forward_modes/pallas_call | solution.py:384
  24.1 5.9 %all-to-all-start = ((bf16[4,128,256]{2,1,0:T(8,128)(2,1)}), bf16[4,128,256]{2,1,0:T(8,128)(2,1)S(1)}, u32[]{:S(2)}, u32[]{:S(2)}) async-start(bf16[4,128,256]{2,1,0:T(8,128)(2,1)} %forward_modes.1), calls=%async_computation | async-start | bytes 524288 | tf_op jit(solution)/shard_map/all_to_all | solution.py:940
  30.1 0.0 collective-permute-done.before
  30.1 0.0 copy-start.3
  30.1 1.5 collective-permute-done.1.after
  31.6 0.0 copy-done.3
  31.6 0.8 copy-done.4
  32.4 10.1 %smooth_low.1.rest_0_ = bf16[4,16,256,256]{3,2,1,0:T(8,128)(2,1)} custom-call(f32[27,32]{1,0:T(8,128)} %taps.7, bf16[16,1,128,128]{3,2,1,0:T(8,128)(2,1)} %copy-done.3, bf16[32,8,128,128]{3,2,1,0:T(8,128)(2,1)} %bitcast.12, bf16[16,1,128,128]{3,2,1,0:T(8,128)(2,1)} %copy-done.4), custom_call_target="tpu_custom_call" | custom-call | flops 10000000 | bytes 100000 | tf_op jit(solution)/shard_map/smooth_low/pallas_call | solution.py:759
  42.5 0.0 all-to-all-done.planar
  42.5 0.0 copy-done.11
  42.5 0.0 copy-start.6
  42.5 3.5 %collective-permute-start.2 = (bf16[16,1,128,128]{3,2,1,0:T(8,128)(2,1)S(1)}, bf16[16,1,128,128]{3,2,1,0:T(8,128)(2,1)S(1)}, u32[]{:S(2)}, u32[]{:S(2)}) collective-permute-start(bf16[16,1,128,128]{3,2,1,0:T(8,128)(2,1)S(1)} %copy-done.11), channel_id=1, source_target_pairs={{0,1},{1,2},{2,3},{4,5},{5,6},{6,7},{8,9},{9,10},{10,11},{12,13},{... | collective-permute-start | bytes 1572872 | tf_op jit(solution)/shard_map/ppermute | solution.py:936
  46.0 0.0 copy-done.10
  46.0 1.3 collective-permute-start.3
  47.3 0.0 copy-done.6
  47.3 7.3 %mix.1 = (bf16[512,128]{1,0:T(8,128)(2,1)}, bf16[4,128,256]{2,1,0:T(8,128)(2,1)}) custom-call(bf16[4,128,256]{2,1,0:T(8,128)(2,1)} %copy-done.6, bf16[1024,2048]{1,0:T(8,128)(2,1)} %bitcast.18, bf16[1024,512]{1,0:T(8,128)(2,1)} %constant.61.clone.z_in, bf16[512,1024]{1,0:T(8,128)(2,1)} %constant.62.clone.z_out, ...), custom_call_target="tpu_custom_call" | custom-call | flops 99999997952 | bytes 100000000 | tf_op jit(solution)/shard_map/mix/pallas_call | solution.py:494
  54.5 4.9 %all-to-all-start.1 = ((bf16[4,128,256]{2,1,0:T(8,128)(2,1)}), bf16[4,128,256]{2,1,0:T(8,128)(2,1)S(1)}, u32[]{:S(2)}, u32[]{:S(2)}) async-start(bf16[4,128,256]{2,1,0:T(8,128)(2,1)} %get-tuple-element.33), calls=%async_computation.1 | async-start | bytes 524288 | tf_op jit(solution)/shard_map/all_to_all | solution.py:940
  59.4 0.0 collective-permute-done.2.before
  59.4 0.6 collective-permute-done.3.after
  60.1 0.2 copy-done.1
  60.2 0.8 copy-done.2
  61.0 10.0 %smooth_high.1.smooth = bf16[4,16,256,256]{3,2,1,0:T(8,128)(2,1)} custom-call(f32[27,32]{1,0:T(8,128)} %taps.7, bf16[16,1,128,128]{3,2,1,0:T(8,128)(2,1)} %copy-done.1, bf16[32,8,128,128]{3,2,1,0:T(8,128)(2,1)} %bitcast.13, bf16[16,1,128,128]{3,2,1,0:T(8,128)(2,1)} %copy-done.2, ...), custom_call_target="tpu_custom_call", output_to_operand_aliasing={{}: (4, {})} | custom-call | flops 10000000 | bytes 100000 | tf_op jit(solution)/shard_map/smooth_high/pallas_call | solution.py:759
  71.0 0.0 all-to-all-done.1.planar
  71.0 0.7 copy-done
  71.8 23.2 %layer.1 = (bf16[32,8,128,128]{3,2,1,0:T(8,128)(2,1)}, bf16[4,128,256]{2,1,0:T(8,128)(2,1)}, bf16[32,1,128,128]{3,2,1,0:T(8,128)(2,1)}, bf16[32,1,128,128]{3,2,1,0:T(8,128)(2,1)}) custom-call(f32[32]{0:T(128)} %bias.1, bf16[4,128,256]{2,1,0:T(8,128)(2,1)} %copy-done, bf16[4,16,256,256]{3,2,1,0:T(8,128)(2,1)} %smooth_high.1.smooth, ...), custom_call_target="tpu_custom_call" | custom-call | flops 10000000 | bytes 100000 | tf_op jit(solution)/shard_map/layer/pallas_call | solution.py:611
  95.0 5.1 %all-to-all-start.2 = ((bf16[4,128,256]{2,1,0:T(8,128)(2,1)}), bf16[4,128,256]{2,1,0:T(8,128)(2,1)S(1)}, u32[]{:S(2)}, u32[]{:S(2)}) async-start(bf16[4,128,256]{2,1,0:T(8,128)(2,1)} %get-tuple-element.40), calls=%async_computation.2 | async-start | bytes 524288 | tf_op jit(solution)/shard_map/all_to_all | solution.py:940
  100.1 4.0 %collective-permute-start.4 = (bf16[32,1,128,128]{3,2,1,0:T(8,128)(2,1)}, bf16[32,1,128,128]{3,2,1,0:T(8,128)(2,1)S(1)}, u32[]{:S(2)}, u32[]{:S(2)}) collective-permute-start(bf16[32,1,128,128]{3,2,1,0:T(8,128)(2,1)} %get-tuple-element.39), channel_id=1, source_target_pairs={{0,1},{1,2},{2,3},{4,5},{5,6},{6,7},{8,9},{9,10},{10,11},{12,13},{... | collective-permute-start | bytes 3145736 | tf_op jit(solution)/shard_map/ppermute | solution.py:936
  104.1 1.3 collective-permute-start.5
  105.4 2.2 %all-to-all-done.2.planar = bf16[4,128,256]{2,1,0:T(8,128)(2,1)S(1)} async-done(((bf16[4,128,256]{2,1,0:T(8,128)(2,1)}), bf16[4,128,256]{2,1,0:T(8,128)(2,1)S(1)}, u32[]{:S(2)}, u32[]{:S(2)}) %all-to-all-start.2) | async-done | bytes 262176 | tf_op jit(solution)/shard_map/all_to_all | solution.py:940
  107.6 0.7 copy-done.7
  108.3 7.7 %mix_back.1 = (bf16[4,128,256]{2,1,0:T(8,128)(2,1)}, bf16[1024,128]{1,0:T(8,128)(2,1)}) custom-call(bf16[4,128,256]{2,1,0:T(8,128)(2,1)} %copy-done.7, bf16[1024,2048]{1,0:T(8,128)(2,1)} %bitcast.19, bf16[1024,512]{1,0:T(8,128)(2,1)} %constant.61.clone.z_in, bf16[512,1024]{1,0:T(8,128)(2,1)} %constant.62.clone.z_out, ...), custom_call_target="tpu_custom_call" | custom-call | flops 99999997952 | bytes 100000000 | tf_op jit(solution)/shard_map/mix_back/pallas_call | solution.py:494
  116.0 4.1 %all-to-all-start.3 = ((bf16[4,128,256]{2,1,0:T(8,128)(2,1)}), bf16[4,128,256]{2,1,0:T(8,128)(2,1)S(1)}, u32[]{:S(2)}, u32[]{:S(2)}) async-start(bf16[4,128,256]{2,1,0:T(8,128)(2,1)} %get-tuple-element.46), calls=%async_computation.3 | async-start | bytes 524288 | tf_op jit(solution)/shard_map/all_to_all | solution.py:940
  120.0 0.0 all-gather.3.cloned.1.call-start
  120.0 0.7 pad_add_fusion.where
  120.7 0.1 all-gather.3.cloned.1.call-update
  120.7 15.2 %near_inner.1.inner = bf16[32,4,128,128]{3,2,1,0:T(8,128)(2,1)} custom-call(f32[27,32]{1,0:T(8,128)} %taps.7, bf16[32,8,128,128]{3,2,1,0:T(8,128)(2,1)} %get-tuple-element.44.field), custom_call_target="tpu_custom_call" | custom-call | flops 10000000 | bytes 100000 | tf_op jit(solution)/shard_map/near_inner/pallas_call | solution.py:789
  136.0 0.0 all-to-all-done.3.planar
  136.0 0.0 collective-permute-done.4.before
  136.0 0.0 copy-start.8
  136.0 0.0 collective-permute-done.5.after
  136.0 0.7 copy-done.5
  136.7 0.4 copy-done.8
  137.1 1.0 copy-done.9
  138.0 17.1 %finish.1 = bf16[32,8,128,128]{3,2,1,0:T(8,128)(2,1)} custom-call(f32[27,32]{1,0:T(8,128)} %taps.7, bf16[32,1,128,128]{3,2,1,0:T(8,128)(2,1)} %copy-done.8, bf16[32,8,128,128]{3,2,1,0:T(8,128)(2,1)} %get-tuple-element.44.field, bf16[32,1,128,128]{3,2,1,0:T(8,128)(2,1)} %copy-done.9, bf16[32,4,128,128]{3,2,1,0:T(8,128)(2,1)} %near_inner.1.inner, ...), custom_call_target="tpu_custom_call" | custom-call | flops 99999997952 | bytes 100000000 | tf_op jit(solution)/shard_map/finish/pallas_call | solution.py:851
  155.1 6.2 %weight_gradient.1 = f32[1024,512]{1,0:T(8,128)} custom-call(s32[2]{0:T(128)} %pad_add_fusion.where, bf16[4,1024,128]{2,1,0:T(8,128)(2,1)} %bitcast.16, bf16[2,128,512]{2,1,0:T(8,128)(2,1)} %constant.73.clone.first, bf16[128,128]{1,0:T(8,128)(2,1)} %constant.69.clone.spread_table.second), custom_call_target="tpu_custom_call" | custom-call | flops 10000000 | bytes 100000 | tf_op jit(solution)/shard_map/weight_gradient/pallas_call | solution.py:913
  (10 shorter events, 0.0 us)
Async XLA Ops:
  11.2 18.9 %collective-permute-start = (bf16[16,1,128,128]{3,2,1,0:T(8,128)(2,1)}, bf16[16,1,128,128]{3,2,1,0:T(8,128)(2,1)S(1)}, u32[]{:S(2)}, u32[]{:S(2)}) collective-permute-start(bf16[16,1,128,128]{3,2,1,0:T(8,128)(2,1)} %get-tuple-element.26), channel_id=1, source_target_pairs={{0,1},{1,2},{2,3},{4,5},{5,6},{6,7},{8,9},{9,10},{10,11},{12,13},{... | collective-permute-start | bytes 1572872 | tf_op jit(solution)/shard_map/ppermute | solution.py:936
  16.1 15.5 %collective-permute-start.1 = (bf16[16,1,128,128]{3,2,1,0:T(8,128)(2,1)}, bf16[16,1,128,128]{3,2,1,0:T(8,128)(2,1)S(1)}, u32[]{:S(2)}, u32[]{:S(2)}) collective-permute-start(bf16[16,1,128,128]{3,2,1,0:T(8,128)(2,1)} %get-tuple-element.27), channel_id=1, source_target_pairs={{1,0},{2,1},{3,2},{5,4},{6,5},{7,6},{9,8},{10,9},{11,10},{13,12},{... | collective-permute-start | bytes 1572872 | tf_op jit(solution)/shard_map/ppermute | solution.py:936
  24.1 18.3 %all-to-all-start = ((bf16[4,128,256]{2,1,0:T(8,128)(2,1)}), bf16[4,128,256]{2,1,0:T(8,128)(2,1)S(1)}, u32[]{:S(2)}, u32[]{:S(2)}) async-start(bf16[4,128,256]{2,1,0:T(8,128)(2,1)} %forward_modes.1), calls=%async_computation | async-start | bytes 524288 | tf_op jit(solution)/shard_map/all_to_all | solution.py:940
  30.1 1.5 copy-start.3
  31.6 0.8 copy-start.4
  32.4 10.1 %copy-start.11 = (bf16[16,1,128,128]{3,2,1,0:T(8,128)(2,1)S(1)}, bf16[16,1,128,128]{3,2,1,0:T(8,128)(2,1)}, u32[]{:S(2)}) copy-start(bf16[16,1,128,128]{3,2,1,0:T(8,128)(2,1)} %get-tuple-element.34) | copy-start | bytes 1572868
  32.4 13.6 %copy-start.10 = (bf16[16,1,128,128]{3,2,1,0:T(8,128)(2,1)S(1)}, bf16[16,1,128,128]{3,2,1,0:T(8,128)(2,1)}, u32[]{:S(2)}) copy-start(bf16[16,1,128,128]{3,2,1,0:T(8,128)(2,1)} %get-tuple-element.35) | copy-start | bytes 1572868
  42.5 4.8 %copy-start.6 = (bf16[4,128,256]{2,1,0:T(8,128)(2,1)}, bf16[4,128,256]{2,1,0:T(8,128)(2,1)S(1)}, u32[]{:S(2)}) copy-start(bf16[4,128,256]{2,1,0:T(8,128)(2,1)S(1)} %all-to-all-done.planar) | copy-start | bytes 786436
  42.5 17.0 %collective-permute-start.2 = (bf16[16,1,128,128]{3,2,1,0:T(8,128)(2,1)S(1)}, bf16[16,1,128,128]{3,2,1,0:T(8,128)(2,1)S(1)}, u32[]{:S(2)}, u32[]{:S(2)}) collective-permute-start(bf16[16,1,128,128]{3,2,1,0:T(8,128)(2,1)S(1)} %copy-done.11), channel_id=1, source_target_pairs={{0,1},{1,2},{2,3},{4,5},{5,6},{6,7},{8,9},{9,10},{10,11},{12,13},{... | collective-permute-start | bytes 1572872 | tf_op jit(solution)/shard_map/ppermute | solution.py:936
  46.0 14.1 %collective-permute-start.3 = (bf16[16,1,128,128]{3,2,1,0:T(8,128)(2,1)S(1)}, bf16[16,1,128,128]{3,2,1,0:T(8,128)(2,1)S(1)}, u32[]{:S(2)}, u32[]{:S(2)}) collective-permute-start(bf16[16,1,128,128]{3,2,1,0:T(8,128)(2,1)S(1)} %copy-done.10), channel_id=1, source_target_pairs={{1,0},{2,1},{3,2},{5,4},{6,5},{7,6},{9,8},{10,9},{11,10},{13,12},{... | collective-permute-start | bytes 1572872 | tf_op jit(solution)/shard_map/ppermute | solution.py:936
  54.5 16.5 %all-to-all-start.1 = ((bf16[4,128,256]{2,1,0:T(8,128)(2,1)}), bf16[4,128,256]{2,1,0:T(8,128)(2,1)S(1)}, u32[]{:S(2)}, u32[]{:S(2)}) async-start(bf16[4,128,256]{2,1,0:T(8,128)(2,1)} %get-tuple-element.33), calls=%async_computation.1 | async-start | bytes 524288 | tf_op jit(solution)/shard_map/all_to_all | solution.py:940
  59.4 0.8 copy-start.1
  60.2 0.8 copy-start.2
  71.0 0.7 copy-start
  95.0 12.6 %all-to-all-start.2 = ((bf16[4,128,256]{2,1,0:T(8,128)(2,1)}), bf16[4,128,256]{2,1,0:T(8,128)(2,1)S(1)}, u32[]{:S(2)}, u32[]{:S(2)}) async-start(bf16[4,128,256]{2,1,0:T(8,128)(2,1)} %get-tuple-element.40), calls=%async_computation.2 | async-start | bytes 524288 | tf_op jit(solution)/shard_map/all_to_all | solution.py:940
  100.1 35.8 %collective-permute-start.4 = (bf16[32,1,128,128]{3,2,1,0:T(8,128)(2,1)}, bf16[32,1,128,128]{3,2,1,0:T(8,128)(2,1)S(1)}, u32[]{:S(2)}, u32[]{:S(2)}) collective-permute-start(bf16[32,1,128,128]{3,2,1,0:T(8,128)(2,1)} %get-tuple-element.39), channel_id=1, source_target_pairs={{0,1},{1,2},{2,3},{4,5},{5,6},{6,7},{8,9},{9,10},{10,11},{12,13},{... | collective-permute-start | bytes 3145736 | tf_op jit(solution)/shard_map/ppermute | solution.py:936
  104.1 31.9 %collective-permute-start.5 = (bf16[32,1,128,128]{3,2,1,0:T(8,128)(2,1)}, bf16[32,1,128,128]{3,2,1,0:T(8,128)(2,1)S(1)}, u32[]{:S(2)}, u32[]{:S(2)}) collective-permute-start(bf16[32,1,128,128]{3,2,1,0:T(8,128)(2,1)} %get-tuple-element.45), channel_id=1, source_target_pairs={{1,0},{2,1},{3,2},{5,4},{6,5},{7,6},{9,8},{10,9},{11,10},{13,12},{... | collective-permute-start | bytes 3145736 | tf_op jit(solution)/shard_map/ppermute | solution.py:936
  107.6 0.7 copy-start.7
  116.0 20.0 %all-to-all-start.3 = ((bf16[4,128,256]{2,1,0:T(8,128)(2,1)}), bf16[4,128,256]{2,1,0:T(8,128)(2,1)S(1)}, u32[]{:S(2)}, u32[]{:S(2)}) async-start(bf16[4,128,256]{2,1,0:T(8,128)(2,1)} %get-tuple-element.46), calls=%async_computation.3 | async-start | bytes 524288 | tf_op jit(solution)/shard_map/all_to_all | solution.py:940
  120.0 35.1 %all-gather.3.cloned.1.call-start = ((), (), s32[]{:S(2)}) async-start(), calls=%async_computation.4 | async-start | bytes 1310720 | tf_op jit(solution)/shard_map/all_gather | solution.py:972
  136.0 0.7 copy-start.5
  136.0 1.1 copy-start.8
  137.1 1.0 copy-start.9
Sparse Core Ops, SparseCore 0:
  122.4 18.1 all-gather.2

commit v9 on v8

--- a/solution.py
+++ b/solution.py
@@ -338,7 +338,7 @@
 
 def cut_rims(field):
     channels, planes = field.shape[:2]
-    steps = 4
+    steps = 2
     rim = jax.ShapeDtypeStruct((channels // 2, 1, NX, NY), jnp.bfloat16)
     block = (channels // steps, 1, NX, NY)
     outs = [
@@ -418,8 +418,9 @@
         spectrum[...] = modes
         total[...] = jnp.zeros_like(total)
         if adjoint:
-            send[: 2 * half] = partner[...]
-            send[2 * half :] = modes
+            for d in range(send.shape[0]):
+                send[d, : 2 * half] = partner[...]
+                send[d, 2 * half :] = modes
 
     lane = lax.broadcasted_iota(jnp.int32, (1, spectrum.shape[1]), 1)
     mine = lane % steps == step
@@ -457,7 +458,7 @@
             out[s] = modes[:, s * width : (s + 1) * width].astype(jnp.bfloat16)
 
 
-def mix(planar, weight, scale_in, scale_out, partner=None):
+def mix(planar, weight, scale_in, scale_out, partner=None, copies=0):
     slabs, lines, width = planar.shape
     adjoint = partner is not None
     depth = KX // slabs
@@ -488,7 +489,7 @@
         in_specs.append(whole(shape))
         operands.append(partner)
         scratch = [pltpu.VMEM(shape, jnp.bfloat16)] + scratch
-        outs = [planar.shape, (2 * shape[0], lines)]
+        outs = [planar.shape, (copies, 2 * shape[0], lines)]
     else:
         outs = [shape, planar.shape]
     return pl.pallas_call(
@@ -738,19 +739,23 @@
         sheets = [before[c, 0]] + [field[c, z] for z in range(planes)] + [after[c, 0]]
         totals.append(apply_band([sheets[z : z + 4] for z in range(0, planes, 2)], band))
 
-    banded(False, taps, start, even, odd, 2)(visit)
-    for p in range(planes // 2):
-        both = [totals[c][p].reshape(NX // 8, 8, 2 * NY) for c in range(2)]
-        out[p] = jnp.concatenate(both, axis=1).astype(jnp.bfloat16)
+        if c % 2 == 1:
+            for p in range(planes // 2):
+                both = [total[p].reshape(NX // 8, 8, 2 * NY) for total in totals[c - 1 : c + 1]]
+                both = jnp.concatenate(both, axis=1).astype(jnp.bfloat16)
+                out[p, :, 8 * (c - 1) : 8 * (c + 1), :] = both
+
+    banded(False, taps, start, even, odd, field.shape[0])(visit)
 
 
 def smooth_planes(field, rims, taps, done=None):
     channels, planes = field.shape[:2]
     pairs = planes // 2
     start = 0 if done is None else channels // 2
-    skip = start // 2
-    rim = pl.BlockSpec((2, 1, NX, NY), lambda c: (c, 0, 0, 0))
-    sheets = pl.BlockSpec((2, planes, NX, NY), lambda c: (c + skip, 0, 0, 0))
+    step = 4
+    skip = start // step
+    rim = pl.BlockSpec((step, 1, NX, NY), lambda c: (c, 0, 0, 0))
+    sheets = pl.BlockSpec((step, planes, NX, NY), lambda c: (c + skip, 0, 0, 0))
     in_specs = [pl.BlockSpec(memory_space=pltpu.SMEM), rim, sheets, rim]
     operands = [taps, rims[0], field, rims[1]]
     if done is not None:
@@ -758,9 +763,9 @@
         operands.append(done)
     return pl.pallas_call(
         functools.partial(smooth_kernel, start),
-        grid=(channels // 4,),
+        grid=(channels // 2 // step,),
         in_specs=in_specs,
-        out_specs=pl.BlockSpec((pairs, NX // 8, 16, 2 * NY), lambda c: (0, 0, c + skip, 0)),
+        out_specs=pl.BlockSpec((pairs, NX // 8, 8 * step, 2 * NY), lambda c: (0, 0, c + skip, 0)),
         out_shape=jax.ShapeDtypeStruct((pairs, NX // 8, 8 * channels, 2 * NY), jnp.bfloat16),
         input_output_aliases={} if done is None else {4: 0},
         scratch_shapes=[pltpu.VMEM((6 * 64, 4 * 64), jnp.bfloat16) for _ in range(2)],
@@ -780,20 +785,21 @@
             out[c, 2 * p] = total[:, :NY]
             out[c, 2 * p + 1] = total[:, NY:]
 
-    banded(True, taps, 0, even, odd, 2)(visit)
+    banded(True, taps, 0, even, odd, field.shape[0])(visit)
 
 
 def near_inner(field, taps):
     channels, planes = field.shape[:2]
+    step = 8
     shape = (channels, planes - 4, NX, NY)
     return pl.pallas_call(
         inner_kernel,
-        grid=(channels // 2,),
+        grid=(channels // step,),
         in_specs=[
             pl.BlockSpec(memory_space=pltpu.SMEM),
-            pl.BlockSpec((2, planes, NX, NY), lambda c: (c, 0, 0, 0)),
+            pl.BlockSpec((step, planes, NX, NY), lambda c: (c, 0, 0, 0)),
         ],
-        out_specs=pl.BlockSpec((2,) + shape[1:], lambda c: (c, 0, 0, 0)),
+        out_specs=pl.BlockSpec((step,) + shape[1:], lambda c: (c, 0, 0, 0)),
         out_shape=jax.ShapeDtypeStruct(shape, jnp.bfloat16),
         scratch_shapes=[pltpu.VMEM((6 * 64, 4 * 64), jnp.bfloat16) for _ in range(2)],
         compiler_params=params(),
@@ -817,7 +823,7 @@
             for s in range(slabs):
                 waves[s, t] = wave[s * lines : (s + 1) * lines]
 
-    rows = 4 * (KX // slabs)
+    rows = field.shape[0] * (KX // slabs)
     here = pl.ds(pl.multiple_of(rows * step, rows), rows)
     right = [waves[s, t, here, :] for s in range(slabs) for t in range(2)]
     right = jnp.concatenate(right, axis=0)
@@ -838,25 +844,26 @@
         for p in range(1, planes // 2 - 1):
             store(c, p, [inner[c, 2 * p - 2 + q].astype(jnp.float32) for q in range(2)])
 
-    banded(True, taps, 0, even, odd, 4)(visit)
+    banded(True, taps, 0, even, odd, field.shape[0])(visit)
 
 
 def finish(planar, spread, rims, inner, taps):
     slabs, lines, width = planar.shape
     channels, planes = spread.shape[:2]
-    ix_table = constant(inverse_x_table(slabs, 4))
+    step = 8
+    ix_table = constant(inverse_x_table(slabs, step))
     iy_table = constant(inverse_y_table(planes, planes))
-    rim = pl.BlockSpec((4, 1, NX, NY), lambda c: (c, 0, 0, 0))
-    sheets = pl.BlockSpec((4, planes, NX, NY), lambda c: (c, 0, 0, 0))
+    rim = pl.BlockSpec((step, 1, NX, NY), lambda c: (c, 0, 0, 0))
+    sheets = pl.BlockSpec((step, planes, NX, NY), lambda c: (c, 0, 0, 0))
     return pl.pallas_call(
         finish_kernel,
-        grid=(channels // 4,),
+        grid=(channels // step,),
         in_specs=[
             pl.BlockSpec(memory_space=pltpu.SMEM),
             rim,
             sheets,
             rim,
-            pl.BlockSpec((4,) + inner.shape[1:], lambda c: (c, 0, 0, 0)),
+            pl.BlockSpec((step,) + inner.shape[1:], lambda c: (c, 0, 0, 0)),
             whole(planar.shape),
             whole(ix_table.shape),
             whole(iy_table.shape),
@@ -964,12 +971,12 @@
     smooth = smooth_planes(field, rims_high, taps, smooth)
     spread, planar, first, last = layer(planar, smooth, cotangent[0], grains[0], bias, point_weight)
     rims = exchange(first, last)
-    planar, send = mix(swap(planar), weight, 0.5 * mode_scale, cell_scale, spectrum)
+    planar, send = mix(swap(planar), weight, 0.5 * mode_scale, cell_scale, spectrum, copies)
     planar = swap(planar)
     send, spread = barrier((send, spread))
     inner = near_inner(spread, taps)
     grad_feats = finish(planar, spread, rims, inner, taps)
-    gathered = lax.all_gather(send, "dp")
+    gathered = lax.all_to_all(send, "dp", split_axis=0, concat_axis=0)
     grad_feats, gathered = barrier((grad_feats, gathered))
     grad_feats = grad_feats[None]
     grad_spec = weight_gradient(gathered, KX // slabs, width, lax.axis_index("dp"))

time: 170 us -> 156 us (0.918)
  between operations: 14.1 us -> 0.78 us
  Pallas kernels: 107 us -> 98.5 us
  waiting for transfers between devices: 4.39 us -> 8.61 us
  starting transfers between devices: 36.3 us -> 39.8 us
    pallas_call x2, Pallas kernels: 32.3 us -> 27 us  [the longest x1 16.5 us: finish(): pl.pallas_call(finish_kernel, grid=(channels // step,), in_specs=[pl.Bloc...]
    all_to_all x4, waiting for transfers between devices: 2.2 us -> 6.48 us  [swap(): return lax.all_to_all(planar, 'slab', split_axis=0, concat_axis=0)]
    all_to_all x0 -> x1, starting transfers between devices: none -> 3.52 us  [local_fast(): gathered = lax.all_to_all(send, 'dp', split_axis=0, concat_axis=0)]
    pallas_call x2, Pallas kernels: 20.1 us -> 17.1 us  [smooth_planes(): pl.pallas_call(functools.partial(smooth_kernel, start), grid=(channels //...]
    unnamed x24 -> x26, local copies, waits for them, and re-layouts: 5.25 us -> 6.12 us
  transfers between devices with their start and end apart: 11 -> 11, of which waited for: 3 -> 4; matrix products, arithmetic and copies ran while one was open for 0% -> 0% of each run, Pallas kernels for 44% -> 43%
where the time goes in v9:
time: 156 us; the launch traced here: 154 us
  Pallas kernels  98.5 us (63%)
  starting transfers between devices  39.8 us (26%)
  waiting for transfers between devices  8.61 us (6%)
  local copies, waits for them, and re-layouts  6.12 us (4%)
    pallas_call x1, Pallas kernels, layer(): pl.pallas_call(layer_kernel, grid=(pairs,), in_specs=[pl.BlockSpec(memory...  23.3 us
    all_to_all x4, starting transfers between devices, swap(): return lax.all_to_all(planar, 'slab', split_axis=0, concat_axis=0)  20 us
    pallas_call x2, Pallas kernels, smooth_planes(): pl.pallas_call(functools.partial(smooth_kernel, start), grid=(channels //...  17.1 us
    pallas_call x1, Pallas kernels, finish(): pl.pallas_call(finish_kernel, grid=(channels // step,), in_specs=[pl.Bloc...  16.5 us
    ppermute x6, starting transfers between devices, exchange(): return (lax.ppermute(last, 'slab', up), lax.ppermute(first, 'slab', down))  16.3 us
    pallas_call x2, Pallas kernels, mix(): pl.pallas_call(functools.partial(mixing_kernel, scale_in, scale_out, adjo...  15.2 us
    pallas_call x1, Pallas kernels, near_inner(): pl.pallas_call(inner_kernel, grid=(channels // step,), in_specs=[pl.Block...  10.5 us
    pallas_call x1, Pallas kernels, forward_modes(): pl.pallas_call(forward_kernel, grid=(planes // 2,), in_specs=[pl.BlockSpe...  6.74 us
  transfers between devices with their start and end apart: 11, of which 4 were waited for; matrix products, arithmetic and copies ran while one was open for 0% of the time, Pallas kernels for 43%

profile of v9, /device:TPU:0, one launch (start us, length us, event | category | flops | bytes accessed | tf_op | source)
XLA Modules:
  0.0 154.4 jit_solution(2015515119638362020)
XLA Ops:
  0.6 3.0 %rims.1 = (bf16[16,1,128,128]{3,2,1,0:T(8,128)(2,1)}, bf16[16,1,128,128]{3,2,1,0:T(8,128)(2,1)}, bf16[16,1,128,128]{3,2,1,0:T(8,128)(2,1)}, bf16[16,1,128,128]{3,2,1,0:T(8,128)(2,1)}) custom-call(bf16[32,8,128,128]{3,2,1,0:T(8,128)(2,1)} %bitcast.8, bf16[32,8,128,128]{3,2,1,0:T(8,128)(2,1)} %bitcast.9), custom_call_target="tpu_custom_call" | custom-call | flops 10000000 | bytes 100000 | tf_op jit(solution)/shard_map/rims/pallas_call | solution.py:348
  3.6 4.9 %collective-permute-start = (bf16[16,1,128,128]{3,2,1,0:T(8,128)(2,1)}, bf16[16,1,128,128]{3,2,1,0:T(8,128)(2,1)S(1)}, u32[]{:S(2)}, u32[]{:S(2)}) collective-permute-start(bf16[16,1,128,128]{3,2,1,0:T(8,128)(2,1)} %get-tuple-element.26), channel_id=1, source_target_pairs={{0,1},{1,2},{2,3},{4,5},{5,6},{6,7},{8,9},{9,10},{10,11},{12,13},{... | collective-permute-start | bytes 1572872 | tf_op jit(solution)/shard_map/ppermute | solution.py:943
  8.6 1.3 collective-permute-start.1
  9.9 6.7 %forward_modes.1 = bf16[4,128,256]{2,1,0:T(8,128)(2,1)} custom-call(bf16[32,8,128,128]{3,2,1,0:T(8,128)(2,1)} %bitcast.10, bf16[64,256]{1,0:T(8,128)(2,1)} %constant.57.clone.x_table, bf16[2048,256]{1,0:T(8,128)(2,1)} %constant.58.clone.y_table), custom_call_target="tpu_custom_call" | custom-call | flops 10000000 | bytes 100000 | tf_op jit(solution)/shard_map/forward_modes/pallas_call | solution.py:384
  16.6 5.9 %all-to-all-start = ((bf16[4,128,256]{2,1,0:T(8,128)(2,1)}), bf16[4,128,256]{2,1,0:T(8,128)(2,1)S(1)}, u32[]{:S(2)}, u32[]{:S(2)}) async-start(bf16[4,128,256]{2,1,0:T(8,128)(2,1)} %forward_modes.1), calls=%async_computation | async-start | bytes 524288 | tf_op jit(solution)/shard_map/all_to_all | solution.py:947
  22.5 0.0 collective-permute-done.before
  22.5 1.5 collective-permute-done.1.after
  24.1 0.0 copy-done.4
  24.1 0.8 copy-done.5
  24.8 8.6 %smooth_low.1.rest_0_ = bf16[4,16,256,256]{3,2,1,0:T(8,128)(2,1)} custom-call(f32[27,32]{1,0:T(8,128)} %taps.7, bf16[16,1,128,128]{3,2,1,0:T(8,128)(2,1)} %copy-done.4, bf16[32,8,128,128]{3,2,1,0:T(8,128)(2,1)} %bitcast.11, bf16[16,1,128,128]{3,2,1,0:T(8,128)(2,1)} %copy-done.5), custom_call_target="tpu_custom_call" | custom-call | flops 10000000 | bytes 100000 | tf_op jit(solution)/shard_map/smooth_low/pallas_call | solution.py:764
  33.5 0.0 all-to-all-done.planar
  33.5 0.0 copy-done.12
  33.5 0.0 copy-start.7
  33.5 3.5 %collective-permute-start.2 = (bf16[16,1,128,128]{3,2,1,0:T(8,128)(2,1)S(1)}, bf16[16,1,128,128]{3,2,1,0:T(8,128)(2,1)S(1)}, u32[]{:S(2)}, u32[]{:S(2)}) collective-permute-start(bf16[16,1,128,128]{3,2,1,0:T(8,128)(2,1)S(1)} %copy-done.12), channel_id=1, source_target_pairs={{0,1},{1,2},{2,3},{4,5},{5,6},{6,7},{8,9},{9,10},{10,11},{12,13},{... | collective-permute-start | bytes 1572872 | tf_op jit(solution)/shard_map/ppermute | solution.py:943
  37.0 0.0 copy-done.11
  37.0 1.3 collective-permute-start.3
  38.3 0.0 copy-done.7
  38.3 7.3 %mix.1 = (bf16[512,128]{1,0:T(8,128)(2,1)}, bf16[4,128,256]{2,1,0:T(8,128)(2,1)}) custom-call(bf16[4,128,256]{2,1,0:T(8,128)(2,1)} %copy-done.7, bf16[1024,2048]{1,0:T(8,128)(2,1)} %bitcast.16, bf16[1024,512]{1,0:T(8,128)(2,1)} %constant.59.clone.z_in, bf16[512,1024]{1,0:T(8,128)(2,1)} %constant.60.clone.z_out, ...), custom_call_target="tpu_custom_call" | custom-call | flops 99999997952 | bytes 100000000 | tf_op jit(solution)/shard_map/mix/pallas_call | solution.py:495
  45.5 4.9 %all-to-all-start.1 = ((bf16[4,128,256]{2,1,0:T(8,128)(2,1)}), bf16[4,128,256]{2,1,0:T(8,128)(2,1)S(1)}, u32[]{:S(2)}, u32[]{:S(2)}) async-start(bf16[4,128,256]{2,1,0:T(8,128)(2,1)} %get-tuple-element.33), calls=%async_computation.1 | async-start | bytes 524288 | tf_op jit(solution)/shard_map/all_to_all | solution.py:947
  50.4 0.0 collective-permute-done.2.before
  50.5 0.6 collective-permute-done.3.after
  51.1 0.2 copy-done.2
  51.2 0.8 copy-done.3
  52.1 8.5 %smooth_high.1.smooth = bf16[4,16,256,256]{3,2,1,0:T(8,128)(2,1)} custom-call(f32[27,32]{1,0:T(8,128)} %taps.7, bf16[16,1,128,128]{3,2,1,0:T(8,128)(2,1)} %copy-done.2, bf16[32,8,128,128]{3,2,1,0:T(8,128)(2,1)} %bitcast.12, bf16[16,1,128,128]{3,2,1,0:T(8,128)(2,1)} %copy-done.3, ...), custom_call_target="tpu_custom_call", output_to_operand_aliasing={{}: (4, {})} | custom-call | flops 10000000 | bytes 100000 | tf_op jit(solution)/shard_map/smooth_high/pallas_call | solution.py:764
  60.6 0.0 all-to-all-done.1.planar
  60.6 0.7 copy-done.1
  61.3 23.3 %layer.1 = (bf16[32,8,128,128]{3,2,1,0:T(8,128)(2,1)}, bf16[4,128,256]{2,1,0:T(8,128)(2,1)}, bf16[32,1,128,128]{3,2,1,0:T(8,128)(2,1)}, bf16[32,1,128,128]{3,2,1,0:T(8,128)(2,1)}) custom-call(f32[32]{0:T(128)} %bias.1, bf16[4,128,256]{2,1,0:T(8,128)(2,1)} %copy-done.1, bf16[4,16,256,256]{3,2,1,0:T(8,128)(2,1)} %smooth_high.1.smooth, ...), custom_call_target="tpu_custom_call" | custom-call | flops 10000000 | bytes 100000 | tf_op jit(solution)/shard_map/layer/pallas_call | solution.py:612
  84.6 5.1 %all-to-all-start.2 = ((bf16[4,128,256]{2,1,0:T(8,128)(2,1)}), bf16[4,128,256]{2,1,0:T(8,128)(2,1)S(1)}, u32[]{:S(2)}, u32[]{:S(2)}) async-start(bf16[4,128,256]{2,1,0:T(8,128)(2,1)} %get-tuple-element.40), calls=%async_computation.2 | async-start | bytes 524288 | tf_op jit(solution)/shard_map/all_to_all | solution.py:947
  89.6 4.0 %collective-permute-start.4 = (bf16[32,1,128,128]{3,2,1,0:T(8,128)(2,1)}, bf16[32,1,128,128]{3,2,1,0:T(8,128)(2,1)S(1)}, u32[]{:S(2)}, u32[]{:S(2)}) collective-permute-start(bf16[32,1,128,128]{3,2,1,0:T(8,128)(2,1)} %get-tuple-element.39), channel_id=1, source_target_pairs={{0,1},{1,2},{2,3},{4,5},{5,6},{6,7},{8,9},{9,10},{10,11},{12,13},{... | collective-permute-start | bytes 3145736 | tf_op jit(solution)/shard_map/ppermute | solution.py:943
  93.6 1.3 collective-permute-start.5
  94.9 2.2 %all-to-all-done.2.planar = bf16[4,128,256]{2,1,0:T(8,128)(2,1)S(1)} async-done(((bf16[4,128,256]{2,1,0:T(8,128)(2,1)}), bf16[4,128,256]{2,1,0:T(8,128)(2,1)S(1)}, u32[]{:S(2)}, u32[]{:S(2)}) %all-to-all-start.2) | async-done | bytes 262176 | tf_op jit(solution)/shard_map/all_to_all | solution.py:947
  97.1 0.7 copy-done.8
  97.8 7.9 %mix_back.1 = (bf16[4,128,256]{2,1,0:T(8,128)(2,1)}, bf16[4,1024,128]{2,1,0:T(8,128)(2,1)}) custom-call(bf16[4,128,256]{2,1,0:T(8,128)(2,1)} %copy-done.8, bf16[1024,2048]{1,0:T(8,128)(2,1)} %bitcast.17, bf16[1024,512]{1,0:T(8,128)(2,1)} %constant.59.clone.z_in, bf16[512,1024]{1,0:T(8,128)(2,1)} %constant.60.clone.z_out, ...), custom_call_target="tpu_custom_call" | custom-call | flops 99999997952 | bytes 100000000 | tf_op jit(solution)/shard_map/mix_back/pallas_call | solution.py:495
  105.8 4.1 %all-to-all-start.3 = ((bf16[4,128,256]{2,1,0:T(8,128)(2,1)}), bf16[4,128,256]{2,1,0:T(8,128)(2,1)S(1)}, u32[]{:S(2)}, u32[]{:S(2)}) async-start(bf16[4,128,256]{2,1,0:T(8,128)(2,1)} %get-tuple-element.46), calls=%async_computation.3 | async-start | bytes 524288 | tf_op jit(solution)/shard_map/all_to_all | solution.py:947
  109.8 0.6 pad_add_fusion.where
  110.4 10.5 %near_inner.1.inner = bf16[32,4,128,128]{3,2,1,0:T(8,128)(2,1)} custom-call(f32[27,32]{1,0:T(8,128)} %taps.7, bf16[32,8,128,128]{3,2,1,0:T(8,128)(2,1)} %get-tuple-element.44.field), custom_call_target="tpu_custom_call" | custom-call | flops 10000000 | bytes 100000 | tf_op jit(solution)/shard_map/near_inner/pallas_call | solution.py:795
  120.9 4.3 %all-to-all-done.3.planar = bf16[4,128,256]{2,1,0:T(8,128)(2,1)S(1)} async-done(((bf16[4,128,256]{2,1,0:T(8,128)(2,1)}), bf16[4,128,256]{2,1,0:T(8,128)(2,1)S(1)}, u32[]{:S(2)}, u32[]{:S(2)}) %all-to-all-start.3) | async-done | bytes 262176 | tf_op jit(solution)/shard_map/all_to_all | solution.py:947
  125.2 3.5 %all-to-all-start.4 = ((bf16[4,1024,128]{2,1,0:T(8,128)(2,1)}), bf16[4,1024,128]{2,1,0:T(8,128)(2,1)S(1)}, u32[]{:S(2)}, u32[]{:S(2)}) async-start(bf16[4,1024,128]{2,1,0:T(8,128)(2,1)} %get-tuple-element.47), calls=%async_computation.4 | async-start | bytes 2097152 | tf_op jit(solution)/shard_map/all_to_all | solution.py:979
  128.7 0.0 collective-permute-done.4.before
  128.8 0.0 copy-start.9
  128.8 0.0 collective-permute-done.5.after
  128.8 1.0 copy-done.9
  129.7 1.0 copy-done.10
  130.7 16.5 %finish.1 = bf16[32,8,128,128]{3,2,1,0:T(8,128)(2,1)} custom-call(f32[27,32]{1,0:T(8,128)} %taps.7, bf16[32,1,128,128]{3,2,1,0:T(8,128)(2,1)} %copy-done.9, bf16[32,8,128,128]{3,2,1,0:T(8,128)(2,1)} %get-tuple-element.44.field, bf16[32,1,128,128]{3,2,1,0:T(8,128)(2,1)} %copy-done.10, bf16[32,4,128,128]{3,2,1,0:T(8,128)(2,1)} %near_inner.1.inner, ...), custom_call_target="tpu_custom_call" | custom-call | flops 99999997952 | bytes 100000000 | tf_op jit(solution)/shard_map/finish/pallas_call | solution.py:858
  147.2 0.0 all-to-all-done.4.gathered
  147.2 0.0 copy-start
  147.2 1.0 copy-done
  148.2 6.2 %weight_gradient.1 = f32[1024,512]{1,0:T(8,128)} custom-call(s32[2]{0:T(128)} %pad_add_fusion.where, bf16[4,1024,128]{2,1,0:T(8,128)(2,1)} %copy-done, bf16[2,128,512]{2,1,0:T(8,128)(2,1)} %constant.70.clone.first, bf16[128,128]{1,0:T(8,128)(2,1)} %constant.67.clone.spread_table.second), custom_call_target="tpu_custom_call" | custom-call | flops 10000000 | bytes 100000 | tf_op jit(solution)/shard_map/weight_gradient/pallas_call | solution.py:920
  (11 shorter events, 0.0 us)
Async XLA Ops:
  3.6 18.9 %collective-permute-start = (bf16[16,1,128,128]{3,2,1,0:T(8,128)(2,1)}, bf16[16,1,128,128]{3,2,1,0:T(8,128)(2,1)S(1)}, u32[]{:S(2)}, u32[]{:S(2)}) collective-permute-start(bf16[16,1,128,128]{3,2,1,0:T(8,128)(2,1)} %get-tuple-element.26), channel_id=1, source_target_pairs={{0,1},{1,2},{2,3},{4,5},{5,6},{6,7},{8,9},{9,10},{10,11},{12,13},{... | collective-permute-start | bytes 1572872 | tf_op jit(solution)/shard_map/ppermute | solution.py:943
  8.6 15.5 %collective-permute-start.1 = (bf16[16,1,128,128]{3,2,1,0:T(8,128)(2,1)}, bf16[16,1,128,128]{3,2,1,0:T(8,128)(2,1)S(1)}, u32[]{:S(2)}, u32[]{:S(2)}) collective-permute-start(bf16[16,1,128,128]{3,2,1,0:T(8,128)(2,1)} %get-tuple-element.27), channel_id=1, source_target_pairs={{1,0},{2,1},{3,2},{5,4},{6,5},{7,6},{9,8},{10,9},{11,10},{13,12},{... | collective-permute-start | bytes 1572872 | tf_op jit(solution)/shard_map/ppermute | solution.py:943
  16.6 16.9 %all-to-all-start = ((bf16[4,128,256]{2,1,0:T(8,128)(2,1)}), bf16[4,128,256]{2,1,0:T(8,128)(2,1)S(1)}, u32[]{:S(2)}, u32[]{:S(2)}) async-start(bf16[4,128,256]{2,1,0:T(8,128)(2,1)} %forward_modes.1), calls=%async_computation | async-start | bytes 524288 | tf_op jit(solution)/shard_map/all_to_all | solution.py:947
  22.5 1.5 copy-start.4
  24.1 0.8 copy-start.5
  24.8 8.6 %copy-start.12 = (bf16[16,1,128,128]{3,2,1,0:T(8,128)(2,1)S(1)}, bf16[16,1,128,128]{3,2,1,0:T(8,128)(2,1)}, u32[]{:S(2)}) copy-start(bf16[16,1,128,128]{3,2,1,0:T(8,128)(2,1)} %get-tuple-element.34) | copy-start | bytes 1572868
  24.8 12.1 %copy-start.11 = (bf16[16,1,128,128]{3,2,1,0:T(8,128)(2,1)S(1)}, bf16[16,1,128,128]{3,2,1,0:T(8,128)(2,1)}, u32[]{:S(2)}) copy-start(bf16[16,1,128,128]{3,2,1,0:T(8,128)(2,1)} %get-tuple-element.35) | copy-start | bytes 1572868
  33.5 4.8 %copy-start.7 = (bf16[4,128,256]{2,1,0:T(8,128)(2,1)}, bf16[4,128,256]{2,1,0:T(8,128)(2,1)S(1)}, u32[]{:S(2)}) copy-start(bf16[4,128,256]{2,1,0:T(8,128)(2,1)S(1)} %all-to-all-done.planar) | copy-start | bytes 786436
  33.5 17.0 %collective-permute-start.2 = (bf16[16,1,128,128]{3,2,1,0:T(8,128)(2,1)S(1)}, bf16[16,1,128,128]{3,2,1,0:T(8,128)(2,1)S(1)}, u32[]{:S(2)}, u32[]{:S(2)}) collective-permute-start(bf16[16,1,128,128]{3,2,1,0:T(8,128)(2,1)S(1)} %copy-done.12), channel_id=1, source_target_pairs={{0,1},{1,2},{2,3},{4,5},{5,6},{6,7},{8,9},{9,10},{10,11},{12,13},{... | collective-permute-start | bytes 1572872 | tf_op jit(solution)/shard_map/ppermute | solution.py:943
  37.0 14.1 %collective-permute-start.3 = (bf16[16,1,128,128]{3,2,1,0:T(8,128)(2,1)S(1)}, bf16[16,1,128,128]{3,2,1,0:T(8,128)(2,1)S(1)}, u32[]{:S(2)}, u32[]{:S(2)}) collective-permute-start(bf16[16,1,128,128]{3,2,1,0:T(8,128)(2,1)S(1)} %copy-done.11), channel_id=1, source_target_pairs={{1,0},{2,1},{3,2},{5,4},{6,5},{7,6},{9,8},{10,9},{11,10},{13,12},{... | collective-permute-start | bytes 1572872 | tf_op jit(solution)/shard_map/ppermute | solution.py:943
  45.5 15.0 %all-to-all-start.1 = ((bf16[4,128,256]{2,1,0:T(8,128)(2,1)}), bf16[4,128,256]{2,1,0:T(8,128)(2,1)S(1)}, u32[]{:S(2)}, u32[]{:S(2)}) async-start(bf16[4,128,256]{2,1,0:T(8,128)(2,1)} %get-tuple-element.33), calls=%async_computation.1 | async-start | bytes 524288 | tf_op jit(solution)/shard_map/all_to_all | solution.py:947
  50.4 0.8 copy-start.2
  51.2 0.8 copy-start.3
  60.6 0.7 copy-start.1
  84.6 12.6 %all-to-all-start.2 = ((bf16[4,128,256]{2,1,0:T(8,128)(2,1)}), bf16[4,128,256]{2,1,0:T(8,128)(2,1)S(1)}, u32[]{:S(2)}, u32[]{:S(2)}) async-start(bf16[4,128,256]{2,1,0:T(8,128)(2,1)} %get-tuple-element.40), calls=%async_computation.2 | async-start | bytes 524288 | tf_op jit(solution)/shard_map/all_to_all | solution.py:947
  89.6 39.1 %collective-permute-start.4 = (bf16[32,1,128,128]{3,2,1,0:T(8,128)(2,1)}, bf16[32,1,128,128]{3,2,1,0:T(8,128)(2,1)S(1)}, u32[]{:S(2)}, u32[]{:S(2)}) collective-permute-start(bf16[32,1,128,128]{3,2,1,0:T(8,128)(2,1)} %get-tuple-element.39), channel_id=1, source_target_pairs={{0,1},{1,2},{2,3},{4,5},{5,6},{6,7},{8,9},{9,10},{10,11},{12,13},{... | collective-permute-start | bytes 3145736 | tf_op jit(solution)/shard_map/ppermute | solution.py:943
  93.6 35.1 %collective-permute-start.5 = (bf16[32,1,128,128]{3,2,1,0:T(8,128)(2,1)}, bf16[32,1,128,128]{3,2,1,0:T(8,128)(2,1)S(1)}, u32[]{:S(2)}, u32[]{:S(2)}) collective-permute-start(bf16[32,1,128,128]{3,2,1,0:T(8,128)(2,1)} %get-tuple-element.45), channel_id=1, source_target_pairs={{1,0},{2,1},{3,2},{5,4},{6,5},{7,6},{9,8},{10,9},{11,10},{13,12},{... | collective-permute-start | bytes 3145736 | tf_op jit(solution)/shard_map/ppermute | solution.py:943
  97.1 0.7 copy-start.8
  105.8 19.4 %all-to-all-start.3 = ((bf16[4,128,256]{2,1,0:T(8,128)(2,1)}), bf16[4,128,256]{2,1,0:T(8,128)(2,1)S(1)}, u32[]{:S(2)}, u32[]{:S(2)}) async-start(bf16[4,128,256]{2,1,0:T(8,128)(2,1)} %get-tuple-element.46), calls=%async_computation.3 | async-start | bytes 524288 | tf_op jit(solution)/shard_map/all_to_all | solution.py:947
  125.2 3.6 %copy-start.6 = (bf16[4,128,256]{2,1,0:T(8,128)(2,1)}, bf16[4,128,256]{2,1,0:T(8,128)(2,1)S(1)}, u32[]{:S(2)}) copy-start(bf16[4,128,256]{2,1,0:T(8,128)(2,1)S(1)} %all-to-all-done.3.planar) | copy-start | bytes 786436
  125.2 22.0 %all-to-all-start.4 = ((bf16[4,1024,128]{2,1,0:T(8,128)(2,1)}), bf16[4,1024,128]{2,1,0:T(8,128)(2,1)S(1)}, u32[]{:S(2)}, u32[]{:S(2)}) async-start(bf16[4,1024,128]{2,1,0:T(8,128)(2,1)} %get-tuple-element.47), calls=%async_computation.4 | async-start | bytes 2097152 | tf_op jit(solution)/shard_map/all_to_all | solution.py:979
  128.8 1.0 copy-start.9
  129.7 1.0 copy-start.10
  147.2 1.0 copy-start

commit v10 on v9

--- a/solution.py
+++ b/solution.py
@@ -233,29 +233,34 @@
     return table.reshape(4 * KX, 2 * NX)
 
 
+def halved(table, planes):
+    table = table.reshape(-1, planes * 2, 2, KY // 2).transpose(0, 2, 1, 3)
+    return table.reshape(-1, planes * 2 * KY)
+
+
 def forward_y_table(planes):
     a = angles(KY, NY)
     cos, sin = np.cos(a).T, np.sin(a).T
     block = np.stack([np.stack([cos, -sin], 1), np.stack([-sin, -cos], 1)])
     pick = np.eye(planes).reshape(planes // 2, 2, planes)
     table = np.einsum("pqz,tyrk->ptqyzrk", pick, block)
-    return table.reshape(planes * 2 * NY, planes * 2 * KY)
+    return halved(table.reshape(planes * 2 * NY, planes * 2 * KY), planes)
 
 
 def forward_z_table():
     a = angles(KZ, NZ)
     cos, sin = np.cos(a).T, np.sin(a).T
     block = np.stack([np.stack([cos, -sin], 1), np.stack([sin, cos], 1)], 1)
-    table = np.einsum("zrqm,kl->zrkqlm", block, np.eye(KY))
-    return table.reshape(NZ * 2 * KY, 2 * KY * KZ)
+    table = np.einsum("zrqm,kl->zrkqlm", block, np.eye(KY // 2))
+    return table.reshape(NZ * KY, KY * KZ)
 
 
 def inverse_z_table():
     a = angles(KZ, NZ)
     cos, sin = np.cos(a), np.sin(a)
     block = np.stack([np.stack([cos, sin], 2), np.stack([-sin, cos], 2)])
-    table = np.einsum("rmzq,kl->rkmzql", block, np.eye(KY))
-    return table.reshape(2 * KY * KZ, NZ * 2 * KY)
+    table = np.einsum("rmzq,kl->rkmzql", block, np.eye(KY // 2))
+    return table.reshape(KY * KZ, NZ * KY)
 
 
 def inverse_y_table(planes, group):
@@ -263,8 +268,9 @@
     cos, sin = np.cos(a), np.sin(a)
     block = np.stack([np.stack([cos, -sin], 1), np.stack([-sin, -cos], 1)])
     pick = np.eye(planes).reshape(planes // group, group, planes)
-    table = np.einsum("pqz,rkty->pzrktqy", pick, block)
-    return table.reshape(planes // group, planes * 2 * KY, 2 * group * NY)
+    table = np.einsum("pqz,rkty->ptqyzrk", pick, block)
+    table = halved(table.reshape(-1, planes * 2 * KY), planes)
+    return table.reshape(planes // group, 2 * group * NY, planes * 2 * KY).transpose(0, 2, 1)
 
 
 def inverse_x_table(slabs, group):
@@ -297,7 +303,7 @@
 
 
 def params(**kw):
-    return pltpu.CompilerParams(vmem_limit_bytes=58 * 2**20, **kw)
+    return pltpu.CompilerParams(vmem_limit_bytes=63438848, **kw)
 
 
 def store_rows(rows, pair, x_table, load):
@@ -406,56 +412,72 @@
         spectrum, out, total, wide, product = rest
     step = pl.program_id(0)
     steps = pl.num_programs(0)
-    slabs = planar.shape[0]
-    width = planar.shape[2]
-    half = spectrum.shape[0] // 2
+    slabs, lines, width = planar.shape
+    half = width // 2
+    quarter = spectrum.shape[0] // 4
     lanes = weight.shape[1] // 2
+    depth = weight.shape[0] // (2 * quarter)
 
     @pl.when(step == 0)
     def _():
-        left = jnp.concatenate([planar[s] for s in range(slabs)], axis=1)
-        modes = (dot(left, z_in[...]).T * scale_in).astype(jnp.bfloat16)
-        spectrum[...] = modes
-        total[...] = jnp.zeros_like(total)
+        left = [
+            jnp.concatenate([planar[s, :, h : h + half] for s in range(slabs)], axis=1)
+            for h in (0, half)
+        ]
+        modes = dot(jnp.concatenate(left, axis=0), z_in[...]) * scale_in
+        for h in range(2):
+            here = modes[h * lines : (h + 1) * lines].T.astype(jnp.bfloat16)
+            spectrum[2 * h * quarter : 2 * (h + 1) * quarter] = here
+            if adjoint:
+                for d in range(send.shape[0]):
+                    send[d, 2 * (h + 2) * quarter : 2 * (h + 3) * quarter] = here
         if adjoint:
             for d in range(send.shape[0]):
-                send[d, : 2 * half] = partner[...]
-                send[d, 2 * half :] = modes
-
-    lane = lax.broadcasted_iota(jnp.int32, (1, spectrum.shape[1]), 1)
-    mine = lane % steps == step
-    wide[...] = dot(jnp.where(mine, spectrum[...], 0), spread_table[...])
+                send[d, : 4 * quarter] = partner[...]
+        total[...] = jnp.zeros_like(total)
+
+    lane = lax.broadcasted_iota(jnp.int32, (1, lines), 1) % (depth * steps)
     block = 32
     tile = wide.shape[1]
-    for at in range(0, half, block):
-        sums = [0.0, 0.0]
-        for column in range(0, lanes, 128):
-            here = slice(column, column + 128) if tile == lanes else slice(None)
-            real_wide = wide[at : at + block, here]
-            imag_wide = wide[half + at : half + at + block, here]
-            w_real = weight[at : at + block, column : column + 128].astype(jnp.float32)
-            imag_column = lanes + column
-            w_imag = weight[at : at + block, imag_column : imag_column + 128].astype(jnp.float32)
-            if adjoint:
-                real = real_wide * w_real + imag_wide * w_imag
-                imag = imag_wide * w_real - real_wide * w_imag
-                product[at : at + block, column : column + 128] = real.astype(jnp.bfloat16)
-                product[half + at : half + at + block, column : column + 128] = imag.astype(
-                    jnp.bfloat16
-                )
-            else:
-                sums[0] = sums[0] + (real_wide * w_real - imag_wide * w_imag)
-                sums[1] = sums[1] + (real_wide * w_imag + imag_wide * w_real)
-        if not adjoint:
-            product[at : at + block] = sums[0].astype(jnp.bfloat16)
-            product[half + at : half + at + block] = sums[1].astype(jnp.bfloat16)
-    total[...] += jnp.where(mine, dot(product[...], sum_table[...]), 0.0)
+    for j in range(depth):
+        mine = lane == depth * step + j
+        wide[...] = dot(jnp.where(mine, spectrum[...], 0), spread_table[...])
+        for at in range(0, 2 * quarter, block):
+            row = 2 * j * quarter + at
+            real_at = at + (at // quarter) * quarter
+            imag_at = real_at + quarter
+            sums = [0.0, 0.0]
+            for column in range(0, lanes, 128):
+                here = slice(column, column + 128) if tile == lanes else slice(None)
+                real_wide = wide[real_at : real_at + block, here]
+                imag_wide = wide[imag_at : imag_at + block, here]
+                w_real = weight[row : row + block, column : column + 128]
+                w_imag = weight[row : row + block, lanes + column : lanes + column + 128]
+                w_real = w_real.astype(jnp.float32)
+                w_imag = w_imag.astype(jnp.float32)
+                if adjoint:
+                    real = real_wide * w_real + imag_wide * w_imag
+                    imag = imag_wide * w_real - real_wide * w_imag
+                    there = slice(column, column + 128)
+                    product[real_at : real_at + block, there] = real.astype(jnp.bfloat16)
+                    product[imag_at : imag_at + block, there] = imag.astype(jnp.bfloat16)
+                else:
+                    sums[0] = sums[0] + (real_wide * w_real - imag_wide * w_imag)
+                    sums[1] = sums[1] + (real_wide * w_imag + imag_wide * w_real)
+            if not adjoint:
+                product[real_at : real_at + block] = sums[0].astype(jnp.bfloat16)
+                product[imag_at : imag_at + block] = sums[1].astype(jnp.bfloat16)
+        total[...] += jnp.where(mine, dot(product[...], sum_table[...]), 0.0)
 
     @pl.when(step == steps - 1)
     def _():
-        modes = dot((total[...] * scale_out).T.astype(jnp.bfloat16), z_out[...])
+        modes = total[...] * scale_out
+        left = [modes[2 * h * quarter : 2 * (h + 1) * quarter].T for h in range(2)]
+        modes = dot(jnp.concatenate(left, axis=0).astype(jnp.bfloat16), z_out[...])
         for s in range(slabs):
-            out[s] = modes[:, s * width : (s + 1) * width].astype(jnp.bfloat16)
+            for h in range(2):
+                here = modes[h * lines : (h + 1) * lines, s * half : (s + 1) * half]
+                out[s, :, h * half : (h + 1) * half] = here.astype(jnp.bfloat16)
 
 
 def mix(planar, weight, scale_in, scale_out, partner=None, copies=0):
@@ -464,6 +486,7 @@
     depth = KX // slabs
     channels = lines // depth
     rows = KY * KZ
+    steps = 2
     z_in = constant(forward_z_table())
     z_out = constant(inverse_z_table())
     first = first_table(channels, depth)
@@ -473,7 +496,7 @@
     shape = (2 * rows, lines)
     in_specs = [
         whole(planar.shape),
-        pl.BlockSpec((rows, weight.shape[1]), lambda j: (j, 0)),
+        pl.BlockSpec((depth // steps * rows, weight.shape[1]), lambda j: (j, 0)),
         whole(z_in.shape),
         whole(z_out.shape),
         whole(spread_table.shape),
@@ -494,7 +517,7 @@
         outs = [shape, planar.shape]
     return pl.pallas_call(
         functools.partial(mixing_kernel, scale_in, scale_out, adjoint),
-        grid=(depth,),
+        grid=(steps,),
         in_specs=in_specs,
         out_specs=[whole(out) for out in outs],
         out_shape=[jax.ShapeDtypeStruct(out, jnp.bfloat16) for out in outs],
@@ -577,7 +600,7 @@
             spread[:, q, pl.ds(x, 16), :] = both[:, :, q * NY : (q + 1) * NY]
         return 0
 
-    lax.fori_loop(0, NX // 16, body, 0, unroll=4)
+    lax.fori_loop(0, NX // 16, body, 0, unroll=8)
 
 
     @pl.when(pair == 0)
@@ -752,7 +775,7 @@
     channels, planes = field.shape[:2]
     pairs = planes // 2
     start = 0 if done is None else channels // 2
-    step = 4
+    step = 8
     skip = start // step
     rim = pl.BlockSpec((step, 1, NX, NY), lambda c: (c, 0, 0, 0))
     sheets = pl.BlockSpec((step, planes, NX, NY), lambda c: (c + skip, 0, 0, 0))
@@ -884,27 +907,33 @@
 def gradient_kernel(depth, where, gathered, first, second, out):
     step = pl.program_id(0)
     samples, rows, lines = gathered.shape
-    half = rows // 4
+    quarter = rows // 8
     lane = lax.broadcasted_iota(jnp.int32, (1, lines), 1)
     mine = lane % depth == step
-    spectra = [gathered[s, : 2 * half] for s in range(samples)]
+    spectra = [gathered[s, : 4 * quarter] for s in range(samples)]
     duals = []
     for s in range(samples):
-        real = gathered[s, 2 * half : 3 * half]
-        imag = gathered[s, 3 * half :]
-        duals.append(jnp.where(where[0] == 0, real, imag))
-        duals.append(jnp.where(where[0] == 0, imag, -real))
+        for h in range(2):
+            at = (2 * h + 4) * quarter
+            real = gathered[s, at : at + quarter]
+            imag = gathered[s, at + quarter : at + 2 * quarter]
+            duals.append(jnp.where(where[0] == 0, real, imag))
+            duals.append(jnp.where(where[0] == 0, imag, -real))
     spectra = jnp.where(mine, jnp.concatenate(spectra, axis=0), 0)
     duals = jnp.where(mine, jnp.concatenate(duals, axis=0), 0)
     wide = dot(duals, second[...])
     for column in range(0, out.shape[1], 256):
         product = dot(spectra, first[0, :, column : column + 256])
         for at in range(0, 256, 128):
-            total = 0.0
-            for s in range(2 * samples):
-                here = slice(s * half, (s + 1) * half)
-                total = total + product[here, at : at + 128] * wide[here]
-            out[:, column + at : column + at + 128] = total * (1.0 / samples)
+            for h in range(2):
+                total = 0.0
+                for s in range(samples):
+                    for part in range(2):
+                        row = (4 * s + 2 * h + part) * quarter
+                        here = slice(row, row + quarter)
+                        total = total + product[here, at : at + 128] * wide[here]
+                there = slice(column + at, column + at + 128)
+                out[h * quarter : (h + 1) * quarter, there] = total * (1.0 / samples)
 
 
 def weight_gradient(gathered, depth, width, index):
@@ -972,14 +1001,14 @@
     spread, planar, first, last = layer(planar, smooth, cotangent[0], grains[0], bias, point_weight)
     rims = exchange(first, last)
     planar, send = mix(swap(planar), weight, 0.5 * mode_scale, cell_scale, spectrum, copies)
-    planar = swap(planar)
     send, spread = barrier((send, spread))
     inner = near_inner(spread, taps)
-    grad_feats = finish(planar, spread, rims, inner, taps)
     gathered = lax.all_to_all(send, "dp", split_axis=0, concat_axis=0)
-    grad_feats, gathered = barrier((grad_feats, gathered))
-    grad_feats = grad_feats[None]
+    planar, gathered, inner, rims = barrier((planar, gathered, inner, rims))
+    planar = swap(planar)
     grad_spec = weight_gradient(gathered, KX // slabs, width, lax.axis_index("dp"))
+    planar, grad_spec = barrier((planar, grad_spec))
+    grad_feats = finish(planar, spread, rims, inner, taps)[None]
     return (grad_feats, grad_spec.reshape(mode_rows, KZ, width))
 
 

time: 156 us -> 151 us (0.968)
  Pallas kernels: 98.5 us -> 94.8 us
  local copies, waits for them, and re-layouts: 6.12 us -> 4.45 us
    all_to_all x1, waiting for transfers between devices: 0.01 us -> 3.41 us  [local_fast(): gathered = lax.all_to_all(send, 'dp', split_axis=0, concat_axis=0)]
    pallas_call x2, Pallas kernels: 15.2 us -> 12.3 us  [mix(): pl.pallas_call(functools.partial(mixing_kernel, scale_in, scale_out, adjo...]
    all_to_all x4, waiting for transfers between devices: 6.48 us -> 4.08 us  [swap(): return lax.all_to_all(planar, 'slab', split_axis=0, concat_axis=0)]
    unnamed x26, local copies, waits for them, and re-layouts: 6.12 us -> 4.45 us
  transfers between devices with their start and end apart: 11 -> 11, of which waited for: 4 -> 5; matrix products, arithmetic and copies ran while one was open for 0% -> 0% of each run, Pallas kernels for 43% -> 36%
where the time goes in v10:
time: 151 us; the launch traced here: 150 us
  Pallas kernels  94.8 us (63%)
  starting transfers between devices  39.9 us (26%)
  waiting for transfers between devices  9.51 us (6%)
  local copies, waits for them, and re-layouts  4.45 us (3%)
    pallas_call x1, Pallas kernels, layer(): pl.pallas_call(layer_kernel, grid=(pairs,), in_specs=[pl.BlockSpec(memory...  21.8 us
    all_to_all x4, starting transfers between devices, swap(): return lax.all_to_all(planar, 'slab', split_axis=0, concat_axis=0)  20 us
    pallas_call x2, Pallas kernels, smooth_planes(): pl.pallas_call(functools.partial(smooth_kernel, start), grid=(channels //...  17.8 us
    pallas_call x1, Pallas kernels, finish(): pl.pallas_call(finish_kernel, grid=(channels // step,), in_specs=[pl.Bloc...  16.5 us
    ppermute x6, starting transfers between devices, exchange(): return (lax.ppermute(last, 'slab', up), lax.ppermute(first, 'slab', down))  16.4 us
    pallas_call x2, Pallas kernels, mix(): pl.pallas_call(functools.partial(mixing_kernel, scale_in, scale_out, adjo...  12.3 us
    pallas_call x1, Pallas kernels, near_inner(): pl.pallas_call(inner_kernel, grid=(channels // step,), in_specs=[pl.Block...  10.5 us
    pallas_call x1, Pallas kernels, forward_modes(): pl.pallas_call(forward_kernel, grid=(planes // 2,), in_specs=[pl.BlockSpe...  6.7 us
  transfers between devices with their start and end apart: 11, of which 5 were waited for; matrix products, arithmetic and copies ran while one was open for 0% of the time, Pallas kernels for 36%

profile of v10, /device:TPU:0, one launch (start us, length us, event | category | flops | bytes accessed | tf_op | source)
XLA Modules:
  0.0 150.1 jit_solution(13212696779230124130)
XLA Ops:
  0.6 3.0 %rims.1 = (bf16[16,1,128,128]{3,2,1,0:T(8,128)(2,1)}, bf16[16,1,128,128]{3,2,1,0:T(8,128)(2,1)}, bf16[16,1,128,128]{3,2,1,0:T(8,128)(2,1)}, bf16[16,1,128,128]{3,2,1,0:T(8,128)(2,1)}) custom-call(bf16[32,8,128,128]{3,2,1,0:T(8,128)(2,1)} %bitcast.8, bf16[32,8,128,128]{3,2,1,0:T(8,128)(2,1)} %bitcast.9), custom_call_target="tpu_custom_call" | custom-call | flops 10000000 | bytes 100000 | tf_op jit(solution)/shard_map/rims/pallas_call | solution.py:354
  3.6 0.0 copy-start.12
  3.6 0.0 copy-start.11
  3.6 5.1 %collective-permute-start = (bf16[16,1,128,128]{3,2,1,0:T(8,128)(2,1)}, bf16[16,1,128,128]{3,2,1,0:T(8,128)(2,1)S(1)}, u32[]{:S(2)}, u32[]{:S(2)}) collective-permute-start(bf16[16,1,128,128]{3,2,1,0:T(8,128)(2,1)} %get-tuple-element.31), channel_id=1, source_target_pairs={{0,1},{1,2},{2,3},{4,5},{5,6},{6,7},{8,9},{9,10},{10,11},{12,13},{... | collective-permute-start | bytes 1572872 | tf_op jit(solution)/shard_map/ppermute | solution.py:972
  8.7 1.3 collective-permute-start.1
  10.0 6.7 %forward_modes.1 = bf16[4,128,256]{2,1,0:T(8,128)(2,1)} custom-call(bf16[32,8,128,128]{3,2,1,0:T(8,128)(2,1)} %bitcast.10, bf16[64,256]{1,0:T(8,128)(2,1)} %constant.57.clone.x_table, bf16[2048,256]{1,0:T(8,128)(2,1)} %constant.58.clone.y_table), custom_call_target="tpu_custom_call" | custom-call | flops 10000000 | bytes 100000 | tf_op jit(solution)/shard_map/forward_modes/pallas_call | solution.py:390
  16.7 5.9 %all-to-all-start = ((bf16[4,128,256]{2,1,0:T(8,128)(2,1)}), bf16[4,128,256]{2,1,0:T(8,128)(2,1)S(1)}, u32[]{:S(2)}, u32[]{:S(2)}) async-start(bf16[4,128,256]{2,1,0:T(8,128)(2,1)} %forward_modes.1), calls=%async_computation | async-start | bytes 524288 | tf_op jit(solution)/shard_map/all_to_all | solution.py:976
  22.6 0.0 collective-permute-done.before
  22.7 1.5 %collective-permute-done.1.after = bf16[16,1,128,128]{3,2,1,0:T(8,128)(2,1)S(1)} collective-permute-done((bf16[16,1,128,128]{3,2,1,0:T(8,128)(2,1)}, bf16[16,1,128,128]{3,2,1,0:T(8,128)(2,1)S(1)}, u32[]{:S(2)}, u32[]{:S(2)}) %collective-permute-start.1) | collective-permute-done | bytes 524320 | tf_op jit(solution)/shard_map/ppermute | solution.py:972
  24.2 0.0 copy-done.12
  24.2 3.5 %collective-permute-start.2 = (bf16[16,1,128,128]{3,2,1,0:T(8,128)(2,1)S(1)}, bf16[16,1,128,128]{3,2,1,0:T(8,128)(2,1)S(1)}, u32[]{:S(2)}, u32[]{:S(2)}) collective-permute-start(bf16[16,1,128,128]{3,2,1,0:T(8,128)(2,1)S(1)} %copy-done.12), channel_id=1, source_target_pairs={{0,1},{1,2},{2,3},{4,5},{5,6},{6,7},{8,9},{9,10},{10,11},{12,13},{... | collective-permute-start | bytes 1572872 | tf_op jit(solution)/shard_map/ppermute | solution.py:972
  27.7 0.0 copy-done.11
  27.7 1.3 collective-permute-start.3
  29.0 0.0 copy-done.4
  29.0 0.0 copy-done.5
  29.0 8.9 %smooth_low.1.rest_0_ = bf16[4,16,256,256]{3,2,1,0:T(8,128)(2,1)} custom-call(f32[27,32]{1,0:T(8,128)} %taps.7, bf16[16,1,128,128]{3,2,1,0:T(8,128)(2,1)} %copy-done.4, bf16[32,8,128,128]{3,2,1,0:T(8,128)(2,1)} %bitcast.11, bf16[16,1,128,128]{3,2,1,0:T(8,128)(2,1)} %copy-done.5), custom_call_target="tpu_custom_call" | custom-call | flops 10000000 | bytes 100000 | tf_op jit(solution)/shard_map/smooth_low/pallas_call | solution.py:787
  37.9 0.0 all-to-all-done.planar
  37.9 0.7 copy-done.7
  38.6 5.9 %mix.1 = (bf16[512,128]{1,0:T(8,128)(2,1)}, bf16[4,128,256]{2,1,0:T(8,128)(2,1)}) custom-call(bf16[4,128,256]{2,1,0:T(8,128)(2,1)} %copy-done.7, bf16[1024,2048]{1,0:T(8,128)(2,1)} %bitcast.16, bf16[512,256]{1,0:T(8,128)(2,1)} %constant.59.clone.z_in, bf16[256,512]{1,0:T(8,128)(2,1)} %constant.60.clone.z_out, bf16[128,1024]{1,0:T(8,128)(2,1)} %constant.61.clone.spread_table, ...), custom_call_target="tpu_custom_call" | custom-call | flops 99999997952 | bytes 100000000 | tf_op jit(solution)/shard_map/mix/pallas_call | solution.py:518
  44.5 4.9 %all-to-all-start.1 = ((bf16[4,128,256]{2,1,0:T(8,128)(2,1)}), bf16[4,128,256]{2,1,0:T(8,128)(2,1)S(1)}, u32[]{:S(2)}, u32[]{:S(2)}) async-start(bf16[4,128,256]{2,1,0:T(8,128)(2,1)} %get-tuple-element.38), calls=%async_computation.1 | async-start | bytes 524288 | tf_op jit(solution)/shard_map/all_to_all | solution.py:976
  49.4 0.0 collective-permute-done.2.before
  49.4 0.0 collective-permute-done.3.after
  49.4 0.8 copy-done.2
  50.2 0.8 copy-done.3
  51.0 8.9 %smooth_high.1.smooth = bf16[4,16,256,256]{3,2,1,0:T(8,128)(2,1)} custom-call(f32[27,32]{1,0:T(8,128)} %taps.7, bf16[16,1,128,128]{3,2,1,0:T(8,128)(2,1)} %copy-done.2, bf16[32,8,128,128]{3,2,1,0:T(8,128)(2,1)} %bitcast.12, bf16[16,1,128,128]{3,2,1,0:T(8,128)(2,1)} %copy-done.3, ...), custom_call_target="tpu_custom_call", output_to_operand_aliasing={{}: (4, {})} | custom-call | flops 10000000 | bytes 100000 | tf_op jit(solution)/shard_map/smooth_high/pallas_call | solution.py:787
  59.9 0.0 all-to-all-done.1.planar
  59.9 0.7 copy-done.1
  60.6 21.8 %layer.1 = (bf16[32,8,128,128]{3,2,1,0:T(8,128)(2,1)}, bf16[4,128,256]{2,1,0:T(8,128)(2,1)}, bf16[32,1,128,128]{3,2,1,0:T(8,128)(2,1)}, bf16[32,1,128,128]{3,2,1,0:T(8,128)(2,1)}) custom-call(f32[32]{0:T(128)} %bias.1, bf16[4,128,256]{2,1,0:T(8,128)(2,1)} %copy-done.1, bf16[4,16,256,256]{3,2,1,0:T(8,128)(2,1)} %smooth_high.1.smooth, ...), custom_call_target="tpu_custom_call" | custom-call | flops 10000000 | bytes 100000 | tf_op jit(solution)/shard_map/layer/pallas_call | solution.py:635
  82.4 5.1 %all-to-all-start.2 = ((bf16[4,128,256]{2,1,0:T(8,128)(2,1)}), bf16[4,128,256]{2,1,0:T(8,128)(2,1)S(1)}, u32[]{:S(2)}, u32[]{:S(2)}) async-start(bf16[4,128,256]{2,1,0:T(8,128)(2,1)} %get-tuple-element.44), calls=%async_computation.2 | async-start | bytes 524288 | tf_op jit(solution)/shard_map/all_to_all | solution.py:976
  87.5 4.0 %collective-permute-start.4 = (bf16[32,1,128,128]{3,2,1,0:T(8,128)(2,1)}, bf16[32,1,128,128]{3,2,1,0:T(8,128)(2,1)S(1)}, u32[]{:S(2)}, u32[]{:S(2)}) collective-permute-start(bf16[32,1,128,128]{3,2,1,0:T(8,128)(2,1)} %get-tuple-element.51), channel_id=1, source_target_pairs={{0,1},{1,2},{2,3},{4,5},{5,6},{6,7},{8,9},{9,10},{10,11},{12,13},{... | collective-permute-start | bytes 3145736 | tf_op jit(solution)/shard_map/ppermute | solution.py:972
  91.5 1.3 collective-permute-start.5
  92.8 2.2 %all-to-all-done.2.planar = bf16[4,128,256]{2,1,0:T(8,128)(2,1)S(1)} async-done(((bf16[4,128,256]{2,1,0:T(8,128)(2,1)}), bf16[4,128,256]{2,1,0:T(8,128)(2,1)S(1)}, u32[]{:S(2)}, u32[]{:S(2)}) %all-to-all-start.2) | async-done | bytes 262176 | tf_op jit(solution)/shard_map/all_to_all | solution.py:976
  95.0 0.7 copy-done.8
  95.7 6.4 %mix_back.1 = (bf16[4,128,256]{2,1,0:T(8,128)(2,1)}, bf16[4,1024,128]{2,1,0:T(8,128)(2,1)}) custom-call(bf16[4,128,256]{2,1,0:T(8,128)(2,1)} %copy-done.8, bf16[1024,2048]{1,0:T(8,128)(2,1)} %bitcast.17, bf16[512,256]{1,0:T(8,128)(2,1)} %constant.59.clone.z_in, bf16[256,512]{1,0:T(8,128)(2,1)} %constant.60.clone.z_out, ...), custom_call_target="tpu_custom_call" | custom-call | flops 99999997952 | bytes 100000000 | tf_op jit(solution)/shard_map/mix_back/pallas_call | solution.py:518
  102.2 3.5 %all-to-all-start.3 = ((bf16[4,1024,128]{2,1,0:T(8,128)(2,1)}), bf16[4,1024,128]{2,1,0:T(8,128)(2,1)S(1)}, u32[]{:S(2)}, u32[]{:S(2)}) async-start(bf16[4,1024,128]{2,1,0:T(8,128)(2,1)} %get-tuple-element.49), calls=%async_computation.3 | async-start | bytes 2097152 | tf_op jit(solution)/shard_map/all_to_all | solution.py:1006
  105.7 10.5 %near_inner.1.inner = bf16[32,4,128,128]{3,2,1,0:T(8,128)(2,1)} custom-call(f32[27,32]{1,0:T(8,128)} %taps.7, bf16[32,8,128,128]{3,2,1,0:T(8,128)(2,1)} %get-tuple-element.50.field), custom_call_target="tpu_custom_call" | custom-call | flops 10000000 | bytes 100000 | tf_op jit(solution)/shard_map/near_inner/pallas_call | solution.py:818
  116.2 0.0 collective-permute-done.4.before
  116.2 0.5 collective-permute-done.5.after
  116.7 3.4 %all-to-all-done.3.gathered = bf16[4,1024,128]{2,1,0:T(8,128)(2,1)S(1)} async-done(((bf16[4,1024,128]{2,1,0:T(8,128)(2,1)}), bf16[4,1024,128]{2,1,0:T(8,128)(2,1)S(1)}, u32[]{:S(2)}, u32[]{:S(2)}) %all-to-all-start.3) | async-done | bytes 1048608 | tf_op jit(solution)/shard_map/all_to_all | solution.py:1006
  120.1 4.0 %all-to-all-start.4 = ((bf16[4,128,256]{2,1,0:T(8,128)(2,1)}), bf16[4,128,256]{2,1,0:T(8,128)(2,1)S(1)}, u32[]{:S(2)}, u32[]{:S(2)}) async-start(bf16[4,128,256]{2,1,0:T(8,128)(2,1)} %get-tuple-element.56), calls=%async_computation.4 | async-start | bytes 524288 | tf_op jit(solution)/shard_map/all_to_all | solution.py:976
  124.2 0.7 pad_add_fusion.where
  124.8 0.0 copy-done
  124.8 6.2 %weight_gradient.1 = f32[1024,512]{1,0:T(8,128)} custom-call(s32[2]{0:T(128)} %pad_add_fusion.where, bf16[4,1024,128]{2,1,0:T(8,128)(2,1)} %copy-done, bf16[2,128,512]{2,1,0:T(8,128)(2,1)} %constant.69.clone.first, bf16[128,128]{1,0:T(8,128)(2,1)} %constant.67.clone.spread_table.second), custom_call_target="tpu_custom_call" | custom-call | flops 10000000 | bytes 100000 | tf_op jit(solution)/shard_map/weight_gradient/pallas_call | solution.py:949
  131.0 1.8 %all-to-all-done.4.planar = bf16[4,128,256]{2,1,0:T(8,128)(2,1)S(1)} async-done(((bf16[4,128,256]{2,1,0:T(8,128)(2,1)}), bf16[4,128,256]{2,1,0:T(8,128)(2,1)S(1)}, u32[]{:S(2)}, u32[]{:S(2)}) %all-to-all-start.4) | async-done | bytes 262176 | tf_op jit(solution)/shard_map/all_to_all | solution.py:976
  132.8 0.0 copy-done.9
  132.9 0.0 copy-done.10
  132.9 0.7 copy-done.6
  133.6 16.5 %finish.1 = bf16[32,8,128,128]{3,2,1,0:T(8,128)(2,1)} custom-call(f32[27,32]{1,0:T(8,128)} %taps.7, bf16[32,1,128,128]{3,2,1,0:T(8,128)(2,1)} %copy-done.9, bf16[32,8,128,128]{3,2,1,0:T(8,128)(2,1)} %get-tuple-element.50.field, bf16[32,1,128,128]{3,2,1,0:T(8,128)(2,1)} %copy-done.10, bf16[32,4,128,128]{3,2,1,0:T(8,128)(2,1)} %near_inner.1.inner, ...), custom_call_target="tpu_custom_call" | custom-call | flops 99999997952 | bytes 100000000 | tf_op jit(solution)/shard_map/finish/pallas_call | solution.py:881
  (11 shorter events, 0.0 us)
Async XLA Ops:
  3.6 20.6 %copy-start.12 = (bf16[16,1,128,128]{3,2,1,0:T(8,128)(2,1)S(1)}, bf16[16,1,128,128]{3,2,1,0:T(8,128)(2,1)}, u32[]{:S(2)}) copy-start(bf16[16,1,128,128]{3,2,1,0:T(8,128)(2,1)} %get-tuple-element.39) | copy-start | bytes 1572868
  3.6 24.1 %copy-start.11 = (bf16[16,1,128,128]{3,2,1,0:T(8,128)(2,1)S(1)}, bf16[16,1,128,128]{3,2,1,0:T(8,128)(2,1)}, u32[]{:S(2)}) copy-start(bf16[16,1,128,128]{3,2,1,0:T(8,128)(2,1)} %get-tuple-element.40) | copy-start | bytes 1572868
  3.6 19.0 %collective-permute-start = (bf16[16,1,128,128]{3,2,1,0:T(8,128)(2,1)}, bf16[16,1,128,128]{3,2,1,0:T(8,128)(2,1)S(1)}, u32[]{:S(2)}, u32[]{:S(2)}) collective-permute-start(bf16[16,1,128,128]{3,2,1,0:T(8,128)(2,1)} %get-tuple-element.31), channel_id=1, source_target_pairs={{0,1},{1,2},{2,3},{4,5},{5,6},{6,7},{8,9},{9,10},{10,11},{12,13},{... | collective-permute-start | bytes 1572872 | tf_op jit(solution)/shard_map/ppermute | solution.py:972
  8.7 15.5 %collective-permute-start.1 = (bf16[16,1,128,128]{3,2,1,0:T(8,128)(2,1)}, bf16[16,1,128,128]{3,2,1,0:T(8,128)(2,1)S(1)}, u32[]{:S(2)}, u32[]{:S(2)}) collective-permute-start(bf16[16,1,128,128]{3,2,1,0:T(8,128)(2,1)} %get-tuple-element.32), channel_id=1, source_target_pairs={{1,0},{2,1},{3,2},{5,4},{6,5},{7,6},{9,8},{10,9},{11,10},{13,12},{... | collective-permute-start | bytes 1572872 | tf_op jit(solution)/shard_map/ppermute | solution.py:972
  16.7 21.2 %all-to-all-start = ((bf16[4,128,256]{2,1,0:T(8,128)(2,1)}), bf16[4,128,256]{2,1,0:T(8,128)(2,1)S(1)}, u32[]{:S(2)}, u32[]{:S(2)}) async-start(bf16[4,128,256]{2,1,0:T(8,128)(2,1)} %forward_modes.1), calls=%async_computation | async-start | bytes 524288 | tf_op jit(solution)/shard_map/all_to_all | solution.py:976
  22.7 6.3 %copy-start.4 = (bf16[16,1,128,128]{3,2,1,0:T(8,128)(2,1)}, bf16[16,1,128,128]{3,2,1,0:T(8,128)(2,1)S(1)}, u32[]{:S(2)}) copy-start(bf16[16,1,128,128]{3,2,1,0:T(8,128)(2,1)S(1)} %collective-permute-done.before) | copy-start | bytes 1572868
  24.2 4.8 %copy-start.5 = (bf16[16,1,128,128]{3,2,1,0:T(8,128)(2,1)}, bf16[16,1,128,128]{3,2,1,0:T(8,128)(2,1)S(1)}, u32[]{:S(2)}) copy-start(bf16[16,1,128,128]{3,2,1,0:T(8,128)(2,1)S(1)} %collective-permute-done.1.after) | copy-start | bytes 1572868
  24.2 25.2 %collective-permute-start.2 = (bf16[16,1,128,128]{3,2,1,0:T(8,128)(2,1)S(1)}, bf16[16,1,128,128]{3,2,1,0:T(8,128)(2,1)S(1)}, u32[]{:S(2)}, u32[]{:S(2)}) collective-permute-start(bf16[16,1,128,128]{3,2,1,0:T(8,128)(2,1)S(1)} %copy-done.12), channel_id=1, source_target_pairs={{0,1},{1,2},{2,3},{4,5},{5,6},{6,7},{8,9},{9,10},{10,11},{12,13},{... | collective-permute-start | bytes 1572872 | tf_op jit(solution)/shard_map/ppermute | solution.py:972
  27.7 21.7 %collective-permute-start.3 = (bf16[16,1,128,128]{3,2,1,0:T(8,128)(2,1)S(1)}, bf16[16,1,128,128]{3,2,1,0:T(8,128)(2,1)S(1)}, u32[]{:S(2)}, u32[]{:S(2)}) collective-permute-start(bf16[16,1,128,128]{3,2,1,0:T(8,128)(2,1)S(1)} %copy-done.11), channel_id=1, source_target_pairs={{1,0},{2,1},{3,2},{5,4},{6,5},{7,6},{9,8},{10,9},{11,10},{13,12},{... | collective-permute-start | bytes 1572872 | tf_op jit(solution)/shard_map/ppermute | solution.py:972
  37.9 0.7 copy-start.7
  44.5 15.4 %all-to-all-start.1 = ((bf16[4,128,256]{2,1,0:T(8,128)(2,1)}), bf16[4,128,256]{2,1,0:T(8,128)(2,1)S(1)}, u32[]{:S(2)}, u32[]{:S(2)}) async-start(bf16[4,128,256]{2,1,0:T(8,128)(2,1)} %get-tuple-element.38), calls=%async_computation.1 | async-start | bytes 524288 | tf_op jit(solution)/shard_map/all_to_all | solution.py:976
  49.4 0.8 copy-start.2
  50.2 0.8 copy-start.3
  59.9 0.7 copy-start.1
  82.4 12.6 %all-to-all-start.2 = ((bf16[4,128,256]{2,1,0:T(8,128)(2,1)}), bf16[4,128,256]{2,1,0:T(8,128)(2,1)S(1)}, u32[]{:S(2)}, u32[]{:S(2)}) async-start(bf16[4,128,256]{2,1,0:T(8,128)(2,1)} %get-tuple-element.44), calls=%async_computation.2 | async-start | bytes 524288 | tf_op jit(solution)/shard_map/all_to_all | solution.py:976
  87.5 28.7 %collective-permute-start.4 = (bf16[32,1,128,128]{3,2,1,0:T(8,128)(2,1)}, bf16[32,1,128,128]{3,2,1,0:T(8,128)(2,1)S(1)}, u32[]{:S(2)}, u32[]{:S(2)}) collective-permute-start(bf16[32,1,128,128]{3,2,1,0:T(8,128)(2,1)} %get-tuple-element.51), channel_id=1, source_target_pairs={{0,1},{1,2},{2,3},{4,5},{5,6},{6,7},{8,9},{9,10},{10,11},{12,13},{... | collective-permute-start | bytes 3145736 | tf_op jit(solution)/shard_map/ppermute | solution.py:972
  91.5 25.2 %collective-permute-start.5 = (bf16[32,1,128,128]{3,2,1,0:T(8,128)(2,1)}, bf16[32,1,128,128]{3,2,1,0:T(8,128)(2,1)S(1)}, u32[]{:S(2)}, u32[]{:S(2)}) collective-permute-start(bf16[32,1,128,128]{3,2,1,0:T(8,128)(2,1)} %get-tuple-element.52), channel_id=1, source_target_pairs={{1,0},{2,1},{3,2},{5,4},{6,5},{7,6},{9,8},{10,9},{11,10},{13,12},{... | collective-permute-start | bytes 3145736 | tf_op jit(solution)/shard_map/ppermute | solution.py:972
  95.0 0.7 copy-start.8
  102.2 18.0 %all-to-all-start.3 = ((bf16[4,1024,128]{2,1,0:T(8,128)(2,1)}), bf16[4,1024,128]{2,1,0:T(8,128)(2,1)S(1)}, u32[]{:S(2)}, u32[]{:S(2)}) async-start(bf16[4,1024,128]{2,1,0:T(8,128)(2,1)} %get-tuple-element.49), calls=%async_computation.3 | async-start | bytes 2097152 | tf_op jit(solution)/shard_map/all_to_all | solution.py:1006
  116.2 16.6 %copy-start.9 = (bf16[32,1,128,128]{3,2,1,0:T(8,128)(2,1)}, bf16[32,1,128,128]{3,2,1,0:T(8,128)(2,1)S(1)}, u32[]{:S(2)}) copy-start(bf16[32,1,128,128]{3,2,1,0:T(8,128)(2,1)S(1)} %collective-permute-done.4.before) | copy-start | bytes 3145732
  116.7 16.1 %copy-start.10 = (bf16[32,1,128,128]{3,2,1,0:T(8,128)(2,1)}, bf16[32,1,128,128]{3,2,1,0:T(8,128)(2,1)S(1)}, u32[]{:S(2)}) copy-start(bf16[32,1,128,128]{3,2,1,0:T(8,128)(2,1)S(1)} %collective-permute-done.5.after) | copy-start | bytes 3145732
  120.1 4.7 %copy-start = (bf16[4,1024,128]{2,1,0:T(8,128)(2,1)}, bf16[4,1024,128]{2,1,0:T(8,128)(2,1)S(1)}, u32[]{:S(2)}) copy-start(bf16[4,1024,128]{2,1,0:T(8,128)(2,1)S(1)} %all-to-all-done.3.gathered) | copy-start | bytes 3145732
  120.1 12.7 %all-to-all-start.4 = ((bf16[4,128,256]{2,1,0:T(8,128)(2,1)}), bf16[4,128,256]{2,1,0:T(8,128)(2,1)S(1)}, u32[]{:S(2)}, u32[]{:S(2)}) async-start(bf16[4,128,256]{2,1,0:T(8,128)(2,1)} %get-tuple-element.56), calls=%async_computation.4 | async-start | bytes 524288 | tf_op jit(solution)/shard_map/all_to_all | solution.py:976
  132.9 0.7 copy-start.6

commit v11 on v10

--- a/solution.py
+++ b/solution.py
@@ -328,42 +328,41 @@
         out[s] = modes[s * lines : (s + 1) * lines].astype(jnp.bfloat16)
 
 
-def rims_kernel(low, high, *rims):
-    step = pl.program_id(0)
-    half = pl.num_programs(0) // 2
-    for k, source in enumerate((low, high)):
-
-        @pl.when(step < half)
-        def _():
-            rims[2 * k][...] = source[...]
-
-        @pl.when(step >= half)
-        def _():
-            rims[2 * k + 1][...] = source[...]
+def rims_kernel(field, *refs):
+    rims, held, got, put = refs[:4], refs[4], refs[5], refs[6]
+    half = field.shape[0] // 2
+    last = field.shape[1] - 1
+    loads, stores = [], []
+    for k in range(4):
+        source = field.at[pl.ds(half * (k % 2), half), pl.ds(last * (k // 2), 1)]
+        loads.append(pltpu.make_async_copy(source, held.at[k], got.at[k]))
+        stores.append(pltpu.make_async_copy(held.at[k], rims[k], put.at[k]))
+    for load in loads:
+        load.start()
+    for load, store in zip(loads, stores):
+        load.wait()
+        store.start()
+    for store in stores:
+        store.wait()
 
 
 def cut_rims(field):
-    channels, planes = field.shape[:2]
-    steps = 2
+    channels = field.shape[0]
     rim = jax.ShapeDtypeStruct((channels // 2, 1, NX, NY), jnp.bfloat16)
-    block = (channels // steps, 1, NX, NY)
-    outs = [
-        pl.BlockSpec(block, lambda c: (jnp.minimum(c, steps // 2 - 1), 0, 0, 0)),
-        pl.BlockSpec(block, lambda c: (jnp.maximum(c - steps // 2, 0), 0, 0, 0)),
-    ]
     return pl.pallas_call(
         rims_kernel,
-        grid=(steps,),
-        in_specs=[
-            pl.BlockSpec(block, lambda c: (c, 0, 0, 0)),
-            pl.BlockSpec(block, lambda c: (c, planes - 1, 0, 0)),
+        in_specs=[pl.BlockSpec(memory_space=pl.ANY)],
+        out_specs=[pl.BlockSpec(memory_space=pl.ANY)] * 4,
+        out_shape=[rim] * 4,
+        scratch_shapes=[
+            pltpu.VMEM((4,) + rim.shape, jnp.bfloat16),
+            pltpu.SemaphoreType.DMA((4,)),
+            pltpu.SemaphoreType.DMA((4,)),
         ],
-        out_specs=outs + outs,
-        out_shape=[rim] * 4,
         compiler_params=params(),
         cost_estimate=LIGHT,
         name="rims",
-    )(field, field)
+    )(field)
 
 
 def forward_kernel(field, x_table, y_table, out, rows):
@@ -430,10 +429,15 @@
             spectrum[2 * h * quarter : 2 * (h + 1) * quarter] = here
             if adjoint:
                 for d in range(send.shape[0]):
-                    send[d, 2 * (h + 2) * quarter : 2 * (h + 3) * quarter] = here
+                    send[d, 2 * (h + 1) * quarter : 2 * (h + 2) * quarter] = here
         if adjoint:
+            rows = [partner[2 * h * quarter : 2 * (h + 1) * quarter] for h in range(2)]
+            rows = [row.astype(jnp.float32) for row in rows]
+            left = lax.broadcasted_iota(jnp.int32, (1, lines), 1) < lines // 2
+            turned = [pltpu.roll(row, lines // 2, axis=1) for row in rows]
+            packed = [jnp.where(left, rows[0], turned[1]), jnp.where(left, turned[0], rows[1])]
             for d in range(send.shape[0]):
-                send[d, : 4 * quarter] = partner[...]
+                send[d, : 2 * quarter] = packed[d % 2].astype(jnp.bfloat16)
         total[...] = jnp.zeros_like(total)
 
     lane = lax.broadcasted_iota(jnp.int32, (1, lines), 1) % (depth * steps)
@@ -512,7 +516,7 @@
         in_specs.append(whole(shape))
         operands.append(partner)
         scratch = [pltpu.VMEM(shape, jnp.bfloat16)] + scratch
-        outs = [planar.shape, (copies, 2 * shape[0], lines)]
+        outs = [planar.shape, (copies, 3 * rows, lines)]
     else:
         outs = [shape, planar.shape]
     return pl.pallas_call(
@@ -775,7 +779,7 @@
     channels, planes = field.shape[:2]
     pairs = planes // 2
     start = 0 if done is None else channels // 2
-    step = 8
+    step = 4
     skip = start // step
     rim = pl.BlockSpec((step, 1, NX, NY), lambda c: (c, 0, 0, 0))
     sheets = pl.BlockSpec((step, planes, NX, NY), lambda c: (c + skip, 0, 0, 0))
@@ -904,65 +908,64 @@
     )(taps, rims[0], spread, rims[1], inner, planar, ix_table, iy_table)
 
 
-def gradient_kernel(depth, where, gathered, first, second, out):
+def gradient_kernel(gathered, first, second, out):
     step = pl.program_id(0)
     samples, rows, lines = gathered.shape
-    quarter = rows // 8
+    quarter = rows // 6
+    depth = out.shape[0] // (2 * quarter)
+    real_part = lax.axis_index("dp") < lax.axis_size("dp") // 2
     lane = lax.broadcasted_iota(jnp.int32, (1, lines), 1)
-    mine = lane % depth == step
-    spectra = [gathered[s, : 4 * quarter] for s in range(samples)]
     duals = []
     for s in range(samples):
         for h in range(2):
-            at = (2 * h + 4) * quarter
+            at = (2 * h + 2) * quarter
             real = gathered[s, at : at + quarter]
             imag = gathered[s, at + quarter : at + 2 * quarter]
-            duals.append(jnp.where(where[0] == 0, real, imag))
-            duals.append(jnp.where(where[0] == 0, imag, -real))
-    spectra = jnp.where(mine, jnp.concatenate(spectra, axis=0), 0)
-    duals = jnp.where(mine, jnp.concatenate(duals, axis=0), 0)
-    wide = dot(duals, second[...])
-    for column in range(0, out.shape[1], 256):
-        product = dot(spectra, first[0, :, column : column + 256])
-        for at in range(0, 256, 128):
+            duals.append(jnp.where(real_part, real, imag))
+            duals.append(jnp.where(real_part, imag, -real))
+    duals = jnp.concatenate(duals, axis=0)
+    for j in range(depth):
+        mine = lane % (depth * pl.num_programs(0)) == depth * step + j
+        spectra = []
+        for s in range(samples):
             for h in range(2):
-                total = 0.0
-                for s in range(samples):
-                    for part in range(2):
-                        row = (4 * s + 2 * h + part) * quarter
-                        here = slice(row, row + quarter)
-                        total = total + product[here, at : at + 128] * wide[here]
-                there = slice(column + at, column + at + 128)
-                out[h * quarter : (h + 1) * quarter, there] = total * (1.0 / samples)
-
-
-def weight_gradient(gathered, depth, width, index):
+                here = mine & (lane // (lines // 2) == h)
+                spectra.append(jnp.where(here, gathered[s, : 2 * quarter], 0))
+        spectra = jnp.concatenate(spectra, axis=0)
+        wide = dot(jnp.where(mine, duals, 0), second[...])
+        for column in range(0, out.shape[1], 256):
+            product = dot(spectra, first[:, column : column + 256])
+            for at in range(0, 256, 128):
+                for h in range(2):
+                    total = 0.0
+                    for s in range(samples):
+                        for part in range(2):
+                            row = (4 * s + 2 * h + part) * quarter
+                            here = slice(row, row + quarter)
+                            total = total + product[here, at : at + 128] * wide[here]
+                    row = (2 * j + h) * quarter
+                    there = slice(column + at, column + at + 128)
+                    out[row : row + quarter, there] = total * (1.0 / samples)
+
+
+def weight_gradient(gathered, depth, width):
     samples, rows, lines = gathered.shape
     channels = lines // depth
-    square = channels * channels
-    cuts = square // width
-    first = first_table(channels, depth).reshape(lines, cuts, width).transpose(1, 0, 2)
-    first = constant(first)
+    first = np.repeat(np.eye(channels // 2), channels, axis=1)
+    first = constant(np.tile(np.repeat(first, depth, axis=0), (2, 1)))
     second = constant(second_table(channels, depth)[:, :128])
-    where = jnp.stack([index // cuts, index % cuts]).astype(jnp.int32)
-    half = rows // 4
+    steps = 2
+    half = rows // 3
     return pl.pallas_call(
-        functools.partial(gradient_kernel, depth),
-        grid_spec=pltpu.PrefetchScalarGridSpec(
-            num_scalar_prefetch=1,
-            grid=(depth,),
-            in_specs=[
-                pl.BlockSpec(gathered.shape, lambda j, w: (0, 0, 0)),
-                pl.BlockSpec((1, lines, width), lambda j, w: (w[1], 0, 0)),
-                pl.BlockSpec(second.shape, lambda j, w: (0, 0)),
-            ],
-            out_specs=pl.BlockSpec((half, width), lambda j, w: (j, 0)),
-        ),
+        gradient_kernel,
+        grid=(steps,),
+        in_specs=[whole(gathered.shape), whole(first.shape), whole(second.shape)],
+        out_specs=pl.BlockSpec((depth // steps * half, width), lambda j: (j, 0)),
         out_shape=jax.ShapeDtypeStruct((depth * half, width), jnp.float32),
         compiler_params=params(),
         cost_estimate=LIGHT,
         name="weight_gradient",
-    )(where, gathered, first, second)
+    )(gathered, first, second)
 
 
 def exchange(first, last):
@@ -1006,7 +1009,7 @@
     gathered = lax.all_to_all(send, "dp", split_axis=0, concat_axis=0)
     planar, gathered, inner, rims = barrier((planar, gathered, inner, rims))
     planar = swap(planar)
-    grad_spec = weight_gradient(gathered, KX // slabs, width, lax.axis_index("dp"))
+    grad_spec = weight_gradient(gathered, KX // slabs, width)
     planar, grad_spec = barrier((planar, grad_spec))
     grad_feats = finish(planar, spread, rims, inner, taps)[None]
     return (grad_feats, grad_spec.reshape(mode_rows, KZ, width))
@@ -1020,8 +1023,7 @@
         and samples == 1
         and channels == 32
         and planes == 8
-        and channels * channels % width == 0
-        and width % 128 == 0
+        and channels * channels == 2 * width
     )
     form = local_fast if fits else local_any
     return form(feats, grains, spec_weight, taps, point_weight, bias, cotangent)

time: 151 us -> 147 us (0.974)
  Pallas kernels: 94.8 us -> 92.5 us
    all_to_all x1, waiting for transfers between devices: 3.41 us -> 1.08 us  [local_fast(): gathered = lax.all_to_all(send, 'dp', split_axis=0, concat_axis=0)]
  transfers between devices with their start and end apart: 11 -> 11, of which waited for: 5 -> 4; matrix products, arithmetic and copies ran while one was open for 0% -> 0% of each run, Pallas kernels for 36% -> 35%
where the time goes in v11:
time: 147 us; the launch traced here: 146 us
  Pallas kernels  92.5 us (63%)
  starting transfers between devices  40 us (27%)
  waiting for transfers between devices  8.14 us (6%)
  local copies, waits for them, and re-layouts  4.46 us (3%)
    pallas_call x1, Pallas kernels, layer(): pl.pallas_call(layer_kernel, grid=(pairs,), in_specs=[pl.BlockSpec(memory...  21.8 us
    all_to_all x4, starting transfers between devices, swap(): return lax.all_to_all(planar, 'slab', split_axis=0, concat_axis=0)  19.9 us
    pallas_call x2, Pallas kernels, smooth_planes(): pl.pallas_call(functools.partial(smooth_kernel, start), grid=(channels //...  17.1 us
    ppermute x6, starting transfers between devices, exchange(): return (lax.ppermute(last, 'slab', up), lax.ppermute(first, 'slab', down))  16.6 us
    pallas_call x1, Pallas kernels, finish(): pl.pallas_call(finish_kernel, grid=(channels // step,), in_specs=[pl.Bloc...  16.5 us
    pallas_call x2, Pallas kernels, mix(): pl.pallas_call(functools.partial(mixing_kernel, scale_in, scale_out, adjo...  12.2 us
    pallas_call x1, Pallas kernels, near_inner(): pl.pallas_call(inner_kernel, grid=(channels // step,), in_specs=[pl.Block...  10.5 us
    pallas_call x1, Pallas kernels, forward_modes(): pl.pallas_call(forward_kernel, grid=(planes // 2,), in_specs=[pl.BlockSpe...  6.7 us
  transfers between devices with their start and end apart: 11, of which 4 were waited for; matrix products, arithmetic and copies ran while one was open for 0% of the time, Pallas kernels for 35%

profile of v11, /device:TPU:0, one launch (start us, length us, event | category | flops | bytes accessed | tf_op | source)
XLA Modules:
  0.0 145.9 jit_solution(4867618077768589036)
XLA Ops:
  0.6 2.4 %rims.1 = (bf16[16,1,128,128]{3,2,1,0:T(8,128)(2,1)}, bf16[16,1,128,128]{3,2,1,0:T(8,128)(2,1)}, bf16[16,1,128,128]{3,2,1,0:T(8,128)(2,1)}, bf16[16,1,128,128]{3,2,1,0:T(8,128)(2,1)}) custom-call(bf16[32,8,128,128]{3,2,1,0:T(8,128)(2,1)} %bitcast.6), custom_call_target="tpu_custom_call" | custom-call | flops 10000000 | bytes 100000 | tf_op jit(solution)/shard_map/rims/pallas_call | solution.py:352
  3.1 0.0 copy-start.12
  3.1 0.0 copy-start.11
  3.1 5.1 %collective-permute-start = (bf16[16,1,128,128]{3,2,1,0:T(8,128)(2,1)}, bf16[16,1,128,128]{3,2,1,0:T(8,128)(2,1)S(1)}, u32[]{:S(2)}, u32[]{:S(2)}) collective-permute-start(bf16[16,1,128,128]{3,2,1,0:T(8,128)(2,1)} %get-tuple-element.31), channel_id=1, source_target_pairs={{0,1},{1,2},{2,3},{4,5},{5,6},{6,7},{8,9},{9,10},{10,11},{12,13},{... | collective-permute-start | bytes 1572872 | tf_op jit(solution)/shard_map/ppermute | solution.py:975
  8.2 1.3 collective-permute-start.1
  9.5 6.7 %forward_modes.1 = bf16[4,128,256]{2,1,0:T(8,128)(2,1)} custom-call(bf16[32,8,128,128]{3,2,1,0:T(8,128)(2,1)} %bitcast.7, bf16[64,256]{1,0:T(8,128)(2,1)} %constant.28.clone.x_table, bf16[2048,256]{1,0:T(8,128)(2,1)} %constant.29.clone.y_table), custom_call_target="tpu_custom_call" | custom-call | flops 10000000 | bytes 100000 | tf_op jit(solution)/shard_map/forward_modes/pallas_call | solution.py:389
  16.2 5.9 %all-to-all-start = ((bf16[4,128,256]{2,1,0:T(8,128)(2,1)}), bf16[4,128,256]{2,1,0:T(8,128)(2,1)S(1)}, u32[]{:S(2)}, u32[]{:S(2)}) async-start(bf16[4,128,256]{2,1,0:T(8,128)(2,1)} %forward_modes.1), calls=%async_computation | async-start | bytes 524288 | tf_op jit(solution)/shard_map/all_to_all | solution.py:979
  22.1 0.0 collective-permute-done.before
  22.1 1.5 %collective-permute-done.1.after = bf16[16,1,128,128]{3,2,1,0:T(8,128)(2,1)S(1)} collective-permute-done((bf16[16,1,128,128]{3,2,1,0:T(8,128)(2,1)}, bf16[16,1,128,128]{3,2,1,0:T(8,128)(2,1)S(1)}, u32[]{:S(2)}, u32[]{:S(2)}) %collective-permute-start.1) | collective-permute-done | bytes 524320 | tf_op jit(solution)/shard_map/ppermute | solution.py:975
  23.7 0.0 copy-done.12
  23.7 3.5 %collective-permute-start.2 = (bf16[16,1,128,128]{3,2,1,0:T(8,128)(2,1)S(1)}, bf16[16,1,128,128]{3,2,1,0:T(8,128)(2,1)S(1)}, u32[]{:S(2)}, u32[]{:S(2)}) collective-permute-start(bf16[16,1,128,128]{3,2,1,0:T(8,128)(2,1)S(1)} %copy-done.12), channel_id=1, source_target_pairs={{0,1},{1,2},{2,3},{4,5},{5,6},{6,7},{8,9},{9,10},{10,11},{12,13},{... | collective-permute-start | bytes 1572872 | tf_op jit(solution)/shard_map/ppermute | solution.py:975
  27.2 0.0 copy-done.11
  27.2 1.3 collective-permute-start.3
  28.5 0.0 copy-done.4
  28.5 0.0 copy-done.5
  28.5 8.5 %smooth_low.1.rest_0_ = bf16[4,16,256,256]{3,2,1,0:T(8,128)(2,1)} custom-call(f32[27,32]{1,0:T(8,128)} %taps.7, bf16[16,1,128,128]{3,2,1,0:T(8,128)(2,1)} %copy-done.4, bf16[32,8,128,128]{3,2,1,0:T(8,128)(2,1)} %bitcast.8, bf16[16,1,128,128]{3,2,1,0:T(8,128)(2,1)} %copy-done.5), custom_call_target="tpu_custom_call" | custom-call | flops 10000000 | bytes 100000 | tf_op jit(solution)/shard_map/smooth_low/pallas_call | solution.py:791
  37.0 0.0 all-to-all-done.planar
  37.0 0.7 copy-done.6
  37.7 5.9 %mix.1 = (bf16[512,128]{1,0:T(8,128)(2,1)}, bf16[4,128,256]{2,1,0:T(8,128)(2,1)}) custom-call(bf16[4,128,256]{2,1,0:T(8,128)(2,1)} %copy-done.6, bf16[1024,2048]{1,0:T(8,128)(2,1)} %bitcast.13, bf16[512,256]{1,0:T(8,128)(2,1)} %constant.30.clone.z_in, bf16[256,512]{1,0:T(8,128)(2,1)} %constant.31.clone.z_out, bf16[128,1024]{1,0:T(8,128)(2,1)} %constant.32.clone.spread_table, ...), custom_call_target="tpu_custom_call" | custom-call | flops 99999997952 | bytes 100000000 | tf_op jit(solution)/shard_map/mix/pallas_call | solution.py:522
  43.6 4.9 %all-to-all-start.1 = ((bf16[4,128,256]{2,1,0:T(8,128)(2,1)}), bf16[4,128,256]{2,1,0:T(8,128)(2,1)S(1)}, u32[]{:S(2)}, u32[]{:S(2)}) async-start(bf16[4,128,256]{2,1,0:T(8,128)(2,1)} %get-tuple-element.38), calls=%async_computation.1 | async-start | bytes 524288 | tf_op jit(solution)/shard_map/all_to_all | solution.py:979
  48.5 0.0 collective-permute-done.2.before
  48.5 0.0 collective-permute-done.3.after
  48.5 0.8 copy-done.2
  49.3 0.8 copy-done.3
  50.1 8.5 %smooth_high.1.smooth = bf16[4,16,256,256]{3,2,1,0:T(8,128)(2,1)} custom-call(f32[27,32]{1,0:T(8,128)} %taps.7, bf16[16,1,128,128]{3,2,1,0:T(8,128)(2,1)} %copy-done.2, bf16[32,8,128,128]{3,2,1,0:T(8,128)(2,1)} %bitcast.9, bf16[16,1,128,128]{3,2,1,0:T(8,128)(2,1)} %copy-done.3, ...), custom_call_target="tpu_custom_call", output_to_operand_aliasing={{}: (4, {})} | custom-call | flops 10000000 | bytes 100000 | tf_op jit(solution)/shard_map/smooth_high/pallas_call | solution.py:791
  58.7 0.0 all-to-all-done.1.planar
  58.7 0.7 copy-done.1
  59.4 21.8 %layer.1 = (bf16[32,8,128,128]{3,2,1,0:T(8,128)(2,1)}, bf16[4,128,256]{2,1,0:T(8,128)(2,1)}, bf16[32,1,128,128]{3,2,1,0:T(8,128)(2,1)}, bf16[32,1,128,128]{3,2,1,0:T(8,128)(2,1)}) custom-call(f32[32]{0:T(128)} %bias.1, bf16[4,128,256]{2,1,0:T(8,128)(2,1)} %copy-done.1, bf16[4,16,256,256]{3,2,1,0:T(8,128)(2,1)} %smooth_high.1.smooth, ...), custom_call_target="tpu_custom_call" | custom-call | flops 10000000 | bytes 100000 | tf_op jit(solution)/shard_map/layer/pallas_call | solution.py:639
  81.2 5.1 %all-to-all-start.2 = ((bf16[4,128,256]{2,1,0:T(8,128)(2,1)}), bf16[4,128,256]{2,1,0:T(8,128)(2,1)S(1)}, u32[]{:S(2)}, u32[]{:S(2)}) async-start(bf16[4,128,256]{2,1,0:T(8,128)(2,1)} %get-tuple-element.44), calls=%async_computation.2 | async-start | bytes 524288 | tf_op jit(solution)/shard_map/all_to_all | solution.py:979
  86.3 4.0 %collective-permute-start.4 = (bf16[32,1,128,128]{3,2,1,0:T(8,128)(2,1)}, bf16[32,1,128,128]{3,2,1,0:T(8,128)(2,1)S(1)}, u32[]{:S(2)}, u32[]{:S(2)}) collective-permute-start(bf16[32,1,128,128]{3,2,1,0:T(8,128)(2,1)} %get-tuple-element.51), channel_id=1, source_target_pairs={{0,1},{1,2},{2,3},{4,5},{5,6},{6,7},{8,9},{9,10},{10,11},{12,13},{... | collective-permute-start | bytes 3145736 | tf_op jit(solution)/shard_map/ppermute | solution.py:975
  90.3 1.5 %collective-permute-start.5 = (bf16[32,1,128,128]{3,2,1,0:T(8,128)(2,1)}, bf16[32,1,128,128]{3,2,1,0:T(8,128)(2,1)S(1)}, u32[]{:S(2)}, u32[]{:S(2)}) collective-permute-start(bf16[32,1,128,128]{3,2,1,0:T(8,128)(2,1)} %get-tuple-element.52), channel_id=1, source_target_pairs={{1,0},{2,1},{3,2},{5,4},{6,5},{7,6},{9,8},{10,9},{11,10},{13,12},{... | collective-permute-start | bytes 3145736 | tf_op jit(solution)/shard_map/ppermute | solution.py:975
  91.7 2.1 %all-to-all-done.2.planar = bf16[4,128,256]{2,1,0:T(8,128)(2,1)S(1)} async-done(((bf16[4,128,256]{2,1,0:T(8,128)(2,1)}), bf16[4,128,256]{2,1,0:T(8,128)(2,1)S(1)}, u32[]{:S(2)}, u32[]{:S(2)}) %all-to-all-start.2) | async-done | bytes 262176 | tf_op jit(solution)/shard_map/all_to_all | solution.py:979
  93.8 0.7 copy-done.7
  94.5 6.3 %mix_back.1 = (bf16[4,128,256]{2,1,0:T(8,128)(2,1)}, bf16[4,768,128]{2,1,0:T(8,128)(2,1)}) custom-call(bf16[4,128,256]{2,1,0:T(8,128)(2,1)} %copy-done.7, bf16[1024,2048]{1,0:T(8,128)(2,1)} %bitcast.14, bf16[512,256]{1,0:T(8,128)(2,1)} %constant.30.clone.z_in, bf16[256,512]{1,0:T(8,128)(2,1)} %constant.31.clone.z_out, ...), custom_call_target="tpu_custom_call" | custom-call | flops 99999997952 | bytes 100000000 | tf_op jit(solution)/shard_map/mix_back/pallas_call | solution.py:522
  100.8 3.5 %all-to-all-start.3 = ((bf16[4,768,128]{2,1,0:T(8,128)(2,1)}), bf16[4,768,128]{2,1,0:T(8,128)(2,1)S(1)}, u32[]{:S(2)}, u32[]{:S(2)}) async-start(bf16[4,768,128]{2,1,0:T(8,128)(2,1)} %get-tuple-element.49), calls=%async_computation.3 | async-start | bytes 1572864 | tf_op jit(solution)/shard_map/all_to_all | solution.py:1009
  104.3 10.5 %near_inner.1.inner = bf16[32,4,128,128]{3,2,1,0:T(8,128)(2,1)} custom-call(f32[27,32]{1,0:T(8,128)} %taps.7, bf16[32,8,128,128]{3,2,1,0:T(8,128)(2,1)} %get-tuple-element.50.field), custom_call_target="tpu_custom_call" | custom-call | flops 10000000 | bytes 100000 | tf_op jit(solution)/shard_map/near_inner/pallas_call | solution.py:822
  114.9 1.1 all-to-all-done.3.gathered
  116.0 0.0 collective-permute-done.4.before
  116.0 0.0 collective-permute-done.5.after
  116.0 0.0 copy-start.10
  116.0 4.0 %all-to-all-start.4 = ((bf16[4,128,256]{2,1,0:T(8,128)(2,1)}), bf16[4,128,256]{2,1,0:T(8,128)(2,1)S(1)}, u32[]{:S(2)}, u32[]{:S(2)}) async-start(bf16[4,128,256]{2,1,0:T(8,128)(2,1)} %get-tuple-element.56), calls=%async_computation.4 | async-start | bytes 524288 | tf_op jit(solution)/shard_map/all_to_all | solution.py:979
  120.0 0.0 copy-done
  120.0 5.2 %weight_gradient.1 = f32[1024,512]{1,0:T(8,128)} custom-call(bf16[4,768,128]{2,1,0:T(8,128)(2,1)} %copy-done, bf16[128,512]{1,0:T(8,128)(2,1)} %constant.40.clone.first, bf16[128,128]{1,0:T(8,128)(2,1)} %constant.38.clone.spread_table.second), custom_call_target="tpu_custom_call" | custom-call | flops 10000000 | bytes 100000 | tf_op jit(solution)/shard_map/weight_gradient/pallas_call | solution.py:959
  125.3 3.4 %all-to-all-done.4.planar = bf16[4,128,256]{2,1,0:T(8,128)(2,1)S(1)} async-done(((bf16[4,128,256]{2,1,0:T(8,128)(2,1)}), bf16[4,128,256]{2,1,0:T(8,128)(2,1)S(1)}, u32[]{:S(2)}, u32[]{:S(2)}) %all-to-all-start.4) | async-done | bytes 262176 | tf_op jit(solution)/shard_map/all_to_all | solution.py:979
  128.7 0.0 copy-done.9
  128.7 0.0 copy-done.10
  128.7 0.7 copy-done.8
  129.4 16.5 %finish.1 = bf16[32,8,128,128]{3,2,1,0:T(8,128)(2,1)} custom-call(f32[27,32]{1,0:T(8,128)} %taps.7, bf16[32,1,128,128]{3,2,1,0:T(8,128)(2,1)} %copy-done.9, bf16[32,8,128,128]{3,2,1,0:T(8,128)(2,1)} %get-tuple-element.50.field, bf16[32,1,128,128]{3,2,1,0:T(8,128)(2,1)} %copy-done.10, bf16[32,4,128,128]{3,2,1,0:T(8,128)(2,1)} %near_inner.1.inner, ...), custom_call_target="tpu_custom_call" | custom-call | flops 99999997952 | bytes 100000000 | tf_op jit(solution)/shard_map/finish/pallas_call | solution.py:885
  (10 shorter events, 0.0 us)
Async XLA Ops:
  3.1 20.6 %copy-start.12 = (bf16[16,1,128,128]{3,2,1,0:T(8,128)(2,1)S(1)}, bf16[16,1,128,128]{3,2,1,0:T(8,128)(2,1)}, u32[]{:S(2)}) copy-start(bf16[16,1,128,128]{3,2,1,0:T(8,128)(2,1)} %get-tuple-element.39) | copy-start | bytes 1572868
  3.1 24.1 %copy-start.11 = (bf16[16,1,128,128]{3,2,1,0:T(8,128)(2,1)S(1)}, bf16[16,1,128,128]{3,2,1,0:T(8,128)(2,1)}, u32[]{:S(2)}) copy-start(bf16[16,1,128,128]{3,2,1,0:T(8,128)(2,1)} %get-tuple-element.40) | copy-start | bytes 1572868
  3.1 19.0 %collective-permute-start = (bf16[16,1,128,128]{3,2,1,0:T(8,128)(2,1)}, bf16[16,1,128,128]{3,2,1,0:T(8,128)(2,1)S(1)}, u32[]{:S(2)}, u32[]{:S(2)}) collective-permute-start(bf16[16,1,128,128]{3,2,1,0:T(8,128)(2,1)} %get-tuple-element.31), channel_id=1, source_target_pairs={{0,1},{1,2},{2,3},{4,5},{5,6},{6,7},{8,9},{9,10},{10,11},{12,13},{... | collective-permute-start | bytes 1572872 | tf_op jit(solution)/shard_map/ppermute | solution.py:975
  8.2 15.5 %collective-permute-start.1 = (bf16[16,1,128,128]{3,2,1,0:T(8,128)(2,1)}, bf16[16,1,128,128]{3,2,1,0:T(8,128)(2,1)S(1)}, u32[]{:S(2)}, u32[]{:S(2)}) collective-permute-start(bf16[16,1,128,128]{3,2,1,0:T(8,128)(2,1)} %get-tuple-element.32), channel_id=1, source_target_pairs={{1,0},{2,1},{3,2},{5,4},{6,5},{7,6},{9,8},{10,9},{11,10},{13,12},{... | collective-permute-start | bytes 1572872 | tf_op jit(solution)/shard_map/ppermute | solution.py:975
  16.2 20.8 %all-to-all-start = ((bf16[4,128,256]{2,1,0:T(8,128)(2,1)}), bf16[4,128,256]{2,1,0:T(8,128)(2,1)S(1)}, u32[]{:S(2)}, u32[]{:S(2)}) async-start(bf16[4,128,256]{2,1,0:T(8,128)(2,1)} %forward_modes.1), calls=%async_computation | async-start | bytes 524288 | tf_op jit(solution)/shard_map/all_to_all | solution.py:979
  22.1 6.3 %copy-start.4 = (bf16[16,1,128,128]{3,2,1,0:T(8,128)(2,1)}, bf16[16,1,128,128]{3,2,1,0:T(8,128)(2,1)S(1)}, u32[]{:S(2)}) copy-start(bf16[16,1,128,128]{3,2,1,0:T(8,128)(2,1)S(1)} %collective-permute-done.before) | copy-start | bytes 1572868
  23.7 4.8 %copy-start.5 = (bf16[16,1,128,128]{3,2,1,0:T(8,128)(2,1)}, bf16[16,1,128,128]{3,2,1,0:T(8,128)(2,1)S(1)}, u32[]{:S(2)}) copy-start(bf16[16,1,128,128]{3,2,1,0:T(8,128)(2,1)S(1)} %collective-permute-done.1.after) | copy-start | bytes 1572868
  23.7 24.8 %collective-permute-start.2 = (bf16[16,1,128,128]{3,2,1,0:T(8,128)(2,1)S(1)}, bf16[16,1,128,128]{3,2,1,0:T(8,128)(2,1)S(1)}, u32[]{:S(2)}, u32[]{:S(2)}) collective-permute-start(bf16[16,1,128,128]{3,2,1,0:T(8,128)(2,1)S(1)} %copy-done.12), channel_id=1, source_target_pairs={{0,1},{1,2},{2,3},{4,5},{5,6},{6,7},{8,9},{9,10},{10,11},{12,13},{... | collective-permute-start | bytes 1572872 | tf_op jit(solution)/shard_map/ppermute | solution.py:975
  27.2 21.4 %collective-permute-start.3 = (bf16[16,1,128,128]{3,2,1,0:T(8,128)(2,1)S(1)}, bf16[16,1,128,128]{3,2,1,0:T(8,128)(2,1)S(1)}, u32[]{:S(2)}, u32[]{:S(2)}) collective-permute-start(bf16[16,1,128,128]{3,2,1,0:T(8,128)(2,1)S(1)} %copy-done.11), channel_id=1, source_target_pairs={{1,0},{2,1},{3,2},{5,4},{6,5},{7,6},{9,8},{10,9},{11,10},{13,12},{... | collective-permute-start | bytes 1572872 | tf_op jit(solution)/shard_map/ppermute | solution.py:975
  37.0 0.7 copy-start.6
  43.6 15.0 %all-to-all-start.1 = ((bf16[4,128,256]{2,1,0:T(8,128)(2,1)}), bf16[4,128,256]{2,1,0:T(8,128)(2,1)S(1)}, u32[]{:S(2)}, u32[]{:S(2)}) async-start(bf16[4,128,256]{2,1,0:T(8,128)(2,1)} %get-tuple-element.38), calls=%async_computation.1 | async-start | bytes 524288 | tf_op jit(solution)/shard_map/all_to_all | solution.py:979
  48.5 0.8 copy-start.2
  49.3 0.8 copy-start.3
  58.7 0.7 copy-start.1
  81.2 12.6 %all-to-all-start.2 = ((bf16[4,128,256]{2,1,0:T(8,128)(2,1)}), bf16[4,128,256]{2,1,0:T(8,128)(2,1)S(1)}, u32[]{:S(2)}, u32[]{:S(2)}) async-start(bf16[4,128,256]{2,1,0:T(8,128)(2,1)} %get-tuple-element.44), calls=%async_computation.2 | async-start | bytes 524288 | tf_op jit(solution)/shard_map/all_to_all | solution.py:979
  86.3 29.7 %collective-permute-start.4 = (bf16[32,1,128,128]{3,2,1,0:T(8,128)(2,1)}, bf16[32,1,128,128]{3,2,1,0:T(8,128)(2,1)S(1)}, u32[]{:S(2)}, u32[]{:S(2)}) collective-permute-start(bf16[32,1,128,128]{3,2,1,0:T(8,128)(2,1)} %get-tuple-element.51), channel_id=1, source_target_pairs={{0,1},{1,2},{2,3},{4,5},{5,6},{6,7},{8,9},{9,10},{10,11},{12,13},{... | collective-permute-start | bytes 3145736 | tf_op jit(solution)/shard_map/ppermute | solution.py:975
  90.3 25.7 %collective-permute-start.5 = (bf16[32,1,128,128]{3,2,1,0:T(8,128)(2,1)}, bf16[32,1,128,128]{3,2,1,0:T(8,128)(2,1)S(1)}, u32[]{:S(2)}, u32[]{:S(2)}) collective-permute-start(bf16[32,1,128,128]{3,2,1,0:T(8,128)(2,1)} %get-tuple-element.52), channel_id=1, source_target_pairs={{1,0},{2,1},{3,2},{5,4},{6,5},{7,6},{9,8},{10,9},{11,10},{13,12},{... | collective-permute-start | bytes 3145736 | tf_op jit(solution)/shard_map/ppermute | solution.py:975
  93.8 0.7 copy-start.7
  100.8 15.1 %all-to-all-start.3 = ((bf16[4,768,128]{2,1,0:T(8,128)(2,1)}), bf16[4,768,128]{2,1,0:T(8,128)(2,1)S(1)}, u32[]{:S(2)}, u32[]{:S(2)}) async-start(bf16[4,768,128]{2,1,0:T(8,128)(2,1)} %get-tuple-element.49), calls=%async_computation.3 | async-start | bytes 1572864 | tf_op jit(solution)/shard_map/all_to_all | solution.py:1009
  116.0 4.1 %copy-start = (bf16[4,768,128]{2,1,0:T(8,128)(2,1)}, bf16[4,768,128]{2,1,0:T(8,128)(2,1)S(1)}, u32[]{:S(2)}) copy-start(bf16[4,768,128]{2,1,0:T(8,128)(2,1)S(1)} %all-to-all-done.3.gathered) | copy-start | bytes 2359300
  116.0 12.7 %copy-start.9 = (bf16[32,1,128,128]{3,2,1,0:T(8,128)(2,1)}, bf16[32,1,128,128]{3,2,1,0:T(8,128)(2,1)S(1)}, u32[]{:S(2)}) copy-start(bf16[32,1,128,128]{3,2,1,0:T(8,128)(2,1)S(1)} %collective-permute-done.4.before) | copy-start | bytes 3145732
  116.0 12.7 %copy-start.10 = (bf16[32,1,128,128]{3,2,1,0:T(8,128)(2,1)}, bf16[32,1,128,128]{3,2,1,0:T(8,128)(2,1)S(1)}, u32[]{:S(2)}) copy-start(bf16[32,1,128,128]{3,2,1,0:T(8,128)(2,1)S(1)} %collective-permute-done.5.after) | copy-start | bytes 3145732
  116.0 12.7 %all-to-all-start.4 = ((bf16[4,128,256]{2,1,0:T(8,128)(2,1)}), bf16[4,128,256]{2,1,0:T(8,128)(2,1)S(1)}, u32[]{:S(2)}, u32[]{:S(2)}) async-start(bf16[4,128,256]{2,1,0:T(8,128)(2,1)} %get-tuple-element.56), calls=%async_computation.4 | async-start | bytes 524288 | tf_op jit(solution)/shard_map/all_to_all | solution.py:979
  128.7 0.7 copy-start.8

commit v12 on v11

--- a/solution.py
+++ b/solution.py
@@ -328,15 +328,19 @@
         out[s] = modes[s * lines : (s + 1) * lines].astype(jnp.bfloat16)
 
 
+def low_channels(channels):
+    return 3 * channels // 8
+
+
 def rims_kernel(field, *refs):
-    rims, held, got, put = refs[:4], refs[4], refs[5], refs[6]
-    half = field.shape[0] // 2
+    rims, held, got, put = refs[:4], refs[4:8], refs[8], refs[9]
     last = field.shape[1] - 1
     loads, stores = [], []
     for k in range(4):
-        source = field.at[pl.ds(half * (k % 2), half), pl.ds(last * (k // 2), 1)]
-        loads.append(pltpu.make_async_copy(source, held.at[k], got.at[k]))
-        stores.append(pltpu.make_async_copy(held.at[k], rims[k], put.at[k]))
+        count = rims[k].shape[0]
+        source = field.at[pl.ds((k % 2) * rims[0].shape[0], count), pl.ds(last * (k // 2), 1)]
+        loads.append(pltpu.make_async_copy(source, held[k], got.at[k]))
+        stores.append(pltpu.make_async_copy(held[k], rims[k], put.at[k]))
     for load in loads:
         load.start()
     for load, store in zip(loads, stores):
@@ -348,14 +352,17 @@
 
 def cut_rims(field):
     channels = field.shape[0]
-    rim = jax.ShapeDtypeStruct((channels // 2, 1, NX, NY), jnp.bfloat16)
+    low = low_channels(channels)
+    rims = [
+        jax.ShapeDtypeStruct((count, 1, NX, NY), jnp.bfloat16) for count in (low, channels - low) * 2
+    ]
     return pl.pallas_call(
         rims_kernel,
         in_specs=[pl.BlockSpec(memory_space=pl.ANY)],
         out_specs=[pl.BlockSpec(memory_space=pl.ANY)] * 4,
-        out_shape=[rim] * 4,
+        out_shape=rims,
         scratch_shapes=[
-            pltpu.VMEM((4,) + rim.shape, jnp.bfloat16),
+            *(pltpu.VMEM(rim.shape, jnp.bfloat16) for rim in rims),
             pltpu.SemaphoreType.DMA((4,)),
             pltpu.SemaphoreType.DMA((4,)),
         ],
@@ -671,47 +678,56 @@
       y_table)
 
 
-def build_band(adjoint, taps, channel, band):
+def build_tile(adjoint, taps, channel, dy, q, planes, span):
     row = lax.broadcasted_iota(jnp.int32, (8, 128), 0)
     lane = lax.broadcasted_iota(jnp.int32, (8, 128), 1)
+    tile = jnp.zeros((8, 128), jnp.float32)
+    for k, plane in enumerate(planes):
+        dz = plane - q
+        if not 0 <= dz <= 2:
+            continue
+        for dx in range(3):
+            number = 9 * dz + 3 * dx + dy
+            tap = taps[26 - number if adjoint else number, channel]
+            tile = jnp.where(lane == (span * k + row + (dx - 1)) % 128, tap, tile)
+    return tile
+
+
+def build_band(adjoint, taps, channel, band, tail):
+    row = lax.broadcasted_iota(jnp.int32, (8, 128), 0)
+    lane = lax.broadcasted_iota(jnp.int32, (8, 128), 1)
+    heads, middles, tails = [], [], []
     for dy in range(3):
         for q in range(2):
-            halves = []
-            for side in range(2):
-                tile = jnp.zeros((8, 128), jnp.float32)
-                for k in range(2):
-                    dz = 2 * side + k - q
-                    if not 0 <= dz <= 2:
-                        continue
-                    for dx in range(3):
-                        number = 9 * dz + 3 * dx + dy
-                        tap = taps[26 - number if adjoint else number, channel]
-                        hit = lane == (64 * k + row + (dx - 1)) % 128
-                        tile = jnp.where(hit, tap, tile)
-                tiles = [pltpu.roll(tile, 8 * k, axis=1) if k > 0 else tile for k in range(8)]
-                low = (row == 0) & (lane % 64 == 63)
-                high = (row == 7) & (lane % 64 == 0)
-                tiles[0] = jnp.where(low, 0.0, tiles[0])
-                tiles[7] = jnp.where(high, 0.0, tiles[7])
-                halves.append(jnp.concatenate(tiles[1:7] + [tiles[0], tiles[7]], axis=0))
-            at = 64 * (2 * dy + q)
-            band[at : at + 64, :] = jnp.concatenate(halves, axis=1).astype(jnp.bfloat16)
+            sides = []
+            for planes in ((0, 1), (2, 3)):
+                tile = build_tile(adjoint, taps, channel, dy, q, planes, 64)
+                tiles = [pltpu.roll(tile, 8 * k, axis=1) for k in range(1, 7)]
+                first = jnp.where((row == 0) & (lane % 64 == 63), 0.0, tile)
+                sides.append([first] + tiles)
+            blocks = [jnp.concatenate(pair, axis=1) for pair in zip(*sides)]
+            heads += blocks
+            middles += blocks[1:]
+            tile = build_tile(adjoint, taps, channel, dy, q, range(4), 32)
+            tiles = [pltpu.roll(tile, 8 * k, axis=1) for k in range(1, 4)]
+            tiles[2] = jnp.where((row == 7) & (lane % 32 == 0), 0.0, tiles[2])
+            tails += tiles
+    band[...] = jnp.concatenate(heads + middles, axis=0).astype(jnp.bfloat16)
+    tail[...] = jnp.concatenate(tails, axis=0).astype(jnp.bfloat16)
 
 
 def apply_band(quads, band):
-    blocks = range(6)
-    lefts = [
-        band[...],
-        jnp.concatenate([band[64 * b : 64 * b + 48, :] for b in blocks], axis=0),
-        jnp.concatenate([band[64 * b + 32 : 64 * b + 64, :] for b in blocks], axis=0),
-    ]
+    band, tail = band
+    counts = (56, 48, 24)
+    ends = (6 * counts[0], 6 * (counts[0] + counts[1]))
+    lefts = (band[: ends[0], :], band[ends[0] : ends[1], :], tail[...])
     lane = lax.broadcasted_iota(jnp.int32, (NX, NY), 1)
     totals = []
     for group in range(0, len(quads), 2):
         products = []
-        for left, x in zip(lefts, (0, 48, 64)):
+        for left, x, span in zip(lefts, (0, 48, 96), (64, 64, 32)):
             right = [
-                jnp.concatenate([sheet[x : x + 64] for sheet in quads[group + p]], axis=0)
+                jnp.concatenate([sheet[x : x + span] for sheet in quads[group + p]], axis=0)
                 for p in range(2)
             ]
             products.append(dot(left, jnp.concatenate(right, axis=1)))
@@ -723,11 +739,8 @@
                 for dy in range(3):
                     b = 2 * dy + q
                     pieces = [
-                        products[0][64 * b + 48 : 64 * b + 56, wide],
-                        products[0][64 * b : 64 * b + 48, wide],
-                        products[1][48 * b : 48 * b + 48, wide],
-                        products[2][32 * b : 32 * b + 16, wide],
-                        products[2][32 * b + 24 : 32 * b + 32, wide],
+                        product[count * b : count * (b + 1), wide]
+                        for product, count in zip(products, counts)
                     ]
                     shifted.append(jnp.concatenate(pieces, axis=0))
                 before = jnp.where(lane == 0, 0.0, pltpu.roll(shifted[0], 1, axis=1))
@@ -737,28 +750,31 @@
     return totals
 
 
-def banded(adjoint, taps, start, even, odd, channels):
+def banded(adjoint, taps, start, bands, channels):
     step = pl.program_id(0)
     final = start + channels * pl.num_programs(0) - 1
-    bands = (even, odd)
 
     @pl.when(step == 0)
     def _():
-        even[...] = jnp.zeros_like(even)
-        odd[...] = jnp.zeros_like(odd)
-        build_band(adjoint, taps, start, even)
+        build_band(adjoint, taps, start, *bands[0])
 
     def run(visit):
         for c in range(channels):
             following = jnp.minimum(start + channels * step + c + 1, final)
-            build_band(adjoint, taps, following, bands[(c + 1) % 2])
+            build_band(adjoint, taps, following, *bands[(c + 1) % 2])
             visit(c, bands[c % 2])
 
     return run
 
 
+def band_scratch():
+    shapes = [(6 * (56 + 48), 256), (6 * 24, 128)]
+    return [pltpu.VMEM(shape, jnp.bfloat16) for shape in shapes * 2]
+
+
 def smooth_kernel(start, taps, before, field, after, *rest):
-    out, even, odd = rest[-3:]
+    out, *bands = rest[-5:]
+    bands = bands[:2], bands[2:]
     planes = field.shape[1]
     totals = []
 
@@ -772,13 +788,15 @@
                 both = jnp.concatenate(both, axis=1).astype(jnp.bfloat16)
                 out[p, :, 8 * (c - 1) : 8 * (c + 1), :] = both
 
-    banded(False, taps, start, even, odd, field.shape[0])(visit)
+    banded(False, taps, start, bands, field.shape[0])(visit)
 
 
 def smooth_planes(field, rims, taps, done=None):
     channels, planes = field.shape[:2]
     pairs = planes // 2
-    start = 0 if done is None else channels // 2
+    low = low_channels(channels)
+    start = 0 if done is None else low
+    count = low if done is None else channels - low
     step = 4
     skip = start // step
     rim = pl.BlockSpec((step, 1, NX, NY), lambda c: (c, 0, 0, 0))
@@ -790,19 +808,20 @@
         operands.append(done)
     return pl.pallas_call(
         functools.partial(smooth_kernel, start),
-        grid=(channels // 2 // step,),
+        grid=(count // step,),
         in_specs=in_specs,
         out_specs=pl.BlockSpec((pairs, NX // 8, 8 * step, 2 * NY), lambda c: (0, 0, c + skip, 0)),
         out_shape=jax.ShapeDtypeStruct((pairs, NX // 8, 8 * channels, 2 * NY), jnp.bfloat16),
         input_output_aliases={} if done is None else {4: 0},
-        scratch_shapes=[pltpu.VMEM((6 * 64, 4 * 64), jnp.bfloat16) for _ in range(2)],
+        scratch_shapes=band_scratch(),
         compiler_params=params(),
         cost_estimate=LIGHT,
         name="smooth_low" if done is None else "smooth_high",
     )(*operands)
 
 
-def inner_kernel(taps, field, out, even, odd):
+def inner_kernel(taps, field, out, *bands):
+    bands = bands[:2], bands[2:]
     planes = field.shape[1]
 
     def visit(c, band):
@@ -812,7 +831,7 @@
             out[c, 2 * p] = total[:, :NY]
             out[c, 2 * p + 1] = total[:, NY:]
 
-    banded(True, taps, 0, even, odd, field.shape[0])(visit)
+    banded(True, taps, 0, bands, field.shape[0])(visit)
 
 
 def near_inner(field, taps):
@@ -828,15 +847,16 @@
         ],
         out_specs=pl.BlockSpec((step,) + shape[1:], lambda c: (c, 0, 0, 0)),
         out_shape=jax.ShapeDtypeStruct(shape, jnp.bfloat16),
-        scratch_shapes=[pltpu.VMEM((6 * 64, 4 * 64), jnp.bfloat16) for _ in range(2)],
+        scratch_shapes=band_scratch(),
         compiler_params=params(),
         cost_estimate=LIGHT,
         name="near_inner",
     )(taps, field)
 
 
-def finish_kernel(taps, before, field, after, inner, planar, ix_table, iy_table, out, waves, even,
-                  odd):
+def finish_kernel(taps, before, field, after, inner, planar, ix_table, iy_table, out, waves,
+                  *bands):
+    bands = bands[:2], bands[2:]
     step = pl.program_id(0)
     slabs, lines = planar.shape[:2]
     planes = field.shape[1]
@@ -871,7 +891,7 @@
         for p in range(1, planes // 2 - 1):
             store(c, p, [inner[c, 2 * p - 2 + q].astype(jnp.float32) for q in range(2)])
 
-    banded(True, taps, 0, even, odd, field.shape[0])(visit)
+    banded(True, taps, 0, bands, field.shape[0])(visit)
 
 
 def finish(planar, spread, rims, inner, taps):
@@ -899,8 +919,7 @@
         out_shape=jax.ShapeDtypeStruct(spread.shape, jnp.bfloat16),
         scratch_shapes=[
             pltpu.VMEM((slabs, 2, lines, planes * NY), jnp.bfloat16),
-            pltpu.VMEM((6 * 64, 4 * 64), jnp.bfloat16),
-            pltpu.VMEM((6 * 64, 4 * 64), jnp.bfloat16),
+            *band_scratch(),
         ],
         compiler_params=params(),
         cost_estimate=HEAVY,

time: 147 us -> 147 us (level)
    ppermute x6, waiting for transfers between devices: 1.55 us -> 0.02 us  [exchange(): return (lax.ppermute(last, 'slab', up), lax.ppermute(first, 'slab', down))]
    unnamed x26 -> x24, local copies, waits for them, and re-layouts: 4.46 us -> 4.51 us
  transfers between devices with their start and end apart: 11 -> 11, of which waited for: 4 -> 3; matrix products, arithmetic and copies ran while one was open for 0% -> 0% of each run, Pallas kernels for 35% -> 36%
where the time goes in v12:
time: 147 us; the launch traced here: 146 us
  Pallas kernels  92.5 us (63%)
  starting transfers between devices  41.4 us (28%)
  waiting for transfers between devices  6.71 us (5%)
  local copies, waits for them, and re-layouts  4.51 us (3%)
    pallas_call x1, Pallas kernels, layer(): pl.pallas_call(layer_kernel, grid=(pairs,), in_specs=[pl.BlockSpec(memory...  21.8 us
    all_to_all x4, starting transfers between devices, swap(): return lax.all_to_all(planar, 'slab', split_axis=0, concat_axis=0)  20.8 us
    pallas_call x2, Pallas kernels, smooth_planes(): pl.pallas_call(functools.partial(smooth_kernel, start), grid=(count // st...  17.3 us
    ppermute x6, starting transfers between devices, exchange(): return (lax.ppermute(last, 'slab', up), lax.ppermute(first, 'slab', down))  17.1 us
    pallas_call x1, Pallas kernels, finish(): pl.pallas_call(finish_kernel, grid=(channels // step,), in_specs=[pl.Bloc...  16.4 us
    pallas_call x2, Pallas kernels, mix(): pl.pallas_call(functools.partial(mixing_kernel, scale_in, scale_out, adjo...  12.2 us
    pallas_call x1, Pallas kernels, near_inner(): pl.pallas_call(inner_kernel, grid=(channels // step,), in_specs=[pl.Block...  10.4 us
    pallas_call x1, Pallas kernels, forward_modes(): pl.pallas_call(forward_kernel, grid=(planes // 2,), in_specs=[pl.BlockSpe...  6.7 us
  transfers between devices with their start and end apart: 11, of which 3 were waited for; matrix products, arithmetic and copies ran while one was open for 0% of the time, Pallas kernels for 36%

profile of v12, /device:TPU:0, one launch (start us, length us, event | category | flops | bytes accessed | tf_op | source)
XLA Modules:
  0.0 145.8 jit_solution(15969281665300235215)
XLA Ops:
  0.6 2.5 %rims.1 = (bf16[12,1,128,128]{3,2,1,0:T(8,128)(2,1)}, bf16[20,1,128,128]{3,2,1,0:T(8,128)(2,1)}, bf16[12,1,128,128]{3,2,1,0:T(8,128)(2,1)}, bf16[20,1,128,128]{3,2,1,0:T(8,128)(2,1)}) custom-call(bf16[32,8,128,128]{3,2,1,0:T(8,128)(2,1)} %bitcast.6), custom_call_target="tpu_custom_call" | custom-call | flops 10000000 | bytes 100000 | tf_op jit(solution)/shard_map/rims/pallas_call | solution.py:359
  3.1 0.0 copy-start.11
  3.1 5.1 %collective-permute-start = (bf16[12,1,128,128]{3,2,1,0:T(8,128)(2,1)}, bf16[12,1,128,128]{3,2,1,0:T(8,128)(2,1)S(1)}, u32[]{:S(2)}, u32[]{:S(2)}) collective-permute-start(bf16[12,1,128,128]{3,2,1,0:T(8,128)(2,1)} %get-tuple-element.31), channel_id=1, source_target_pairs={{0,1},{1,2},{2,3},{4,5},{5,6},{6,7},{8,9},{9,10},{10,11},{12,13},{... | collective-permute-start | bytes 1179656 | tf_op jit(solution)/shard_map/ppermute | solution.py:994
  8.2 1.3 collective-permute-start.1
  9.5 6.7 %forward_modes.1 = bf16[4,128,256]{2,1,0:T(8,128)(2,1)} custom-call(bf16[32,8,128,128]{3,2,1,0:T(8,128)(2,1)} %bitcast.7, bf16[64,256]{1,0:T(8,128)(2,1)} %constant.28.clone.x_table, bf16[2048,256]{1,0:T(8,128)(2,1)} %constant.29.clone.y_table), custom_call_target="tpu_custom_call" | custom-call | flops 10000000 | bytes 100000 | tf_op jit(solution)/shard_map/forward_modes/pallas_call | solution.py:396
  16.2 5.9 %all-to-all-start = ((bf16[4,128,256]{2,1,0:T(8,128)(2,1)}), bf16[4,128,256]{2,1,0:T(8,128)(2,1)S(1)}, u32[]{:S(2)}, u32[]{:S(2)}) async-start(bf16[4,128,256]{2,1,0:T(8,128)(2,1)} %forward_modes.1), calls=%async_computation | async-start | bytes 524288 | tf_op jit(solution)/shard_map/all_to_all | solution.py:998
  22.1 0.0 collective-permute-done.before
  22.1 0.0 copy-start.4
  22.1 0.0 collective-permute-done.1.after
  22.1 0.0 copy-start.5
  22.2 4.0 %collective-permute-start.2 = (bf16[20,1,128,128]{3,2,1,0:T(8,128)(2,1)}, bf16[20,1,128,128]{3,2,1,0:T(8,128)(2,1)S(1)}, u32[]{:S(2)}, u32[]{:S(2)}) collective-permute-start(bf16[20,1,128,128]{3,2,1,0:T(8,128)(2,1)} %get-tuple-element.39), channel_id=1, source_target_pairs={{0,1},{1,2},{2,3},{4,5},{5,6},{6,7},{8,9},{9,10},{10,11},{12,13},{... | collective-permute-start | bytes 1966088 | tf_op jit(solution)/shard_map/ppermute | solution.py:994
  26.1 0.0 copy-done.11
  26.1 1.3 collective-permute-start.3
  27.4 0.0 copy-done.4
  27.4 0.0 copy-done.5
  27.5 7.1 %smooth_low.1.rest_0_ = bf16[4,16,256,256]{3,2,1,0:T(8,128)(2,1)} custom-call(f32[27,32]{1,0:T(8,128)} %taps.7, bf16[12,1,128,128]{3,2,1,0:T(8,128)(2,1)} %copy-done.4, bf16[32,8,128,128]{3,2,1,0:T(8,128)(2,1)} %bitcast.8, bf16[12,1,128,128]{3,2,1,0:T(8,128)(2,1)} %copy-done.5), custom_call_target="tpu_custom_call" | custom-call | flops 10000000 | bytes 100000 | tf_op jit(solution)/shard_map/smooth_low/pallas_call | solution.py:809
  34.5 0.0 all-to-all-done.planar
  34.5 0.7 copy-done.6
  35.2 5.9 %mix.1 = (bf16[512,128]{1,0:T(8,128)(2,1)}, bf16[4,128,256]{2,1,0:T(8,128)(2,1)}) custom-call(bf16[4,128,256]{2,1,0:T(8,128)(2,1)} %copy-done.6, bf16[1024,2048]{1,0:T(8,128)(2,1)} %bitcast.13, bf16[512,256]{1,0:T(8,128)(2,1)} %constant.30.clone.z_in, bf16[256,512]{1,0:T(8,128)(2,1)} %constant.31.clone.z_out, bf16[128,1024]{1,0:T(8,128)(2,1)} %constant.32.clone.spread_table, ...), custom_call_target="tpu_custom_call" | custom-call | flops 99999997952 | bytes 100000000 | tf_op jit(solution)/shard_map/mix/pallas_call | solution.py:529
  41.1 5.7 %all-to-all-start.1 = ((bf16[4,128,256]{2,1,0:T(8,128)(2,1)}), bf16[4,128,256]{2,1,0:T(8,128)(2,1)S(1)}, u32[]{:S(2)}, u32[]{:S(2)}) async-start(bf16[4,128,256]{2,1,0:T(8,128)(2,1)} %get-tuple-element.38), calls=%async_computation.1 | async-start | bytes 524288 | tf_op jit(solution)/shard_map/all_to_all | solution.py:998
  46.8 0.0 collective-permute-done.2.before
  46.8 0.0 collective-permute-done.3.after
  46.8 0.8 copy-done.2
  47.7 0.8 copy-done.3
  48.5 10.2 %smooth_high.1.smooth = bf16[4,16,256,256]{3,2,1,0:T(8,128)(2,1)} custom-call(f32[27,32]{1,0:T(8,128)} %taps.7, bf16[20,1,128,128]{3,2,1,0:T(8,128)(2,1)} %copy-done.2, bf16[32,8,128,128]{3,2,1,0:T(8,128)(2,1)} %bitcast.9, bf16[20,1,128,128]{3,2,1,0:T(8,128)(2,1)} %copy-done.3, ...), custom_call_target="tpu_custom_call", output_to_operand_aliasing={{}: (4, {})} | custom-call | flops 10000000 | bytes 100000 | tf_op jit(solution)/shard_map/smooth_high/pallas_call | solution.py:809
  58.7 0.0 all-to-all-done.1.planar
  58.7 0.7 copy-done.1
  59.5 21.8 %layer.1 = (bf16[32,8,128,128]{3,2,1,0:T(8,128)(2,1)}, bf16[4,128,256]{2,1,0:T(8,128)(2,1)}, bf16[32,1,128,128]{3,2,1,0:T(8,128)(2,1)}, bf16[32,1,128,128]{3,2,1,0:T(8,128)(2,1)}) custom-call(f32[32]{0:T(128)} %bias.1, bf16[4,128,256]{2,1,0:T(8,128)(2,1)} %copy-done.1, bf16[4,16,256,256]{3,2,1,0:T(8,128)(2,1)} %smooth_high.1.smooth, ...), custom_call_target="tpu_custom_call" | custom-call | flops 10000000 | bytes 100000 | tf_op jit(solution)/shard_map/layer/pallas_call | solution.py:646
  81.2 5.1 %all-to-all-start.2 = ((bf16[4,128,256]{2,1,0:T(8,128)(2,1)}), bf16[4,128,256]{2,1,0:T(8,128)(2,1)S(1)}, u32[]{:S(2)}, u32[]{:S(2)}) async-start(bf16[4,128,256]{2,1,0:T(8,128)(2,1)} %get-tuple-element.44), calls=%async_computation.2 | async-start | bytes 524288 | tf_op jit(solution)/shard_map/all_to_all | solution.py:998
  86.3 4.0 %collective-permute-start.4 = (bf16[32,1,128,128]{3,2,1,0:T(8,128)(2,1)}, bf16[32,1,128,128]{3,2,1,0:T(8,128)(2,1)S(1)}, u32[]{:S(2)}, u32[]{:S(2)}) collective-permute-start(bf16[32,1,128,128]{3,2,1,0:T(8,128)(2,1)} %get-tuple-element.51), channel_id=1, source_target_pairs={{0,1},{1,2},{2,3},{4,5},{5,6},{6,7},{8,9},{9,10},{10,11},{12,13},{... | collective-permute-start | bytes 3145736 | tf_op jit(solution)/shard_map/ppermute | solution.py:994
  90.3 1.5 %collective-permute-start.5 = (bf16[32,1,128,128]{3,2,1,0:T(8,128)(2,1)}, bf16[32,1,128,128]{3,2,1,0:T(8,128)(2,1)S(1)}, u32[]{:S(2)}, u32[]{:S(2)}) collective-permute-start(bf16[32,1,128,128]{3,2,1,0:T(8,128)(2,1)} %get-tuple-element.52), channel_id=1, source_target_pairs={{1,0},{2,1},{3,2},{5,4},{6,5},{7,6},{9,8},{10,9},{11,10},{13,12},{... | collective-permute-start | bytes 3145736 | tf_op jit(solution)/shard_map/ppermute | solution.py:994
  91.8 2.0 %all-to-all-done.2.planar = bf16[4,128,256]{2,1,0:T(8,128)(2,1)S(1)} async-done(((bf16[4,128,256]{2,1,0:T(8,128)(2,1)}), bf16[4,128,256]{2,1,0:T(8,128)(2,1)S(1)}, u32[]{:S(2)}, u32[]{:S(2)}) %all-to-all-start.2) | async-done | bytes 262176 | tf_op jit(solution)/shard_map/all_to_all | solution.py:998
  93.8 0.7 copy-done.7
  94.5 6.3 %mix_back.1 = (bf16[4,128,256]{2,1,0:T(8,128)(2,1)}, bf16[4,768,128]{2,1,0:T(8,128)(2,1)}) custom-call(bf16[4,128,256]{2,1,0:T(8,128)(2,1)} %copy-done.7, bf16[1024,2048]{1,0:T(8,128)(2,1)} %bitcast.14, bf16[512,256]{1,0:T(8,128)(2,1)} %constant.30.clone.z_in, bf16[256,512]{1,0:T(8,128)(2,1)} %constant.31.clone.z_out, ...), custom_call_target="tpu_custom_call" | custom-call | flops 99999997952 | bytes 100000000 | tf_op jit(solution)/shard_map/mix_back/pallas_call | solution.py:529
  100.9 3.5 %all-to-all-start.3 = ((bf16[4,768,128]{2,1,0:T(8,128)(2,1)}), bf16[4,768,128]{2,1,0:T(8,128)(2,1)S(1)}, u32[]{:S(2)}, u32[]{:S(2)}) async-start(bf16[4,768,128]{2,1,0:T(8,128)(2,1)} %get-tuple-element.49), calls=%async_computation.3 | async-start | bytes 1572864 | tf_op jit(solution)/shard_map/all_to_all | solution.py:1028
  104.4 10.4 %near_inner.1.inner = bf16[32,4,128,128]{3,2,1,0:T(8,128)(2,1)} custom-call(f32[27,32]{1,0:T(8,128)} %taps.7, bf16[32,8,128,128]{3,2,1,0:T(8,128)(2,1)} %get-tuple-element.50.field), custom_call_target="tpu_custom_call" | custom-call | flops 10000000 | bytes 100000 | tf_op jit(solution)/shard_map/near_inner/pallas_call | solution.py:841
  114.8 1.2 all-to-all-done.3.gathered
  116.0 0.0 collective-permute-done.4.before
  116.0 0.0 collective-permute-done.5.after
  116.0 0.0 copy-start.10
  116.0 4.1 %all-to-all-start.4 = ((bf16[4,128,256]{2,1,0:T(8,128)(2,1)}), bf16[4,128,256]{2,1,0:T(8,128)(2,1)S(1)}, u32[]{:S(2)}, u32[]{:S(2)}) async-start(bf16[4,128,256]{2,1,0:T(8,128)(2,1)} %get-tuple-element.56), calls=%async_computation.4 | async-start | bytes 524288 | tf_op jit(solution)/shard_map/all_to_all | solution.py:998
  120.1 0.0 copy-done
  120.1 5.2 %weight_gradient.1 = f32[1024,512]{1,0:T(8,128)} custom-call(bf16[4,768,128]{2,1,0:T(8,128)(2,1)} %copy-done, bf16[128,512]{1,0:T(8,128)(2,1)} %constant.40.clone.first, bf16[128,128]{1,0:T(8,128)(2,1)} %constant.38.clone.spread_table.second), custom_call_target="tpu_custom_call" | custom-call | flops 10000000 | bytes 100000 | tf_op jit(solution)/shard_map/weight_gradient/pallas_call | solution.py:978
  125.3 3.4 %all-to-all-done.4.planar = bf16[4,128,256]{2,1,0:T(8,128)(2,1)S(1)} async-done(((bf16[4,128,256]{2,1,0:T(8,128)(2,1)}), bf16[4,128,256]{2,1,0:T(8,128)(2,1)S(1)}, u32[]{:S(2)}, u32[]{:S(2)}) %all-to-all-start.4) | async-done | bytes 262176 | tf_op jit(solution)/shard_map/all_to_all | solution.py:998
  128.7 0.0 copy-done.9
  128.7 0.0 copy-done.10
  128.7 0.7 copy-done.8
  129.5 16.4 %finish.1 = bf16[32,8,128,128]{3,2,1,0:T(8,128)(2,1)} custom-call(f32[27,32]{1,0:T(8,128)} %taps.7, bf16[32,1,128,128]{3,2,1,0:T(8,128)(2,1)} %copy-done.9, bf16[32,8,128,128]{3,2,1,0:T(8,128)(2,1)} %get-tuple-element.50.field, bf16[32,1,128,128]{3,2,1,0:T(8,128)(2,1)} %copy-done.10, bf16[32,4,128,128]{3,2,1,0:T(8,128)(2,1)} %near_inner.1.inner, ...), custom_call_target="tpu_custom_call" | custom-call | flops 99999997952 | bytes 100000000 | tf_op jit(solution)/shard_map/finish/pallas_call | solution.py:905
  (8 shorter events, 0.0 us)
Async XLA Ops:
  3.1 23.0 %copy-start.11 = (bf16[20,1,128,128]{3,2,1,0:T(8,128)(2,1)S(1)}, bf16[20,1,128,128]{3,2,1,0:T(8,128)(2,1)}, u32[]{:S(2)}) copy-start(bf16[20,1,128,128]{3,2,1,0:T(8,128)(2,1)} %get-tuple-element.40) | copy-start | bytes 1966084
  3.1 19.0 %collective-permute-start = (bf16[12,1,128,128]{3,2,1,0:T(8,128)(2,1)}, bf16[12,1,128,128]{3,2,1,0:T(8,128)(2,1)S(1)}, u32[]{:S(2)}, u32[]{:S(2)}) collective-permute-start(bf16[12,1,128,128]{3,2,1,0:T(8,128)(2,1)} %get-tuple-element.31), channel_id=1, source_target_pairs={{0,1},{1,2},{2,3},{4,5},{5,6},{6,7},{8,9},{9,10},{10,11},{12,13},{... | collective-permute-start | bytes 1179656 | tf_op jit(solution)/shard_map/ppermute | solution.py:994
  8.2 13.9 %collective-permute-start.1 = (bf16[12,1,128,128]{3,2,1,0:T(8,128)(2,1)}, bf16[12,1,128,128]{3,2,1,0:T(8,128)(2,1)S(1)}, u32[]{:S(2)}, u32[]{:S(2)}) collective-permute-start(bf16[12,1,128,128]{3,2,1,0:T(8,128)(2,1)} %get-tuple-element.32), channel_id=1, source_target_pairs={{1,0},{2,1},{3,2},{5,4},{6,5},{7,6},{9,8},{10,9},{11,10},{13,12},{... | collective-permute-start | bytes 1179656 | tf_op jit(solution)/shard_map/ppermute | solution.py:994
  16.2 18.3 %all-to-all-start = ((bf16[4,128,256]{2,1,0:T(8,128)(2,1)}), bf16[4,128,256]{2,1,0:T(8,128)(2,1)S(1)}, u32[]{:S(2)}, u32[]{:S(2)}) async-start(bf16[4,128,256]{2,1,0:T(8,128)(2,1)} %forward_modes.1), calls=%async_computation | async-start | bytes 524288 | tf_op jit(solution)/shard_map/all_to_all | solution.py:998
  22.1 5.3 %copy-start.4 = (bf16[12,1,128,128]{3,2,1,0:T(8,128)(2,1)}, bf16[12,1,128,128]{3,2,1,0:T(8,128)(2,1)S(1)}, u32[]{:S(2)}) copy-start(bf16[12,1,128,128]{3,2,1,0:T(8,128)(2,1)S(1)} %collective-permute-done.before) | copy-start | bytes 1179652
  22.1 5.3 %copy-start.5 = (bf16[12,1,128,128]{3,2,1,0:T(8,128)(2,1)}, bf16[12,1,128,128]{3,2,1,0:T(8,128)(2,1)S(1)}, u32[]{:S(2)}) copy-start(bf16[12,1,128,128]{3,2,1,0:T(8,128)(2,1)S(1)} %collective-permute-done.1.after) | copy-start | bytes 1179652
  22.2 24.7 %collective-permute-start.2 = (bf16[20,1,128,128]{3,2,1,0:T(8,128)(2,1)}, bf16[20,1,128,128]{3,2,1,0:T(8,128)(2,1)S(1)}, u32[]{:S(2)}, u32[]{:S(2)}) collective-permute-start(bf16[20,1,128,128]{3,2,1,0:T(8,128)(2,1)} %get-tuple-element.39), channel_id=1, source_target_pairs={{0,1},{1,2},{2,3},{4,5},{5,6},{6,7},{8,9},{9,10},{10,11},{12,13},{... | collective-permute-start | bytes 1966088 | tf_op jit(solution)/shard_map/ppermute | solution.py:994
  26.1 20.7 %collective-permute-start.3 = (bf16[20,1,128,128]{3,2,1,0:T(8,128)(2,1)S(1)}, bf16[20,1,128,128]{3,2,1,0:T(8,128)(2,1)S(1)}, u32[]{:S(2)}, u32[]{:S(2)}) collective-permute-start(bf16[20,1,128,128]{3,2,1,0:T(8,128)(2,1)S(1)} %copy-done.11), channel_id=1, source_target_pairs={{1,0},{2,1},{3,2},{5,4},{6,5},{7,6},{9,8},{10,9},{11,10},{13,12},{... | collective-permute-start | bytes 1966088 | tf_op jit(solution)/shard_map/ppermute | solution.py:994
  34.5 0.7 copy-start.6
  41.1 17.6 %all-to-all-start.1 = ((bf16[4,128,256]{2,1,0:T(8,128)(2,1)}), bf16[4,128,256]{2,1,0:T(8,128)(2,1)S(1)}, u32[]{:S(2)}, u32[]{:S(2)}) async-start(bf16[4,128,256]{2,1,0:T(8,128)(2,1)} %get-tuple-element.38), calls=%async_computation.1 | async-start | bytes 524288 | tf_op jit(solution)/shard_map/all_to_all | solution.py:998
  46.8 0.8 copy-start.2
  47.7 0.8 copy-start.3
  58.7 0.7 copy-start.1
  81.2 12.6 %all-to-all-start.2 = ((bf16[4,128,256]{2,1,0:T(8,128)(2,1)}), bf16[4,128,256]{2,1,0:T(8,128)(2,1)S(1)}, u32[]{:S(2)}, u32[]{:S(2)}) async-start(bf16[4,128,256]{2,1,0:T(8,128)(2,1)} %get-tuple-element.44), calls=%async_computation.2 | async-start | bytes 524288 | tf_op jit(solution)/shard_map/all_to_all | solution.py:998
  86.3 29.7 %collective-permute-start.4 = (bf16[32,1,128,128]{3,2,1,0:T(8,128)(2,1)}, bf16[32,1,128,128]{3,2,1,0:T(8,128)(2,1)S(1)}, u32[]{:S(2)}, u32[]{:S(2)}) collective-permute-start(bf16[32,1,128,128]{3,2,1,0:T(8,128)(2,1)} %get-tuple-element.51), channel_id=1, source_target_pairs={{0,1},{1,2},{2,3},{4,5},{5,6},{6,7},{8,9},{9,10},{10,11},{12,13},{... | collective-permute-start | bytes 3145736 | tf_op jit(solution)/shard_map/ppermute | solution.py:994
  90.3 25.7 %collective-permute-start.5 = (bf16[32,1,128,128]{3,2,1,0:T(8,128)(2,1)}, bf16[32,1,128,128]{3,2,1,0:T(8,128)(2,1)S(1)}, u32[]{:S(2)}, u32[]{:S(2)}) collective-permute-start(bf16[32,1,128,128]{3,2,1,0:T(8,128)(2,1)} %get-tuple-element.52), channel_id=1, source_target_pairs={{1,0},{2,1},{3,2},{5,4},{6,5},{7,6},{9,8},{10,9},{11,10},{13,12},{... | collective-permute-start | bytes 3145736 | tf_op jit(solution)/shard_map/ppermute | solution.py:994
  93.8 0.7 copy-start.7
  100.9 15.1 %all-to-all-start.3 = ((bf16[4,768,128]{2,1,0:T(8,128)(2,1)}), bf16[4,768,128]{2,1,0:T(8,128)(2,1)S(1)}, u32[]{:S(2)}, u32[]{:S(2)}) async-start(bf16[4,768,128]{2,1,0:T(8,128)(2,1)} %get-tuple-element.49), calls=%async_computation.3 | async-start | bytes 1572864 | tf_op jit(solution)/shard_map/all_to_all | solution.py:1028
  116.0 4.1 %copy-start = (bf16[4,768,128]{2,1,0:T(8,128)(2,1)}, bf16[4,768,128]{2,1,0:T(8,128)(2,1)S(1)}, u32[]{:S(2)}) copy-start(bf16[4,768,128]{2,1,0:T(8,128)(2,1)S(1)} %all-to-all-done.3.gathered) | copy-start | bytes 2359300
  116.0 12.7 %copy-start.9 = (bf16[32,1,128,128]{3,2,1,0:T(8,128)(2,1)}, bf16[32,1,128,128]{3,2,1,0:T(8,128)(2,1)S(1)}, u32[]{:S(2)}) copy-start(bf16[32,1,128,128]{3,2,1,0:T(8,128)(2,1)S(1)} %collective-permute-done.4.before) | copy-start | bytes 3145732
  116.0 12.7 %copy-start.10 = (bf16[32,1,128,128]{3,2,1,0:T(8,128)(2,1)}, bf16[32,1,128,128]{3,2,1,0:T(8,128)(2,1)S(1)}, u32[]{:S(2)}) copy-start(bf16[32,1,128,128]{3,2,1,0:T(8,128)(2,1)S(1)} %collective-permute-done.5.after) | copy-start | bytes 3145732
  116.0 12.7 %all-to-all-start.4 = ((bf16[4,128,256]{2,1,0:T(8,128)(2,1)}), bf16[4,128,256]{2,1,0:T(8,128)(2,1)S(1)}, u32[]{:S(2)}, u32[]{:S(2)}) async-start(bf16[4,128,256]{2,1,0:T(8,128)(2,1)} %get-tuple-element.56), calls=%async_computation.4 | async-start | bytes 524288 | tf_op jit(solution)/shard_map/all_to_all | solution.py:998
  128.7 0.7 copy-start.8

commit v13 on v12

--- a/solution.py
+++ b/solution.py
@@ -302,8 +302,11 @@
     return pl.BlockSpec(shape, lambda *_: (0,) * len(shape))
 
 
-def params(**kw):
-    return pltpu.CompilerParams(vmem_limit_bytes=63438848, **kw)
+def params(limit=63438848):
+    return pltpu.CompilerParams(vmem_limit_bytes=limit)
+
+
+ROOMY = 48 * 2**20
 
 
 def store_rows(rows, pair, x_table, load):
@@ -533,7 +536,7 @@
         out_specs=[whole(out) for out in outs],
         out_shape=[jax.ShapeDtypeStruct(out, jnp.bfloat16) for out in outs],
         scratch_shapes=scratch,
-        compiler_params=params(),
+        compiler_params=params(ROOMY),
         cost_estimate=HEAVY,
         name="mix_back" if adjoint else "mix",
     )(*operands)
@@ -761,20 +764,24 @@
     def run(visit):
         for c in range(channels):
             following = jnp.minimum(start + channels * step + c + 1, final)
-            build_band(adjoint, taps, following, *bands[(c + 1) % 2])
-            visit(c, bands[c % 2])
+            build_band(adjoint, taps, following, *bands[(c + 1) % channels])
+            visit(c, bands[c])
 
     return run
 
 
-def band_scratch():
+def band_scratch(channels):
     shapes = [(6 * (56 + 48), 256), (6 * 24, 128)]
-    return [pltpu.VMEM(shape, jnp.bfloat16) for shape in shapes * 2]
+    return [pltpu.VMEM(shape, jnp.bfloat16) for shape in shapes * channels]
+
+
+def paired(refs):
+    return list(zip(refs[0::2], refs[1::2]))
 
 
 def smooth_kernel(start, taps, before, field, after, *rest):
-    out, *bands = rest[-5:]
-    bands = bands[:2], bands[2:]
+    out, *bands = rest[-2 * field.shape[0] - 1 :]
+    bands = paired(bands)
     planes = field.shape[1]
     totals = []
 
@@ -813,15 +820,15 @@
         out_specs=pl.BlockSpec((pairs, NX // 8, 8 * step, 2 * NY), lambda c: (0, 0, c + skip, 0)),
         out_shape=jax.ShapeDtypeStruct((pairs, NX // 8, 8 * channels, 2 * NY), jnp.bfloat16),
         input_output_aliases={} if done is None else {4: 0},
-        scratch_shapes=band_scratch(),
-        compiler_params=params(),
+        scratch_shapes=band_scratch(step),
+        compiler_params=params(ROOMY),
         cost_estimate=LIGHT,
         name="smooth_low" if done is None else "smooth_high",
     )(*operands)
 
 
 def inner_kernel(taps, field, out, *bands):
-    bands = bands[:2], bands[2:]
+    bands = paired(bands)
     planes = field.shape[1]
 
     def visit(c, band):
@@ -847,8 +854,8 @@
         ],
         out_specs=pl.BlockSpec((step,) + shape[1:], lambda c: (c, 0, 0, 0)),
         out_shape=jax.ShapeDtypeStruct(shape, jnp.bfloat16),
-        scratch_shapes=band_scratch(),
-        compiler_params=params(),
+        scratch_shapes=band_scratch(step),
+        compiler_params=params(ROOMY),
         cost_estimate=LIGHT,
         name="near_inner",
     )(taps, field)
@@ -856,7 +863,7 @@
 
 def finish_kernel(taps, before, field, after, inner, planar, ix_table, iy_table, out, waves,
                   *bands):
-    bands = bands[:2], bands[2:]
+    bands = paired(bands)
     step = pl.program_id(0)
     slabs, lines = planar.shape[:2]
     planes = field.shape[1]
@@ -919,7 +926,7 @@
         out_shape=jax.ShapeDtypeStruct(spread.shape, jnp.bfloat16),
         scratch_shapes=[
             pltpu.VMEM((slabs, 2, lines, planes * NY), jnp.bfloat16),
-            *band_scratch(),
+            *band_scratch(step),
         ],
         compiler_params=params(),
         cost_estimate=HEAVY,
@@ -981,7 +988,7 @@
         in_specs=[whole(gathered.shape), whole(first.shape), whole(second.shape)],
         out_specs=pl.BlockSpec((depth // steps * half, width), lambda j: (j, 0)),
         out_shape=jax.ShapeDtypeStruct((depth * half, width), jnp.float32),
-        compiler_params=params(),
+        compiler_params=params(ROOMY),
         cost_estimate=LIGHT,
         name="weight_gradient",
     )(gathered, first, second)

time: 147 us -> 145 us (0.986)
  Pallas kernels: 92.5 us -> 87.8 us
    pallas_call x2, Pallas kernels: 12.2 us -> 10 us  [mix(): pl.pallas_call(functools.partial(mixing_kernel, scale_in, scale_out, adjo...]
    all_to_all x4, waiting for transfers between devices: 5.48 us -> 7.26 us  [swap(): return lax.all_to_all(planar, 'slab', split_axis=0, concat_axis=0)]
    unnamed x24 -> x26, local copies, waits for them, and re-layouts: 4.51 us -> 5.67 us
  transfers between devices with their start and end apart: 11 -> 11, of which waited for: 3 -> 4; matrix products, arithmetic and copies ran while one was open for 0% -> 0% of each run, Pallas kernels for 36% -> 33%
where the time goes in v13:
time: 145 us; the launch traced here: 144 us
  Pallas kernels  87.8 us (61%)
  starting transfers between devices  41.3 us (28%)
  waiting for transfers between devices  8.12 us (6%)
  local copies, waits for them, and re-layouts  5.67 us (4%)
    pallas_call x1, Pallas kernels, layer(): pl.pallas_call(layer_kernel, grid=(pairs,), in_specs=[pl.BlockSpec(memory...  21.8 us
    all_to_all x4, starting transfers between devices, swap(): return lax.all_to_all(planar, 'slab', split_axis=0, concat_axis=0)  20.6 us
    pallas_call x2, Pallas kernels, smooth_planes(): pl.pallas_call(functools.partial(smooth_kernel, start), grid=(count // st...  17.1 us
    ppermute x6, starting transfers between devices, exchange(): return (lax.ppermute(last, 'slab', up), lax.ppermute(first, 'slab', down))  17.1 us
    pallas_call x1, Pallas kernels, finish(): pl.pallas_call(finish_kernel, grid=(channels // step,), in_specs=[pl.Bloc...  16.3 us
    pallas_call x2, Pallas kernels, mix(): pl.pallas_call(functools.partial(mixing_kernel, scale_in, scale_out, adjo...  10 us
    pallas_call x1, Pallas kernels, near_inner(): pl.pallas_call(inner_kernel, grid=(channels // step,), in_specs=[pl.Block...  9.29 us
    all_to_all x4, waiting for transfers between devices, swap(): return lax.all_to_all(planar, 'slab', split_axis=0, concat_axis=0)  7.26 us
  transfers between devices with their start and end apart: 11, of which 4 were waited for; matrix products, arithmetic and copies ran while one was open for 0% of the time, Pallas kernels for 33%

profile of v13, /device:TPU:0, one launch (start us, length us, event | category | flops | bytes accessed | tf_op | source)
XLA Modules:
  0.0 143.8 jit_solution(2420624358786571277)
XLA Ops:
  0.6 0.0 copy-start.1
  0.6 2.5 %rims.1 = (bf16[12,1,128,128]{3,2,1,0:T(8,128)(2,1)}, bf16[20,1,128,128]{3,2,1,0:T(8,128)(2,1)}, bf16[12,1,128,128]{3,2,1,0:T(8,128)(2,1)}, bf16[20,1,128,128]{3,2,1,0:T(8,128)(2,1)}) custom-call(bf16[32,8,128,128]{3,2,1,0:T(8,128)(2,1)} %bitcast.8), custom_call_target="tpu_custom_call" | custom-call | flops 10000000 | bytes 100000 | tf_op jit(solution)/shard_map/rims/pallas_call | solution.py:362
  3.1 5.0 %collective-permute-start = (bf16[12,1,128,128]{3,2,1,0:T(8,128)(2,1)}, bf16[12,1,128,128]{3,2,1,0:T(8,128)(2,1)S(1)}, u32[]{:S(2)}, u32[]{:S(2)}) collective-permute-start(bf16[12,1,128,128]{3,2,1,0:T(8,128)(2,1)} %get-tuple-element.31), channel_id=1, source_target_pairs={{0,1},{1,2},{2,3},{4,5},{5,6},{6,7},{8,9},{9,10},{10,11},{12,13},{... | collective-permute-start | bytes 1179656 | tf_op jit(solution)/shard_map/ppermute | solution.py:1001
  8.1 1.3 collective-permute-start.1
  9.4 6.7 %forward_modes.1 = bf16[4,128,256]{2,1,0:T(8,128)(2,1)} custom-call(bf16[32,8,128,128]{3,2,1,0:T(8,128)(2,1)} %bitcast.9, bf16[64,256]{1,0:T(8,128)(2,1)} %constant.28.clone.x_table, bf16[2048,256]{1,0:T(8,128)(2,1)} %constant.29.clone.y_table), custom_call_target="tpu_custom_call" | custom-call | flops 10000000 | bytes 100000 | tf_op jit(solution)/shard_map/forward_modes/pallas_call | solution.py:399
  16.1 5.9 %all-to-all-start = ((bf16[4,128,256]{2,1,0:T(8,128)(2,1)}), bf16[4,128,256]{2,1,0:T(8,128)(2,1)S(1)}, u32[]{:S(2)}, u32[]{:S(2)}) async-start(bf16[4,128,256]{2,1,0:T(8,128)(2,1)} %forward_modes.1), calls=%async_computation | async-start | bytes 524288 | tf_op jit(solution)/shard_map/all_to_all | solution.py:1005
  22.0 0.0 collective-permute-done.before
  22.0 0.0 collective-permute-done.1.after
  22.0 0.0 copy-start.5
  22.0 0.0 copy-start.6
  22.1 0.0 copy-start.8
  22.1 0.0 copy-start.9
  22.1 4.1 %collective-permute-start.2 = (bf16[20,1,128,128]{3,2,1,0:T(8,128)(2,1)}, bf16[20,1,128,128]{3,2,1,0:T(8,128)(2,1)S(1)}, u32[]{:S(2)}, u32[]{:S(2)}) collective-permute-start(bf16[20,1,128,128]{3,2,1,0:T(8,128)(2,1)} %get-tuple-element.39), channel_id=1, source_target_pairs={{0,1},{1,2},{2,3},{4,5},{5,6},{6,7},{8,9},{9,10},{10,11},{12,13},{... | collective-permute-start | bytes 1966088 | tf_op jit(solution)/shard_map/ppermute | solution.py:1001
  26.2 1.3 collective-permute-start.3
  27.5 0.0 copy-done.1
  27.5 7.0 %smooth_low.1.rest_0_ = bf16[4,16,256,256]{3,2,1,0:T(8,128)(2,1)} custom-call(f32[27,32]{1,0:T(8,128)S(1)} %copy-done.1, bf16[12,1,128,128]{3,2,1,0:T(8,128)(2,1)S(1)} %collective-permute-done.before, bf16[32,8,128,128]{3,2,1,0:T(8,128)(2,1)} %bitcast.10, bf16[12,1,128,128]{3,2,1,0:T(8,128)(2,1)S(1)} %collective-permute-done.1.after), custom_call_target="tpu_custom_call" | custom-call | flops 10000000 | bytes 100000 | tf_op jit(solution)/shard_map/smooth_low/pallas_call | solution.py:816
  34.5 0.0 all-to-all-done.planar
  34.5 0.0 copy-done.5
  34.5 0.0 copy-done.6
  34.5 0.0 copy-done.8
  34.5 0.0 copy-done.9
  34.5 0.0 copy-start.4
  34.5 2.2 %copy-done.4 = bf16[64,16,2048]{2,1,0:T(8,128)(2,1)S(1)} copy-done((bf16[64,16,2048]{2,1,0:T(8,128)(2,1)S(1)}, bf16[64,16,2048]{2,1,0:T(8,128)(2,1)}, u32[]{:S(2)}) %copy-start.4) | copy-done | bytes 4194328
  36.7 4.0 %mix.1 = (bf16[512,128]{1,0:T(8,128)(2,1)S(1)}, bf16[4,128,256]{2,1,0:T(8,128)(2,1)}) custom-call(bf16[4,128,256]{2,1,0:T(8,128)(2,1)S(1)} %all-to-all-done.planar, bf16[1024,2048]{1,0:T(8,128)(2,1)S(1)} %bitcast.7, bf16[512,256]{1,0:T(8,128)(2,1)S(1)} %copy-done.6, bf16[256,512]{1,0:T(8,128)(2,1)S(1)} %copy-done.5, bf16[128,1024]{1,0:T(8,128)(2,1)S(1)} %copy-done.8, ...), custom_call_target="tpu_custom_call" | custom-call | flops 99999997952 | bytes 100000000 | tf_op jit(solution)/shard_map/mix/pallas_call | solution.py:532
  40.7 5.7 %all-to-all-start.1 = ((bf16[4,128,256]{2,1,0:T(8,128)(2,1)}), bf16[4,128,256]{2,1,0:T(8,128)(2,1)S(1)}, u32[]{:S(2)}, u32[]{:S(2)}) async-start(bf16[4,128,256]{2,1,0:T(8,128)(2,1)} %get-tuple-element.38), calls=%async_computation.1 | async-start | bytes 524288 | tf_op jit(solution)/shard_map/all_to_all | solution.py:1005
  46.4 0.0 collective-permute-done.2.before
  46.4 0.0 collective-permute-done.3.after
  46.4 10.1 %smooth_high.1.smooth = bf16[4,16,256,256]{3,2,1,0:T(8,128)(2,1)} custom-call(f32[27,32]{1,0:T(8,128)S(1)} %copy-done.1, bf16[20,1,128,128]{3,2,1,0:T(8,128)(2,1)S(1)} %collective-permute-done.2.before, bf16[32,8,128,128]{3,2,1,0:T(8,128)(2,1)} %bitcast.11, ...), custom_call_target="tpu_custom_call", output_to_operand_aliasing={{}: (4, {})} | custom-call | flops 10000000 | bytes 100000 | tf_op jit(solution)/shard_map/smooth_high/pallas_call | solution.py:816
  56.6 0.0 all-to-all-done.1.planar
  56.6 0.7 copy-done.10
  57.3 21.8 %layer.1 = (bf16[32,8,128,128]{3,2,1,0:T(8,128)(2,1)}, bf16[4,128,256]{2,1,0:T(8,128)(2,1)}, bf16[32,1,128,128]{3,2,1,0:T(8,128)(2,1)}, bf16[32,1,128,128]{3,2,1,0:T(8,128)(2,1)}) custom-call(f32[32]{0:T(128)} %bias.1, bf16[4,128,256]{2,1,0:T(8,128)(2,1)} %copy-done.10, bf16[4,16,256,256]{3,2,1,0:T(8,128)(2,1)} %smooth_high.1.smooth, ...), custom_call_target="tpu_custom_call" | custom-call | flops 10000000 | bytes 100000 | tf_op jit(solution)/shard_map/layer/pallas_call | solution.py:649
  79.1 5.1 %all-to-all-start.2 = ((bf16[4,128,256]{2,1,0:T(8,128)(2,1)}), bf16[4,128,256]{2,1,0:T(8,128)(2,1)S(1)}, u32[]{:S(2)}, u32[]{:S(2)}) async-start(bf16[4,128,256]{2,1,0:T(8,128)(2,1)} %get-tuple-element.44), calls=%async_computation.2 | async-start | bytes 524288 | tf_op jit(solution)/shard_map/all_to_all | solution.py:1005
  84.2 4.0 %collective-permute-start.4 = (bf16[32,1,128,128]{3,2,1,0:T(8,128)(2,1)}, bf16[32,1,128,128]{3,2,1,0:T(8,128)(2,1)S(1)}, u32[]{:S(2)}, u32[]{:S(2)}) collective-permute-start(bf16[32,1,128,128]{3,2,1,0:T(8,128)(2,1)} %get-tuple-element.51), channel_id=1, source_target_pairs={{0,1},{1,2},{2,3},{4,5},{5,6},{6,7},{8,9},{9,10},{10,11},{12,13},{... | collective-permute-start | bytes 3145736 | tf_op jit(solution)/shard_map/ppermute | solution.py:1001
  88.2 1.5 %collective-permute-start.5 = (bf16[32,1,128,128]{3,2,1,0:T(8,128)(2,1)}, bf16[32,1,128,128]{3,2,1,0:T(8,128)(2,1)}, u32[]{:S(2)}, u32[]{:S(2)}) collective-permute-start(bf16[32,1,128,128]{3,2,1,0:T(8,128)(2,1)} %get-tuple-element.52), channel_id=1, source_target_pairs={{1,0},{2,1},{3,2},{5,4},{6,5},{7,6},{9,8},{10,9},{11,10},{13,12},{... | collective-permute-start | bytes 3145736 | tf_op jit(solution)/shard_map/ppermute | solution.py:1001
  89.7 2.1 %all-to-all-done.2.planar = bf16[4,128,256]{2,1,0:T(8,128)(2,1)S(1)} async-done(((bf16[4,128,256]{2,1,0:T(8,128)(2,1)}), bf16[4,128,256]{2,1,0:T(8,128)(2,1)S(1)}, u32[]{:S(2)}, u32[]{:S(2)}) %all-to-all-start.2) | async-done | bytes 262176 | tf_op jit(solution)/shard_map/all_to_all | solution.py:1005
  91.7 6.0 %mix_back.1 = (bf16[4,128,256]{2,1,0:T(8,128)(2,1)}, bf16[4,768,128]{2,1,0:T(8,128)(2,1)}) custom-call(bf16[4,128,256]{2,1,0:T(8,128)(2,1)S(1)} %all-to-all-done.2.planar, bf16[1024,2048]{1,0:T(8,128)(2,1)} %bitcast.6, bf16[512,256]{1,0:T(8,128)(2,1)S(1)} %copy-done.6, bf16[256,512]{1,0:T(8,128)(2,1)S(1)} %copy-done.5, bf16[128,128]{1,0:T(8,128)(2,1)S(1)} %copy-done.3, ...), custom_call_target="tpu_custom_call" | custom-call | flops 99999997952 | bytes 100000000 | tf_op jit(solution)/shard_map/mix_back/pallas_call | solution.py:532
  97.8 3.6 %all-to-all-start.3 = ((bf16[4,768,128]{2,1,0:T(8,128)(2,1)}), bf16[4,768,128]{2,1,0:T(8,128)(2,1)S(1)}, u32[]{:S(2)}, u32[]{:S(2)}) async-start(bf16[4,768,128]{2,1,0:T(8,128)(2,1)} %get-tuple-element.49), calls=%async_computation.3 | async-start | bytes 1572864 | tf_op jit(solution)/shard_map/all_to_all | solution.py:1035
  101.4 9.3 %near_inner.1.inner = bf16[32,4,128,128]{3,2,1,0:T(8,128)(2,1)S(1)} custom-call(f32[27,32]{1,0:T(8,128)S(1)} %copy-done.1, bf16[32,8,128,128]{3,2,1,0:T(8,128)(2,1)} %get-tuple-element.50.field), custom_call_target="tpu_custom_call" | custom-call | flops 10000000 | bytes 100000 | tf_op jit(solution)/shard_map/near_inner/pallas_call | solution.py:848
  110.7 2.0 %copy-done = bf16[32,4,128,128]{3,2,1,0:T(8,128)(2,1)} copy-done((bf16[32,4,128,128]{3,2,1,0:T(8,128)(2,1)}, bf16[32,4,128,128]{3,2,1,0:T(8,128)(2,1)S(1)}, u32[]{:S(2)}) %copy-start) | copy-done | bytes 4194328
  112.7 0.3 all-to-all-done.3.gathered
  113.0 0.0 collective-permute-done.4.before
  113.0 0.5 collective-permute-done.5.after
  113.6 3.9 %all-to-all-start.4 = ((bf16[4,128,256]{2,1,0:T(8,128)(2,1)}), bf16[4,128,256]{2,1,0:T(8,128)(2,1)S(1)}, u32[]{:S(2)}, u32[]{:S(2)}) async-start(bf16[4,128,256]{2,1,0:T(8,128)(2,1)} %get-tuple-element.56), calls=%async_computation.4 | async-start | bytes 524288 | tf_op jit(solution)/shard_map/all_to_all | solution.py:1005
  117.5 4.0 %weight_gradient.1 = f32[1024,512]{1,0:T(8,128)} custom-call(bf16[4,768,128]{2,1,0:T(8,128)(2,1)S(1)} %all-to-all-done.3.gathered, bf16[128,512]{1,0:T(8,128)(2,1)S(1)} %copy-done.2, bf16[128,128]{1,0:T(8,128)(2,1)S(1)} %copy-done.3), custom_call_target="tpu_custom_call" | custom-call | flops 10000000 | bytes 100000 | tf_op jit(solution)/shard_map/weight_gradient/pallas_call | solution.py:985
  121.5 5.2 %all-to-all-done.4.planar = bf16[4,128,256]{2,1,0:T(8,128)(2,1)S(1)} async-done(((bf16[4,128,256]{2,1,0:T(8,128)(2,1)}), bf16[4,128,256]{2,1,0:T(8,128)(2,1)S(1)}, u32[]{:S(2)}, u32[]{:S(2)}) %all-to-all-start.4) | async-done | bytes 262176 | tf_op jit(solution)/shard_map/all_to_all | solution.py:1005
  126.7 0.0 copy-done.12
  126.7 0.7 copy-done.11
  127.4 16.3 %finish.1 = bf16[32,8,128,128]{3,2,1,0:T(8,128)(2,1)} custom-call(f32[27,32]{1,0:T(8,128)} %taps.7, bf16[32,1,128,128]{3,2,1,0:T(8,128)(2,1)} %copy-done.12, bf16[32,8,128,128]{3,2,1,0:T(8,128)(2,1)} %get-tuple-element.50.field, bf16[32,1,128,128]{3,2,1,0:T(8,128)(2,1)} %collective-permute-done.5.after, bf16[32,4,128,128]{3,2,1,0:T(8,128)(2,1)} %copy-done, ...), custom_call_target="tpu_custom_call" | custom-call | flops 99999997952 | bytes 100000000 | tf_op jit(solution)/shard_map/finish/pallas_call | solution.py:912
  (10 shorter events, 0.0 us)
Async XLA Ops:
  0.6 26.9 %copy-start.1 = (f32[27,32]{1,0:T(8,128)S(1)}, f32[27,32]{1,0:T(8,128)}, u32[]{:S(2)}) copy-start(f32[27,32]{1,0:T(8,128)} %taps.7) | copy-start | bytes 10372
  3.1 18.9 %collective-permute-start = (bf16[12,1,128,128]{3,2,1,0:T(8,128)(2,1)}, bf16[12,1,128,128]{3,2,1,0:T(8,128)(2,1)S(1)}, u32[]{:S(2)}, u32[]{:S(2)}) collective-permute-start(bf16[12,1,128,128]{3,2,1,0:T(8,128)(2,1)} %get-tuple-element.31), channel_id=1, source_target_pairs={{0,1},{1,2},{2,3},{4,5},{5,6},{6,7},{8,9},{9,10},{10,11},{12,13},{... | collective-permute-start | bytes 1179656 | tf_op jit(solution)/shard_map/ppermute | solution.py:1001
  8.1 13.9 %collective-permute-start.1 = (bf16[12,1,128,128]{3,2,1,0:T(8,128)(2,1)}, bf16[12,1,128,128]{3,2,1,0:T(8,128)(2,1)S(1)}, u32[]{:S(2)}, u32[]{:S(2)}) collective-permute-start(bf16[12,1,128,128]{3,2,1,0:T(8,128)(2,1)} %get-tuple-element.32), channel_id=1, source_target_pairs={{1,0},{2,1},{3,2},{5,4},{6,5},{7,6},{9,8},{10,9},{11,10},{13,12},{... | collective-permute-start | bytes 1179656 | tf_op jit(solution)/shard_map/ppermute | solution.py:1001
  16.1 18.4 %all-to-all-start = ((bf16[4,128,256]{2,1,0:T(8,128)(2,1)}), bf16[4,128,256]{2,1,0:T(8,128)(2,1)S(1)}, u32[]{:S(2)}, u32[]{:S(2)}) async-start(bf16[4,128,256]{2,1,0:T(8,128)(2,1)} %forward_modes.1), calls=%async_computation | async-start | bytes 524288 | tf_op jit(solution)/shard_map/all_to_all | solution.py:1005
  22.0 12.5 %copy-start.5 = (bf16[256,512]{1,0:T(8,128)(2,1)S(1)}, bf16[256,512]{1,0:T(8,128)(2,1)}, u32[]{:S(2)}) copy-start(bf16[256,512]{1,0:T(8,128)(2,1)} %constant.31.clone.z_out) | copy-start | bytes 786436
  22.0 12.5 %copy-start.6 = (bf16[512,256]{1,0:T(8,128)(2,1)S(1)}, bf16[512,256]{1,0:T(8,128)(2,1)}, u32[]{:S(2)}) copy-start(bf16[512,256]{1,0:T(8,128)(2,1)} %constant.30.clone.z_in) | copy-start | bytes 786436
  22.1 12.5 %copy-start.8 = (bf16[128,1024]{1,0:T(8,128)(2,1)S(1)}, bf16[128,1024]{1,0:T(8,128)(2,1)}, u32[]{:S(2)}) copy-start(bf16[128,1024]{1,0:T(8,128)(2,1)} %constant.32.clone.spread_table) | copy-start | bytes 786436
  22.1 12.4 %copy-start.9 = (bf16[128,128]{1,0:T(8,128)(2,1)S(1)}, bf16[128,128]{1,0:T(8,128)(2,1)}, u32[]{:S(2)}) copy-start(bf16[128,128]{1,0:T(8,128)(2,1)} %constant.33.clone.sum_table) | copy-start | bytes 98308
  22.1 24.4 %collective-permute-start.2 = (bf16[20,1,128,128]{3,2,1,0:T(8,128)(2,1)}, bf16[20,1,128,128]{3,2,1,0:T(8,128)(2,1)S(1)}, u32[]{:S(2)}, u32[]{:S(2)}) collective-permute-start(bf16[20,1,128,128]{3,2,1,0:T(8,128)(2,1)} %get-tuple-element.39), channel_id=1, source_target_pairs={{0,1},{1,2},{2,3},{4,5},{5,6},{6,7},{8,9},{9,10},{10,11},{12,13},{... | collective-permute-start | bytes 1966088 | tf_op jit(solution)/shard_map/ppermute | solution.py:1001
  26.2 20.3 %collective-permute-start.3 = (bf16[20,1,128,128]{3,2,1,0:T(8,128)(2,1)}, bf16[20,1,128,128]{3,2,1,0:T(8,128)(2,1)S(1)}, u32[]{:S(2)}, u32[]{:S(2)}) collective-permute-start(bf16[20,1,128,128]{3,2,1,0:T(8,128)(2,1)} %get-tuple-element.40), channel_id=1, source_target_pairs={{1,0},{2,1},{3,2},{5,4},{6,5},{7,6},{9,8},{10,9},{11,10},{13,12},{... | collective-permute-start | bytes 1966088 | tf_op jit(solution)/shard_map/ppermute | solution.py:1001
  34.5 2.2 %copy-start.4 = (bf16[64,16,2048]{2,1,0:T(8,128)(2,1)S(1)}, bf16[64,16,2048]{2,1,0:T(8,128)(2,1)}, u32[]{:S(2)}) copy-start(bf16[64,16,2048]{2,1,0:T(8,128)(2,1)} %param.28) | copy-start | bytes 12582916
  40.7 15.8 %all-to-all-start.1 = ((bf16[4,128,256]{2,1,0:T(8,128)(2,1)}), bf16[4,128,256]{2,1,0:T(8,128)(2,1)S(1)}, u32[]{:S(2)}, u32[]{:S(2)}) async-start(bf16[4,128,256]{2,1,0:T(8,128)(2,1)} %get-tuple-element.38), calls=%async_computation.1 | async-start | bytes 524288 | tf_op jit(solution)/shard_map/all_to_all | solution.py:1005
  56.6 0.7 copy-start.10
  57.3 34.4 %copy-start.3 = (bf16[128,128]{1,0:T(8,128)(2,1)S(1)}, bf16[128,128]{1,0:T(8,128)(2,1)}, u32[]{:S(2)}) copy-start(bf16[128,128]{1,0:T(8,128)(2,1)} %constant.38.clone.spread_table.second) | copy-start | bytes 98308
  57.3 34.4 %copy-start.7 = (bf16[1024,128]{1,0:T(8,128)(2,1)S(1)}, bf16[1024,128]{1,0:T(8,128)(2,1)}, u32[]{:S(2)}) copy-start(bf16[1024,128]{1,0:T(8,128)(2,1)} %constant.39.clone.sum_table) | copy-start | bytes 786436
  79.1 12.6 %all-to-all-start.2 = ((bf16[4,128,256]{2,1,0:T(8,128)(2,1)}), bf16[4,128,256]{2,1,0:T(8,128)(2,1)S(1)}, u32[]{:S(2)}, u32[]{:S(2)}) async-start(bf16[4,128,256]{2,1,0:T(8,128)(2,1)} %get-tuple-element.44), calls=%async_computation.2 | async-start | bytes 524288 | tf_op jit(solution)/shard_map/all_to_all | solution.py:1005
  84.2 28.8 %collective-permute-start.4 = (bf16[32,1,128,128]{3,2,1,0:T(8,128)(2,1)}, bf16[32,1,128,128]{3,2,1,0:T(8,128)(2,1)S(1)}, u32[]{:S(2)}, u32[]{:S(2)}) collective-permute-start(bf16[32,1,128,128]{3,2,1,0:T(8,128)(2,1)} %get-tuple-element.51), channel_id=1, source_target_pairs={{0,1},{1,2},{2,3},{4,5},{5,6},{6,7},{8,9},{9,10},{10,11},{12,13},{... | collective-permute-start | bytes 3145736 | tf_op jit(solution)/shard_map/ppermute | solution.py:1001
  88.2 25.4 %collective-permute-start.5 = (bf16[32,1,128,128]{3,2,1,0:T(8,128)(2,1)}, bf16[32,1,128,128]{3,2,1,0:T(8,128)(2,1)}, u32[]{:S(2)}, u32[]{:S(2)}) collective-permute-start(bf16[32,1,128,128]{3,2,1,0:T(8,128)(2,1)} %get-tuple-element.52), channel_id=1, source_target_pairs={{1,0},{2,1},{3,2},{5,4},{6,5},{7,6},{9,8},{10,9},{11,10},{13,12},{... | collective-permute-start | bytes 3145736 | tf_op jit(solution)/shard_map/ppermute | solution.py:1001
  97.8 19.7 %copy-start.2 = (bf16[128,512]{1,0:T(8,128)(2,1)S(1)}, bf16[128,512]{1,0:T(8,128)(2,1)}, u32[]{:S(2)}) copy-start(bf16[128,512]{1,0:T(8,128)(2,1)} %constant.40.clone.first) | copy-start | bytes 393220
  97.8 15.3 %all-to-all-start.3 = ((bf16[4,768,128]{2,1,0:T(8,128)(2,1)}), bf16[4,768,128]{2,1,0:T(8,128)(2,1)S(1)}, u32[]{:S(2)}, u32[]{:S(2)}) async-start(bf16[4,768,128]{2,1,0:T(8,128)(2,1)} %get-tuple-element.49), calls=%async_computation.3 | async-start | bytes 1572864 | tf_op jit(solution)/shard_map/all_to_all | solution.py:1035
  110.7 2.0 %copy-start = (bf16[32,4,128,128]{3,2,1,0:T(8,128)(2,1)}, bf16[32,4,128,128]{3,2,1,0:T(8,128)(2,1)S(1)}, u32[]{:S(2)}) copy-start(bf16[32,4,128,128]{3,2,1,0:T(8,128)(2,1)S(1)} %near_inner.1.inner) | copy-start | bytes 12582916
  113.0 13.7 %copy-start.12 = (bf16[32,1,128,128]{3,2,1,0:T(8,128)(2,1)}, bf16[32,1,128,128]{3,2,1,0:T(8,128)(2,1)S(1)}, u32[]{:S(2)}) copy-start(bf16[32,1,128,128]{3,2,1,0:T(8,128)(2,1)S(1)} %collective-permute-done.4.before) | copy-start | bytes 3145732
  113.6 13.1 %all-to-all-start.4 = ((bf16[4,128,256]{2,1,0:T(8,128)(2,1)}), bf16[4,128,256]{2,1,0:T(8,128)(2,1)S(1)}, u32[]{:S(2)}, u32[]{:S(2)}) async-start(bf16[4,128,256]{2,1,0:T(8,128)(2,1)} %get-tuple-element.56), calls=%async_computation.4 | async-start | bytes 524288 | tf_op jit(solution)/shard_map/all_to_all | solution.py:1005
  126.7 0.7 copy-start.11

commit v14 on v13

--- a/solution.py
+++ b/solution.py
@@ -292,6 +292,7 @@
 
 LIGHT = pl.CostEstimate(flops=10**7, bytes_accessed=10**5, transcendentals=0)
 HEAVY = pl.CostEstimate(flops=10**11, bytes_accessed=10**8, transcendentals=0)
+MIDDLE = pl.CostEstimate(flops=10**10, bytes_accessed=2 * 10**7, transcendentals=0)
 
 
 def dot(a, b):
@@ -674,7 +675,7 @@
             pltpu.VMEM((8 * channels, 8 * channels), jnp.bfloat16),
             pltpu.VMEM((8 * channels, 8 * channels), jnp.bfloat16),
         ],
-        compiler_params=params(),
+        compiler_params=params(ROOMY),
         cost_estimate=LIGHT,
         name="layer",
     )(bias, planar, smooth, cotangent, grains, point_weight, repeat, ix_table, iy_table, x_table,
@@ -822,7 +823,7 @@
         input_output_aliases={} if done is None else {4: 0},
         scratch_shapes=band_scratch(step),
         compiler_params=params(ROOMY),
-        cost_estimate=LIGHT,
+        cost_estimate=MIDDLE,
         name="smooth_low" if done is None else "smooth_high",
     )(*operands)
 
@@ -855,7 +856,7 @@
         out_specs=pl.BlockSpec((step,) + shape[1:], lambda c: (c, 0, 0, 0)),
         out_shape=jax.ShapeDtypeStruct(shape, jnp.bfloat16),
         scratch_shapes=band_scratch(step),
-        compiler_params=params(ROOMY),
+        compiler_params=params(),
         cost_estimate=LIGHT,
         name="near_inner",
     )(taps, field)
@@ -928,7 +929,7 @@
             pltpu.VMEM((slabs, 2, lines, planes * NY), jnp.bfloat16),
             *band_scratch(step),
         ],
-        compiler_params=params(),
+        compiler_params=params(ROOMY),
         cost_estimate=HEAVY,
         name="finish",
     )(taps, rims[0], spread, rims[1], inner, planar, ix_table, iy_table)
@@ -989,7 +990,7 @@
         out_specs=pl.BlockSpec((depth // steps * half, width), lambda j: (j, 0)),
         out_shape=jax.ShapeDtypeStruct((depth * half, width), jnp.float32),
         compiler_params=params(ROOMY),
-        cost_estimate=LIGHT,
+        cost_estimate=MIDDLE,
         name="weight_gradient",
     )(gathered, first, second)
 

time: 145 us -> 151 us (1.041)
  local copies, waits for them, and re-layouts: 5.67 us -> 11.3 us
    unnamed x26 -> x54, local copies, waits for them, and re-layouts: 5.67 us -> 11.3 us
  transfers between devices with their start and end apart: 11 -> 11, of which waited for: 4 -> 3; matrix products, arithmetic and copies ran while one was open for 0% -> 0% of each run, Pallas kernels for 33% -> 33%
where the time goes in v14:
time: 151 us; the launch traced here: 149 us
  Pallas kernels  86.6 us (57%)
  starting transfers between devices  42.6 us (28%)
  local copies, waits for them, and re-layouts  11.3 us (7%)
  waiting for transfers between devices  7.84 us (5%)
    all_to_all x4, starting transfers between devices, swap(): return lax.all_to_all(planar, 'slab', split_axis=0, concat_axis=0)  21.1 us
    pallas_call x1, Pallas kernels, layer(): pl.pallas_call(layer_kernel, grid=(pairs,), in_specs=[pl.BlockSpec(memory...  20.3 us
    ppermute x6, starting transfers between devices, exchange(): return (lax.ppermute(last, 'slab', up), lax.ppermute(first, 'slab', down))  17.9 us
    pallas_call x2, Pallas kernels, smooth_planes(): pl.pallas_call(functools.partial(smooth_kernel, start), grid=(count // st...  17.4 us
    pallas_call x1, Pallas kernels, finish(): pl.pallas_call(finish_kernel, grid=(channels // step,), in_specs=[pl.Bloc...  15.1 us
    unnamed x54, local copies, waits for them, and re-layouts  11.3 us
    pallas_call x1, Pallas kernels, near_inner(): pl.pallas_call(inner_kernel, grid=(channels // step,), in_specs=[pl.Block...  10.5 us
    pallas_call x2, Pallas kernels, mix(): pl.pallas_call(functools.partial(mixing_kernel, scale_in, scale_out, adjo...  10.1 us
  transfers between devices with their start and end apart: 11, of which 3 were waited for; matrix products, arithmetic and copies ran while one was open for 0% of the time, Pallas kernels for 33%

profile of v14, /device:TPU:0, one launch (start us, length us, event | category | flops | bytes accessed | tf_op | source)
XLA Modules:
  0.0 149.3 jit_solution(3909577570529555558)
XLA Ops:
  0.6 0.0 copy-start.7
  0.6 2.5 %rims.1 = (bf16[12,1,128,128]{3,2,1,0:T(8,128)(2,1)}, bf16[20,1,128,128]{3,2,1,0:T(8,128)(2,1)}, bf16[12,1,128,128]{3,2,1,0:T(8,128)(2,1)}, bf16[20,1,128,128]{3,2,1,0:T(8,128)(2,1)}) custom-call(bf16[32,8,128,128]{3,2,1,0:T(8,128)(2,1)} %bitcast.9), custom_call_target="tpu_custom_call" | custom-call | flops 10000000 | bytes 100000 | tf_op jit(solution)/shard_map/rims/pallas_call | solution.py:363
  3.1 5.0 %collective-permute-start = (bf16[12,1,128,128]{3,2,1,0:T(8,128)(2,1)}, bf16[12,1,128,128]{3,2,1,0:T(8,128)(2,1)S(1)}, u32[]{:S(2)}, u32[]{:S(2)}) collective-permute-start(bf16[12,1,128,128]{3,2,1,0:T(8,128)(2,1)} %get-tuple-element.31), channel_id=1, source_target_pairs={{0,1},{1,2},{2,3},{4,5},{5,6},{6,7},{8,9},{9,10},{10,11},{12,13},{... | collective-permute-start | bytes 1179656 | tf_op jit(solution)/shard_map/ppermute | solution.py:1002
  8.1 1.3 collective-permute-start.1
  9.4 6.7 %forward_modes.1 = bf16[4,128,256]{2,1,0:T(8,128)(2,1)} custom-call(bf16[32,8,128,128]{3,2,1,0:T(8,128)(2,1)} %bitcast.10, bf16[64,256]{1,0:T(8,128)(2,1)} %constant.28.clone.x_table, bf16[2048,256]{1,0:T(8,128)(2,1)} %constant.29.clone.y_table), custom_call_target="tpu_custom_call" | custom-call | flops 10000000 | bytes 100000 | tf_op jit(solution)/shard_map/forward_modes/pallas_call | solution.py:400
  16.1 5.9 %all-to-all-start = ((bf16[4,128,256]{2,1,0:T(8,128)(2,1)}), bf16[4,128,256]{2,1,0:T(8,128)(2,1)S(1)}, u32[]{:S(2)}, u32[]{:S(2)}) async-start(bf16[4,128,256]{2,1,0:T(8,128)(2,1)} %forward_modes.1), calls=%async_computation | async-start | bytes 524288 | tf_op jit(solution)/shard_map/all_to_all | solution.py:1006
  22.0 0.0 collective-permute-done.before
  22.0 0.0 collective-permute-done.1.after
  22.0 0.0 copy-start.15
  22.0 0.0 copy-start.17
  22.0 0.0 copy-start.20
  22.1 0.0 copy-start.24
  22.1 4.9 %collective-permute-start.2 = (bf16[20,1,128,128]{3,2,1,0:T(8,128)(2,1)}, bf16[20,1,128,128]{3,2,1,0:T(8,128)(2,1)}, u32[]{:S(2)}, u32[]{:S(2)}) collective-permute-start(bf16[20,1,128,128]{3,2,1,0:T(8,128)(2,1)} %get-tuple-element.39), channel_id=1, source_target_pairs={{0,1},{1,2},{2,3},{4,5},{5,6},{6,7},{8,9},{9,10},{10,11},{12,13},{... | collective-permute-start | bytes 1966088 | tf_op jit(solution)/shard_map/ppermute | solution.py:1002
  27.0 1.3 collective-permute-start.3
  28.3 7.0 %smooth_low.1.rest_0_ = bf16[4,16,256,256]{3,2,1,0:T(8,128)(2,1)} custom-call(f32[27,32]{1,0:T(8,128)S(1)} %copy-done.7, bf16[12,1,128,128]{3,2,1,0:T(8,128)(2,1)S(1)} %collective-permute-done.before, bf16[32,8,128,128]{3,2,1,0:T(8,128)(2,1)} %bitcast.11, bf16[12,1,128,128]{3,2,1,0:T(8,128)(2,1)S(1)} %collective-permute-done.1.after), custom_call_target="tpu_custom_call" | custom-call | flops 10000000000 | bytes 20000000 | tf_op jit(solution)/shard_map/smooth_low/pallas_call | solution.py:817
  35.3 0.0 copy-start.11
  35.3 2.2 %copy-done.11 = bf16[64,16,2048]{2,1,0:T(8,128)(2,1)S(1)} copy-done((bf16[64,16,2048]{2,1,0:T(8,128)(2,1)S(1)}, bf16[64,16,2048]{2,1,0:T(8,128)(2,1)}, u32[]{:S(2)}) %copy-start.11) | copy-done | bytes 4194328
  37.5 4.0 %mix.1 = (bf16[512,128]{1,0:T(8,128)(2,1)S(1)}, bf16[4,128,256]{2,1,0:T(8,128)(2,1)}) custom-call(bf16[4,128,256]{2,1,0:T(8,128)(2,1)S(1)} %all-to-all-done.planar, bf16[1024,2048]{1,0:T(8,128)(2,1)S(1)} %bitcast.8, bf16[512,256]{1,0:T(8,128)(2,1)S(1)} %copy-done.17, bf16[256,512]{1,0:T(8,128)(2,1)S(1)} %copy-done.15, bf16[128,1024]{1,0:T(8,128)(2,1)S(1)} %copy-done.20, ...), custom_call_target="tpu_custom_call" | custom-call | flops 99999997952 | bytes 100000000 | tf_op jit(solution)/shard_map/mix/pallas_call | solution.py:533
  41.5 0.7 copy-done.25
  42.2 5.7 %all-to-all-start.1 = ((bf16[4,128,256]{2,1,0:T(8,128)(2,1)}), bf16[4,128,256]{2,1,0:T(8,128)(2,1)S(1)}, u32[]{:S(2)}, u32[]{:S(2)}) async-start(bf16[4,128,256]{2,1,0:T(8,128)(2,1)} %get-tuple-element.38), calls=%async_computation.1 | async-start | bytes 524288 | tf_op jit(solution)/shard_map/all_to_all | solution.py:1006
  47.9 0.0 copy-start.3
  47.9 0.0 copy-start.5
  47.9 0.0 copy-start.6
  47.9 0.0 copy-start.9
  47.9 0.0 copy-start.10
  47.9 10.4 %smooth_high.1.smooth = bf16[4,16,256,256]{3,2,1,0:T(8,128)(2,1)} custom-call(f32[27,32]{1,0:T(8,128)S(1)} %copy-done.7, bf16[20,1,128,128]{3,2,1,0:T(8,128)(2,1)} %collective-permute-done.2.before, bf16[32,8,128,128]{3,2,1,0:T(8,128)(2,1)} %bitcast.12, bf16[20,1,128,128]{3,2,1,0:T(8,128)(2,1)} %collective-permute-done.3.after, ...), custom_call_target="tpu_custom_call", output_to_operand_aliasing={{}: (4, {})} | custom-call | flops 10000000000 | bytes 20000000 | tf_op jit(solution)/shard_map/smooth_high/pallas_call | solution.py:817
  58.4 20.3 %layer.1 = (bf16[32,8,128,128]{3,2,1,0:T(8,128)(2,1)}, bf16[4,128,256]{2,1,0:T(8,128)(2,1)S(1)}, bf16[32,1,128,128]{3,2,1,0:T(8,128)(2,1)S(1)}, bf16[32,1,128,128]{3,2,1,0:T(8,128)(2,1)S(1)}) custom-call(f32[32]{0:T(128)S(1)} %copy-done.10, bf16[4,128,256]{2,1,0:T(8,128)(2,1)S(1)} %all-to-all-done.1.planar, bf16[4,16,256,256]{3,2,1,0:T(8,128)(2,1)} %smooth_high.1.smooth, ...), custom_call_target="tpu_custom_call" | custom-call | flops 10000000 | bytes 100000 | tf_op jit(solution)/shard_map/layer/pallas_call | solution.py:650
  78.7 0.7 copy-done.4
  79.5 1.0 copy-done.12
  80.4 1.0 copy-done.13
  81.4 5.1 %all-to-all-start.2 = ((bf16[4,128,256]{2,1,0:T(8,128)(2,1)}), bf16[4,128,256]{2,1,0:T(8,128)(2,1)S(1)}, u32[]{:S(2)}, u32[]{:S(2)}) async-start(bf16[4,128,256]{2,1,0:T(8,128)(2,1)} %copy-done.4), calls=%async_computation.2 | async-start | bytes 524288 | tf_op jit(solution)/shard_map/all_to_all | solution.py:1006
  86.5 4.0 %collective-permute-start.4 = (bf16[32,1,128,128]{3,2,1,0:T(8,128)(2,1)}, bf16[32,1,128,128]{3,2,1,0:T(8,128)(2,1)S(1)}, u32[]{:S(2)}, u32[]{:S(2)}) collective-permute-start(bf16[32,1,128,128]{3,2,1,0:T(8,128)(2,1)} %copy-done.13), channel_id=1, source_target_pairs={{0,1},{1,2},{2,3},{4,5},{5,6},{6,7},{8,9},{9,10},{10,11},{12,13},{... | collective-permute-start | bytes 3145736 | tf_op jit(solution)/shard_map/ppermute | solution.py:1002
  90.5 1.5 collective-permute-start.5
  92.0 2.0 %all-to-all-done.2.planar = bf16[4,128,256]{2,1,0:T(8,128)(2,1)S(1)} async-done(((bf16[4,128,256]{2,1,0:T(8,128)(2,1)}), bf16[4,128,256]{2,1,0:T(8,128)(2,1)S(1)}, u32[]{:S(2)}, u32[]{:S(2)}) %all-to-all-start.2) | async-done | bytes 262176 | tf_op jit(solution)/shard_map/all_to_all | solution.py:1006
  94.0 0.9 copy-done.16
  95.0 0.9 copy-done.18
  95.9 0.9 copy-done.19
  96.9 0.8 copy-done.22
  97.6 0.9 copy-done.26
  98.5 6.1 %mix_back.1 = (bf16[4,128,256]{2,1,0:T(8,128)(2,1)}, bf16[4,768,128]{2,1,0:T(8,128)(2,1)}) custom-call(bf16[4,128,256]{2,1,0:T(8,128)(2,1)S(1)} %all-to-all-done.2.planar, bf16[1024,2048]{1,0:T(8,128)(2,1)} %bitcast.7, bf16[512,256]{1,0:T(8,128)(2,1)S(1)} %copy-done.18, bf16[256,512]{1,0:T(8,128)(2,1)S(1)} %copy-done.16, bf16[128,128]{1,0:T(8,128)(2,1)S(1)} %copy-done.22, ...), custom_call_target="tpu_custom_call" | custom-call | flops 99999997952 | bytes 100000000 | tf_op jit(solution)/shard_map/mix_back/pallas_call | solution.py:533
  104.6 3.6 %all-to-all-start.3 = ((bf16[4,768,128]{2,1,0:T(8,128)(2,1)}), bf16[4,768,128]{2,1,0:T(8,128)(2,1)S(1)}, u32[]{:S(2)}, u32[]{:S(2)}) async-start(bf16[4,768,128]{2,1,0:T(8,128)(2,1)} %get-tuple-element.49), calls=%async_computation.3 | async-start | bytes 1572864 | tf_op jit(solution)/shard_map/all_to_all | solution.py:1036
  108.2 10.5 %near_inner.1.inner = bf16[32,4,128,128]{3,2,1,0:T(8,128)(2,1)} custom-call(f32[27,32]{1,0:T(8,128)} %taps.7, bf16[32,8,128,128]{3,2,1,0:T(8,128)(2,1)} %get-tuple-element.50.field), custom_call_target="tpu_custom_call" | custom-call | flops 10000000 | bytes 100000 | tf_op jit(solution)/shard_map/near_inner/pallas_call | solution.py:849
  118.7 1.2 all-to-all-done.3.gathered
  119.8 4.4 %all-to-all-start.4 = ((bf16[4,128,256]{2,1,0:T(8,128)(2,1)}), bf16[4,128,256]{2,1,0:T(8,128)(2,1)S(1)}, u32[]{:S(2)}, u32[]{:S(2)}) async-start(bf16[4,128,256]{2,1,0:T(8,128)(2,1)} %get-tuple-element.56), calls=%async_computation.4 | async-start | bytes 524288 | tf_op jit(solution)/shard_map/all_to_all | solution.py:1006
  124.2 4.0 %weight_gradient.1 = f32[1024,512]{1,0:T(8,128)} custom-call(bf16[4,768,128]{2,1,0:T(8,128)(2,1)S(1)} %all-to-all-done.3.gathered, bf16[128,512]{1,0:T(8,128)(2,1)S(1)} %copy-done.21, bf16[128,128]{1,0:T(8,128)(2,1)S(1)} %copy-done.23), custom_call_target="tpu_custom_call" | custom-call | flops 10000000000 | bytes 20000000 | tf_op jit(solution)/shard_map/weight_gradient/pallas_call | solution.py:986
  128.3 4.6 %all-to-all-done.4.planar = bf16[4,128,256]{2,1,0:T(8,128)(2,1)S(1)} async-done(((bf16[4,128,256]{2,1,0:T(8,128)(2,1)}), bf16[4,128,256]{2,1,0:T(8,128)(2,1)S(1)}, u32[]{:S(2)}, u32[]{:S(2)}) %all-to-all-start.4) | async-done | bytes 262176 | tf_op jit(solution)/shard_map/all_to_all | solution.py:1006
  132.9 1.2 copy-done.14
  134.1 15.1 %finish.1 = bf16[32,8,128,128]{3,2,1,0:T(8,128)(2,1)} custom-call(f32[27,32]{1,0:T(8,128)S(1)} %copy-done.8, bf16[32,1,128,128]{3,2,1,0:T(8,128)(2,1)S(1)} %collective-permute-done.4.before, bf16[32,8,128,128]{3,2,1,0:T(8,128)(2,1)} %get-tuple-element.50.field, bf16[32,1,128,128]{3,2,1,0:T(8,128)(2,1)} %collective-permute-done.5.after, ...), custom_call_target="tpu_custom_call" | custom-call | flops 99999997952 | bytes 100000000 | tf_op jit(solution)/shard_map/finish/pallas_call | solution.py:913
  (38 shorter events, 0.1 us)
Async XLA Ops:
  0.6 27.7 %copy-start.7 = (f32[27,32]{1,0:T(8,128)S(1)}, f32[27,32]{1,0:T(8,128)}, u32[]{:S(2)}) copy-start(f32[27,32]{1,0:T(8,128)} %taps.7) | copy-start | bytes 10372
  3.1 18.9 %collective-permute-start = (bf16[12,1,128,128]{3,2,1,0:T(8,128)(2,1)}, bf16[12,1,128,128]{3,2,1,0:T(8,128)(2,1)S(1)}, u32[]{:S(2)}, u32[]{:S(2)}) collective-permute-start(bf16[12,1,128,128]{3,2,1,0:T(8,128)(2,1)} %get-tuple-element.31), channel_id=1, source_target_pairs={{0,1},{1,2},{2,3},{4,5},{5,6},{6,7},{8,9},{9,10},{10,11},{12,13},{... | collective-permute-start | bytes 1179656 | tf_op jit(solution)/shard_map/ppermute | solution.py:1002
  8.1 13.9 %collective-permute-start.1 = (bf16[12,1,128,128]{3,2,1,0:T(8,128)(2,1)}, bf16[12,1,128,128]{3,2,1,0:T(8,128)(2,1)S(1)}, u32[]{:S(2)}, u32[]{:S(2)}) collective-permute-start(bf16[12,1,128,128]{3,2,1,0:T(8,128)(2,1)} %get-tuple-element.32), channel_id=1, source_target_pairs={{1,0},{2,1},{3,2},{5,4},{6,5},{7,6},{9,8},{10,9},{11,10},{13,12},{... | collective-permute-start | bytes 1179656 | tf_op jit(solution)/shard_map/ppermute | solution.py:1002
  16.1 19.2 %all-to-all-start = ((bf16[4,128,256]{2,1,0:T(8,128)(2,1)}), bf16[4,128,256]{2,1,0:T(8,128)(2,1)S(1)}, u32[]{:S(2)}, u32[]{:S(2)}) async-start(bf16[4,128,256]{2,1,0:T(8,128)(2,1)} %forward_modes.1), calls=%async_computation | async-start | bytes 524288 | tf_op jit(solution)/shard_map/all_to_all | solution.py:1006
  22.0 13.3 %copy-start.15 = (bf16[256,512]{1,0:T(8,128)(2,1)S(1)}, bf16[256,512]{1,0:T(8,128)(2,1)}, u32[]{:S(2)}) copy-start(bf16[256,512]{1,0:T(8,128)(2,1)} %constant.31.clone.z_out) | copy-start | bytes 786436
  22.0 13.3 %copy-start.17 = (bf16[512,256]{1,0:T(8,128)(2,1)S(1)}, bf16[512,256]{1,0:T(8,128)(2,1)}, u32[]{:S(2)}) copy-start(bf16[512,256]{1,0:T(8,128)(2,1)} %constant.30.clone.z_in) | copy-start | bytes 786436
  22.0 13.3 %copy-start.20 = (bf16[128,1024]{1,0:T(8,128)(2,1)S(1)}, bf16[128,1024]{1,0:T(8,128)(2,1)}, u32[]{:S(2)}) copy-start(bf16[128,1024]{1,0:T(8,128)(2,1)} %constant.32.clone.spread_table) | copy-start | bytes 786436
  22.1 13.3 %copy-start.24 = (bf16[128,128]{1,0:T(8,128)(2,1)S(1)}, bf16[128,128]{1,0:T(8,128)(2,1)}, u32[]{:S(2)}) copy-start(bf16[128,128]{1,0:T(8,128)(2,1)} %constant.33.clone.sum_table) | copy-start | bytes 98308
  22.1 25.8 %collective-permute-start.2 = (bf16[20,1,128,128]{3,2,1,0:T(8,128)(2,1)}, bf16[20,1,128,128]{3,2,1,0:T(8,128)(2,1)}, u32[]{:S(2)}, u32[]{:S(2)}) collective-permute-start(bf16[20,1,128,128]{3,2,1,0:T(8,128)(2,1)} %get-tuple-element.39), channel_id=1, source_target_pairs={{0,1},{1,2},{2,3},{4,5},{5,6},{6,7},{8,9},{9,10},{10,11},{12,13},{... | collective-permute-start | bytes 1966088 | tf_op jit(solution)/shard_map/ppermute | solution.py:1002
  27.0 20.9 %collective-permute-start.3 = (bf16[20,1,128,128]{3,2,1,0:T(8,128)(2,1)}, bf16[20,1,128,128]{3,2,1,0:T(8,128)(2,1)}, u32[]{:S(2)}, u32[]{:S(2)}) collective-permute-start(bf16[20,1,128,128]{3,2,1,0:T(8,128)(2,1)} %get-tuple-element.40), channel_id=1, source_target_pairs={{1,0},{2,1},{3,2},{5,4},{6,5},{7,6},{9,8},{10,9},{11,10},{13,12},{... | collective-permute-start | bytes 1966088 | tf_op jit(solution)/shard_map/ppermute | solution.py:1002
  35.3 2.2 %copy-start.11 = (bf16[64,16,2048]{2,1,0:T(8,128)(2,1)S(1)}, bf16[64,16,2048]{2,1,0:T(8,128)(2,1)}, u32[]{:S(2)}) copy-start(bf16[64,16,2048]{2,1,0:T(8,128)(2,1)} %param.28) | copy-start | bytes 12582916
  41.5 0.7 copy-start.25
  42.2 16.2 %all-to-all-start.1 = ((bf16[4,128,256]{2,1,0:T(8,128)(2,1)}), bf16[4,128,256]{2,1,0:T(8,128)(2,1)S(1)}, u32[]{:S(2)}, u32[]{:S(2)}) async-start(bf16[4,128,256]{2,1,0:T(8,128)(2,1)} %get-tuple-element.38), calls=%async_computation.1 | async-start | bytes 524288 | tf_op jit(solution)/shard_map/all_to_all | solution.py:1006
  47.8 10.5 %copy-start = (bf16[2048,256]{1,0:T(8,128)(2,1)S(1)}, bf16[2048,256]{1,0:T(8,128)(2,1)}, u32[]{:S(2)}) copy-start(bf16[2048,256]{1,0:T(8,128)(2,1)} %constant.29.clone.y_table) | copy-start | bytes 3145732
  47.9 10.5 %copy-start.1 = (bf16[4,256,512]{2,1,0:T(8,128)(2,1)S(1)}, bf16[4,256,512]{2,1,0:T(8,128)(2,1)}, u32[]{:S(2)}) copy-start(bf16[4,256,512]{2,1,0:T(8,128)(2,1)} %constant.36.clone.iy_table) | copy-start | bytes 3145732
  47.9 10.5 %copy-start.2 = (s32[1,8,128,128]{3,2,1,0:T(8,128)S(1)}, s32[1,8,128,128]{3,2,1,0:T(8,128)}, u32[]{:S(2)}) copy-start(s32[1,8,128,128]{3,2,1,0:T(8,128)} %param.27) | copy-start | bytes 1572868
  47.9 10.5 %copy-start.3 = (bf16[1024,256]{1,0:T(8,128)(2,1)S(1)}, bf16[1024,256]{1,0:T(8,128)(2,1)}, u32[]{:S(2)}) copy-start(bf16[1024,256]{1,0:T(8,128)(2,1)} %constant.35.clone.ix_table) | copy-start | bytes 1572868
  47.9 10.5 %copy-start.5 = (bf16[256,32]{1,0:T(8,128)(2,1)S(1)}, bf16[256,32]{1,0:T(8,128)(2,1)}, u32[]{:S(2)}) copy-start(bf16[256,32]{1,0:T(8,128)(2,1)} %constant.34.clone.repeat) | copy-start | bytes 49156
  47.9 10.5 %copy-start.6 = (bf16[64,256]{1,0:T(8,128)(2,1)S(1)}, bf16[64,256]{1,0:T(8,128)(2,1)}, u32[]{:S(2)}) copy-start(bf16[64,256]{1,0:T(8,128)(2,1)} %constant.37.clone.x_table) | copy-start | bytes 98308
  47.9 10.5 %copy-start.9 = (bf16[32,32]{1,0:T(8,128)(2,1)S(1)}, bf16[32,32]{1,0:T(8,128)(2,1)}, u32[]{:S(2)}) copy-start(bf16[32,32]{1,0:T(8,128)(2,1)} %point_weight.1) | copy-start | bytes 6148
  47.9 10.5 %copy-start.10 = (f32[32]{0:T(128)S(1)}, f32[32]{0:T(128)}, u32[]{:S(2)}) copy-start(f32[32]{0:T(128)} %bias.1) | copy-start | bytes 388
  78.7 0.7 copy-start.4
  79.5 1.0 copy-start.12
  80.4 1.0 copy-start.13
  81.4 12.6 %all-to-all-start.2 = ((bf16[4,128,256]{2,1,0:T(8,128)(2,1)}), bf16[4,128,256]{2,1,0:T(8,128)(2,1)S(1)}, u32[]{:S(2)}, u32[]{:S(2)}) async-start(bf16[4,128,256]{2,1,0:T(8,128)(2,1)} %copy-done.4), calls=%async_computation.2 | async-start | bytes 524288 | tf_op jit(solution)/shard_map/all_to_all | solution.py:1006
  86.5 33.3 %collective-permute-start.4 = (bf16[32,1,128,128]{3,2,1,0:T(8,128)(2,1)}, bf16[32,1,128,128]{3,2,1,0:T(8,128)(2,1)S(1)}, u32[]{:S(2)}, u32[]{:S(2)}) collective-permute-start(bf16[32,1,128,128]{3,2,1,0:T(8,128)(2,1)} %copy-done.13), channel_id=1, source_target_pairs={{0,1},{1,2},{2,3},{4,5},{5,6},{6,7},{8,9},{9,10},{10,11},{12,13},{... | collective-permute-start | bytes 3145736 | tf_op jit(solution)/shard_map/ppermute | solution.py:1002
  90.5 29.4 %collective-permute-start.5 = (bf16[32,1,128,128]{3,2,1,0:T(8,128)(2,1)}, bf16[32,1,128,128]{3,2,1,0:T(8,128)(2,1)}, u32[]{:S(2)}, u32[]{:S(2)}) collective-permute-start(bf16[32,1,128,128]{3,2,1,0:T(8,128)(2,1)} %copy-done.12), channel_id=1, source_target_pairs={{1,0},{2,1},{3,2},{5,4},{6,5},{7,6},{9,8},{10,9},{11,10},{13,12},{... | collective-permute-start | bytes 3145736 | tf_op jit(solution)/shard_map/ppermute | solution.py:1002
  94.0 1.0 copy-start.16
  94.9 0.9 copy-start.18
  95.9 0.9 copy-start.19
  96.8 0.8 copy-start.22
  97.6 0.9 copy-start.26
  104.6 19.7 %copy-start.21 = (bf16[128,512]{1,0:T(8,128)(2,1)S(1)}, bf16[128,512]{1,0:T(8,128)(2,1)}, u32[]{:S(2)}) copy-start(bf16[128,512]{1,0:T(8,128)(2,1)} %constant.40.clone.first) | copy-start | bytes 393220
  104.6 19.7 %copy-start.23 = (bf16[128,128]{1,0:T(8,128)(2,1)S(1)}, bf16[128,128]{1,0:T(8,128)(2,1)}, u32[]{:S(2)}) copy-start(bf16[128,128]{1,0:T(8,128)(2,1)} %constant.38.clone.spread_table.second) | copy-start | bytes 98308
  104.6 15.3 %all-to-all-start.3 = ((bf16[4,768,128]{2,1,0:T(8,128)(2,1)}), bf16[4,768,128]{2,1,0:T(8,128)(2,1)S(1)}, u32[]{:S(2)}, u32[]{:S(2)}) async-start(bf16[4,768,128]{2,1,0:T(8,128)(2,1)} %get-tuple-element.49), calls=%async_computation.3 | async-start | bytes 1572864 | tf_op jit(solution)/shard_map/all_to_all | solution.py:1036
  119.8 13.1 %all-to-all-start.4 = ((bf16[4,128,256]{2,1,0:T(8,128)(2,1)}), bf16[4,128,256]{2,1,0:T(8,128)(2,1)S(1)}, u32[]{:S(2)}, u32[]{:S(2)}) async-start(bf16[4,128,256]{2,1,0:T(8,128)(2,1)} %get-tuple-element.56), calls=%async_computation.4 | async-start | bytes 524288 | tf_op jit(solution)/shard_map/all_to_all | solution.py:1006
  124.2 8.7 %copy-start.8 = (f32[27,32]{1,0:T(8,128)S(1)}, f32[27,32]{1,0:T(8,128)}, u32[]{:S(2)}) copy-start(f32[27,32]{1,0:T(8,128)} %taps.7) | copy-start | bytes 10372
  132.9 1.2 copy-start.14

commit v15 on v13

--- a/solution.py
+++ b/solution.py
@@ -855,7 +855,7 @@
         out_specs=pl.BlockSpec((step,) + shape[1:], lambda c: (c, 0, 0, 0)),
         out_shape=jax.ShapeDtypeStruct(shape, jnp.bfloat16),
         scratch_shapes=band_scratch(step),
-        compiler_params=params(ROOMY),
+        compiler_params=params(),
         cost_estimate=LIGHT,
         name="near_inner",
     )(taps, field)
@@ -928,7 +928,7 @@
             pltpu.VMEM((slabs, 2, lines, planes * NY), jnp.bfloat16),
             *band_scratch(step),
         ],
-        compiler_params=params(),
+        compiler_params=params(ROOMY),
         cost_estimate=HEAVY,
         name="finish",
     )(taps, rims[0], spread, rims[1], inner, planar, ix_table, iy_table)

time: 145 us -> 144 us (level)
  local copies, waits for them, and re-layouts: 5.67 us -> 4.19 us
    unnamed x26, local copies, waits for them, and re-layouts: 5.67 us -> 4.19 us
  transfers between devices with their start and end apart: 11 -> 11, of which waited for: 4 -> 4; matrix products, arithmetic and copies ran while one was open for 0% -> 0% of each run, Pallas kernels for 33% -> 34%
where the time goes in v15:
time: 144 us; the launch traced here: 142 us
  Pallas kernels  87.8 us (61%)
  starting transfers between devices  41.3 us (29%)
  waiting for transfers between devices  8.38 us (6%)
  local copies, waits for them, and re-layouts  4.19 us (3%)
    pallas_call x1, Pallas kernels, layer(): pl.pallas_call(layer_kernel, grid=(pairs,), in_specs=[pl.BlockSpec(memory...  21.8 us
    all_to_all x4, starting transfers between devices, swap(): return lax.all_to_all(planar, 'slab', split_axis=0, concat_axis=0)  20.6 us
    pallas_call x2, Pallas kernels, smooth_planes(): pl.pallas_call(functools.partial(smooth_kernel, start), grid=(count // st...  17.1 us
    ppermute x6, starting transfers between devices, exchange(): return (lax.ppermute(last, 'slab', up), lax.ppermute(first, 'slab', down))  17.1 us
    pallas_call x1, Pallas kernels, finish(): pl.pallas_call(finish_kernel, grid=(channels // step,), in_specs=[pl.Bloc...  15.1 us
    pallas_call x1, Pallas kernels, near_inner(): pl.pallas_call(inner_kernel, grid=(channels // step,), in_specs=[pl.Block...  10.5 us
    pallas_call x2, Pallas kernels, mix(): pl.pallas_call(functools.partial(mixing_kernel, scale_in, scale_out, adjo...  10 us
    all_to_all x4, waiting for transfers between devices, swap(): return lax.all_to_all(planar, 'slab', split_axis=0, concat_axis=0)  6.71 us
  transfers between devices with their start and end apart: 11, of which 4 were waited for; matrix products, arithmetic and copies ran while one was open for 0% of the time, Pallas kernels for 34%

profile of v15, /device:TPU:0, one launch (start us, length us, event | category | flops | bytes accessed | tf_op | source)
XLA Modules:
  0.0 142.5 jit_solution(14807192626997418497)
XLA Ops:
  0.6 0.0 copy-start.1
  0.6 2.5 %rims.1 = (bf16[12,1,128,128]{3,2,1,0:T(8,128)(2,1)}, bf16[20,1,128,128]{3,2,1,0:T(8,128)(2,1)}, bf16[12,1,128,128]{3,2,1,0:T(8,128)(2,1)}, bf16[20,1,128,128]{3,2,1,0:T(8,128)(2,1)}) custom-call(bf16[32,8,128,128]{3,2,1,0:T(8,128)(2,1)} %bitcast.8), custom_call_target="tpu_custom_call" | custom-call | flops 10000000 | bytes 100000 | tf_op jit(solution)/shard_map/rims/pallas_call | solution.py:362
  3.1 5.0 %collective-permute-start = (bf16[12,1,128,128]{3,2,1,0:T(8,128)(2,1)}, bf16[12,1,128,128]{3,2,1,0:T(8,128)(2,1)S(1)}, u32[]{:S(2)}, u32[]{:S(2)}) collective-permute-start(bf16[12,1,128,128]{3,2,1,0:T(8,128)(2,1)} %get-tuple-element.31), channel_id=1, source_target_pairs={{0,1},{1,2},{2,3},{4,5},{5,6},{6,7},{8,9},{9,10},{10,11},{12,13},{... | collective-permute-start | bytes 1179656 | tf_op jit(solution)/shard_map/ppermute | solution.py:1001
  8.1 1.3 collective-permute-start.1
  9.4 6.7 %forward_modes.1 = bf16[4,128,256]{2,1,0:T(8,128)(2,1)} custom-call(bf16[32,8,128,128]{3,2,1,0:T(8,128)(2,1)} %bitcast.9, bf16[64,256]{1,0:T(8,128)(2,1)} %constant.28.clone.x_table, bf16[2048,256]{1,0:T(8,128)(2,1)} %constant.29.clone.y_table), custom_call_target="tpu_custom_call" | custom-call | flops 10000000 | bytes 100000 | tf_op jit(solution)/shard_map/forward_modes/pallas_call | solution.py:399
  16.1 5.9 %all-to-all-start = ((bf16[4,128,256]{2,1,0:T(8,128)(2,1)}), bf16[4,128,256]{2,1,0:T(8,128)(2,1)S(1)}, u32[]{:S(2)}, u32[]{:S(2)}) async-start(bf16[4,128,256]{2,1,0:T(8,128)(2,1)} %forward_modes.1), calls=%async_computation | async-start | bytes 524288 | tf_op jit(solution)/shard_map/all_to_all | solution.py:1005
  22.0 0.0 collective-permute-done.before
  22.0 0.0 collective-permute-done.1.after
  22.0 0.0 copy-start.7
  22.0 0.0 copy-start.8
  22.1 0.0 copy-start.10
  22.1 0.0 copy-start.11
  22.1 4.1 %collective-permute-start.2 = (bf16[20,1,128,128]{3,2,1,0:T(8,128)(2,1)}, bf16[20,1,128,128]{3,2,1,0:T(8,128)(2,1)S(1)}, u32[]{:S(2)}, u32[]{:S(2)}) collective-permute-start(bf16[20,1,128,128]{3,2,1,0:T(8,128)(2,1)} %get-tuple-element.39), channel_id=1, source_target_pairs={{0,1},{1,2},{2,3},{4,5},{5,6},{6,7},{8,9},{9,10},{10,11},{12,13},{... | collective-permute-start | bytes 1966088 | tf_op jit(solution)/shard_map/ppermute | solution.py:1001
  26.2 1.3 collective-permute-start.3
  27.5 0.0 copy-done.1
  27.5 7.0 %smooth_low.1.rest_0_ = bf16[4,16,256,256]{3,2,1,0:T(8,128)(2,1)} custom-call(f32[27,32]{1,0:T(8,128)S(1)} %copy-done.1, bf16[12,1,128,128]{3,2,1,0:T(8,128)(2,1)S(1)} %collective-permute-done.before, bf16[32,8,128,128]{3,2,1,0:T(8,128)(2,1)} %bitcast.10, bf16[12,1,128,128]{3,2,1,0:T(8,128)(2,1)S(1)} %collective-permute-done.1.after), custom_call_target="tpu_custom_call" | custom-call | flops 10000000 | bytes 100000 | tf_op jit(solution)/shard_map/smooth_low/pallas_call | solution.py:816
  34.5 0.0 all-to-all-done.planar
  34.5 0.0 copy-done.7
  34.5 0.0 copy-done.8
  34.5 0.0 copy-done.10
  34.5 0.0 copy-start.5
  34.5 2.2 %copy-done.5 = bf16[64,16,2048]{2,1,0:T(8,128)(2,1)S(1)} copy-done((bf16[64,16,2048]{2,1,0:T(8,128)(2,1)S(1)}, bf16[64,16,2048]{2,1,0:T(8,128)(2,1)}, u32[]{:S(2)}) %copy-start.5) | copy-done | bytes 4194328
  36.7 4.0 %mix.1 = (bf16[512,128]{1,0:T(8,128)(2,1)S(1)}, bf16[4,128,256]{2,1,0:T(8,128)(2,1)}) custom-call(bf16[4,128,256]{2,1,0:T(8,128)(2,1)S(1)} %all-to-all-done.planar, bf16[1024,2048]{1,0:T(8,128)(2,1)S(1)} %bitcast.7, bf16[512,256]{1,0:T(8,128)(2,1)S(1)} %copy-done.8, bf16[256,512]{1,0:T(8,128)(2,1)S(1)} %copy-done.7, bf16[128,1024]{1,0:T(8,128)(2,1)S(1)} %copy-done.10, ...), custom_call_target="tpu_custom_call" | custom-call | flops 99999997952 | bytes 100000000 | tf_op jit(solution)/shard_map/mix/pallas_call | solution.py:532
  40.7 5.7 %all-to-all-start.1 = ((bf16[4,128,256]{2,1,0:T(8,128)(2,1)}), bf16[4,128,256]{2,1,0:T(8,128)(2,1)S(1)}, u32[]{:S(2)}, u32[]{:S(2)}) async-start(bf16[4,128,256]{2,1,0:T(8,128)(2,1)} %get-tuple-element.38), calls=%async_computation.1 | async-start | bytes 524288 | tf_op jit(solution)/shard_map/all_to_all | solution.py:1005
  46.4 0.0 collective-permute-done.2.before
  46.4 0.0 collective-permute-done.3.after
  46.4 10.1 %smooth_high.1.smooth = bf16[4,16,256,256]{3,2,1,0:T(8,128)(2,1)} custom-call(f32[27,32]{1,0:T(8,128)S(1)} %copy-done.1, bf16[20,1,128,128]{3,2,1,0:T(8,128)(2,1)S(1)} %collective-permute-done.2.before, bf16[32,8,128,128]{3,2,1,0:T(8,128)(2,1)} %bitcast.11, ...), custom_call_target="tpu_custom_call", output_to_operand_aliasing={{}: (4, {})} | custom-call | flops 10000000 | bytes 100000 | tf_op jit(solution)/shard_map/smooth_high/pallas_call | solution.py:816
  56.6 0.0 all-to-all-done.1.planar
  56.6 0.7 copy-done.12
  57.3 21.8 %layer.1 = (bf16[32,8,128,128]{3,2,1,0:T(8,128)(2,1)}, bf16[4,128,256]{2,1,0:T(8,128)(2,1)}, bf16[32,1,128,128]{3,2,1,0:T(8,128)(2,1)}, bf16[32,1,128,128]{3,2,1,0:T(8,128)(2,1)}) custom-call(f32[32]{0:T(128)} %bias.1, bf16[4,128,256]{2,1,0:T(8,128)(2,1)} %copy-done.12, bf16[4,16,256,256]{3,2,1,0:T(8,128)(2,1)} %smooth_high.1.smooth, ...), custom_call_target="tpu_custom_call" | custom-call | flops 10000000 | bytes 100000 | tf_op jit(solution)/shard_map/layer/pallas_call | solution.py:649
  79.1 5.1 %all-to-all-start.2 = ((bf16[4,128,256]{2,1,0:T(8,128)(2,1)}), bf16[4,128,256]{2,1,0:T(8,128)(2,1)S(1)}, u32[]{:S(2)}, u32[]{:S(2)}) async-start(bf16[4,128,256]{2,1,0:T(8,128)(2,1)} %get-tuple-element.44), calls=%async_computation.2 | async-start | bytes 524288 | tf_op jit(solution)/shard_map/all_to_all | solution.py:1005
  84.2 4.0 %collective-permute-start.4 = (bf16[32,1,128,128]{3,2,1,0:T(8,128)(2,1)}, bf16[32,1,128,128]{3,2,1,0:T(8,128)(2,1)S(1)}, u32[]{:S(2)}, u32[]{:S(2)}) collective-permute-start(bf16[32,1,128,128]{3,2,1,0:T(8,128)(2,1)} %get-tuple-element.51), channel_id=1, source_target_pairs={{0,1},{1,2},{2,3},{4,5},{5,6},{6,7},{8,9},{9,10},{10,11},{12,13},{... | collective-permute-start | bytes 3145736 | tf_op jit(solution)/shard_map/ppermute | solution.py:1001
  88.2 1.5 %collective-permute-start.5 = (bf16[32,1,128,128]{3,2,1,0:T(8,128)(2,1)}, bf16[32,1,128,128]{3,2,1,0:T(8,128)(2,1)}, u32[]{:S(2)}, u32[]{:S(2)}) collective-permute-start(bf16[32,1,128,128]{3,2,1,0:T(8,128)(2,1)} %get-tuple-element.52), channel_id=1, source_target_pairs={{1,0},{2,1},{3,2},{5,4},{6,5},{7,6},{9,8},{10,9},{11,10},{13,12},{... | collective-permute-start | bytes 3145736 | tf_op jit(solution)/shard_map/ppermute | solution.py:1001
  89.7 2.1 %all-to-all-done.2.planar = bf16[4,128,256]{2,1,0:T(8,128)(2,1)S(1)} async-done(((bf16[4,128,256]{2,1,0:T(8,128)(2,1)}), bf16[4,128,256]{2,1,0:T(8,128)(2,1)S(1)}, u32[]{:S(2)}, u32[]{:S(2)}) %all-to-all-start.2) | async-done | bytes 262176 | tf_op jit(solution)/shard_map/all_to_all | solution.py:1005
  91.7 6.0 %mix_back.1 = (bf16[4,128,256]{2,1,0:T(8,128)(2,1)}, bf16[4,768,128]{2,1,0:T(8,128)(2,1)}) custom-call(bf16[4,128,256]{2,1,0:T(8,128)(2,1)S(1)} %all-to-all-done.2.planar, bf16[1024,2048]{1,0:T(8,128)(2,1)} %bitcast.6, bf16[512,256]{1,0:T(8,128)(2,1)S(1)} %copy-done.8, bf16[256,512]{1,0:T(8,128)(2,1)S(1)} %copy-done.7, bf16[128,128]{1,0:T(8,128)(2,1)S(1)} %copy-done.4, ...), custom_call_target="tpu_custom_call" | custom-call | flops 99999997952 | bytes 100000000 | tf_op jit(solution)/shard_map/mix_back/pallas_call | solution.py:532
  97.8 3.6 %all-to-all-start.3 = ((bf16[4,768,128]{2,1,0:T(8,128)(2,1)}), bf16[4,768,128]{2,1,0:T(8,128)(2,1)S(1)}, u32[]{:S(2)}, u32[]{:S(2)}) async-start(bf16[4,768,128]{2,1,0:T(8,128)(2,1)} %get-tuple-element.49), calls=%async_computation.3 | async-start | bytes 1572864 | tf_op jit(solution)/shard_map/all_to_all | solution.py:1035
  101.4 0.0 copy-start
  101.4 0.0 copy-start.2
  101.4 10.5 %near_inner.1.inner = bf16[32,4,128,128]{3,2,1,0:T(8,128)(2,1)} custom-call(f32[27,32]{1,0:T(8,128)} %taps.7, bf16[32,8,128,128]{3,2,1,0:T(8,128)(2,1)} %get-tuple-element.50.field), custom_call_target="tpu_custom_call" | custom-call | flops 10000000 | bytes 100000 | tf_op jit(solution)/shard_map/near_inner/pallas_call | solution.py:848
  111.9 1.1 all-to-all-done.3.gathered
  113.0 0.0 collective-permute-done.4.before
  113.0 0.5 collective-permute-done.5.after
  113.6 3.9 %all-to-all-start.4 = ((bf16[4,128,256]{2,1,0:T(8,128)(2,1)}), bf16[4,128,256]{2,1,0:T(8,128)(2,1)S(1)}, u32[]{:S(2)}, u32[]{:S(2)}) async-start(bf16[4,128,256]{2,1,0:T(8,128)(2,1)} %get-tuple-element.56), calls=%async_computation.4 | async-start | bytes 524288 | tf_op jit(solution)/shard_map/all_to_all | solution.py:1005
  117.5 4.0 %weight_gradient.1 = f32[1024,512]{1,0:T(8,128)} custom-call(bf16[4,768,128]{2,1,0:T(8,128)(2,1)S(1)} %all-to-all-done.3.gathered, bf16[128,512]{1,0:T(8,128)(2,1)S(1)} %copy-done.3, bf16[128,128]{1,0:T(8,128)(2,1)S(1)} %copy-done.4), custom_call_target="tpu_custom_call" | custom-call | flops 10000000 | bytes 100000 | tf_op jit(solution)/shard_map/weight_gradient/pallas_call | solution.py:985
  121.5 4.6 %all-to-all-done.4.planar = bf16[4,128,256]{2,1,0:T(8,128)(2,1)S(1)} async-done(((bf16[4,128,256]{2,1,0:T(8,128)(2,1)}), bf16[4,128,256]{2,1,0:T(8,128)(2,1)S(1)}, u32[]{:S(2)}, u32[]{:S(2)}) %all-to-all-start.4) | async-done | bytes 262176 | tf_op jit(solution)/shard_map/all_to_all | solution.py:1005
  126.1 0.0 copy-done.2
  126.1 1.2 copy-done.6
  127.4 15.1 %finish.1 = bf16[32,8,128,128]{3,2,1,0:T(8,128)(2,1)} custom-call(f32[27,32]{1,0:T(8,128)S(1)} %copy-done.2, bf16[32,1,128,128]{3,2,1,0:T(8,128)(2,1)S(1)} %collective-permute-done.4.before, bf16[32,8,128,128]{3,2,1,0:T(8,128)(2,1)} %get-tuple-element.50.field, bf16[32,1,128,128]{3,2,1,0:T(8,128)(2,1)} %collective-permute-done.5.after, ...), custom_call_target="tpu_custom_call" | custom-call | flops 99999997952 | bytes 100000000 | tf_op jit(solution)/shard_map/finish/pallas_call | solution.py:912
  (10 shorter events, 0.0 us)
Async XLA Ops:
  0.6 26.9 %copy-start.1 = (f32[27,32]{1,0:T(8,128)S(1)}, f32[27,32]{1,0:T(8,128)}, u32[]{:S(2)}) copy-start(f32[27,32]{1,0:T(8,128)} %taps.7) | copy-start | bytes 10372
  3.1 18.9 %collective-permute-start = (bf16[12,1,128,128]{3,2,1,0:T(8,128)(2,1)}, bf16[12,1,128,128]{3,2,1,0:T(8,128)(2,1)S(1)}, u32[]{:S(2)}, u32[]{:S(2)}) collective-permute-start(bf16[12,1,128,128]{3,2,1,0:T(8,128)(2,1)} %get-tuple-element.31), channel_id=1, source_target_pairs={{0,1},{1,2},{2,3},{4,5},{5,6},{6,7},{8,9},{9,10},{10,11},{12,13},{... | collective-permute-start | bytes 1179656 | tf_op jit(solution)/shard_map/ppermute | solution.py:1001
  8.1 13.9 %collective-permute-start.1 = (bf16[12,1,128,128]{3,2,1,0:T(8,128)(2,1)}, bf16[12,1,128,128]{3,2,1,0:T(8,128)(2,1)S(1)}, u32[]{:S(2)}, u32[]{:S(2)}) collective-permute-start(bf16[12,1,128,128]{3,2,1,0:T(8,128)(2,1)} %get-tuple-element.32), channel_id=1, source_target_pairs={{1,0},{2,1},{3,2},{5,4},{6,5},{7,6},{9,8},{10,9},{11,10},{13,12},{... | collective-permute-start | bytes 1179656 | tf_op jit(solution)/shard_map/ppermute | solution.py:1001
  16.1 18.4 %all-to-all-start = ((bf16[4,128,256]{2,1,0:T(8,128)(2,1)}), bf16[4,128,256]{2,1,0:T(8,128)(2,1)S(1)}, u32[]{:S(2)}, u32[]{:S(2)}) async-start(bf16[4,128,256]{2,1,0:T(8,128)(2,1)} %forward_modes.1), calls=%async_computation | async-start | bytes 524288 | tf_op jit(solution)/shard_map/all_to_all | solution.py:1005
  22.0 12.5 %copy-start.7 = (bf16[256,512]{1,0:T(8,128)(2,1)S(1)}, bf16[256,512]{1,0:T(8,128)(2,1)}, u32[]{:S(2)}) copy-start(bf16[256,512]{1,0:T(8,128)(2,1)} %constant.31.clone.z_out) | copy-start | bytes 786436
  22.0 12.5 %copy-start.8 = (bf16[512,256]{1,0:T(8,128)(2,1)S(1)}, bf16[512,256]{1,0:T(8,128)(2,1)}, u32[]{:S(2)}) copy-start(bf16[512,256]{1,0:T(8,128)(2,1)} %constant.30.clone.z_in) | copy-start | bytes 786436
  22.1 12.5 %copy-start.10 = (bf16[128,1024]{1,0:T(8,128)(2,1)S(1)}, bf16[128,1024]{1,0:T(8,128)(2,1)}, u32[]{:S(2)}) copy-start(bf16[128,1024]{1,0:T(8,128)(2,1)} %constant.32.clone.spread_table) | copy-start | bytes 786436
  22.1 12.4 %copy-start.11 = (bf16[128,128]{1,0:T(8,128)(2,1)S(1)}, bf16[128,128]{1,0:T(8,128)(2,1)}, u32[]{:S(2)}) copy-start(bf16[128,128]{1,0:T(8,128)(2,1)} %constant.33.clone.sum_table) | copy-start | bytes 98308
  22.1 24.4 %collective-permute-start.2 = (bf16[20,1,128,128]{3,2,1,0:T(8,128)(2,1)}, bf16[20,1,128,128]{3,2,1,0:T(8,128)(2,1)S(1)}, u32[]{:S(2)}, u32[]{:S(2)}) collective-permute-start(bf16[20,1,128,128]{3,2,1,0:T(8,128)(2,1)} %get-tuple-element.39), channel_id=1, source_target_pairs={{0,1},{1,2},{2,3},{4,5},{5,6},{6,7},{8,9},{9,10},{10,11},{12,13},{... | collective-permute-start | bytes 1966088 | tf_op jit(solution)/shard_map/ppermute | solution.py:1001
  26.2 20.3 %collective-permute-start.3 = (bf16[20,1,128,128]{3,2,1,0:T(8,128)(2,1)}, bf16[20,1,128,128]{3,2,1,0:T(8,128)(2,1)S(1)}, u32[]{:S(2)}, u32[]{:S(2)}) collective-permute-start(bf16[20,1,128,128]{3,2,1,0:T(8,128)(2,1)} %get-tuple-element.40), channel_id=1, source_target_pairs={{1,0},{2,1},{3,2},{5,4},{6,5},{7,6},{9,8},{10,9},{11,10},{13,12},{... | collective-permute-start | bytes 1966088 | tf_op jit(solution)/shard_map/ppermute | solution.py:1001
  34.5 2.2 %copy-start.5 = (bf16[64,16,2048]{2,1,0:T(8,128)(2,1)S(1)}, bf16[64,16,2048]{2,1,0:T(8,128)(2,1)}, u32[]{:S(2)}) copy-start(bf16[64,16,2048]{2,1,0:T(8,128)(2,1)} %param.28) | copy-start | bytes 12582916
  40.7 15.8 %all-to-all-start.1 = ((bf16[4,128,256]{2,1,0:T(8,128)(2,1)}), bf16[4,128,256]{2,1,0:T(8,128)(2,1)S(1)}, u32[]{:S(2)}, u32[]{:S(2)}) async-start(bf16[4,128,256]{2,1,0:T(8,128)(2,1)} %get-tuple-element.38), calls=%async_computation.1 | async-start | bytes 524288 | tf_op jit(solution)/shard_map/all_to_all | solution.py:1005
  56.6 0.7 copy-start.12
  57.3 34.4 %copy-start.4 = (bf16[128,128]{1,0:T(8,128)(2,1)S(1)}, bf16[128,128]{1,0:T(8,128)(2,1)}, u32[]{:S(2)}) copy-start(bf16[128,128]{1,0:T(8,128)(2,1)} %constant.38.clone.spread_table.second) | copy-start | bytes 98308
  57.3 34.4 %copy-start.9 = (bf16[1024,128]{1,0:T(8,128)(2,1)S(1)}, bf16[1024,128]{1,0:T(8,128)(2,1)}, u32[]{:S(2)}) copy-start(bf16[1024,128]{1,0:T(8,128)(2,1)} %constant.39.clone.sum_table) | copy-start | bytes 786436
  79.1 12.6 %all-to-all-start.2 = ((bf16[4,128,256]{2,1,0:T(8,128)(2,1)}), bf16[4,128,256]{2,1,0:T(8,128)(2,1)S(1)}, u32[]{:S(2)}, u32[]{:S(2)}) async-start(bf16[4,128,256]{2,1,0:T(8,128)(2,1)} %get-tuple-element.44), calls=%async_computation.2 | async-start | bytes 524288 | tf_op jit(solution)/shard_map/all_to_all | solution.py:1005
  84.2 28.8 %collective-permute-start.4 = (bf16[32,1,128,128]{3,2,1,0:T(8,128)(2,1)}, bf16[32,1,128,128]{3,2,1,0:T(8,128)(2,1)S(1)}, u32[]{:S(2)}, u32[]{:S(2)}) collective-permute-start(bf16[32,1,128,128]{3,2,1,0:T(8,128)(2,1)} %get-tuple-element.51), channel_id=1, source_target_pairs={{0,1},{1,2},{2,3},{4,5},{5,6},{6,7},{8,9},{9,10},{10,11},{12,13},{... | collective-permute-start | bytes 3145736 | tf_op jit(solution)/shard_map/ppermute | solution.py:1001
  88.2 25.4 %collective-permute-start.5 = (bf16[32,1,128,128]{3,2,1,0:T(8,128)(2,1)}, bf16[32,1,128,128]{3,2,1,0:T(8,128)(2,1)}, u32[]{:S(2)}, u32[]{:S(2)}) collective-permute-start(bf16[32,1,128,128]{3,2,1,0:T(8,128)(2,1)} %get-tuple-element.52), channel_id=1, source_target_pairs={{1,0},{2,1},{3,2},{5,4},{6,5},{7,6},{9,8},{10,9},{11,10},{13,12},{... | collective-permute-start | bytes 3145736 | tf_op jit(solution)/shard_map/ppermute | solution.py:1001
  97.8 19.7 %copy-start.3 = (bf16[128,512]{1,0:T(8,128)(2,1)S(1)}, bf16[128,512]{1,0:T(8,128)(2,1)}, u32[]{:S(2)}) copy-start(bf16[128,512]{1,0:T(8,128)(2,1)} %constant.40.clone.first) | copy-start | bytes 393220
  97.8 15.3 %all-to-all-start.3 = ((bf16[4,768,128]{2,1,0:T(8,128)(2,1)}), bf16[4,768,128]{2,1,0:T(8,128)(2,1)S(1)}, u32[]{:S(2)}, u32[]{:S(2)}) async-start(bf16[4,768,128]{2,1,0:T(8,128)(2,1)} %get-tuple-element.49), calls=%async_computation.3 | async-start | bytes 1572864 | tf_op jit(solution)/shard_map/all_to_all | solution.py:1035
  101.4 24.7 %copy-start = (bf16[1024,256]{1,0:T(8,128)(2,1)S(1)}, bf16[1024,256]{1,0:T(8,128)(2,1)}, u32[]{:S(2)}) copy-start(bf16[1024,256]{1,0:T(8,128)(2,1)} %constant.35.clone.ix_table) | copy-start | bytes 1572868
  101.4 24.7 %copy-start.2 = (f32[27,32]{1,0:T(8,128)S(1)}, f32[27,32]{1,0:T(8,128)}, u32[]{:S(2)}) copy-start(f32[27,32]{1,0:T(8,128)} %taps.7) | copy-start | bytes 10372
  113.6 12.6 %all-to-all-start.4 = ((bf16[4,128,256]{2,1,0:T(8,128)(2,1)}), bf16[4,128,256]{2,1,0:T(8,128)(2,1)S(1)}, u32[]{:S(2)}, u32[]{:S(2)}) async-start(bf16[4,128,256]{2,1,0:T(8,128)(2,1)} %get-tuple-element.56), calls=%async_computation.4 | async-start | bytes 524288 | tf_op jit(solution)/shard_map/all_to_all | solution.py:1005
  126.1 1.2 copy-start.6
